TPU v7x, 32 devices: a whole 2x2x4 slice. The times are simulated.
32 devices in a mesh: occ: 8 (over z, y), ao: 4 (over x, core).
Axes of the slice: x: 2, y: 2, z: 4, core: 2. Of those that a mesh axis runs over, the one named last changes fastest.
Arguments:
- amplitudes: bfloat16 [256, 256, 256], P('occ', None, 'ao'), may hold values from -6 to 6
- orbitals: bfloat16 [512, 256], replicated, may hold values from -0.375 to 0.375
- tiles: bfloat16 [512, 512, 512], P('occ', None, 'ao'), may hold values from -0.125 to 0.125
- tile_count: int32 [8], replicated, may hold values from 1 to 64, 256 in all
- tile_row: int32 [512], replicated, may hold values from 0 to 63
- tile_src: int32 [512, 1], replicated, may hold values from 0 to 7; in each aligned block of 64 rows (0 to 63, 64 to 127, ...) at most 8 rows name the same one
- tile_sub: int32 [512], replicated, may hold values from 0 to 63
Outputs:
- sigma_out: bfloat16 [256, 256, 256], P('occ', None, 'ao')
Inputs may be any that keep to these rules, and one draw needn't show every extreme that they name: `tile_count`: each occ index owns between 1 and 64 live slots, the first ones of its 64 slots; some index owns exactly 64. `tile_src`: among the 64 slots of one owner no source index is named more than 8 times, and some owner names one source exactly 8 times.
All inputs are finite; a program needn't handle non-finite values.
Results may differ from a plain program's by a relative error of at most 0.024.
Values may be sent and summed in bfloat16 or wider, within the bound.
No kernel may reach another device: no remote copies, remote signals or barrier semaphores. Data moves between devices by JAX's collectives and lax.ppermute only.
A program may use at most 128 MiB of HBM per device.

v0:
```python
import jax
import jax.numpy as jnp
from jax import lax
from jax.sharding import PartitionSpec as P


def shards(amplitudes, orbitals, tiles, tile_count, tile_row, tile_src, tile_sub):
    node_count = lax.axis_size("occ")
    own_index = lax.axis_index("occ")
    quarter = lax.axis_index("ao")
    local_occ, vir_count, vir_part = amplitudes.shape
    ao_count = orbitals.shape[0]
    ao_part = ao_count // lax.axis_size("ao")
    slot_count = tiles.shape[0]
    blocks = ao_count // node_count
    nu_rows = lax.dynamic_slice_in_dim(orbitals, quarter * ao_part, ao_part, 0)
    vir_cols = lax.dynamic_slice_in_dim(orbitals, quarter * vir_part, vir_part, 1)
    partial_x = jnp.einsum("icd,nd->icn", amplitudes, vir_cols, preferred_element_type=jnp.float32)
    half_pairs = lax.psum_scatter(
        partial_x.astype(jnp.bfloat16), "ao", scatter_dimension=2, tiled=True
    )
    pair_rows = jnp.einsum(
        "mc,icn->imn", orbitals, half_pairs, preferred_element_type=jnp.float32
    ).astype(jnp.bfloat16)
    sources = tile_src[:, 0].reshape(node_count, slot_count)
    sub_blocks = tile_sub.reshape(node_count, slot_count)
    wanted = (sources * blocks + sub_blocks).reshape(-1)
    picked = jnp.take(pair_rows, wanted, axis=1).reshape(local_occ, node_count, slot_count, ao_part)
    arrived = lax.all_to_all(picked, "occ", split_axis=1, concat_axis=0, tiled=True)
    fetched = arrived.reshape(local_occ * node_count, slot_count, ao_part)
    live_mask = jnp.arange(slot_count, dtype=jnp.int32) < tile_count[own_index]
    own_row = lax.dynamic_index_in_dim(
        tile_row.reshape(node_count, slot_count), own_index, 0, keepdims=False
    )
    onehot = (
        (own_row[:, None] == jnp.arange(blocks, dtype=jnp.int32)[None, :]) & live_mask[:, None]
    ).astype(jnp.bfloat16)
    products = jnp.einsum("itn,tsn->tis", fetched, tiles, preferred_element_type=jnp.float32)
    upper_part = products.astype(jnp.bfloat16)
    lower_part = (products - upper_part.astype(jnp.float32)).astype(jnp.bfloat16)
    partial_z = jnp.einsum("tr,tis->irs", onehot, upper_part, preferred_element_type=jnp.float32)
    partial_z = partial_z + jnp.einsum(
        "tr,tis->irs", onehot, lower_part, preferred_element_type=jnp.float32
    )
    ladder = lax.psum_scatter(partial_z.astype(jnp.bfloat16), "ao", scatter_dimension=2, tiled=True)
    back_rows = lax.all_to_all(ladder, "occ", split_axis=0, concat_axis=1, tiled=True)
    mixed = jnp.einsum(
        "la,ils->ias", orbitals, back_rows, preferred_element_type=jnp.float32
    ).astype(jnp.bfloat16)
    partial_s = jnp.einsum("ias,sb->iab", mixed, nu_rows, preferred_element_type=jnp.float32)
    return lax.psum_scatter(partial_s.astype(jnp.bfloat16), "ao", scatter_dimension=2, tiled=True)


def solution(mesh):
    placed = (P("occ", None, "ao"), P(), P("occ", None, "ao"), P(), P(), P(), P())
    return jax.shard_map(
        shards, mesh=mesh, in_specs=placed, out_specs=P("occ", None, "ao"), check_vma=False
    )
```

profile of v0, /device:TPU:0, one launch (start us, length us, event | category | flops | bytes accessed | tf_op | source)
XLA Modules:
  0.0 685.1 jit_solution(1520868862342144110)
XLA Ops:
  6.5 0.0 copy-start
  6.5 0.0 reduce-scatter.6.cloned.1.call-start
  6.5 1.2 copy-done
  7.8 6.5 convert_bitcast_fusion
  14.3 0.0 copy-start.4
  14.3 0.0 copy-start.5
  14.3 0.0 copy-start.2
  14.3 0.0 reduce-scatter.6.cloned.1.call-update
  14.3 0.7 copy-done.4
  15.0 0.0 copy-done.5
  15.0 0.1 broadcast_in_dim.17
  15.1 73.8 %reduce-scatter.6.cloned.1.call-done = bf16[32,256,128]{1,2,0:T(8,128)(2,1)} async-done(((bf16[32,256,512]{1,2,0:T(8,128)(2,1)}), bf16[32,256,128]{1,2,0:T(8,128)(2,1)}) %reduce-scatter.6.cloned.1.call-update) | async-done | bytes 2097168 | tf_op jit(solution)/shard_map/reduce_scatter | solution.py:19
  88.9 0.0 copy-done.2
  88.9 4.8 convert_bitcast_fusion.1
  93.7 7.9 %copy.30 = bf16[32,512,128]{2,0,1:T(8,128)(2,1)} copy(bf16[32,512,128]{1,2,0:T(8,128)(2,1)} %convert_bitcast_fusion.1) | data formatting | bytes 8388608 | tf_op jit(solution)/shard_map/convert_element_type | solution.py:24
  101.6 5.3 gather_fusion
  107.0 3.8 copy.31
  110.8 0.5 broadcast_select_fusion
  111.3 2.9 copy.32
  114.2 0.0 copy-start.3
  114.2 0.0 copy-start.6
  114.2 5.6 all-to-all-start
  119.8 0.2 reduce-scatter.10.cloned.1.call-start
  120.1 0.0 copy-done.3
  120.1 0.1 reshape.28
  120.1 0.0 copy-done.6
  120.1 0.6 dynamic_slice.15
  120.7 0.6 iota_compare_fusion.1
  121.4 91.7 %all-to-all-done = bf16[32,8,64,128]{3,2,0,1:T(8,128)(2,1)} async-done(((bf16[32,8,64,128]{3,2,0,1:T(8,128)(2,1)}), bf16[32,8,64,128]{3,2,0,1:T(8,128)(2,1)}, u32[]{:S(2)}, u32[]{:S(2)}) %all-to-all-start) | async-done | bytes 4194336 | tf_op jit(solution)/shard_map/all_to_all | solution.py:29
  213.1 6.8 copy.33
  219.9 19.1 %subtract_convert_fusion = (bf16[64,256,512]{2,1,0:T(8,128)(2,1)}, bf16[64,256,512]{2,1,0:T(8,128)(2,1)}) fusion(bf16[256,64,128]{2,0,1:T(8,128)(2,1)} %bitcast.50, bf16[64,512,128]{2,1,0:T(8,128)(2,1)} %param.9), kind=kOutput, calls=%fused_computation.2 | convolution fusion | flops 2181038080 | bytes 46137344 | tf_op jit(solution)/shard_map/itn,tsn->tis/dot_general | solution.py:38
  239.1 25.5 %fusion.1 = f32[256,512,64]{1,2,0:T(8,128)} fusion(bf16[64,256,512]{2,1,0:T(8,128)(2,1)} %get-tuple-element.5, s32[64]{0:T(128)S(1)} %fusion.28, pred[64]{0:T(512)(128)(4,1)S(1)} %iota_compare_fusion.1), kind=kOutput, calls=%fused_computation.4 | convolution fusion | flops 1073750016 | bytes 50331968 | tf_op jit(solution)/shard_map/tr,tis->irs/dot_general | solution.py:42
  264.6 27.4 %fusion = bf16[256,64,512]{2,1,0:T(8,128)(2,1)} fusion(f32[256,512,64]{1,2,0:T(8,128)} %fusion.1, bf16[64,256,512]{2,1,0:T(8,128)(2,1)} %get-tuple-element.6, s32[64]{0:T(128)S(1)} %fusion.28, pred[64]{0:T(512)(128)(4,1)S(1)} %iota_compare_fusion.1), kind=kOutput, calls=%fused_computation.3 | convolution fusion | flops 1090527232 | bytes 67109184 | tf_op jit(solution)/shard_map/tr,tis->irs/dot_general | solution.py:41
  292.0 46.0 %copy.42 = bf16[256,64,512]{1,0,2:T(8,128)(2,1)} copy(bf16[256,64,512]{2,1,0:T(8,128)(2,1)} %fusion) | data formatting | bytes 33554432
  338.0 38.3 %reshape.42 = bf16[512,16384]{1,0:T(8,128)(2,1)} reshape(bf16[512,256,64]{2,1,0:T(8,128)(2,1)} %bitcast.48) | data formatting | bytes 33554432
  376.3 0.0 reduce-scatter.10.cloned.1.call-update
  376.3 124.4 %reduce-scatter.10.cloned.1.call-done = bf16[128,16384]{1,0:T(8,128)(2,1)} async-done(((bf16[512,16384]{1,0:T(8,128)(2,1)}), bf16[128,16384]{1,0:T(8,128)(2,1)}) %reduce-scatter.10.cloned.1.call-update) | async-done | bytes 4194320
  500.7 11.4 %reshape.43 = bf16[128,256,64]{2,1,0:T(8,128)(2,1)} reshape(bf16[128,16384]{1,0:T(8,128)(2,1)} %reduce-scatter.10.cloned.1.call-done) | data formatting | bytes 8388608
  512.1 11.5 %copy.43 = bf16[256,64,128]{2,1,0:T(8,128)(2,1)} copy(bf16[256,64,128]{1,0,2:T(8,128)(2,1)} %bitcast.49) | data formatting | bytes 8388608
  523.6 5.5 all-to-all-start.1
  529.2 0.3 reduce-scatter.8.cloned.1.call-start
  529.5 93.0 %all-to-all-done.1 = bf16[256,64,128]{2,1,0:T(8,128)(2,1)} async-done(((bf16[256,64,128]{2,1,0:T(8,128)(2,1)}), bf16[256,64,128]{2,1,0:T(8,128)(2,1)}, u32[]{:S(2)}, u32[]{:S(2)}) %all-to-all-start.1) | async-done | bytes 4194336 | tf_op jit(solution)/shard_map/all_to_all | solution.py:46
  622.4 5.6 copy.36
  628.0 0.0 copy-start.1
  628.0 7.8 %convolution_convert_fusion = bf16[32,256,256]{1,2,0:T(8,128)(2,1)} fusion(bf16[32,512,128]{2,1,0:T(8,128)(2,1)} %bitcast.53, bf16[512,256]{1,0:T(8,128)(2,1)S(1)} %copy-done.2, s32[]{:T(128)S(6)} %select_n.25), kind=kOutput, calls=%fused_computation.11 | convolution fusion | flops 1613758464 | bytes 8716292 | tf_op jit(solution)/shard_map/ias,sb->iab/dot_general | solution.py:50
  635.8 0.0 reduce-scatter.8.cloned.1.call-update
  635.8 42.8 %reduce-scatter.8.cloned.1.call-done = bf16[32,256,64]{1,2,0:T(8,128)(2,1)} async-done(((bf16[32,256,256]{1,2,0:T(8,128)(2,1)}), bf16[32,256,64]{1,2,0:T(8,128)(2,1)}) %reduce-scatter.8.cloned.1.call-update) | async-done | bytes 1048592 | tf_op jit(solution)/shard_map/reduce_scatter | solution.py:51
  678.6 0.0 copy-done.1
  (4 shorter events, 0.0 us)
Async XLA Ops:
  6.5 1.2 copy-start
  6.5 82.3 %reduce-scatter.6.cloned.1.call-start = ((), (), s32[]{:S(2)}) async-start(), calls=%async_computation.5 | async-start | bytes 10485760 | tf_op jit(solution)/shard_map/reduce_scatter | solution.py:19
  14.3 0.7 copy-start.4
  14.3 0.7 copy-start.5
  14.3 74.6 %copy-start.2 = (bf16[512,256]{1,0:T(8,128)(2,1)S(1)}, bf16[512,256]{1,0:T(8,128)(2,1)}, u32[]{:S(2)}) copy-start(bf16[512,256]{1,0:T(8,128)(2,1)} %param.8) | copy-start | bytes 786436
  114.2 5.9 copy-start.3
  114.2 6.0 copy-start.6
  114.2 98.9 %all-to-all-start = ((bf16[32,8,64,128]{3,2,0,1:T(8,128)(2,1)}), bf16[32,8,64,128]{3,2,0,1:T(8,128)(2,1)}, u32[]{:S(2)}, u32[]{:S(2)}) async-start(bf16[32,8,64,128]{3,2,0,1:T(8,128)(2,1)} %copy.32), calls=%async_computation.1 | async-start | bytes 8388608 | tf_op jit(solution)/shard_map/all_to_all | solution.py:29
  119.8 380.9 %reduce-scatter.10.cloned.1.call-start = ((), (), s32[]{:S(2)}) async-start(), calls=%async_computation.7 | async-start | bytes 20971520
  523.6 98.8 %all-to-all-start.1 = ((bf16[256,64,128]{2,1,0:T(8,128)(2,1)}), bf16[256,64,128]{2,1,0:T(8,128)(2,1)}, u32[]{:S(2)}, u32[]{:S(2)}) async-start(bf16[256,64,128]{2,1,0:T(8,128)(2,1)} %copy.43), calls=%async_computation.2 | async-start | bytes 8388608 | tf_op jit(solution)/shard_map/all_to_all | solution.py:46
  529.2 149.4 %reduce-scatter.8.cloned.1.call-start = ((), (), s32[]{:S(2)}) async-start(), calls=%async_computation.6 | async-start | bytes 5242880 | tf_op jit(solution)/shard_map/reduce_scatter | solution.py:51
  628.0 50.6 %copy-start.1 = (bf16[32,256,64]{1,2,0:T(8,128)(2,1)S(1)}, bf16[32,256,64]{1,2,0:T(8,128)(2,1)}, u32[]{:S(2)}) copy-start(bf16[32,256,64]{1,2,0:T(8,128)(2,1)} %param.7) | copy-start | bytes 3145732
Sparse Core Ops, SparseCore 0:
  14.4 74.3 reduce-scatter.5
  376.5 124.2 reduce-scatter.9
  636.0 42.5 reduce-scatter.7
where the time goes:
time: 688 us; the launch traced here: 685 us
  waiting for transfers between devices  426 us (62%)
  local copies, waits for them, and re-layouts  142 us (21%)
  matrix products  91.2 us (13%)
  between operations  13.2 us (2%)
  starting transfers between devices  11.7 us (2%)
    unnamed x4, waiting for transfers between devices  124 us
    unnamed x18, local copies, waits for them, and re-layouts  109 us
    all_to_all x1, waiting for transfers between devices, shards(): lax.all_to_all(ladder, 'occ', split_axis=0, concat_axis=1, tiled=True)  93 us
    all_to_all x1, waiting for transfers between devices, shards(): lax.all_to_all(picked, 'occ', split_axis=1, concat_axis=0, tiled=True)  91.7 us
    reduce_scatter x1, waiting for transfers between devices, shards(): lax.psum_scatter(partial_x.astype(jnp.bfloat16), 'ao', scatter_dimension=...  73.8 us
    reduce_scatter x1, waiting for transfers between devices, shards(): lax.psum_scatter(partial_s.astype(jnp.bfloat16), 'ao', scatter_dimension=...  42.8 us
    dot_general x1, matrix products, shards(): jnp.einsum('tr,tis->irs', onehot, upper_part, preferred_element_type=jnp....  27.4 us
    dot_general x1, matrix products, shards(): jnp.einsum('tr,tis->irs', onehot, lower_part, preferred_element_type=jnp....  25.5 us
  transfers between devices with their start and end apart: 5, of which 5 were waited for; matrix products, arithmetic and copies ran while one was open for 0% of the time, Pallas kernels for 0%

commit v1 on v0

v1 whole, which is shorter than its diff:
```python
import jax
import jax.numpy as jnp
from jax import lax
from jax.sharding import PartitionSpec as P

CHUNKS = 4


def shards(amplitudes, orbitals, tiles, tile_count, tile_row, tile_src, tile_sub):
    nodes = lax.axis_size("occ")
    own = lax.axis_index("occ")
    parts = lax.axis_size("ao")
    part = lax.axis_index("ao")
    core, side = part % 2, part // 2
    near = [(q, q ^ 1) for q in range(parts)]
    far = [(q, (q + 2) % parts) for q in range(parts)]
    local_occ, vir, vir_part = amplitudes.shape
    ao_count = orbitals.shape[0]
    nu_part = tiles.shape[2]
    slots = tiles.shape[0]
    half = slots // 2
    step = half // CHUNKS
    blocks = ao_count // nodes
    f32, bf16 = jnp.float32, jnp.bfloat16
    pick = lax.dynamic_slice_in_dim

    def join(mine, other, axis):
        return jnp.where(
            core == 0,
            jnp.concatenate([mine, other], axis),
            jnp.concatenate([other, mine], axis),
        )

    def mine_of(table):
        return pick(table.reshape(nodes, slots), core * half, half, 1)

    source = mine_of(tile_src[:, 0]) * blocks + mine_of(tile_sub)
    target = jnp.arange(nodes, dtype=jnp.int32)[:, None] * blocks + mine_of(tile_row)
    place = core * half + jnp.arange(half, dtype=jnp.int32)
    live = place[None, :] < tile_count[:, None]
    source_rows = jnp.take(orbitals, source, axis=0)
    target_rows = jnp.where(live[:, :, None], jnp.take(orbitals, target, axis=0), 0)

    paired = join(amplitudes, lax.ppermute(amplitudes, "ao", near), 2)
    nu_rows = pick(orbitals, side * 2 * nu_part, 2 * nu_part, 0)
    side_vir = 2 * vir_part
    far_side = (side + 1) % (parts // 2)

    dressed = []
    for n in range(CHUNKS):
        first = pick(tiles, core * half + n * step, step, 0)
        second = pick(tiles, (1 - core) * half + n * step, step, 0)
        keep = jnp.einsum("sb,tsn->tbn", orbitals, first, preferred_element_type=f32).astype(bf16)
        give = jnp.einsum("sb,tsn->tbn", orbitals, second, preferred_element_type=f32).astype(bf16)
        whole = join(keep, lax.ppermute(give, "ao", near), 2)
        both = jnp.einsum("tbn,nd->tbd", whole, nu_rows, preferred_element_type=f32)
        here = pick(both, side * side_vir, side_vir, 2)
        there = pick(both, far_side * side_vir, side_vir, 2).astype(bf16)
        dressed.append((here + lax.ppermute(there, "ao", far).astype(f32)).astype(bf16))

    total = jnp.zeros((local_occ, vir, side_vir), f32)
    arrived = []
    for n in range(CHUNKS):
        rows = source_rows[:, n * step:(n + 1) * step]
        sent = jnp.einsum("otc,icd->otid", rows, paired, preferred_element_type=f32).astype(bf16)
        arrived.append(lax.all_to_all(sent, "occ", split_axis=0, concat_axis=0, tiled=True))
    for n in range(CHUNKS):
        both = jnp.einsum("otid,tbd->otib", arrived[n], dressed[n], preferred_element_type=f32)
        here = pick(both, side * side_vir, side_vir, 3)
        there = pick(both, far_side * side_vir, side_vir, 3).astype(bf16)
        summed = (here + lax.ppermute(there, "ao", far).astype(f32)).astype(bf16)
        back = lax.all_to_all(summed, "occ", split_axis=0, concat_axis=0, tiled=True)
        rows = target_rows[:, n * step:(n + 1) * step]
        total = total + jnp.einsum("ota,otib->iab", rows, back, preferred_element_type=f32)
    low, high = total[:, :, :vir_part], total[:, :, vir_part:]
    keep = jnp.where(core == 0, low, high)
    give = jnp.where(core == 0, high, low).astype(bf16)
    return (keep + lax.ppermute(give, "ao", near).astype(f32)).astype(bf16)


def solution(mesh):
    placed = (P("occ", None, "ao"), P(), P("occ", None, "ao"), P(), P(), P(), P())
    return jax.shard_map(
        shards, mesh=mesh, in_specs=placed, out_specs=P("occ", None, "ao"), check_vma=False
    )
```

time: 688 us -> 189 us (0.27)
  waiting for transfers between devices: 426 us -> 48.7 us
  local copies, waits for them, and re-layouts: 142 us -> 20.7 us
  starting transfers between devices: 11.7 us -> 55.3 us
  matrix products: 91.2 us -> 57.3 us
  between operations: 13.2 us -> 0.36 us
    all_to_all x2 -> x8, waiting for transfers between devices: 185 us -> 11.6 us  [the longest x4 9.77 us: shards(): lax.all_to_all(sent, 'occ', split_axis=0, concat_axis=0, tiled=True)]
    unnamed x4 -> x0, waiting for transfers between devices: 124 us -> none
    reduce_scatter x2 -> x0, waiting for transfers between devices: 117 us -> none  [the longest x1 73.8 us: shards(): lax.psum_scatter(partial_x.astype(jnp.bfloat16), 'ao', scatter_dimension=...]
    unnamed x18 -> x43, local copies, waits for them, and re-layouts: 109 us -> 6.02 us
    ppermute x0 -> x14, waiting for transfers between devices: none -> 37.1 us  [the longest x4 26.8 us: shards(): summed = (here + lax.ppermute(there, 'ao', far).astype(f32)).astype(bf16)]
    dot_general x6 -> x24, matrix products: 91.2 us -> 57.3 us  [the longest x4 15.1 us: shards(): jnp.einsum('ota,otib->iab', rows, back, preferred_element_type=f32)]
    all_to_all x2 -> x8, starting transfers between devices: 11.2 us -> 42 us  [the longest x4 23.1 us: shards(): lax.all_to_all(summed, 'occ', split_axis=0, concat_axis=0, tiled=True)]
    ppermute x0 -> x14, starting transfers between devices: none -> 13.3 us  [the longest x4 6.88 us: shards(): summed = (here + lax.ppermute(there, 'ao', far).astype(f32)).astype(bf16)]
  transfers between devices with their start and end apart: 5 -> 22, of which waited for: 5 -> 11; matrix products, arithmetic and copies ran while one was open for 0% -> 38% of each run, Pallas kernels for 0% -> 0%
where the time goes in v1:
time: 189 us; the launch traced here: 188 us
  matrix products  57.3 us (30%)
  starting transfers between devices  55.3 us (29%)
  waiting for transfers between devices  48.7 us (26%)
  local copies, waits for them, and re-layouts  20.7 us (11%)
  other arithmetic  5.43 us (3%)
    ppermute x4, waiting for transfers between devices, shards(): summed = (here + lax.ppermute(there, 'ao', far).astype(f32)).astype(bf16)  26.8 us
    all_to_all x4, starting transfers between devices, shards(): lax.all_to_all(summed, 'occ', split_axis=0, concat_axis=0, tiled=True)  23.1 us
    all_to_all x4, starting transfers between devices, shards(): lax.all_to_all(sent, 'occ', split_axis=0, concat_axis=0, tiled=True)  18.9 us
    dot_general x4, matrix products, shards(): jnp.einsum('ota,otib->iab', rows, back, preferred_element_type=f32)  15.1 us
    dot_general x4, matrix products, shards(): jnp.einsum('otc,icd->otid', rows, paired, preferred_element_type=f32)  10.1 us
    all_to_all x4, waiting for transfers between devices, shards(): lax.all_to_all(sent, 'occ', split_axis=0, concat_axis=0, tiled=True)  9.77 us
    dot_general x4, matrix products, shards(): jnp.einsum('sb,tsn->tbn', orbitals, first, preferred_element_type=f32)  9.25 us
    dot_general x4, matrix products, shards(): jnp.einsum('sb,tsn->tbn', orbitals, second, preferred_element_type=f32)  8.43 us
  transfers between devices with their start and end apart: 22, of which 11 were waited for; matrix products, arithmetic and copies ran while one was open for 38% of the time, Pallas kernels for 0%

profile of v1, /device:TPU:0, one launch (start us, length us, event | category | flops | bytes accessed | tf_op | source)
XLA Modules:
  0.0 187.7 jit_solution(3770032345305196984)
XLA Ops:
  1.0 1.7 fusion.3
  3.2 2.5 %fusion.9 = bf16[8,256,128]{1,2,0:T(8,128)(2,1)} fusion(bf16[64,512,128]{2,1,0:T(8,128)(2,1)} %param.11, s32[]{:T(128)S(6)} %select_n.137, bf16[512,256]{1,0:T(8,128)(2,1)S(1)} %copy-done), kind=kOutput, calls=%fused_computation.25 | convolution fusion | flops 268697600 | bytes 1835012 | tf_op jit(solution)/shard_map/sb,tsn->tbn/dot_general | solution.py:54
  8.7 2.3 %fusion.96 = bf16[8,8,32,128]{3,1,2,0:T(8,128)(2,1)S(1)} fusion(bf16[8,32,256]{2,1,0:T(8,128)(2,1)S(1)} %broadcast_select_fusion, bf16[32,256,64]{1,2,0:T(8,128)(2,1)} %collective-permute-done.2, bf16[32,256,64]{1,2,0:T(8,128)(2,1)S(1)} %copy-done.18, pred[]{:T(512)S(6)} %eq.5), kind=kOutput, calls=%fused_computation.142 | convolution fusion | flops 143654912 | bytes 2654209 | tf_op jit(solution)/shard_map/otc,icd->otid/dot_general | solution.py:65
  11.9 7.2 %all-to-all-start = ((bf16[8,8,32,128]{3,2,1,0:T(8,128)(2,1)}), bf16[8,8,32,128]{3,2,1,0:T(8,128)(2,1)S(1)}, u32[]{:S(2)}, u32[]{:S(2)}) async-start(bf16[8,8,32,128]{3,2,1,0:T(8,128)(2,1)} %copy.99), calls=%async_computation | async-start | bytes 1048576 | tf_op jit(solution)/shard_map/all_to_all | solution.py:66
  19.1 1.7 fusion.5
  20.9 2.5 %fusion.7 = bf16[8,256,128]{1,2,0:T(8,128)(2,1)} fusion(bf16[64,512,128]{2,1,0:T(8,128)(2,1)} %param.11, s32[]{:T(128)S(6)} %select_n.134, bf16[512,256]{1,0:T(8,128)(2,1)S(1)} %copy-done), kind=kOutput, calls=%fused_computation.23 | convolution fusion | flops 268697600 | bytes 1835012 | tf_op jit(solution)/shard_map/sb,tsn->tbn/dot_general | solution.py:54
  23.9 1.7 fusion.2
  25.6 3.2 %fusion.93 = bf16[8,8,32,128]{3,1,2,0:T(8,128)(2,1)S(1)} fusion(bf16[8,32,256]{2,1,0:T(8,128)(2,1)S(1)} %broadcast_select_fusion, bf16[32,256,64]{1,2,0:T(8,128)(2,1)} %collective-permute-done.2, bf16[32,256,64]{1,2,0:T(8,128)(2,1)} %param.9, pred[]{:T(512)S(6)} %eq.5), kind=kOutput, calls=%fused_computation.133 | convolution fusion | flops 143654912 | bytes 2654209 | tf_op jit(solution)/shard_map/otc,icd->otid/dot_general | solution.py:65
  29.8 4.1 %all-to-all-done = bf16[8,8,32,128]{3,2,1,0:T(8,128)(2,1)S(1)} async-done(((bf16[8,8,32,128]{3,2,1,0:T(8,128)(2,1)}), bf16[8,8,32,128]{3,2,1,0:T(8,128)(2,1)S(1)}, u32[]{:S(2)}, u32[]{:S(2)}) %all-to-all-start) | async-done | bytes 524320 | tf_op jit(solution)/shard_map/all_to_all | solution.py:66
  33.9 3.6 %all-to-all-start.6 = ((bf16[8,8,32,128]{3,2,1,0:T(8,128)(2,1)}), bf16[8,8,32,128]{3,2,1,0:T(8,128)(2,1)S(1)}, u32[]{:S(2)}, u32[]{:S(2)}) async-start(bf16[8,8,32,128]{3,2,1,0:T(8,128)(2,1)} %copy.96), calls=%async_computation.6 | async-start | bytes 1048576 | tf_op jit(solution)/shard_map/all_to_all | solution.py:66
  37.5 2.5 %fusion.8 = bf16[8,256,128]{1,2,0:T(8,128)(2,1)} fusion(bf16[64,512,128]{2,1,0:T(8,128)(2,1)} %param.11, s32[]{:T(128)S(6)} %select_n.136, bf16[512,256]{1,0:T(8,128)(2,1)S(1)} %copy-done), kind=kOutput, calls=%fused_computation.24 | convolution fusion | flops 268697600 | bytes 1835012 | tf_op jit(solution)/shard_map/sb,tsn->tbn/dot_general | solution.py:53
  40.0 2.5 %fusion.4 = bf16[8,256,128]{1,2,0:T(8,128)(2,1)} fusion(bf16[64,512,128]{2,1,0:T(8,128)(2,1)} %param.11, s32[]{:T(128)S(6)} %select_n.130, bf16[512,256]{1,0:T(8,128)(2,1)S(1)} %copy-done), kind=kOutput, calls=%fused_computation.20 | convolution fusion | flops 268697600 | bytes 1835012 | tf_op jit(solution)/shard_map/sb,tsn->tbn/dot_general | solution.py:53
  42.5 1.8 fusion.10
  45.7 1.6 collective-permute-start.1
  47.3 2.3 %fusion.95 = bf16[8,8,32,128]{3,1,2,0:T(8,128)(2,1)S(1)} fusion(bf16[8,32,256]{2,1,0:T(8,128)(2,1)S(1)} %broadcast_select_fusion, bf16[32,256,64]{1,2,0:T(8,128)(2,1)} %collective-permute-done.2, bf16[32,256,64]{1,2,0:T(8,128)(2,1)S(1)} %copy-done.19, pred[]{:T(512)S(6)} %eq.5), kind=kOutput, calls=%fused_computation.139 | convolution fusion | flops 143654912 | bytes 2654209 | tf_op jit(solution)/shard_map/otc,icd->otid/dot_general | solution.py:65
  50.6 1.6 all-to-all-done.6
  52.2 4.4 %all-to-all-start.2 = ((bf16[8,8,32,128]{3,2,1,0:T(8,128)(2,1)}), bf16[8,8,32,128]{3,2,1,0:T(8,128)(2,1)}, u32[]{:S(2)}, u32[]{:S(2)}) async-start(bf16[8,8,32,128]{3,2,1,0:T(8,128)(2,1)} %copy.98), calls=%async_computation.2 | async-start | bytes 1048576 | tf_op jit(solution)/shard_map/all_to_all | solution.py:66
  56.6 1.8 fusion.16
  61.9 2.3 %fusion.94 = bf16[8,8,32,128]{3,1,2,0:T(8,128)(2,1)S(1)} fusion(bf16[8,32,256]{2,1,0:T(8,128)(2,1)S(1)} %broadcast_select_fusion, bf16[32,256,64]{1,2,0:T(8,128)(2,1)} %collective-permute-done.2, bf16[32,256,64]{1,2,0:T(8,128)(2,1)S(1)} %copy-done.20, pred[]{:T(512)S(6)} %eq.5), kind=kOutput, calls=%fused_computation.136 | convolution fusion | flops 143654912 | bytes 2654209 | tf_op jit(solution)/shard_map/otc,icd->otid/dot_general | solution.py:65
  66.6 4.0 %all-to-all-done.2 = bf16[8,8,32,128]{3,2,1,0:T(8,128)(2,1)} async-done(((bf16[8,8,32,128]{3,2,1,0:T(8,128)(2,1)}), bf16[8,8,32,128]{3,2,1,0:T(8,128)(2,1)}, u32[]{:S(2)}, u32[]{:S(2)}) %all-to-all-start.2) | async-done | bytes 524320 | tf_op jit(solution)/shard_map/all_to_all | solution.py:66
  70.7 3.6 %all-to-all-start.4 = ((bf16[8,8,32,128]{3,2,1,0:T(8,128)(2,1)}), bf16[8,8,32,128]{3,2,1,0:T(8,128)(2,1)S(1)}, u32[]{:S(2)}, u32[]{:S(2)}) async-start(bf16[8,8,32,128]{3,2,1,0:T(8,128)(2,1)} %copy.97), calls=%async_computation.4 | async-start | bytes 1048576 | tf_op jit(solution)/shard_map/all_to_all | solution.py:66
  75.9 2.5 %fusion.6 = bf16[8,256,128]{1,2,0:T(8,128)(2,1)} fusion(bf16[64,512,128]{2,1,0:T(8,128)(2,1)} %param.11, s32[]{:T(128)S(6)} %select_n.133, bf16[512,256]{1,0:T(8,128)(2,1)S(1)} %copy-done), kind=kOutput, calls=%fused_computation.22 | convolution fusion | flops 268697600 | bytes 1835012 | tf_op jit(solution)/shard_map/sb,tsn->tbn/dot_general | solution.py:53
  78.5 1.8 fusion.55
  80.3 7.3 %collective-permute-done.3 = bf16[8,8,32,128]{3,2,0,1:T(8,128)(2,1)S(1)} collective-permute-done((bf16[8,8,32,128]{3,2,0,1:T(8,128)(2,1)S(1)}, bf16[8,8,32,128]{3,2,0,1:T(8,128)(2,1)S(1)}, u32[]{:S(2)}, u32[]{:S(2)}) %collective-permute-start.3) | collective-permute-done | bytes 524320 | tf_op jit(solution)/shard_map/ppermute | solution.py:71
  89.5 5.7 %all-to-all-start.1 = ((bf16[8,8,32,128]{3,2,1,0:T(8,128)(2,1)}), bf16[8,8,32,128]{3,2,1,0:T(8,128)(2,1)S(1)}, u32[]{:S(2)}, u32[]{:S(2)}) async-start(bf16[8,8,32,128]{3,2,1,0:T(8,128)(2,1)} %copy.28), calls=%async_computation.1 | async-start | bytes 1048576 | tf_op jit(solution)/shard_map/all_to_all | solution.py:72
  95.3 1.8 collective-permute-start.6
  97.2 2.0 %fusion.22 = f32[8,256,256]{2,1,0:T(8,128)S(1)} fusion(bf16[8,256,128]{1,2,0:T(8,128)(2,1)} %collective-permute-done.7, bf16[8,256,128]{1,2,0:T(8,128)(2,1)} %fusion.6, pred[]{:T(512)S(6)} %eq.5, bf16[512,256]{1,0:T(8,128)(2,1)S(1)} %copy-done, s32[]{:T(128)S(6)} %select_n.123), kind=kOutput, calls=%fused_computation.41 | convolution fusion | flops 273154048 | bytes 3276805 | tf_op jit(solution)/shard_map/tbn,nd->tbd/dot_general | solution.py:56
  100.7 1.7 fusion.28
  105.0 5.3 %collective-permute-done.6 = bf16[8,8,32,128]{3,2,0,1:T(8,128)(2,1)S(1)} collective-permute-done((bf16[8,8,32,128]{3,2,0,1:T(8,128)(2,1)S(1)}, bf16[8,8,32,128]{3,2,0,1:T(8,128)(2,1)S(1)}, u32[]{:S(2)}, u32[]{:S(2)}) %collective-permute-start.6) | collective-permute-done | bytes 524320 | tf_op jit(solution)/shard_map/ppermute | solution.py:71
  111.3 6.0 %all-to-all-start.3 = ((bf16[8,8,32,128]{3,2,1,0:T(8,128)(2,1)}), bf16[8,8,32,128]{3,2,1,0:T(8,128)(2,1)}, u32[]{:S(2)}, u32[]{:S(2)}) async-start(bf16[8,8,32,128]{3,2,1,0:T(8,128)(2,1)} %copy.34), calls=%async_computation.3 | async-start | bytes 1048576 | tf_op jit(solution)/shard_map/all_to_all | solution.py:72
  117.3 4.3 %collective-permute-done.8 = bf16[8,256,128]{2,1,0:T(8,128)(2,1)} collective-permute-done((bf16[8,256,128]{2,1,0:T(8,128)(2,1)}, bf16[8,256,128]{2,1,0:T(8,128)(2,1)}, u32[]{:S(2)}, u32[]{:S(2)}) %collective-permute-start.8) | collective-permute-done | bytes 524320 | tf_op jit(solution)/shard_map/ppermute | solution.py:59
  121.6 2.0 %fusion.59 = f32[8,256,8,32]{1,3,2,0:T(8,128)S(1)} fusion(bf16[8,256,128]{2,1,0:T(8,128)(2,1)} %collective-permute-done.8, f32[8,256,256]{2,1,0:T(8,128)} %copy-done.7, s32[]{:T(128)S(6)} %select_n.124, bf16[8,8,32,128]{3,2,1,0:T(8,128)(2,1)} %copy-done.5), kind=kOutput, calls=%fused_computation.97 | convolution fusion | flops 135004160 | bytes 4194308 | tf_op jit(solution)/shard_map/otid,tbd->otib/dot_general | solution.py:68
  125.8 1.8 collective-permute-start.9
  127.6 1.8 gather_fusion.1
  129.4 3.4 %collective-permute-done.11 = bf16[8,256,128]{2,1,0:T(8,128)(2,1)} collective-permute-done((bf16[8,256,128]{2,1,0:T(8,128)(2,1)}, bf16[8,256,128]{2,1,0:T(8,128)(2,1)}, u32[]{:S(2)}, u32[]{:S(2)}) %collective-permute-start.11) | collective-permute-done | bytes 524320 | tf_op jit(solution)/shard_map/ppermute | solution.py:59
  132.8 1.8 fusion.63
  134.7 6.5 %collective-permute-done.9 = bf16[8,8,32,128]{3,2,0,1:T(8,128)(2,1)} collective-permute-done((bf16[8,8,32,128]{3,2,0,1:T(8,128)(2,1)}, bf16[8,8,32,128]{3,2,0,1:T(8,128)(2,1)}, u32[]{:S(2)}, u32[]{:S(2)}) %collective-permute-start.9) | collective-permute-done | bytes 524320 | tf_op jit(solution)/shard_map/ppermute | solution.py:71
  143.3 5.7 %all-to-all-start.5 = ((bf16[8,8,32,128]{3,2,1,0:T(8,128)(2,1)}), bf16[8,8,32,128]{3,2,1,0:T(8,128)(2,1)S(1)}, u32[]{:S(2)}, u32[]{:S(2)}) async-start(bf16[8,8,32,128]{3,2,1,0:T(8,128)(2,1)} %copy.40), calls=%async_computation.5 | async-start | bytes 1048576 | tf_op jit(solution)/shard_map/all_to_all | solution.py:72
  149.1 1.8 collective-permute-start.12
  152.0 7.7 %collective-permute-done.12 = bf16[8,8,32,128]{3,2,0,1:T(8,128)(2,1)S(1)} collective-permute-done((bf16[8,8,32,128]{3,2,0,1:T(8,128)(2,1)S(1)}, bf16[8,8,32,128]{3,2,0,1:T(8,128)(2,1)S(1)}, u32[]{:S(2)}, u32[]{:S(2)}) %collective-permute-start.12) | collective-permute-done | bytes 524320 | tf_op jit(solution)/shard_map/ppermute | solution.py:71
  160.7 5.7 %all-to-all-start.7 = ((bf16[8,8,32,128]{3,2,1,0:T(8,128)(2,1)}), bf16[8,8,32,128]{3,2,1,0:T(8,128)(2,1)S(1)}, u32[]{:S(2)}, u32[]{:S(2)}) async-start(bf16[8,8,32,128]{3,2,1,0:T(8,128)(2,1)} %copy.46), calls=%async_computation.7 | async-start | bytes 1048576 | tf_op jit(solution)/shard_map/all_to_all | solution.py:72
  166.4 2.8 %fusion.74 = f32[32,128,256,1]{2,1,3,0:T(8,128)} fusion(bf16[8,8,32,128]{3,2,1,0:T(8,128)(2,1)S(1)} %all-to-all-done.1, bf16[8,32,256]{2,1,0:T(8,128)(2,1)S(1)} %select_select_fusion), kind=kOutput, calls=%fused_computation.110 | convolution fusion | flops 134217728 | bytes 4751360 | tf_op jit(solution)/shard_map/ota,otib->iab/dot_general | solution.py:74
  169.2 3.8 %fusion.71 = f32[32,128,256,1]{2,1,3,0:T(8,128)} fusion(bf16[8,8,32,128]{3,2,1,0:T(8,128)(2,1)} %all-to-all-done.3, bf16[8,32,256]{2,1,0:T(8,128)(2,1)S(1)} %select_select_fusion), kind=kOutput, calls=%fused_computation.107 | convolution fusion | flops 134217728 | bytes 4751360 | tf_op jit(solution)/shard_map/ota,otib->iab/dot_general | solution.py:74
  172.9 2.8 %fusion.68 = f32[32,128,256,1]{2,1,3,0:T(8,128)} fusion(bf16[8,8,32,128]{3,2,1,0:T(8,128)(2,1)S(1)} %all-to-all-done.5, bf16[8,32,256]{2,1,0:T(8,128)(2,1)S(1)} %select_select_fusion), kind=kOutput, calls=%fused_computation.104 | convolution fusion | flops 134217728 | bytes 4751360 | tf_op jit(solution)/shard_map/ota,otib->iab/dot_general | solution.py:74
  175.7 1.8 all-to-all-done.7
  177.5 5.7 %fusion = f32[32,256,128]{1,2,0:T(8,128)S(1)} fusion(f32[32,128,256,1]{2,1,3,0:T(8,128)} %fusion.68, f32[32,128,256,1]{2,1,3,0:T(8,128)} %fusion.71, f32[32,128,256,1]{2,1,3,0:T(8,128)} %fusion.74, bf16[8,8,32,128]{3,2,1,0:T(8,128)(2,1)S(1)} %all-to-all-done.7, bf16[8,32,256]{2,1,0:T(8,128)(2,1)S(1)} %select_select_fusion), kind=kOutput, calls=%fused_computation.3 | convolution fusion | flops 137363456 | bytes 17334272 | tf_op jit(solution)/shard_map/ota,otib->iab/dot_general | solution.py:74
  183.5 2.6 %collective-permute-done.13 = bf16[32,256,64]{1,2,0:T(8,128)(2,1)S(1)} collective-permute-done((bf16[32,256,64]{1,2,0:T(8,128)(2,1)S(1)}, bf16[32,256,64]{1,2,0:T(8,128)(2,1)S(1)}, u32[]{:S(2)}, u32[]{:S(2)}) %collective-permute-start.13) | collective-permute-done | bytes 1048608 | tf_op jit(solution)/shard_map/ppermute | solution.py:78
  186.2 1.6 add_convert_fusion
  (101 shorter events, 30.7 us)
Async XLA Ops:
  0.0 1.0 copy-start
  0.0 6.3 %copy-start.16 = (s32[512,1]{0,1:T(1,128)S(1)}, s32[512,1]{0,1:T(1,128)}, u32[]{:S(2)}) copy-start(s32[512,1]{0,1:T(1,128)} %param.14) | copy-start | bytes 6148
  0.0 7.1 %copy-start.14 = (s32[512]{0:T(512)S(1)}, s32[512]{0:T(512)}, u32[]{:S(2)}) copy-start(s32[512]{0:T(512)} %param.15) | copy-start | bytes 6148
  0.0 7.2 %copy-start.15 = (s32[512]{0:T(512)S(1)}, s32[512]{0:T(512)}, u32[]{:S(2)}) copy-start(s32[512]{0:T(512)} %param.13) | copy-start | bytes 6148
  0.0 8.7 %collective-permute-start.2 = (bf16[32,256,64]{1,2,0:T(8,128)(2,1)}, bf16[32,256,64]{1,2,0:T(8,128)(2,1)}, u32[]{:S(2)}, u32[]{:S(2)}) collective-permute-start(bf16[32,256,64]{1,2,0:T(8,128)(2,1)} %param.9), channel_id=1, source_target_pairs={{0,1},{1,0},{2,3},{3,2},{4,5},{5,4},{6,7},{7,6},{8,9},{9,8},{10,11... | collective-permute-start | bytes 3145736 | tf_op jit(solution)/shard_map/ppermute | solution.py:44
  2.7 6.0 %copy-start.18 = (bf16[32,256,64]{1,2,0:T(8,128)(2,1)S(1)}, bf16[32,256,64]{1,2,0:T(8,128)(2,1)}, u32[]{:S(2)}) copy-start(bf16[32,256,64]{1,2,0:T(8,128)(2,1)} %param.9) | copy-start | bytes 3145732
  2.7 39.9 %collective-permute-start = (bf16[8,256,128]{1,2,0:T(8,128)(2,1)S(1)}, bf16[8,256,128]{1,2,0:T(8,128)(2,1)}, u32[]{:S(2)}, u32[]{:S(2)}) collective-permute-start(bf16[8,256,128]{1,2,0:T(8,128)(2,1)S(1)} %fusion.3), channel_id=1, source_target_pairs={{0,1},{1,0},{2,3},{3,2},{4,5},{5,4},{6,7},{7,6},{8,9},{9,8},{10,11... | collective-permute-start | bytes 1572872 | tf_op jit(solution)/shard_map/ppermute | solution.py:55
  5.7 95.0 %collective-permute-start.10 = (bf16[8,256,128]{1,2,0:T(8,128)(2,1)}, bf16[8,256,128]{1,2,0:T(8,128)(2,1)}, u32[]{:S(2)}, u32[]{:S(2)}) collective-permute-start(bf16[8,256,128]{1,2,0:T(8,128)(2,1)} %fusion.9), channel_id=1, source_target_pairs={{0,1},{1,0},{2,3},{3,2},{4,5},{5,4},{6,7},{7,6},{8,9},{9,8},{10,11... | collective-permute-start | bytes 1572872 | tf_op jit(solution)/shard_map/ppermute | solution.py:55
  11.9 22.0 %all-to-all-start = ((bf16[8,8,32,128]{3,2,1,0:T(8,128)(2,1)}), bf16[8,8,32,128]{3,2,1,0:T(8,128)(2,1)S(1)}, u32[]{:S(2)}, u32[]{:S(2)}) async-start(bf16[8,8,32,128]{3,2,1,0:T(8,128)(2,1)} %copy.99), calls=%async_computation | async-start | bytes 1048576 | tf_op jit(solution)/shard_map/all_to_all | solution.py:66
  20.9 35.7 %collective-permute-start.4 = (bf16[8,256,128]{1,2,0:T(8,128)(2,1)S(1)}, bf16[8,256,128]{1,2,0:T(8,128)(2,1)}, u32[]{:S(2)}, u32[]{:S(2)}) collective-permute-start(bf16[8,256,128]{1,2,0:T(8,128)(2,1)S(1)} %fusion.5), channel_id=1, source_target_pairs={{0,1},{1,0},{2,3},{3,2},{4,5},{5,4},{6,7},{7,6},{8,9},{9,8},{10,11... | collective-permute-start | bytes 1572872 | tf_op jit(solution)/shard_map/ppermute | solution.py:55
  23.4 73.7 %collective-permute-start.7 = (bf16[8,256,128]{1,2,0:T(8,128)(2,1)}, bf16[8,256,128]{1,2,0:T(8,128)(2,1)}, u32[]{:S(2)}, u32[]{:S(2)}) collective-permute-start(bf16[8,256,128]{1,2,0:T(8,128)(2,1)} %fusion.7), channel_id=1, source_target_pairs={{0,1},{1,0},{2,3},{3,2},{4,5},{5,4},{6,7},{7,6},{8,9},{9,8},{10,11... | collective-permute-start | bytes 1572872 | tf_op jit(solution)/shard_map/ppermute | solution.py:55
  33.9 18.3 %all-to-all-start.6 = ((bf16[8,8,32,128]{3,2,1,0:T(8,128)(2,1)}), bf16[8,8,32,128]{3,2,1,0:T(8,128)(2,1)S(1)}, u32[]{:S(2)}, u32[]{:S(2)}) async-start(bf16[8,8,32,128]{3,2,1,0:T(8,128)(2,1)} %copy.96), calls=%async_computation.6 | async-start | bytes 1048576 | tf_op jit(solution)/shard_map/all_to_all | solution.py:66
  42.5 4.8 %copy-start.19 = (bf16[32,256,64]{1,2,0:T(8,128)(2,1)S(1)}, bf16[32,256,64]{1,2,0:T(8,128)(2,1)}, u32[]{:S(2)}) copy-start(bf16[32,256,64]{1,2,0:T(8,128)(2,1)} %param.9) | copy-start | bytes 3145732
  44.3 1.3 copy-start.8
  45.7 19.4 %collective-permute-start.1 = (bf16[8,256,128]{2,1,0:T(8,128)(2,1)S(1)}, bf16[8,256,128]{2,1,0:T(8,128)(2,1)}, u32[]{:S(2)}, u32[]{:S(2)}) collective-permute-start(bf16[8,256,128]{2,1,0:T(8,128)(2,1)S(1)} %dynamic-slice_convert_fusion.7), channel_id=1, source_target_pairs={{0,2},{1,3},{2,0},{3,1},{4,6},{5,7},{6,4},{7,5},{8,10},{9,11},{10,... | collective-permute-start | bytes 1572872 | tf_op jit(solution)/shard_map/ppermute | solution.py:59
  49.6 7.0 %copy-start.13 = (bf16[8,256,128]{1,2,0:T(8,128)(2,1)S(1)}, bf16[8,256,128]{1,2,0:T(8,128)(2,1)}, u32[]{:S(2)}) copy-start(bf16[8,256,128]{1,2,0:T(8,128)(2,1)} %fusion.4) | copy-start | bytes 1572868
  52.2 18.5 %all-to-all-start.2 = ((bf16[8,8,32,128]{3,2,1,0:T(8,128)(2,1)}), bf16[8,8,32,128]{3,2,1,0:T(8,128)(2,1)}, u32[]{:S(2)}, u32[]{:S(2)}) async-start(bf16[8,8,32,128]{3,2,1,0:T(8,128)(2,1)} %copy.98), calls=%async_computation.2 | async-start | bytes 1048576 | tf_op jit(solution)/shard_map/all_to_all | solution.py:66
  56.6 5.3 %copy-start.20 = (bf16[32,256,64]{1,2,0:T(8,128)(2,1)S(1)}, bf16[32,256,64]{1,2,0:T(8,128)(2,1)}, u32[]{:S(2)}) copy-start(bf16[32,256,64]{1,2,0:T(8,128)(2,1)} %param.9) | copy-start | bytes 3145732
  58.4 1.3 copy-start.10
  60.6 4.5 %copy-start.9 = (f32[8,256,256]{2,1,0:T(8,128)S(1)}, f32[8,256,256]{2,1,0:T(8,128)}, u32[]{:S(2)}) copy-start(f32[8,256,256]{2,1,0:T(8,128)} %copy-done.8) | copy-start | bytes 6291460
  60.6 17.9 %collective-permute-start.5 = (bf16[8,256,128]{2,1,0:T(8,128)(2,1)}, bf16[8,256,128]{2,1,0:T(8,128)(2,1)}, u32[]{:S(2)}, u32[]{:S(2)}) collective-permute-start(bf16[8,256,128]{2,1,0:T(8,128)(2,1)} %dynamic-slice_convert_fusion.5), channel_id=1, source_target_pairs={{0,2},{1,3},{2,0},{3,1},{4,6},{5,7},{6,4},{7,5},{8,10},{9,11},{10,... | collective-permute-start | bytes 1572872 | tf_op jit(solution)/shard_map/ppermute | solution.py:59
  66.6 11.8 %copy-start.1 = (f32[8,256,8,32]{1,3,2,0:T(8,128)}, f32[8,256,8,32]{1,3,2,0:T(8,128)S(1)}, u32[]{:S(2)}) copy-start(f32[8,256,8,32]{1,3,2,0:T(8,128)S(1)} %fusion.51) | copy-start | bytes 6291460
  70.7 18.0 %all-to-all-start.4 = ((bf16[8,8,32,128]{3,2,1,0:T(8,128)(2,1)}), bf16[8,8,32,128]{3,2,1,0:T(8,128)(2,1)S(1)}, u32[]{:S(2)}, u32[]{:S(2)}) async-start(bf16[8,8,32,128]{3,2,1,0:T(8,128)(2,1)} %copy.97), calls=%async_computation.4 | async-start | bytes 1048576 | tf_op jit(solution)/shard_map/all_to_all | solution.py:66
  74.3 4.2 %copy-start.11 = (f32[8,256,256]{2,1,0:T(8,128)S(1)}, f32[8,256,256]{2,1,0:T(8,128)}, u32[]{:S(2)}) copy-start(f32[8,256,256]{2,1,0:T(8,128)} %copy-done.10) | copy-start | bytes 6291460
  74.4 13.2 %collective-permute-start.3 = (bf16[8,8,32,128]{3,2,0,1:T(8,128)(2,1)S(1)}, bf16[8,8,32,128]{3,2,0,1:T(8,128)(2,1)S(1)}, u32[]{:S(2)}, u32[]{:S(2)}) collective-permute-start(bf16[8,8,32,128]{3,2,0,1:T(8,128)(2,1)S(1)} %fusion.53), channel_id=1, source_target_pairs={{0,2},{1,3},{2,0},{3,1},{4,6},{5,7},{6,4},{7,5},{8,10},{9,11},{10,... | collective-permute-start | bytes 1572872 | tf_op jit(solution)/shard_map/ppermute | solution.py:71
  78.5 9.1 %copy-start.2 = (f32[8,256,8,32]{1,3,2,0:T(8,128)S(1)}, f32[8,256,8,32]{1,3,2,0:T(8,128)}, u32[]{:S(2)}) copy-start(f32[8,256,8,32]{1,3,2,0:T(8,128)} %copy-done.1) | copy-start | bytes 6291460
  88.7 0.8 copy-start.5
  89.5 21.8 %all-to-all-start.1 = ((bf16[8,8,32,128]{3,2,1,0:T(8,128)(2,1)}), bf16[8,8,32,128]{3,2,1,0:T(8,128)(2,1)S(1)}, u32[]{:S(2)}, u32[]{:S(2)}) async-start(bf16[8,8,32,128]{3,2,1,0:T(8,128)(2,1)} %copy.28), calls=%async_computation.1 | async-start | bytes 1048576 | tf_op jit(solution)/shard_map/all_to_all | solution.py:72
  95.3 5.4 %copy-start.12 = (bf16[8,256,128]{1,2,0:T(8,128)(2,1)S(1)}, bf16[8,256,128]{1,2,0:T(8,128)(2,1)}, u32[]{:S(2)}) copy-start(bf16[8,256,128]{1,2,0:T(8,128)(2,1)} %fusion.8) | copy-start | bytes 1572868
  95.3 14.9 %collective-permute-start.6 = (bf16[8,8,32,128]{3,2,0,1:T(8,128)(2,1)S(1)}, bf16[8,8,32,128]{3,2,0,1:T(8,128)(2,1)S(1)}, u32[]{:S(2)}, u32[]{:S(2)}) collective-permute-start(bf16[8,8,32,128]{3,2,0,1:T(8,128)(2,1)S(1)} %fusion.57), channel_id=1, source_target_pairs={{0,2},{1,3},{2,0},{3,1},{4,6},{5,7},{6,4},{7,5},{8,10},{9,11},{10,... | collective-permute-start | bytes 1572872 | tf_op jit(solution)/shard_map/ppermute | solution.py:71
  99.2 1.5 copy-start.7
  100.2 21.4 %collective-permute-start.8 = (bf16[8,256,128]{2,1,0:T(8,128)(2,1)}, bf16[8,256,128]{2,1,0:T(8,128)(2,1)}, u32[]{:S(2)}, u32[]{:S(2)}) collective-permute-start(bf16[8,256,128]{2,1,0:T(8,128)(2,1)} %dynamic-slice_convert_fusion.3), channel_id=1, source_target_pairs={{0,2},{1,3},{2,0},{3,1},{4,6},{5,7},{6,4},{7,5},{8,10},{9,11},{10,... | collective-permute-start | bytes 1572872 | tf_op jit(solution)/shard_map/ppermute | solution.py:59
  102.4 8.0 %copy-start.6 = (f32[8,256,256]{2,1,0:T(8,128)}, f32[8,256,256]{2,1,0:T(8,128)S(1)}, u32[]{:S(2)}) copy-start(f32[8,256,256]{2,1,0:T(8,128)S(1)} %fusion.28) | copy-start | bytes 6291460
  103.4 29.4 %collective-permute-start.11 = (bf16[8,256,128]{2,1,0:T(8,128)(2,1)}, bf16[8,256,128]{2,1,0:T(8,128)(2,1)}, u32[]{:S(2)}, u32[]{:S(2)}) collective-permute-start(bf16[8,256,128]{2,1,0:T(8,128)(2,1)} %dynamic-slice_convert_fusion.1), channel_id=1, source_target_pairs={{0,2},{1,3},{2,0},{3,1},{4,6},{5,7},{6,4},{7,5},{8,10},{9,11},{10,... | collective-permute-start | bytes 1572872 | tf_op jit(solution)/shard_map/ppermute | solution.py:59
  111.3 31.9 %all-to-all-start.3 = ((bf16[8,8,32,128]{3,2,1,0:T(8,128)(2,1)}), bf16[8,8,32,128]{3,2,1,0:T(8,128)(2,1)}, u32[]{:S(2)}, u32[]{:S(2)}) async-start(bf16[8,8,32,128]{3,2,1,0:T(8,128)(2,1)} %copy.34), calls=%async_computation.3 | async-start | bytes 1048576 | tf_op jit(solution)/shard_map/all_to_all | solution.py:72
  123.5 1.3 copy-start.3
  125.8 15.4 %collective-permute-start.9 = (bf16[8,8,32,128]{3,2,0,1:T(8,128)(2,1)}, bf16[8,8,32,128]{3,2,0,1:T(8,128)(2,1)}, u32[]{:S(2)}, u32[]{:S(2)}) collective-permute-start(bf16[8,8,32,128]{3,2,0,1:T(8,128)(2,1)} %fusion.61), channel_id=1, source_target_pairs={{0,2},{1,3},{2,0},{3,1},{4,6},{5,7},{6,4},{7,5},{8,10},{9,11},{10,... | collective-permute-start | bytes 1572872 | tf_op jit(solution)/shard_map/ppermute | solution.py:71
  129.4 11.8 %copy-start.4 = (f32[8,256,8,32]{1,3,2,0:T(8,128)S(1)}, f32[8,256,8,32]{1,3,2,0:T(8,128)}, u32[]{:S(2)}) copy-start(f32[8,256,8,32]{1,3,2,0:T(8,128)} %copy-done.3) | copy-start | bytes 6291460
  142.4 8.5 %copy-start.17 = (s32[8]{0:T(128)S(1)}, s32[8]{0:T(128)}, u32[]{:S(2)}) copy-start(s32[8]{0:T(128)} %param.12) | copy-start | bytes 100
  143.3 17.4 %all-to-all-start.5 = ((bf16[8,8,32,128]{3,2,1,0:T(8,128)(2,1)}), bf16[8,8,32,128]{3,2,1,0:T(8,128)(2,1)S(1)}, u32[]{:S(2)}, u32[]{:S(2)}) async-start(bf16[8,8,32,128]{3,2,1,0:T(8,128)(2,1)} %copy.40), calls=%async_computation.5 | async-start | bytes 1048576 | tf_op jit(solution)/shard_map/all_to_all | solution.py:72
  149.1 10.6 %collective-permute-start.12 = (bf16[8,8,32,128]{3,2,0,1:T(8,128)(2,1)S(1)}, bf16[8,8,32,128]{3,2,0,1:T(8,128)(2,1)S(1)}, u32[]{:S(2)}, u32[]{:S(2)}) collective-permute-start(bf16[8,8,32,128]{3,2,0,1:T(8,128)(2,1)S(1)} %fusion.65), channel_id=1, source_target_pairs={{0,2},{1,3},{2,0},{3,1},{4,6},{5,7},{6,4},{7,5},{8,10},{9,11},{10,... | collective-permute-start | bytes 1572872 | tf_op jit(solution)/shard_map/ppermute | solution.py:71
  160.7 16.8 %all-to-all-start.7 = ((bf16[8,8,32,128]{3,2,1,0:T(8,128)(2,1)}), bf16[8,8,32,128]{3,2,1,0:T(8,128)(2,1)S(1)}, u32[]{:S(2)}, u32[]{:S(2)}) async-start(bf16[8,8,32,128]{3,2,1,0:T(8,128)(2,1)} %copy.46), calls=%async_computation.7 | async-start | bytes 1048576 | tf_op jit(solution)/shard_map/all_to_all | solution.py:72
  183.5 2.7 %collective-permute-start.13 = (bf16[32,256,64]{1,2,0:T(8,128)(2,1)S(1)}, bf16[32,256,64]{1,2,0:T(8,128)(2,1)S(1)}, u32[]{:S(2)}, u32[]{:S(2)}) collective-permute-start(bf16[32,256,64]{1,2,0:T(8,128)(2,1)S(1)} %select_convert_fusion), channel_id=1, source_target_pairs={{0,1},{1,0},{2,3},{3,2},{4,5},{5,4},{6,7},{7,6},{8,9},{9,8},{10,11... | collective-permute-start | bytes 3145736 | tf_op jit(solution)/shard_map/ppermute | solution.py:78

commit v2 on v1

v2 whole, which is shorter than its diff:
```python
import functools

import jax
import jax.numpy as jnp
from jax import lax
from jax.experimental import pallas as pl
from jax.experimental.pallas import tpu as pltpu
from jax.sharding import PartitionSpec as P

F32, BF16 = jnp.float32, jnp.bfloat16
TILE_PARTS = 4
VMEM_LIMIT = 50 * 1024 * 1024


def dot(a, b, dims=(((1,), (0,)), ((), ()))):
    return lax.dot_general(a, b, dims, preferred_element_type=F32)


def call(body, outs, ins, flops, scratch=(), early=()):
    whole = pl.BlockSpec(memory_space=pltpu.VMEM)
    moved = sum(2 * x.size for x in ins) + sum(2 * x.size for x in outs)
    return pl.pallas_call(
        body,
        out_shape=outs,
        in_specs=[whole] * len(ins) + [pl.BlockSpec(memory_space=pl.ANY)] * len(early),
        out_specs=[whole] * len(outs),
        scratch_shapes=list(scratch),
        cost_estimate=pl.CostEstimate(flops=flops, bytes_accessed=moved, transcendentals=0),
        compiler_params=pltpu.CompilerParams(vmem_limit_bytes=VMEM_LIMIT),
    )(*ins, *early)


def order_body(orbitals, left, side_rows, held):
    vir = orbitals.shape[1]
    part = lax.axis_index("ao")
    nu_part = side_rows.shape[0] // 2
    line = orbitals[...]
    left[...] = line.T
    quarters = [line[:, q:q + vir // 4] for q in (vir // 4, 0, 3 * vir // 4, vir // 2)]
    line = jnp.where(part % 2 == 0, line, jnp.concatenate(quarters, 1))
    line = jnp.where(part // 2 == 0, line, jnp.concatenate([line[:, vir // 2:], line[:, :vir // 2]], 1))
    held[...] = line
    for q in range(2):
        start = pl.multiple_of((part ^ q) * nu_part, nu_part)
        side_rows[pl.ds(q * nu_part, nu_part), :] = held[pl.ds(start, nu_part), :]


def order_orbitals(orbitals, nu_part):
    count, vir = orbitals.shape
    outs = [jax.ShapeDtypeStruct((vir, count), BF16), jax.ShapeDtypeStruct((2 * nu_part, vir), BF16)]
    return call(order_body, outs, (orbitals,), count * vir, [pltpu.VMEM((count, vir), BF16)])


def gather_body(src, sub, row, count, orbitals, early, source, target, held, ahead, back):
    held[...] = orbitals[...].astype(F32)
    nodes = count.shape[0]
    slots = src.shape[0] // nodes
    half = slots // 2
    blocks = held.shape[0] // nodes
    own, core = lax.axis_index("occ"), lax.axis_index("ao") % 2
    for k in range(nodes):
        partner = own ^ k

        def step(j, carry):
            place = core * half + j
            slot = k * slots + place
            ahead[pl.ds(k * half + j, 1), :] = held[pl.ds(src[slot] * blocks + sub[slot], 1), :]
            line = held[pl.ds(partner * blocks + row[partner * slots + place], 1), :]
            back[pl.ds(k * half + j, 1), :] = jnp.where(place < count[partner], line, 0.0)
            return carry

        lax.fori_loop(0, half, step, 0, unroll=8)
    source[...] = ahead[...].astype(BF16)
    target[...] = back[...].astype(BF16)


def gather_rows(src, sub, row, count, orbitals, early):
    slots, vir = src.shape[0] // 2, orbitals.shape[1]
    scalar = pl.BlockSpec(memory_space=pltpu.SMEM)
    whole = pl.BlockSpec(memory_space=pltpu.VMEM)
    return pl.pallas_call(
        gather_body,
        out_shape=[jax.ShapeDtypeStruct((slots, vir), BF16)] * 2,
        in_specs=[scalar] * 4 + [whole, pl.BlockSpec(memory_space=pl.ANY)],
        out_specs=[whole] * 2,
        scratch_shapes=[pltpu.VMEM(orbitals.shape, F32)] + [pltpu.VMEM((slots, vir), F32)] * 2,
        cost_estimate=pl.CostEstimate(flops=slots * vir, bytes_accessed=8 * slots * vir, transcendentals=0),
        compiler_params=pltpu.CompilerParams(vmem_limit_bytes=VMEM_LIMIT),
    )(src, sub, row, count, orbitals, early)


def rows_body(rows_ref, mine_ref, other_ref, *rest):
    out, scratch = rest[-2:]
    occ = mine_ref.shape[0]
    count, _ = rows_ref.shape
    width = scratch.shape[1]
    rows = rows_ref[...]

    def step(n, carry):
        i = 2 * n
        right = jnp.concatenate([mine_ref[i], other_ref[i], mine_ref[i + 1], other_ref[i + 1]], 0)
        product = dot(rows, right, (((1,), (1,)), ((), ())))
        scratch[pl.ds(i, count, stride=occ), :] = product[:, :width]
        scratch[pl.ds(i + 1, count, stride=occ), :] = product[:, width:]
        return carry

    lax.fori_loop(0, occ // 2, step, 0, unroll=4)
    block = count // out.shape[0] * occ
    for k in range(out.shape[0]):
        out[k] = scratch[k * block:(k + 1) * block, :].reshape(out.shape[1:]).astype(BF16)


def pair_rows(rows, mine, other, nodes, early):
    occ, part, vir = mine.shape
    count = rows.shape[0]
    outs = [jax.ShapeDtypeStruct((nodes, count // nodes, occ, 2 * part), BF16)]
    scratch = [pltpu.VMEM((count * occ, 2 * part), F32)]
    return call(rows_body, outs, (rows, mine, other), 4 * count * occ * vir * part, scratch, early)[0]


def start_copies(other_core, start, tiles, held, sems):
    core = lax.axis_index("ao") % 2
    offset = (1 - core if other_core else core) * (tiles.shape[0] // 2) + start
    pieces = sems.shape[0]
    size = held.shape[0] // pieces
    copies = []
    for n in range(pieces):
        source = tiles.at[pl.ds(offset + n * size, size)]
        copies.append(pltpu.make_async_copy(source, held.at[pl.ds(n * size, size)], sems.at[n]))
        copies[n].start()
    return copies


def pair_dot(left, held, t):
    product = dot(left, jnp.concatenate([held[t], held[t + 1]], 1))
    width = held.shape[2]
    return product[:, :width].astype(BF16), product[:, width:].astype(BF16)


def give_kernel(start, left_ref, tiles, *rest):
    out, held, sems = rest[-3:]
    copies = start_copies(True, start, tiles, held, sems)
    size = out.shape[0] // len(copies)
    left = left_ref[...]
    for n, copy in enumerate(copies):
        copy.wait()
        for t in range(n * size, (n + 1) * size, 2):
            out[t], out[t + 1] = pair_dot(left, held, t)


def finish_kernel(start, skip, left_ref, tiles, other, right_ref, *rest):
    here, there, held, sems = rest[-4:]
    copies = start_copies(False, start, tiles, held, sems)
    size = here.shape[0] // len(copies)
    width = here.shape[1]
    left, right = left_ref[...], right_ref[...]
    side = lax.axis_index("ao") // 2
    for n, copy in enumerate(copies):
        copy.wait()
        rows = []
        for t in range(n * size, (n + 1) * size, 2):
            for j, mine in enumerate(pair_dot(left, held, t)):
                rows.append(jnp.concatenate([mine, other[skip + t + j]], 1))
        both = dot(jnp.concatenate(rows, 0), right).reshape(size, -1, right.shape[1]).astype(BF16)
        piece = pl.ds(n * size, size)
        low, high = both[:, :width], both[:, width:]
        here[piece] = jnp.where(side == 0, low, high)
        away = jnp.where(side == 0, high, low)
        there[piece] = jnp.concatenate([away[:, :, width:], away[:, :, :width]], 2)


PIECE = 4


def tile_call(body, count, tiles, ins, outs, early=()):
    _, sig, nu = tiles.shape
    vir = ins[0].shape[0]
    whole = pl.BlockSpec(memory_space=pltpu.VMEM)
    away = pl.BlockSpec(memory_space=pl.ANY)
    flops = 2 * count * vir * nu * (sig + 2 * vir * (len(outs) - 1))
    return pl.pallas_call(
        body,
        out_shape=outs,
        in_specs=[whole, away] + [whole] * (len(ins) - 1) + [away] * len(early),
        out_specs=[whole] * len(outs),
        scratch_shapes=[pltpu.VMEM((count, sig, nu), BF16), pltpu.SemaphoreType.DMA((count // PIECE,))],
        cost_estimate=pl.CostEstimate(
            flops=flops, bytes_accessed=2 * count * sig * nu * 2, transcendentals=0
        ),
        compiler_params=pltpu.CompilerParams(vmem_limit_bytes=VMEM_LIMIT),
    )(ins[0], tiles, *ins[1:], *early)


def dress_body(parts, *refs):
    out = refs[-1]
    t = 0
    for n in range(parts):
        size = refs[2 * n].shape[0]
        out[t:t + size] = refs[2 * n][...] + refs[2 * n + 1][...]
        t += size


def dress(parts):
    slots = sum(x.shape[0] for x in parts[::2])
    outs = [jax.ShapeDtypeStruct((slots,) + parts[0].shape[1:], BF16)]
    return call(functools.partial(dress_body, len(parts) // 2), outs, parts, slots)[0]


def product_body(near_ref, far_ref, dressed, last, last_far, *refs):
    scratch = refs[-1]
    groups, slots, occ, _ = near_ref.shape
    outs = refs[-1 - groups:-1]
    first = dressed.shape[0]
    for t in range(slots):
        tile = dressed[t] if t < first else last[t - first] + last_far[t - first]
        rows = [jnp.concatenate([near_ref[n, t], far_ref[n, t]], 1) for n in range(groups)]
        product = dot(jnp.concatenate(rows, 0), tile, (((1,), (1,)), ((), ())))
        scratch[pl.ds(t, groups * occ, stride=slots), :] = product
    for n, out in enumerate(outs):
        block = occ * slots
        out[...] = scratch[n * block:(n + 1) * block, :].reshape(out.shape).astype(BF16)


def products(near_rows, far_rows, tiles, early):
    groups, slots, occ, width = near_rows.shape
    outs = [jax.ShapeDtypeStruct((occ, slots, width), BF16)] * groups
    scratch = [pltpu.VMEM((groups * occ * slots, width), F32)]
    flops = 4 * groups * occ * slots * width * width
    return call(product_body, outs, (near_rows, far_rows, *tiles), flops, scratch, early)


def back_body(nodes, rows_ref, *refs):
    values, (keep, give) = refs[:nodes], refs[nodes:]
    occ = values[0].shape[0]
    part = keep.shape[1]
    core = lax.axis_index("ao") % 2
    rows = rows_ref[...]

    def step(i, carry):
        left = jnp.concatenate([v[i] for v in values], 0)
        product = dot(left, rows, (((0,), (0,)), ((), ())))
        low, high = product[:part].astype(BF16), product[part:].astype(BF16)
        keep[i] = jnp.where(core == 0, low, high)
        give[i] = jnp.where(core == 0, high, low)
        return carry

    lax.fori_loop(0, occ, step, 0, unroll=4)


def back_transform(rows, values):
    occ, _, width = values[0].shape
    count, vir = rows.shape
    outs = [jax.ShapeDtypeStruct((occ, width // 2, vir), BF16)] * 2
    return call(
        functools.partial(back_body, len(values)), outs, (rows, *values), 2 * occ * vir * count * width
    )


def shards(amplitudes, orbitals, tiles, tile_count, tile_row, tile_src, tile_sub):
    nodes = lax.axis_size("occ")
    own = lax.axis_index("occ")
    parts = lax.axis_size("ao")
    part = lax.axis_index("ao")
    core = part % 2
    near = [(q, q ^ 1) for q in range(parts)]
    far = [(q, q ^ 2) for q in range(parts)]
    local_occ, vir, vir_part = amplitudes.shape
    nu_part = tiles.shape[2]
    slots = tiles.shape[0]
    half = slots // 2
    blocks = orbitals.shape[0] // nodes
    pick = lax.dynamic_slice_in_dim

    mine = jnp.swapaxes(amplitudes, 1, 2)
    other = lax.ppermute(mine, "ao", near)
    left, side_rows = order_orbitals(orbitals, nu_part)
    def tile_shape(count, width):
        return jax.ShapeDtypeStruct((count, vir, width), BF16)

    def give(start, early):
        outs = [tile_shape(half // 2, nu_part)]
        body = functools.partial(give_kernel, start)
        (given,) = tile_call(body, half // 2, tiles, (left,), outs, early)
        return given, lax.ppermute(given, "ao", near)

    given, first_parts = give(0, ())
    given, second_parts = give(half // 2, [given])
    source_rows, target_rows = gather_rows(tile_src[:, 0], tile_sub, tile_row, tile_count, orbitals, given)
    sent = pair_rows(source_rows, mine, other, nodes, (first_parts, second_parts))
    arrived = lax.all_to_all(sent, "occ", split_axis=0, concat_axis=0, tiled=True)
    parts, early = [], [sent]
    step = half // TILE_PARTS
    for n in range(TILE_PARTS):
        if n >= 2:
            early.append(parts[2 * n - 3])
        other_parts = first_parts if 2 * n < TILE_PARTS else second_parts
        here, there = tile_call(
            functools.partial(finish_kernel, n * step, n * step % (half // 2)), step, tiles,
            (left, other_parts, side_rows), [jax.ShapeDtypeStruct((step, vir // 2, vir), BF16)] * 2, early,
        )
        early = [there]
        parts += [here, lax.ppermute(there, "ao", far)]
    tiles_done = [dress(parts[:-2]), *parts[-2:]]
    units = [[nodes - 1 - n, (n + nodes // 2 - 2) % (nodes // 2)] for n in range(nodes // 2)]
    blocks_of = [jnp.stack([arrived[own ^ k] for k in unit]) for unit in units]
    far_blocks = [lax.ppermute(x, "ao", far) for x in blocks_of]
    returned, early = {}, []
    for n, unit in enumerate(units):
        made = products(blocks_of[n], far_blocks[n], tiles_done, early)
        early = [made[0]]
        if n >= 1:
            early += [returned[k] for k in units[n - 1]]
        for k, x in zip(unit, made):
            returned[k] = lax.ppermute(x, "occ", [(o, o ^ k) for o in range(nodes)]) if k else x
    returned = [returned[k] for k in range(nodes)]
    keep, give_up = back_transform(target_rows, returned)
    return jnp.swapaxes(keep + lax.ppermute(give_up, "ao", near), 1, 2)


def plain_shards(amplitudes, orbitals, tiles, tile_count, tile_row, tile_src, tile_sub):
    nodes = lax.axis_size("occ")
    parts = lax.axis_size("ao")
    part = lax.axis_index("ao")
    core = part % 2
    near = [(q, q ^ 1) for q in range(parts)]
    far = [(q, q ^ 2) for q in range(parts)]
    vir_part = amplitudes.shape[2]
    nu_part = tiles.shape[2]
    slots = tiles.shape[0]
    half = slots // 2
    blocks = orbitals.shape[0] // nodes
    pick = lax.dynamic_slice_in_dim
    ordered = jnp.concatenate([pick(orbitals, (part ^ q) * vir_part, vir_part, 1) for q in range(parts)], 1)
    side_rows = jnp.concatenate([pick(ordered, (part ^ q) * nu_part, nu_part, 0) for q in range(2)], 0)

    def mine_of(table):
        return pick(table.reshape(nodes, slots), core * half, half, 1)

    def product(form, a, b):
        return jnp.einsum(form, a, b, preferred_element_type=F32)

    def split(x, at, axis):
        size = x.shape[axis] // 2
        return pick(x, at * size, size, axis), pick(x, (1 - at) * size, size, axis)

    source = mine_of(tile_src[:, 0]) * blocks + mine_of(tile_sub)
    target = jnp.arange(nodes, dtype=jnp.int32)[:, None] * blocks + mine_of(tile_row)
    place = core * half + jnp.arange(half, dtype=jnp.int32)
    live = place[None, :] < tile_count[:, None]
    source_rows = jnp.take(orbitals, source, axis=0)
    target_rows = jnp.where(live[:, :, None], jnp.take(orbitals, target, axis=0), 0)
    paired = jnp.concatenate([amplitudes, lax.ppermute(amplitudes, "ao", near)], 2)
    sent = product("otc,icd->otid", source_rows, paired).astype(BF16)
    arrived = lax.all_to_all(sent, "occ", split_axis=0, concat_axis=0, tiled=True)
    keep, give = split(product("sb,tsn->tbn", orbitals, tiles).astype(BF16), core, 0)
    whole = jnp.concatenate([keep, lax.ppermute(give, "ao", near)], 2)
    both = product("tbn,nd->tbd", whole, side_rows).astype(BF16)
    dressed = both[:, :, :2 * vir_part] + lax.ppermute(both[:, :, 2 * vir_part:], "ao", far)
    both = product("otid,tbd->otib", arrived, dressed).astype(BF16)
    here, there = split(both, part // 2, 3)
    summed = here + lax.ppermute(there, "ao", far)
    back = lax.all_to_all(summed, "occ", split_axis=0, concat_axis=0, tiled=True)
    total = product("ota,otib->iab", target_rows, back).astype(BF16)
    keep, give = split(total, core, 2)
    return keep + lax.ppermute(give, "ao", near)


def solution(mesh):
    placed = (P("occ", None, "ao"), P(), P("occ", None, "ao"), P(), P(), P(), P())

    def whole(amplitudes, *rest):
        nodes = mesh.shape["occ"]
        rows = amplitudes.shape[0] // nodes
        body = shards if rows % 16 == 0 and nodes <= 16 else plain_shards
        return jax.shard_map(
            body, mesh=mesh, in_specs=placed, out_specs=P("occ", None, "ao"), check_vma=False
        )(amplitudes, *rest)

    return whole
```

time: 189 us -> 157 us (0.83)
  matrix products: 57.3 us -> 0 us
  Pallas kernels: 0 us -> 40.4 us
  waiting for transfers between devices: 48.7 us -> 81.1 us
  starting transfers between devices: 55.3 us -> 27.4 us
  local copies, waits for them, and re-layouts: 20.7 us -> 6.14 us
  other arithmetic: 5.43 us -> 1.28 us
    dot_general x24 -> x0, matrix products: 57.3 us -> none  [the longest x4 15.1 us: shards(): jnp.einsum('ota,otib->iab', rows, back, preferred_element_type=f32)]
    pallas_call x0 -> x15, Pallas kernels: none -> 40.4 us  [the longest x8 20.9 us: call(): pl.pallas_call(body, out_shape=outs, in_specs=[whole] * len(ins) + [pl.Bl...]
    ppermute x14 -> x19, waiting for transfers between devices: 37.1 us -> 66.7 us  [the longest x4 26.9 us: shards(): far_blocks = [lax.ppermute(x, 'ao', far) for x in blocks_of]]
    all_to_all x4 -> x0, starting transfers between devices: 23.1 us -> none  [shards(): lax.all_to_all(summed, 'occ', split_axis=0, concat_axis=0, tiled=True)]
    all_to_all x4 -> x1, starting transfers between devices: 18.9 us -> 6.92 us  [shards(): lax.all_to_all(sent, 'occ', split_axis=0, concat_axis=0, tiled=True)]
    convert_element_type x12 -> x0, local copies, waits for them, and re-layouts: 7.6 us -> none  [the longest x4 3.47 us: shards(): summed = (here + lax.ppermute(there, 'ao', far).astype(f32)).astype(bf16)]
    ppermute x14 -> x19, starting transfers between devices: 13.3 us -> 20.4 us  [the longest x7 9.88 us: shards(): lax.ppermute(x, 'occ', [(o, o ^ k) for o in range(nodes)])]
    all_to_all x4 -> x1, waiting for transfers between devices: 9.77 us -> 14.3 us  [shards(): lax.all_to_all(sent, 'occ', split_axis=0, concat_axis=0, tiled=True)]
  transfers between devices with their start and end apart: 22 -> 20, of which waited for: 11 -> 11; matrix products, arithmetic and copies ran while one was open for 38% -> 1% of each run, Pallas kernels for 0% -> 17%
where the time goes in v2:
time: 157 us
  waiting for transfers between devices  81.1 us (52%)
  Pallas kernels  40.4 us (26%)
  starting transfers between devices  27.4 us (17%)
  local copies, waits for them, and re-layouts  6.14 us (4%)
    ppermute x4, waiting for transfers between devices, shards(): far_blocks = [lax.ppermute(x, 'ao', far) for x in blocks_of]  26.9 us
    ppermute x7, waiting for transfers between devices, shards(): lax.ppermute(x, 'occ', [(o, o ^ k) for o in range(nodes)])  21.2 us
    pallas_call x8, Pallas kernels, call(): pl.pallas_call(body, out_shape=outs, in_specs=[whole] * len(ins) + [pl.Bl...  20.9 us
    pallas_call x6, Pallas kernels, tile_call(): pl.pallas_call(body, out_shape=outs, in_specs=[whole, away] + [whole] * (...  16.6 us
    ppermute x4, waiting for transfers between devices, shards(): parts += [here, lax.ppermute(there, 'ao', far)]  15.8 us
    all_to_all x1, waiting for transfers between devices, shards(): lax.all_to_all(sent, 'occ', split_axis=0, concat_axis=0, tiled=True)  14.3 us
    ppermute x7, starting transfers between devices, shards(): lax.ppermute(x, 'occ', [(o, o ^ k) for o in range(nodes)])  9.88 us
    all_to_all x1, starting transfers between devices, shards(): lax.all_to_all(sent, 'occ', split_axis=0, concat_axis=0, tiled=True)  6.92 us
  transfers between devices with their start and end apart: 20, of which 11 were waited for; matrix products, arithmetic and copies ran while one was open for 1% of the time, Pallas kernels for 17%

profile of v2, /device:TPU:0, one launch (start us, length us, event | category | flops | bytes accessed | tf_op | source)
XLA Modules:
  0.0 156.6 jit_solution(6334989137977470421)
XLA Ops:
  0.0 0.9 copy-done.3
  1.2 2.3 %shard_map.74.rest_0_ = bf16[16,256,128]{2,1,0:T(8,128)(2,1)S(1)} custom-call(bf16[256,512]{1,0:T(8,128)(2,1)S(1)} %get-tuple-element.27.left_ref, bf16[64,512,128]{2,1,0:T(8,128)(2,1)} %tiles.11), custom_call_target="tpu_custom_call" | custom-call | flops 536870912 | bytes 4194304 | tf_op jit(solution)/shard_map/pallas_call | solution.py:181
  3.6 0.5 collective-permute-start.1
  4.1 2.3 %shard_map.75.early = bf16[16,256,128]{2,1,0:T(8,128)(2,1)S(1)} custom-call(bf16[256,512]{1,0:T(8,128)(2,1)S(1)} %get-tuple-element.27.left_ref, bf16[64,512,128]{2,1,0:T(8,128)(2,1)} %tiles.11, bf16[16,256,128]{2,1,0:T(8,128)(2,1)S(1)} %shard_map.74.rest_0_), custom_call_target="tpu_custom_call" | custom-call | flops 536870912 | bytes 4194304 | tf_op jit(solution)/shard_map/pallas_call | solution.py:181
  7.0 2.9 %shard_map.76 = (bf16[256,256]{1,0:T(8,128)(2,1)S(1)}, bf16[256,256]{1,0:T(8,128)(2,1)S(1)}) custom-call(s32[512]{0:T(512)S(1)} %bitcast.6, s32[512]{0:T(512)S(1)} %copy-done.13, s32[512]{0:T(512)S(1)} %copy-done.14, s32[8]{0:T(128)S(1)} %copy-done.15, bf16[512,256]{1,0:T(8,128)(2,1)S(1)} %copy-done.3, bf16[16,256,128]{2,1,0:T(8,128)(2,1)S(1)} %shard_map.75.early), custom_call_target="tpu_custom_call" | custom-call | flops 65536 | bytes 524288 | tf_op jit(solution)/shard_map/pallas_call | solution.py:81
  9.9 0.6 copy-done.10
  10.6 0.9 copy-done
  11.6 4.8 %shard_map.77.rest_0_ = bf16[8,32,32,128]{3,2,1,0:T(8,128)(2,1)} custom-call(bf16[256,256]{1,0:T(8,128)(2,1)S(1)} %get-tuple-element.29.rows_ref, bf16[32,64,256]{2,1,0:T(8,128)(2,1)S(1)} %bitcast.5, bf16[32,64,256]{2,1,0:T(8,128)(2,1)S(1)} %collective-permute-done.other_ref, bf16[16,256,128]{2,1,0:T(8,128)(2,1)S(1)} %collective-permute-done.1.rest_0_.other, ...), custom_call_target="tpu_custom_call" | custom-call | flops 536870912 | bytes 4325376 | tf_op jit(solution)/shard_map/pallas_call | solution.py:22
  16.3 6.9 %all-to-all-start = ((bf16[8,32,32,128]{3,2,1,0:T(8,128)(2,1)}), bf16[8,32,32,128]{3,2,1,0:T(8,128)(2,1)}, u32[]{:S(2)}, u32[]{:S(2)}) async-start(bf16[8,32,32,128]{3,2,1,0:T(8,128)(2,1)} %shard_map.77.rest_0_), calls=%async_computation | async-start | bytes 4194304 | tf_op jit(solution)/shard_map/all_to_all | solution.py:290
  23.2 3.0 %shard_map.78 = (bf16[8,128,256]{2,1,0:T(8,128)(2,1)S(1)}, bf16[8,128,256]{2,1,0:T(8,128)(2,1)}) custom-call(bf16[256,512]{1,0:T(8,128)(2,1)S(1)} %get-tuple-element.27.left_ref, bf16[64,512,128]{2,1,0:T(8,128)(2,1)} %tiles.11, bf16[16,256,128]{2,1,0:T(8,128)(2,1)S(1)} %collective-permute-done.1.rest_0_.other, ...), custom_call_target="tpu_custom_call" | custom-call | flops 536870912 | bytes 2097152 | tf_op jit(solution)/shard_map/pallas_call | solution.py:181
  26.3 0.8 copy-done.4
  27.1 1.5 collective-permute-start.4
  28.6 3.0 %shard_map.79 = (bf16[8,128,256]{2,1,0:T(8,128)(2,1)S(1)}, bf16[8,128,256]{2,1,0:T(8,128)(2,1)}) custom-call(bf16[256,512]{1,0:T(8,128)(2,1)S(1)} %get-tuple-element.27.left_ref, bf16[64,512,128]{2,1,0:T(8,128)(2,1)} %tiles.11, bf16[16,256,128]{2,1,0:T(8,128)(2,1)S(1)} %collective-permute-done.1.rest_0_.other, ...), custom_call_target="tpu_custom_call" | custom-call | flops 536870912 | bytes 2097152 | tf_op jit(solution)/shard_map/pallas_call | solution.py:181
  31.6 0.8 copy-done.6
  32.4 0.5 collective-permute-start.5
  32.9 9.1 %collective-permute-done.4.rest_1_.refs_1_ = bf16[8,128,256]{2,1,0:T(8,128)(2,1)S(1)} collective-permute-done((bf16[8,128,256]{2,1,0:T(8,128)(2,1)}, bf16[8,128,256]{2,1,0:T(8,128)(2,1)S(1)}, u32[]{:S(2)}, u32[]{:S(2)}) %collective-permute-start.4) | collective-permute-done | bytes 524320 | tf_op jit(solution)/shard_map/ppermute | solution.py:302
  42.1 3.0 %shard_map.80 = (bf16[8,128,256]{2,1,0:T(8,128)(2,1)S(1)}, bf16[8,128,256]{2,1,0:T(8,128)(2,1)}) custom-call(bf16[256,512]{1,0:T(8,128)(2,1)S(1)} %get-tuple-element.27.left_ref, bf16[64,512,128]{2,1,0:T(8,128)(2,1)} %tiles.11, bf16[16,256,128]{2,1,0:T(8,128)(2,1)S(1)} %copy-done.1, bf16[256,256]{1,0:T(8,128)(2,1)S(1)} %get-tuple-element.30.right_ref, ...), custom_call_target="tpu_custom_call" | custom-call | flops 536870912 | bytes 2097152 | tf_op jit(solution)/shard_map/pallas_call | solution.py:181
  45.1 1.6 collective-permute-start.6
  46.6 6.7 %collective-permute-done.5.refs_3_.rest_1_ = bf16[8,128,256]{2,1,0:T(8,128)(2,1)S(1)} collective-permute-done((bf16[8,128,256]{2,1,0:T(8,128)(2,1)}, bf16[8,128,256]{2,1,0:T(8,128)(2,1)S(1)}, u32[]{:S(2)}, u32[]{:S(2)}) %collective-permute-start.5) | collective-permute-done | bytes 524320 | tf_op jit(solution)/shard_map/ppermute | solution.py:302
  53.3 3.0 %shard_map.82 = (bf16[8,128,256]{2,1,0:T(8,128)(2,1)S(1)}, bf16[8,128,256]{2,1,0:T(8,128)(2,1)}) custom-call(bf16[256,512]{1,0:T(8,128)(2,1)S(1)} %get-tuple-element.27.left_ref, bf16[64,512,128]{2,1,0:T(8,128)(2,1)} %tiles.11, bf16[16,256,128]{2,1,0:T(8,128)(2,1)S(1)} %copy-done.1, bf16[256,256]{1,0:T(8,128)(2,1)S(1)} %get-tuple-element.30.right_ref, ...), custom_call_target="tpu_custom_call" | custom-call | flops 536870912 | bytes 2097152 | tf_op jit(solution)/shard_map/pallas_call | solution.py:181
  56.3 1.6 collective-permute-start.7
  57.8 14.3 %all-to-all-done = bf16[8,32,32,128]{3,2,1,0:T(8,128)(2,1)} async-done(((bf16[8,32,32,128]{3,2,1,0:T(8,128)(2,1)}), bf16[8,32,32,128]{3,2,1,0:T(8,128)(2,1)}, u32[]{:S(2)}, u32[]{:S(2)}) %all-to-all-start) | async-done | bytes 2097184 | tf_op jit(solution)/shard_map/all_to_all | solution.py:290
  72.2 1.9 %constant_dynamic-slice_fusion.1 = (bf16[1,32,32,128]{3,2,1,0:T(8,128)(2,1)S(1)}, bf16[1,32,32,128]{3,2,1,0:T(8,128)(2,1)S(1)}, bf16[1,32,32,128]{3,2,1,0:T(8,12...) fusion(bf16[8,32,32,128]{3,2,1,0:T(8,128)(2,1)} %all-to-all-don, ...), kind=kLoop, calls=%fused_computation.6 | loop fusion | bytes 4194336 | tf_op jit(solution)/shard_map/dynamic_slice | solution.py:305
  74.2 1.6 collective-permute-start.9
  75.8 0.6 collective-permute-start.8
  76.5 1.5 collective-permute-start.3
  78.1 0.6 collective-permute-start.12
  78.7 2.4 %shard_map.81.dressed = bf16[24,128,256]{2,1,0:T(8,128)(2,1)} custom-call(bf16[8,128,256]{2,1,0:T(8,128)(2,1)S(1)} %copy-done.5, bf16[8,128,256]{2,1,0:T(8,128)(2,1)S(1)} %collective-permute-done.4.rest_1_.refs_1_, bf16[8,128,256]{2,1,0:T(8,128)(2,1)S(1)} %copy-done.7, bf16[8,128,256]{2,1,0:T(8,128)(2,1)S(1)} %collective-permute-done.5.refs_3_.rest_1_, ...), custom_call_target="tpu_custom_call" | custom-call | flops 24 | bytes 4718592 | tf_op jit(solution)/shard_map/pallas_call | solution.py:22
  81.1 8.0 %collective-permute-done.9.far_ref = bf16[2,32,32,128]{3,2,1,0:T(8,128)(2,1)S(1)} collective-permute-done((bf16[2,32,32,128]{3,2,1,0:T(8,128)(2,1)S(1)}, bf16[2,32,32,128]{3,2,1,0:T(8,128)(2,1)S(1)}, u32[]{:S(2)}, u32[]{:S(2)}) %collective-permute-start.9) | collective-permute-done | bytes 524320 | tf_op jit(solution)/shard_map/ppermute | solution.py:306
  89.1 2.6 %shard_map.83 = (bf16[32,32,128]{2,1,0:T(8,128)(2,1)S(1)}, bf16[32,32,128]{2,1,0:T(8,128)(2,1)S(1)}) custom-call(bf16[2,32,32,128]{3,2,1,0:T(8,128)(2,1)S(1)} %pad_maximum_fusion.2.near_ref, bf16[2,32,32,128]{3,2,1,0:T(8,128)(2,1)S(1)} %collective-permute-done.9.far_ref, bf16[24,128,256]{2,1,0:T(8,128)(2,1)} %shard_map.81.dressed, ...), custom_call_target="tpu_custom_call" | custom-call | flops 134217728 | bytes 4194304 | tf_op jit(solution)/shard_map/pallas_call | solution.py:22
  91.7 2.4 %collective-permute-start.10 = (bf16[32,32,128]{2,1,0:T(8,128)(2,1)S(1)}, bf16[32,32,128]{2,1,0:T(8,128)(2,1)S(1)}, u32[]{:S(2)}, u32[]{:S(2)}) collective-permute-start(bf16[32,32,128]{2,1,0:T(8,128)(2,1)S(1)} %get-tuple-element.39.refs_0_), channel_id=1, source_target_pairs={{0,28},{4,24},{8,20},{12,16},{16,12},{20,8},{24,4},{28,0},{1,29},{... | collective-permute-start | bytes 786440 | tf_op jit(solution)/shard_map/ppermute | solution.py:314
  94.1 6.3 %collective-permute-done.8.far_ref = bf16[2,32,32,128]{3,2,1,0:T(8,128)(2,1)S(1)} collective-permute-done((bf16[2,32,32,128]{3,2,1,0:T(8,128)(2,1)S(1)}, bf16[2,32,32,128]{3,2,1,0:T(8,128)(2,1)S(1)}, u32[]{:S(2)}, u32[]{:S(2)}) %collective-permute-start.8) | collective-permute-done | bytes 524320 | tf_op jit(solution)/shard_map/ppermute | solution.py:306
  100.4 2.6 %shard_map.84 = (bf16[32,32,128]{2,1,0:T(8,128)(2,1)S(1)}, bf16[32,32,128]{2,1,0:T(8,128)(2,1)S(1)}) custom-call(bf16[2,32,32,128]{3,2,1,0:T(8,128)(2,1)S(1)} %pad_maximum_fusion.1.near_ref, bf16[2,32,32,128]{3,2,1,0:T(8,128)(2,1)S(1)} %collective-permute-done.8.far_ref, bf16[24,128,256]{2,1,0:T(8,128)(2,1)} %shard_map.81.dressed, ...), custom_call_target="tpu_custom_call" | custom-call | flops 134217728 | bytes 4194304 | tf_op jit(solution)/shard_map/pallas_call | solution.py:22
  103.0 2.3 %collective-permute-start.13 = (bf16[32,32,128]{2,1,0:T(8,128)(2,1)S(1)}, bf16[32,32,128]{2,1,0:T(8,128)(2,1)S(1)}, u32[]{:S(2)}, u32[]{:S(2)}) collective-permute-start(bf16[32,32,128]{2,1,0:T(8,128)(2,1)S(1)} %get-tuple-element.40.refs_0_), channel_id=1, source_target_pairs={{0,24},{4,28},{8,16},{12,20},{16,8},{20,12},{24,0},{28,4},{1,25},{... | collective-permute-start | bytes 786440 | tf_op jit(solution)/shard_map/ppermute | solution.py:314
  105.2 6.4 %collective-permute-done.3.far_ref = bf16[2,32,32,128]{3,2,1,0:T(8,128)(2,1)S(1)} collective-permute-done((bf16[2,32,32,128]{3,2,1,0:T(8,128)(2,1)S(1)}, bf16[2,32,32,128]{3,2,1,0:T(8,128)(2,1)S(1)}, u32[]{:S(2)}, u32[]{:S(2)}) %collective-permute-start.3) | collective-permute-done | bytes 524320 | tf_op jit(solution)/shard_map/ppermute | solution.py:306
  111.6 0.8 collective-permute-start.14
  112.4 2.6 %shard_map.85 = (bf16[32,32,128]{2,1,0:T(8,128)(2,1)S(1)}, bf16[32,32,128]{2,1,0:T(8,128)(2,1)S(1)}) custom-call(bf16[2,32,32,128]{3,2,1,0:T(8,128)(2,1)S(1)} %pad_maximum_fusion.near_ref, bf16[2,32,32,128]{3,2,1,0:T(8,128)(2,1)S(1)} %collective-permute-done.3.far_ref, bf16[24,128,256]{2,1,0:T(8,128)(2,1)} %shard_map.81.dressed, ...), custom_call_target="tpu_custom_call" | custom-call | flops 134217728 | bytes 4194304 | tf_op jit(solution)/shard_map/pallas_call | solution.py:22
  115.0 6.1 %collective-permute-done.12.far_ref = bf16[2,32,32,128]{3,2,1,0:T(8,128)(2,1)S(1)} collective-permute-done((bf16[2,32,32,128]{3,2,1,0:T(8,128)(2,1)S(1)}, bf16[2,32,32,128]{3,2,1,0:T(8,128)(2,1)S(1)}, u32[]{:S(2)}, u32[]{:S(2)}) %collective-permute-start.12) | collective-permute-done | bytes 524320 | tf_op jit(solution)/shard_map/ppermute | solution.py:306
  121.2 2.6 %shard_map.86 = (bf16[32,32,128]{2,1,0:T(8,128)(2,1)S(1)}, bf16[32,32,128]{2,1,0:T(8,128)(2,1)S(1)}) custom-call(bf16[2,32,32,128]{3,2,1,0:T(8,128)(2,1)S(1)} %pad_maximum_fusion.3.near_ref, bf16[2,32,32,128]{3,2,1,0:T(8,128)(2,1)S(1)} %collective-permute-done.12.far_ref, bf16[24,128,256]{2,1,0:T(8,128)(2,1)} %shard_map.81.dressed, ...), custom_call_target="tpu_custom_call" | custom-call | flops 134217728 | bytes 4194304 | tf_op jit(solution)/shard_map/pallas_call | solution.py:22
  123.8 1.5 collective-permute-start.15
  125.3 1.4 collective-permute-start.16
  126.7 1.5 collective-permute-start.17
  128.2 2.2 %collective-permute-done.15.refs_1_ = bf16[32,32,128]{2,1,0:T(8,128)(2,1)S(1)} collective-permute-done((bf16[32,32,128]{2,1,0:T(8,128)(2,1)S(1)}, bf16[32,32,128]{2,1,0:T(8,128)(2,1)S(1)}, u32[]{:S(2)}, u32[]{:S(2)}) %collective-permute-start.15) | collective-permute-done | bytes 262176 | tf_op jit(solution)/shard_map/ppermute | solution.py:314
  130.4 14.1 %collective-permute-done.16.refs_4_ = bf16[32,32,128]{2,1,0:T(8,128)(2,1)S(1)} collective-permute-done((bf16[32,32,128]{2,1,0:T(8,128)(2,1)S(1)}, bf16[32,32,128]{2,1,0:T(8,128)(2,1)S(1)}, u32[]{:S(2)}, u32[]{:S(2)}) %collective-permute-start.16) | collective-permute-done | bytes 262176 | tf_op jit(solution)/shard_map/ppermute | solution.py:314
  144.5 4.9 %collective-permute-done.17.refs_5_ = bf16[32,32,128]{2,1,0:T(8,128)(2,1)S(1)} collective-permute-done((bf16[32,32,128]{2,1,0:T(8,128)(2,1)S(1)}, bf16[32,32,128]{2,1,0:T(8,128)(2,1)S(1)}, u32[]{:S(2)}, u32[]{:S(2)}) %collective-permute-start.17) | collective-permute-done | bytes 262176 | tf_op jit(solution)/shard_map/ppermute | solution.py:314
  149.4 3.2 %shard_map.87 = (bf16[32,64,256]{2,1,0:T(8,128)(2,1)S(1)}, bf16[32,64,256]{2,1,0:T(8,128)(2,1)}) custom-call(bf16[256,256]{1,0:T(8,128)(2,1)S(1)} %copy-done.11, bf16[32,32,128]{2,1,0:T(8,128)(2,1)S(1)} %get-tuple-element.42.refs_0_, bf16[32,32,128]{2,1,0:T(8,128)(2,1)S(1)} %collective-permute-done.15.refs_1_, ...), custom_call_target="tpu_custom_call" | custom-call | flops 536870912 | bytes 4325376 | tf_op jit(solution)/shard_map/pallas_call | solution.py:22
  152.6 2.9 %collective-permute-done.18 = bf16[32,64,256]{2,1,0:T(8,128)(2,1)S(1)} collective-permute-done((bf16[32,64,256]{2,1,0:T(8,128)(2,1)}, bf16[32,64,256]{2,1,0:T(8,128)(2,1)S(1)}, u32[]{:S(2)}, u32[]{:S(2)}) %collective-permute-start.18) | collective-permute-done | bytes 1048608 | tf_op jit(solution)/shard_map/ppermute | solution.py:317
  155.5 1.1 add_bitcast_fusion
  (45 shorter events, 1.1 us)
Async XLA Ops:
  0.0 0.9 copy-start.3
  3.5 3.1 %copy-start.2 = (bf16[32,256,64]{1,2,0:T(8,128)(2,1)S(1)}, bf16[32,256,64]{1,2,0:T(8,128)(2,1)}, u32[]{:S(2)}) copy-start(bf16[32,256,64]{1,2,0:T(8,128)(2,1)} %param.7) | copy-start | bytes 3145732
  3.5 3.5 %copy-start.12 = (s32[512,1]{0,1:T(1,128)S(1)}, s32[512,1]{0,1:T(1,128)}, u32[]{:S(2)}) copy-start(s32[512,1]{0,1:T(1,128)} %param.12) | copy-start | bytes 6148
  3.5 3.5 %copy-start.13 = (s32[512]{0:T(512)S(1)}, s32[512]{0:T(512)}, u32[]{:S(2)}) copy-start(s32[512]{0:T(512)} %sub.1) | copy-start | bytes 6148
  3.5 3.4 %copy-start.14 = (s32[512]{0:T(512)S(1)}, s32[512]{0:T(512)}, u32[]{:S(2)}) copy-start(s32[512]{0:T(512)} %row.1) | copy-start | bytes 6148
  3.6 3.4 %copy-start.15 = (s32[8]{0:T(128)S(1)}, s32[8]{0:T(128)}, u32[]{:S(2)}) copy-start(s32[8]{0:T(128)} %count.1) | copy-start | bytes 100
  3.6 7.0 %collective-permute-start.1 = (bf16[16,256,128]{2,1,0:T(8,128)(2,1)S(1)}, bf16[16,256,128]{2,1,0:T(8,128)(2,1)S(1)}, u32[]{:S(2)}, u32[]{:S(2)}) collective-permute-start(bf16[16,256,128]{2,1,0:T(8,128)(2,1)S(1)} %shard_map.74.rest_0_), channel_id=1, source_target_pairs={{0,1},{1,0},{2,3},{3,2},{4,5},{5,4},{6,7},{7,6},{8,9},{9,8},{10,11... | collective-permute-start | bytes 3145736 | tf_op jit(solution)/shard_map/ppermute | solution.py:284
  6.4 4.2 %collective-permute-start.2 = (bf16[16,256,128]{2,1,0:T(8,128)(2,1)S(1)}, bf16[16,256,128]{2,1,0:T(8,128)(2,1)S(1)}, u32[]{:S(2)}, u32[]{:S(2)}) collective-permute-start(bf16[16,256,128]{2,1,0:T(8,128)(2,1)S(1)} %shard_map.75.early), channel_id=1, source_target_pairs={{0,1},{1,0},{2,3},{3,2},{4,5},{5,4},{6,7},{7,6},{8,9},{9,8},{10,11... | collective-permute-start | bytes 3145736 | tf_op jit(solution)/shard_map/ppermute | solution.py:284
  6.6 4.0 %collective-permute-start = (bf16[32,64,256]{2,1,0:T(8,128)(2,1)S(1)}, bf16[32,64,256]{2,1,0:T(8,128)(2,1)S(1)}, u32[]{:S(2)}, u32[]{:S(2)}) collective-permute-start(bf16[32,64,256]{2,1,0:T(8,128)(2,1)S(1)} %bitcast.4), channel_id=1, source_target_pairs={{0,1},{1,0},{2,3},{3,2},{4,5},{5,4},{6,7},{7,6},{8,9},{9,8},{10,11... | collective-permute-start | bytes 3145736 | tf_op jit(solution)/shard_map/ppermute | solution.py:275
  9.9 0.7 copy-start.10
  10.6 1.0 copy-start
  16.3 55.9 %all-to-all-start = ((bf16[8,32,32,128]{3,2,1,0:T(8,128)(2,1)}), bf16[8,32,32,128]{3,2,1,0:T(8,128)(2,1)}, u32[]{:S(2)}, u32[]{:S(2)}) async-start(bf16[8,32,32,128]{3,2,1,0:T(8,128)(2,1)} %shard_map.77.rest_0_), calls=%async_computation | async-start | bytes 4194304 | tf_op jit(solution)/shard_map/all_to_all | solution.py:290
  26.3 0.8 copy-start.4
  27.1 15.0 %copy-start.1 = (bf16[16,256,128]{2,1,0:T(8,128)(2,1)S(1)}, bf16[16,256,128]{2,1,0:T(8,128)(2,1)}, u32[]{:S(2)}) copy-start(bf16[16,256,128]{2,1,0:T(8,128)(2,1)} %copy-done) | copy-start | bytes 3145732
  27.1 15.0 %collective-permute-start.4 = (bf16[8,128,256]{2,1,0:T(8,128)(2,1)}, bf16[8,128,256]{2,1,0:T(8,128)(2,1)S(1)}, u32[]{:S(2)}, u32[]{:S(2)}) collective-permute-start(bf16[8,128,256]{2,1,0:T(8,128)(2,1)} %get-tuple-element.32.rest_0_), channel_id=1, source_target_pairs={{0,2},{1,3},{2,0},{3,1},{4,6},{5,7},{6,4},{7,5},{8,10},{9,11},{10,... | collective-permute-start | bytes 1572872 | tf_op jit(solution)/shard_map/ppermute | solution.py:302
  31.6 0.8 copy-start.6
  32.4 20.9 %collective-permute-start.5 = (bf16[8,128,256]{2,1,0:T(8,128)(2,1)}, bf16[8,128,256]{2,1,0:T(8,128)(2,1)S(1)}, u32[]{:S(2)}, u32[]{:S(2)}) collective-permute-start(bf16[8,128,256]{2,1,0:T(8,128)(2,1)} %get-tuple-element.34.rest_0_), channel_id=1, source_target_pairs={{0,2},{1,3},{2,0},{3,1},{4,6},{5,7},{6,4},{7,5},{8,10},{9,11},{10,... | collective-permute-start | bytes 1572872 | tf_op jit(solution)/shard_map/ppermute | solution.py:302
  45.1 11.2 %copy-start.8 = (bf16[8,128,256]{2,1,0:T(8,128)(2,1)}, bf16[8,128,256]{2,1,0:T(8,128)(2,1)S(1)}, u32[]{:S(2)}) copy-start(bf16[8,128,256]{2,1,0:T(8,128)(2,1)S(1)} %get-tuple-element.35.refs_4_) | copy-start | bytes 1572868
  45.1 33.0 %collective-permute-start.6 = (bf16[8,128,256]{2,1,0:T(8,128)(2,1)}, bf16[8,128,256]{2,1,0:T(8,128)(2,1)}, u32[]{:S(2)}, u32[]{:S(2)}) collective-permute-start(bf16[8,128,256]{2,1,0:T(8,128)(2,1)} %get-tuple-element.36.rest_0_), channel_id=1, source_target_pairs={{0,2},{1,3},{2,0},{3,1},{4,6},{5,7},{6,4},{7,5},{8,10},{9,11},{10,... | collective-permute-start | bytes 1572872 | tf_op jit(solution)/shard_map/ppermute | solution.py:302
  56.3 24.8 %collective-permute-start.7 = (bf16[8,128,256]{2,1,0:T(8,128)(2,1)}, bf16[8,128,256]{2,1,0:T(8,128)(2,1)S(1)}, u32[]{:S(2)}, u32[]{:S(2)}) collective-permute-start(bf16[8,128,256]{2,1,0:T(8,128)(2,1)} %get-tuple-element.38), channel_id=1, source_target_pairs={{0,2},{1,3},{2,0},{3,1},{4,6},{5,7},{6,4},{7,5},{8,10},{9,11},{10,... | collective-permute-start | bytes 1572872 | tf_op jit(solution)/shard_map/ppermute | solution.py:302
  74.1 4.6 %copy-start.5 = (bf16[8,128,256]{2,1,0:T(8,128)(2,1)S(1)}, bf16[8,128,256]{2,1,0:T(8,128)(2,1)}, u32[]{:S(2)}) copy-start(bf16[8,128,256]{2,1,0:T(8,128)(2,1)} %copy-done.4) | copy-start | bytes 1572868
  74.1 4.6 %copy-start.7 = (bf16[8,128,256]{2,1,0:T(8,128)(2,1)S(1)}, bf16[8,128,256]{2,1,0:T(8,128)(2,1)}, u32[]{:S(2)}) copy-start(bf16[8,128,256]{2,1,0:T(8,128)(2,1)} %copy-done.6) | copy-start | bytes 1572868
  74.2 4.6 %copy-start.9 = (bf16[8,128,256]{2,1,0:T(8,128)(2,1)S(1)}, bf16[8,128,256]{2,1,0:T(8,128)(2,1)}, u32[]{:S(2)}) copy-start(bf16[8,128,256]{2,1,0:T(8,128)(2,1)} %copy-done.8) | copy-start | bytes 1572868
  74.2 14.9 %collective-permute-start.9 = (bf16[2,32,32,128]{3,2,1,0:T(8,128)(2,1)S(1)}, bf16[2,32,32,128]{3,2,1,0:T(8,128)(2,1)S(1)}, u32[]{:S(2)}, u32[]{:S(2)}) collective-permute-start(bf16[2,32,32,128]{3,2,1,0:T(8,128)(2,1)S(1)} %pad_maximum_fusion.2.near_ref), channel_id=1, source_target_pairs={{0,2},{1,3},{2,0},{3,1},{4,6},{5,7},{6,4},{7,5},{8,10},{9,11},{10,... | collective-permute-start | bytes 1572872 | tf_op jit(solution)/shard_map/ppermute | solution.py:306
  75.8 24.6 %collective-permute-start.8 = (bf16[2,32,32,128]{3,2,1,0:T(8,128)(2,1)S(1)}, bf16[2,32,32,128]{3,2,1,0:T(8,128)(2,1)S(1)}, u32[]{:S(2)}, u32[]{:S(2)}) collective-permute-start(bf16[2,32,32,128]{3,2,1,0:T(8,128)(2,1)S(1)} %pad_maximum_fusion.1.near_ref), channel_id=1, source_target_pairs={{0,2},{1,3},{2,0},{3,1},{4,6},{5,7},{6,4},{7,5},{8,10},{9,11},{10,... | collective-permute-start | bytes 1572872 | tf_op jit(solution)/shard_map/ppermute | solution.py:306
  76.5 35.1 %collective-permute-start.3 = (bf16[2,32,32,128]{3,2,1,0:T(8,128)(2,1)S(1)}, bf16[2,32,32,128]{3,2,1,0:T(8,128)(2,1)S(1)}, u32[]{:S(2)}, u32[]{:S(2)}) collective-permute-start(bf16[2,32,32,128]{3,2,1,0:T(8,128)(2,1)S(1)} %pad_maximum_fusion.near_ref), channel_id=1, source_target_pairs={{0,2},{1,3},{2,0},{3,1},{4,6},{5,7},{6,4},{7,5},{8,10},{9,11},{10,... | collective-permute-start | bytes 1572872 | tf_op jit(solution)/shard_map/ppermute | solution.py:306
  78.1 43.0 %collective-permute-start.12 = (bf16[2,32,32,128]{3,2,1,0:T(8,128)(2,1)S(1)}, bf16[2,32,32,128]{3,2,1,0:T(8,128)(2,1)S(1)}, u32[]{:S(2)}, u32[]{:S(2)}) collective-permute-start(bf16[2,32,32,128]{3,2,1,0:T(8,128)(2,1)S(1)} %pad_maximum_fusion.3.near_ref), channel_id=1, source_target_pairs={{0,2},{1,3},{2,0},{3,1},{4,6},{5,7},{6,4},{7,5},{8,10},{9,11},{10,... | collective-permute-start | bytes 1572872 | tf_op jit(solution)/shard_map/ppermute | solution.py:306
  91.7 20.7 %collective-permute-start.10 = (bf16[32,32,128]{2,1,0:T(8,128)(2,1)S(1)}, bf16[32,32,128]{2,1,0:T(8,128)(2,1)S(1)}, u32[]{:S(2)}, u32[]{:S(2)}) collective-permute-start(bf16[32,32,128]{2,1,0:T(8,128)(2,1)S(1)} %get-tuple-element.39.refs_0_), channel_id=1, source_target_pairs={{0,28},{4,24},{8,20},{12,16},{16,12},{20,8},{24,4},{28,0},{1,29},{... | collective-permute-start | bytes 786440 | tf_op jit(solution)/shard_map/ppermute | solution.py:314
  94.1 18.4 %collective-permute-start.11 = (bf16[32,32,128]{2,1,0:T(8,128)(2,1)S(1)}, bf16[32,32,128]{2,1,0:T(8,128)(2,1)S(1)}, u32[]{:S(2)}, u32[]{:S(2)}) collective-permute-start(bf16[32,32,128]{2,1,0:T(8,128)(2,1)S(1)} %get-tuple-element.41), channel_id=1, source_target_pairs={{0,8},{4,12},{8,0},{12,4},{16,24},{20,28},{24,16},{28,20},{1,9},{5... | collective-permute-start | bytes 786440 | tf_op jit(solution)/shard_map/ppermute | solution.py:314
  103.0 18.2 %collective-permute-start.13 = (bf16[32,32,128]{2,1,0:T(8,128)(2,1)S(1)}, bf16[32,32,128]{2,1,0:T(8,128)(2,1)S(1)}, u32[]{:S(2)}, u32[]{:S(2)}) collective-permute-start(bf16[32,32,128]{2,1,0:T(8,128)(2,1)S(1)} %get-tuple-element.40.refs_0_), channel_id=1, source_target_pairs={{0,24},{4,28},{8,16},{12,20},{16,8},{20,12},{24,0},{28,4},{1,25},{... | collective-permute-start | bytes 786440 | tf_op jit(solution)/shard_map/ppermute | solution.py:314
  111.6 9.5 %collective-permute-start.14 = (bf16[32,32,128]{2,1,0:T(8,128)(2,1)S(1)}, bf16[32,32,128]{2,1,0:T(8,128)(2,1)S(1)}, u32[]{:S(2)}, u32[]{:S(2)}) collective-permute-start(bf16[32,32,128]{2,1,0:T(8,128)(2,1)S(1)} %get-tuple-element.44), channel_id=1, source_target_pairs={{0,12},{4,8},{8,4},{12,0},{16,28},{20,24},{24,20},{28,16},{1,13},{... | collective-permute-start | bytes 786440 | tf_op jit(solution)/shard_map/ppermute | solution.py:314
  121.1 28.2 %copy-start.11 = (bf16[256,256]{1,0:T(8,128)(2,1)S(1)}, bf16[256,256]{1,0:T(8,128)(2,1)}, u32[]{:S(2)}) copy-start(bf16[256,256]{1,0:T(8,128)(2,1)} %copy-done.10) | copy-start | bytes 393220
  123.8 6.7 %collective-permute-start.15 = (bf16[32,32,128]{2,1,0:T(8,128)(2,1)S(1)}, bf16[32,32,128]{2,1,0:T(8,128)(2,1)S(1)}, u32[]{:S(2)}, u32[]{:S(2)}) collective-permute-start(bf16[32,32,128]{2,1,0:T(8,128)(2,1)S(1)} %get-tuple-element.45), channel_id=1, source_target_pairs={{0,4},{4,0},{8,12},{12,8},{16,20},{20,16},{24,28},{28,24},{1,5},{5... | collective-permute-start | bytes 786440 | tf_op jit(solution)/shard_map/ppermute | solution.py:314
  125.3 19.2 %collective-permute-start.16 = (bf16[32,32,128]{2,1,0:T(8,128)(2,1)S(1)}, bf16[32,32,128]{2,1,0:T(8,128)(2,1)S(1)}, u32[]{:S(2)}, u32[]{:S(2)}) collective-permute-start(bf16[32,32,128]{2,1,0:T(8,128)(2,1)S(1)} %get-tuple-element.46), channel_id=1, source_target_pairs={{0,16},{4,20},{8,24},{12,28},{16,0},{20,4},{24,8},{28,12},{1,17},{... | collective-permute-start | bytes 786440 | tf_op jit(solution)/shard_map/ppermute | solution.py:314
  126.7 22.7 %collective-permute-start.17 = (bf16[32,32,128]{2,1,0:T(8,128)(2,1)S(1)}, bf16[32,32,128]{2,1,0:T(8,128)(2,1)S(1)}, u32[]{:S(2)}, u32[]{:S(2)}) collective-permute-start(bf16[32,32,128]{2,1,0:T(8,128)(2,1)S(1)} %get-tuple-element.43.refs_0_), channel_id=1, source_target_pairs={{0,20},{4,16},{8,28},{12,24},{16,4},{20,0},{24,12},{28,8},{1,21},{... | collective-permute-start | bytes 786440 | tf_op jit(solution)/shard_map/ppermute | solution.py:314
  152.6 2.9 %collective-permute-start.18 = (bf16[32,64,256]{2,1,0:T(8,128)(2,1)}, bf16[32,64,256]{2,1,0:T(8,128)(2,1)S(1)}, u32[]{:S(2)}, u32[]{:S(2)}) collective-permute-start(bf16[32,64,256]{2,1,0:T(8,128)(2,1)} %get-tuple-element.48), channel_id=1, source_target_pairs={{0,1},{1,0},{2,3},{3,2},{4,5},{5,4},{6,7},{7,6},{8,9},{9,8},{10,11... | collective-permute-start | bytes 3145736 | tf_op jit(solution)/shard_map/ppermute | solution.py:317

commit v3 on v2

--- a/solution.py
+++ b/solution.py
@@ -9,14 +9,15 @@
 
 F32, BF16 = jnp.float32, jnp.bfloat16
 TILE_PARTS = 4
-VMEM_LIMIT = 50 * 1024 * 1024
+VMEM_LIMIT = 16 * 1024 * 1024
+TILE_VMEM_LIMIT = 50 * 1024 * 1024
 
 
 def dot(a, b, dims=(((1,), (0,)), ((), ()))):
     return lax.dot_general(a, b, dims, preferred_element_type=F32)
 
 
-def call(body, outs, ins, flops, scratch=(), early=()):
+def call(body, outs, ins, flops, scratch=(), early=(), limit=VMEM_LIMIT):
     whole = pl.BlockSpec(memory_space=pltpu.VMEM)
     moved = sum(2 * x.size for x in ins) + sum(2 * x.size for x in outs)
     return pl.pallas_call(
@@ -26,7 +27,7 @@
         out_specs=[whole] * len(outs),
         scratch_shapes=list(scratch),
         cost_estimate=pl.CostEstimate(flops=flops, bytes_accessed=moved, transcendentals=0),
-        compiler_params=pltpu.CompilerParams(vmem_limit_bytes=VMEM_LIMIT),
+        compiler_params=pltpu.CompilerParams(vmem_limit_bytes=limit),
     )(*ins, *early)
 
 
@@ -51,10 +52,28 @@
     return call(order_body, outs, (orbitals,), count * vir, [pltpu.VMEM((count, vir), BF16)])
 
 
-def gather_body(src, sub, row, count, orbitals, early, source, target, held, ahead, back):
+def source_body(src, sub, orbitals, early, source, held, ahead):
+    held[...] = orbitals[...].astype(F32)
+    nodes = lax.axis_size("occ")
+    slots = src.shape[0] // nodes
+    half = slots // 2
+    blocks = held.shape[0] // nodes
+    core = lax.axis_index("ao") % 2
+    for k in range(nodes):
+
+        def step(j, carry):
+            slot = k * slots + core * half + j
+            ahead[pl.ds(k * half + j, 1), :] = held[pl.ds(src[slot] * blocks + sub[slot], 1), :]
+            return carry
+
+        lax.fori_loop(0, half, step, 0, unroll=8)
+    source[...] = ahead[...].astype(BF16)
+
+
+def target_body(row, count, orbitals, early, target, held, back):
     held[...] = orbitals[...].astype(F32)
     nodes = count.shape[0]
-    slots = src.shape[0] // nodes
+    slots = row.shape[0] // nodes
     half = slots // 2
     blocks = held.shape[0] // nodes
     own, core = lax.axis_index("occ"), lax.axis_index("ao") % 2
@@ -63,59 +82,83 @@
 
         def step(j, carry):
             place = core * half + j
-            slot = k * slots + place
-            ahead[pl.ds(k * half + j, 1), :] = held[pl.ds(src[slot] * blocks + sub[slot], 1), :]
             line = held[pl.ds(partner * blocks + row[partner * slots + place], 1), :]
             back[pl.ds(k * half + j, 1), :] = jnp.where(place < count[partner], line, 0.0)
             return carry
 
         lax.fori_loop(0, half, step, 0, unroll=8)
-    source[...] = ahead[...].astype(BF16)
     target[...] = back[...].astype(BF16)
 
 
-def gather_rows(src, sub, row, count, orbitals, early):
-    slots, vir = src.shape[0] // 2, orbitals.shape[1]
+def gather(body, tables, orbitals, early):
+    slots, vir = tables[0].shape[0] // 2, orbitals.shape[1]
     scalar = pl.BlockSpec(memory_space=pltpu.SMEM)
     whole = pl.BlockSpec(memory_space=pltpu.VMEM)
     return pl.pallas_call(
-        gather_body,
-        out_shape=[jax.ShapeDtypeStruct((slots, vir), BF16)] * 2,
-        in_specs=[scalar] * 4 + [whole, pl.BlockSpec(memory_space=pl.ANY)],
-        out_specs=[whole] * 2,
-        scratch_shapes=[pltpu.VMEM(orbitals.shape, F32)] + [pltpu.VMEM((slots, vir), F32)] * 2,
-        cost_estimate=pl.CostEstimate(flops=slots * vir, bytes_accessed=8 * slots * vir, transcendentals=0),
+        body,
+        out_shape=jax.ShapeDtypeStruct((slots, vir), BF16),
+        in_specs=[scalar] * 2 + [whole, pl.BlockSpec(memory_space=pl.ANY)],
+        out_specs=whole,
+        scratch_shapes=[pltpu.VMEM(orbitals.shape, F32), pltpu.VMEM((slots, vir), F32)],
+        cost_estimate=pl.CostEstimate(flops=slots * vir, bytes_accessed=4 * slots * vir, transcendentals=0),
         compiler_params=pltpu.CompilerParams(vmem_limit_bytes=VMEM_LIMIT),
-    )(src, sub, row, count, orbitals, early)
+    )(*tables, orbitals, early)
 
 
 def rows_body(rows_ref, mine_ref, other_ref, *rest):
-    out, scratch = rest[-2:]
-    occ = mine_ref.shape[0]
-    count, _ = rows_ref.shape
-    width = scratch.shape[1]
+    out = rest[-1]
+    nodes, occ, slots, width = out.shape
     rows = rows_ref[...]
 
     def step(n, carry):
         i = 2 * n
         right = jnp.concatenate([mine_ref[i], other_ref[i], mine_ref[i + 1], other_ref[i + 1]], 0)
-        product = dot(rows, right, (((1,), (1,)), ((), ())))
-        scratch[pl.ds(i, count, stride=occ), :] = product[:, :width]
-        scratch[pl.ds(i + 1, count, stride=occ), :] = product[:, width:]
+        product = dot(rows, right, (((1,), (1,)), ((), ()))).astype(BF16)
+        for j in range(2):
+            out[:, i + j] = product[:, j * width:(j + 1) * width].reshape(nodes, slots, width)
         return carry
 
     lax.fori_loop(0, occ // 2, step, 0, unroll=4)
-    block = count // out.shape[0] * occ
-    for k in range(out.shape[0]):
-        out[k] = scratch[k * block:(k + 1) * block, :].reshape(out.shape[1:]).astype(BF16)
 
 
 def pair_rows(rows, mine, other, nodes, early):
     occ, part, vir = mine.shape
     count = rows.shape[0]
-    outs = [jax.ShapeDtypeStruct((nodes, count // nodes, occ, 2 * part), BF16)]
-    scratch = [pltpu.VMEM((count * occ, 2 * part), F32)]
-    return call(rows_body, outs, (rows, mine, other), 4 * count * occ * vir * part, scratch, early)[0]
+    outs = [jax.ShapeDtypeStruct((nodes, occ, count // nodes, 2 * part), BF16)]
+    return call(rows_body, outs, (rows, mine, other), 4 * count * occ * vir * part, (), early, TILE_VMEM_LIMIT)[0]
+
+
+def turn_body(groups, meta, *refs):
+    blocks, (out, held) = refs[:groups], refs[-2:]
+    _, occ, slots, width = blocks[0].shape
+    for n in range(groups):
+        base = n * occ * slots
+        held[base:base + occ * slots, :] = blocks[n][0].astype(F32).reshape(occ * slots, width)
+        for t in range(slots):
+            out[n, t] = held[pl.ds(base + t, occ, stride=slots), :].astype(BF16)
+
+
+def turn(own, arrived, partners, early):
+    groups = len(partners)
+    _, occ, slots, width = arrived.shape
+    specs = [
+        pl.BlockSpec((1, occ, slots, width), lambda n, ref, k=k: (ref[0] ^ k, 0, 0, 0)) for k in partners
+    ]
+    return pl.pallas_call(
+        functools.partial(turn_body, groups),
+        out_shape=jax.ShapeDtypeStruct((groups, slots, occ, width), BF16),
+        grid_spec=pltpu.PrefetchScalarGridSpec(
+            num_scalar_prefetch=1,
+            grid=(1,),
+            in_specs=specs + [pl.BlockSpec(memory_space=pl.ANY)] * len(early),
+            out_specs=pl.BlockSpec(memory_space=pltpu.VMEM),
+            scratch_shapes=[pltpu.VMEM((groups * occ * slots, width), F32)],
+        ),
+        cost_estimate=pl.CostEstimate(
+            flops=groups * occ * slots * width, bytes_accessed=4 * groups * occ * slots * width, transcendentals=0
+        ),
+        compiler_params=pltpu.CompilerParams(vmem_limit_bytes=VMEM_LIMIT),
+    )(jnp.reshape(own, (1,)), *[arrived] * groups, *early)
 
 
 def start_copies(other_core, start, tiles, held, sems):
@@ -187,7 +230,7 @@
         cost_estimate=pl.CostEstimate(
             flops=flops, bytes_accessed=2 * count * sig * nu * 2, transcendentals=0
         ),
-        compiler_params=pltpu.CompilerParams(vmem_limit_bytes=VMEM_LIMIT),
+        compiler_params=pltpu.CompilerParams(vmem_limit_bytes=TILE_VMEM_LIMIT),
     )(ins[0], tiles, *ins[1:], *early)
 
 
@@ -227,6 +270,14 @@
     scratch = [pltpu.VMEM((groups * occ * slots, width), F32)]
     flops = 4 * groups * occ * slots * width * width
     return call(product_body, outs, (near_rows, far_rows, *tiles), flops, scratch, early)
+
+
+def copy_body(rows, *rest):
+    rest[-1][...] = rows[...]
+
+
+def rows_after(rows, early):
+    return call(copy_body, [jax.ShapeDtypeStruct(rows.shape, BF16)], (rows,), rows.size, (), early)[0]
 
 
 def back_body(nodes, rows_ref, *refs):
@@ -285,7 +336,7 @@
 
     given, first_parts = give(0, ())
     given, second_parts = give(half // 2, [given])
-    source_rows, target_rows = gather_rows(tile_src[:, 0], tile_sub, tile_row, tile_count, orbitals, given)
+    source_rows = gather(source_body, (tile_src[:, 0], tile_sub), orbitals, given)
     sent = pair_rows(source_rows, mine, other, nodes, (first_parts, second_parts))
     arrived = lax.all_to_all(sent, "occ", split_axis=0, concat_axis=0, tiled=True)
     parts, early = [], [sent]
@@ -300,18 +351,24 @@
         )
         early = [there]
         parts += [here, lax.ppermute(there, "ao", far)]
+    target_rows = gather(target_body, (tile_row, tile_count), orbitals, early[0])
     tiles_done = [dress(parts[:-2]), *parts[-2:]]
     units = [[nodes - 1 - n, (n + nodes // 2 - 2) % (nodes // 2)] for n in range(nodes // 2)]
-    blocks_of = [jnp.stack([arrived[own ^ k] for k in unit]) for unit in units]
-    far_blocks = [lax.ppermute(x, "ao", far) for x in blocks_of]
+    wait_for = {2: (0,), 3: (1,)}
+    blocks_of, far_blocks = [], []
+    for unit in units:
+        blocks_of.append(turn(own, arrived, unit, blocks_of[-1:]))
+        far_blocks.append(lax.ppermute(blocks_of[-1], "ao", far))
     returned, early = {}, []
     for n, unit in enumerate(units):
         made = products(blocks_of[n], far_blocks[n], tiles_done, early)
         early = [made[0]]
-        if n >= 1:
-            early += [returned[k] for k in units[n - 1]]
+        for m in wait_for.get(n, ()):
+            early += [returned[k] for k in units[m]]
         for k, x in zip(unit, made):
             returned[k] = lax.ppermute(x, "occ", [(o, o ^ k) for o in range(nodes)]) if k else x
+    tied = [returned[k] for m in (2,) for k in units[m]]
+    target_rows = rows_after(target_rows, tied)
     returned = [returned[k] for k in range(nodes)]
     keep, give_up = back_transform(target_rows, returned)
     return jnp.swapaxes(keep + lax.ppermute(give_up, "ao", near), 1, 2)

time: 157 us -> 140 us (0.89)
  waiting for transfers between devices: 81.1 us -> 71.2 us
  Pallas kernels: 40.4 us -> 33.9 us
  local copies, waits for them, and re-layouts: 6.14 us -> 3.41 us
  starting transfers between devices: 27.4 us -> 30.1 us
    ppermute x7, waiting for transfers between devices: 21.2 us -> 8.96 us  [shards(): lax.ppermute(x, 'occ', [(o, o ^ k) for o in range(nodes)])]
    pallas_call x8 -> x9, Pallas kernels: 20.9 us -> 11.3 us  [call(): pl.pallas_call(body, out_shape=outs, in_specs=[whole] * len(ins) + [pl.Bl...]
    pallas_call x1 -> x6, Pallas kernels: 2.92 us -> 6.6 us  [the longest x2 4.05 us: gather(): pl.pallas_call(body, out_shape=jax.ShapeDtypeStruct((slots, vir), BF16),...]
    ppermute x7, starting transfers between devices: 9.88 us -> 12.6 us  [shards(): lax.ppermute(x, 'occ', [(o, o ^ k) for o in range(nodes)])]
    dynamic_slice x1 -> x0, local copies, waits for them, and re-layouts: 1.94 us -> none  [shards(): blocks_of = [jnp.stack([arrived[own ^ k] for k in unit]) for unit in units]]
    unnamed x32 -> x42, local copies, waits for them, and re-layouts: 4.2 us -> 3.41 us
  transfers between devices with their start and end apart: 20 -> 20, of which waited for: 11 -> 13; matrix products, arithmetic and copies ran while one was open for 1% -> 0% of each run, Pallas kernels for 17% -> 19%
where the time goes in v3:
time: 140 us
  waiting for transfers between devices  71.2 us (51%)
  Pallas kernels  33.9 us (24%)
  starting transfers between devices  30.1 us (22%)
  local copies, waits for them, and re-layouts  3.41 us (2%)
    ppermute x4, waiting for transfers between devices, shards(): far_blocks.append(lax.ppermute(blocks_of[-1], 'ao', far))  28.1 us
    pallas_call x6, Pallas kernels, tile_call(): pl.pallas_call(body, out_shape=outs, in_specs=[whole, away] + [whole] * (...  16 us
    ppermute x4, waiting for transfers between devices, shards(): parts += [here, lax.ppermute(there, 'ao', far)]  15.5 us
    all_to_all x1, waiting for transfers between devices, shards(): lax.all_to_all(sent, 'occ', split_axis=0, concat_axis=0, tiled=True)  14.3 us
    ppermute x7, starting transfers between devices, shards(): lax.ppermute(x, 'occ', [(o, o ^ k) for o in range(nodes)])  12.6 us
    pallas_call x9, Pallas kernels, call(): pl.pallas_call(body, out_shape=outs, in_specs=[whole] * len(ins) + [pl.Bl...  11.3 us
    ppermute x7, waiting for transfers between devices, shards(): lax.ppermute(x, 'occ', [(o, o ^ k) for o in range(nodes)])  8.96 us
    all_to_all x1, starting transfers between devices, shards(): lax.all_to_all(sent, 'occ', split_axis=0, concat_axis=0, tiled=True)  6.98 us
  transfers between devices with their start and end apart: 20, of which 13 were waited for; matrix products, arithmetic and copies ran while one was open for 0% of the time, Pallas kernels for 19%

profile of v3, /device:TPU:0, one launch (start us, length us, event | category | flops | bytes accessed | tf_op | source)
XLA Modules:
  0.0 140.1 jit_solution(1403310382243726850)
XLA Ops:
  0.0 0.9 copy-done.5
  1.2 2.3 %shard_map.74.rest_0_ = bf16[16,256,128]{2,1,0:T(8,128)(2,1)S(1)} custom-call(bf16[256,512]{1,0:T(8,128)(2,1)S(1)} %get-tuple-element.25.left_ref, bf16[64,512,128]{2,1,0:T(8,128)(2,1)} %tiles.11), custom_call_target="tpu_custom_call" | custom-call | flops 536870912 | bytes 4194304 | tf_op jit(solution)/shard_map/pallas_call | solution.py:224
  4.1 2.3 %shard_map.75.early = bf16[16,256,128]{2,1,0:T(8,128)(2,1)S(1)} custom-call(bf16[256,512]{1,0:T(8,128)(2,1)S(1)} %get-tuple-element.25.left_ref, bf16[64,512,128]{2,1,0:T(8,128)(2,1)} %tiles.11, bf16[16,256,128]{2,1,0:T(8,128)(2,1)S(1)} %shard_map.74.rest_0_), custom_call_target="tpu_custom_call" | custom-call | flops 536870912 | bytes 4194304 | tf_op jit(solution)/shard_map/pallas_call | solution.py:224
  7.0 1.9 %shard_map.76.rows_ref = bf16[256,256]{1,0:T(8,128)(2,1)S(1)} custom-call(s32[512]{0:T(512)S(1)} %bitcast.7, s32[512]{0:T(512)S(1)} %copy-done.18, bf16[512,256]{1,0:T(8,128)(2,1)S(1)} %copy-done.6, bf16[16,256,128]{2,1,0:T(8,128)(2,1)S(1)} %shard_map.75.early), custom_call_target="tpu_custom_call" | custom-call | flops 65536 | bytes 262144 | tf_op jit(solution)/shard_map/pallas_call | solution.py:97
  9.1 1.5 %collective-permute-done.2.other_ref = bf16[32,64,256]{2,1,0:T(8,128)(2,1)S(1)} collective-permute-done((bf16[32,64,256]{2,1,0:T(8,128)(2,1)S(1)}, bf16[32,64,256]{2,1,0:T(8,128)(2,1)S(1)}, u32[]{:S(2)}, u32[]{:S(2)}) %collective-permute-start.2) | collective-permute-done | bytes 1048608 | tf_op jit(solution)/shard_map/ppermute | solution.py:326
  10.6 2.7 %shard_map.77.rest_0_ = bf16[8,32,32,128]{3,2,1,0:T(8,128)(2,1)} custom-call(bf16[256,256]{1,0:T(8,128)(2,1)S(1)} %shard_map.76.rows_ref, bf16[32,64,256]{2,1,0:T(8,128)(2,1)S(1)} %bitcast.6, bf16[32,64,256]{2,1,0:T(8,128)(2,1)S(1)} %collective-permute-done.2.other_ref, bf16[16,256,128]{2,1,0:T(8,128)(2,1)S(1)} %collective-permute-done.1.rest_0_.other, ...), custom_call_target="tpu_custom_call" | custom-call | flops 536870912 | bytes 4325376 | tf_op jit(solution)/shard_map/pallas_call | solution.py:23
  13.3 7.0 %all-to-all-start = ((bf16[8,32,32,128]{3,2,1,0:T(8,128)(2,1)}), bf16[8,32,32,128]{3,2,1,0:T(8,128)(2,1)S(1)}, u32[]{:S(2)}, u32[]{:S(2)}) async-start(bf16[8,32,32,128]{3,2,1,0:T(8,128)(2,1)} %shard_map.77.rest_0_), calls=%async_computation | async-start | bytes 4194304 | tf_op jit(solution)/shard_map/all_to_all | solution.py:341
  20.3 2.2 %shard_map.78 = (bf16[8,128,256]{2,1,0:T(8,128)(2,1)S(1)}, bf16[8,128,256]{2,1,0:T(8,128)(2,1)S(1)}) custom-call(bf16[256,512]{1,0:T(8,128)(2,1)S(1)} %get-tuple-element.25.left_ref, bf16[64,512,128]{2,1,0:T(8,128)(2,1)} %tiles.11, bf16[16,256,128]{2,1,0:T(8,128)(2,1)S(1)} %collective-permute-done.1.rest_0_.other, ...), custom_call_target="tpu_custom_call" | custom-call | flops 536870912 | bytes 2097152 | tf_op jit(solution)/shard_map/pallas_call | solution.py:224
  22.5 0.8 copy-done.11
  23.3 1.5 %collective-permute-start.3 = (bf16[8,128,256]{2,1,0:T(8,128)(2,1)S(1)}, bf16[8,128,256]{2,1,0:T(8,128)(2,1)S(1)}, u32[]{:S(2)}, u32[]{:S(2)}) collective-permute-start(bf16[8,128,256]{2,1,0:T(8,128)(2,1)S(1)} %get-tuple-element.27.rest_0_), channel_id=1, source_target_pairs={{0,2},{1,3},{2,0},{3,1},{4,6},{5,7},{6,4},{7,5},{8,10},{9,11},{10,... | collective-permute-start | bytes 1572872 | tf_op jit(solution)/shard_map/ppermute | solution.py:353
  24.8 3.0 %shard_map.79 = (bf16[8,128,256]{2,1,0:T(8,128)(2,1)S(1)}, bf16[8,128,256]{2,1,0:T(8,128)(2,1)}) custom-call(bf16[256,512]{1,0:T(8,128)(2,1)S(1)} %get-tuple-element.25.left_ref, bf16[64,512,128]{2,1,0:T(8,128)(2,1)} %tiles.11, bf16[16,256,128]{2,1,0:T(8,128)(2,1)S(1)} %collective-permute-done.1.rest_0_.other, ...), custom_call_target="tpu_custom_call" | custom-call | flops 536870912 | bytes 2097152 | tf_op jit(solution)/shard_map/pallas_call | solution.py:224
  28.4 9.7 %collective-permute-done.3.rest_1_.refs_1_ = bf16[8,128,256]{2,1,0:T(8,128)(2,1)S(1)} collective-permute-done((bf16[8,128,256]{2,1,0:T(8,128)(2,1)S(1)}, bf16[8,128,256]{2,1,0:T(8,128)(2,1)S(1)}, u32[]{:S(2)}, u32[]{:S(2)}) %collective-permute-start.3) | collective-permute-done | bytes 524320 | tf_op jit(solution)/shard_map/ppermute | solution.py:353
  38.1 3.2 %shard_map.80 = (bf16[8,128,256]{2,1,0:T(8,128)(2,1)S(1)}, bf16[8,128,256]{2,1,0:T(8,128)(2,1)}) custom-call(bf16[256,512]{1,0:T(8,128)(2,1)S(1)} %get-tuple-element.25.left_ref, bf16[64,512,128]{2,1,0:T(8,128)(2,1)} %tiles.11, bf16[16,256,128]{2,1,0:T(8,128)(2,1)S(1)} %copy-done.1, bf16[256,256]{1,0:T(8,128)(2,1)S(1)} %get-tuple-element.26.right_ref, ...), custom_call_target="tpu_custom_call" | custom-call | flops 536870912 | bytes 2097152 | tf_op jit(solution)/shard_map/pallas_call | solution.py:224
  41.3 0.8 copy-done.15
  42.1 1.5 %collective-permute-start.6 = (bf16[8,128,256]{2,1,0:T(8,128)(2,1)}, bf16[8,128,256]{2,1,0:T(8,128)(2,1)}, u32[]{:S(2)}, u32[]{:S(2)}) collective-permute-start(bf16[8,128,256]{2,1,0:T(8,128)(2,1)} %get-tuple-element.29.rest_0_), channel_id=1, source_target_pairs={{0,2},{1,3},{2,0},{3,1},{4,6},{5,7},{6,4},{7,5},{8,10},{9,11},{10,... | collective-permute-start | bytes 1572872 | tf_op jit(solution)/shard_map/ppermute | solution.py:353
  43.6 5.8 %collective-permute-done.4.rest_1_.refs_3_ = bf16[8,128,256]{2,1,0:T(8,128)(2,1)} collective-permute-done((bf16[8,128,256]{2,1,0:T(8,128)(2,1)}, bf16[8,128,256]{2,1,0:T(8,128)(2,1)}, u32[]{:S(2)}, u32[]{:S(2)}) %collective-permute-start.4) | collective-permute-done | bytes 524320 | tf_op jit(solution)/shard_map/ppermute | solution.py:353
  49.4 3.0 %shard_map.81 = (bf16[8,128,256]{2,1,0:T(8,128)(2,1)S(1)}, bf16[8,128,256]{2,1,0:T(8,128)(2,1)}) custom-call(bf16[256,512]{1,0:T(8,128)(2,1)S(1)} %get-tuple-element.25.left_ref, bf16[64,512,128]{2,1,0:T(8,128)(2,1)} %tiles.11, bf16[16,256,128]{2,1,0:T(8,128)(2,1)S(1)} %copy-done.2, bf16[256,256]{1,0:T(8,128)(2,1)S(1)} %get-tuple-element.26.right_ref, ...), custom_call_target="tpu_custom_call" | custom-call | flops 536870912 | bytes 2097152 | tf_op jit(solution)/shard_map/pallas_call | solution.py:224
  52.4 0.8 copy-done.3
  53.2 1.5 %collective-permute-start.7 = (bf16[8,128,256]{2,1,0:T(8,128)(2,1)}, bf16[8,128,256]{2,1,0:T(8,128)(2,1)S(1)}, u32[]{:S(2)}, u32[]{:S(2)}) collective-permute-start(bf16[8,128,256]{2,1,0:T(8,128)(2,1)} %get-tuple-element.30.early), channel_id=1, source_target_pairs={{0,2},{1,3},{2,0},{3,1},{4,6},{5,7},{6,4},{7,5},{8,10},{9,11},{10,... | collective-permute-start | bytes 1572872 | tf_op jit(solution)/shard_map/ppermute | solution.py:353
  54.7 14.3 %all-to-all-done.refs_0_.refs_1_ = bf16[8,32,32,128]{3,2,1,0:T(8,128)(2,1)S(1)} async-done(((bf16[8,32,32,128]{3,2,1,0:T(8,128)(2,1)}), bf16[8,32,32,128]{3,2,1,0:T(8,128)(2,1)S(1)}, u32[]{:S(2)}, u32[]{:S(2)}) %all-to-all-start) | async-done | bytes 2097184 | tf_op jit(solution)/shard_map/all_to_all | solution.py:341
  69.1 0.6 shard_map.83.refs_2_.near_ref
  69.7 1.6 %collective-permute-start.9 = (bf16[2,32,32,128]{3,2,1,0:T(8,128)(2,1)S(1)}, bf16[2,32,32,128]{3,2,1,0:T(8,128)(2,1)S(1)}, u32[]{:S(2)}, u32[]{:S(2)}) collective-permute-start(bf16[2,32,32,128]{3,2,1,0:T(8,128)(2,1)S(1)} %shard_map.83.refs_2_.near_ref), channel_id=1, source_target_pairs={{0,2},{1,3},{2,0},{3,1},{4,6},{5,7},{6,4},{7,5},{8,10},{9,11},{10,... | collective-permute-start | bytes 1572872 | tf_op jit(solution)/shard_map/ppermute | solution.py:361
  71.3 0.6 shard_map.84.refs_2_.near_ref
  72.5 0.6 shard_map.85.near_ref.refs_2_
  73.2 1.6 %collective-permute-start.5 = (bf16[2,32,32,128]{3,2,1,0:T(8,128)(2,1)S(1)}, bf16[2,32,32,128]{3,2,1,0:T(8,128)(2,1)S(1)}, u32[]{:S(2)}, u32[]{:S(2)}) collective-permute-start(bf16[2,32,32,128]{3,2,1,0:T(8,128)(2,1)S(1)} %shard_map.85.near_ref.refs_2_), channel_id=1, source_target_pairs={{0,2},{1,3},{2,0},{3,1},{4,6},{5,7},{6,4},{7,5},{8,10},{9,11},{10,... | collective-permute-start | bytes 1572872 | tf_op jit(solution)/shard_map/ppermute | solution.py:361
  74.7 0.6 shard_map.91.near_ref
  76.0 1.4 %shard_map.86.dressed = bf16[24,128,256]{2,1,0:T(8,128)(2,1)S(1)} custom-call(bf16[8,128,256]{2,1,0:T(8,128)(2,1)S(1)} %copy-done.12, bf16[8,128,256]{2,1,0:T(8,128)(2,1)S(1)} %copy-done.9, bf16[8,128,256]{2,1,0:T(8,128)(2,1)S(1)} %copy-done.14, bf16[8,128,256]{2,1,0:T(8,128)(2,1)} %collective-permute-done.4.rest_1_.refs_3_, ...), custom_call_target="tpu_custom_call" | custom-call | flops 24 | bytes 4718592 | tf_op jit(solution)/shard_map/pallas_call | solution.py:23
  77.5 7.2 %collective-permute-done.9.far_ref = bf16[2,32,32,128]{3,2,1,0:T(8,128)(2,1)S(1)} collective-permute-done((bf16[2,32,32,128]{3,2,1,0:T(8,128)(2,1)S(1)}, bf16[2,32,32,128]{3,2,1,0:T(8,128)(2,1)S(1)}, u32[]{:S(2)}, u32[]{:S(2)}) %collective-permute-start.9) | collective-permute-done | bytes 524320 | tf_op jit(solution)/shard_map/ppermute | solution.py:361
  84.6 1.2 shard_map.87
  85.8 2.6 %collective-permute-start.12 = (bf16[32,32,128]{2,1,0:T(8,128)(2,1)S(1)}, bf16[32,32,128]{2,1,0:T(8,128)(2,1)S(1)}, u32[]{:S(2)}, u32[]{:S(2)}) collective-permute-start(bf16[32,32,128]{2,1,0:T(8,128)(2,1)S(1)} %get-tuple-element.35.refs_0_), channel_id=1, source_target_pairs={{0,28},{4,24},{8,20},{12,16},{16,12},{20,8},{24,4},{28,0},{1,29},{... | collective-permute-start | bytes 786440 | tf_op jit(solution)/shard_map/ppermute | solution.py:369
  88.7 7.2 %collective-permute-done.8.far_ref = bf16[2,32,32,128]{3,2,1,0:T(8,128)(2,1)S(1)} collective-permute-done((bf16[2,32,32,128]{3,2,1,0:T(8,128)(2,1)S(1)}, bf16[2,32,32,128]{3,2,1,0:T(8,128)(2,1)S(1)}, u32[]{:S(2)}, u32[]{:S(2)}) %collective-permute-start.8) | collective-permute-done | bytes 524320 | tf_op jit(solution)/shard_map/ppermute | solution.py:361
  95.9 1.2 shard_map.88
  97.0 2.3 %collective-permute-start.17 = (bf16[32,32,128]{2,1,0:T(8,128)(2,1)S(1)}, bf16[32,32,128]{2,1,0:T(8,128)(2,1)S(1)}, u32[]{:S(2)}, u32[]{:S(2)}) collective-permute-start(bf16[32,32,128]{2,1,0:T(8,128)(2,1)S(1)} %get-tuple-element.36.refs_0_), channel_id=1, source_target_pairs={{0,24},{4,28},{8,16},{12,20},{16,8},{20,12},{24,0},{28,4},{1,25},{... | collective-permute-start | bytes 786440 | tf_op jit(solution)/shard_map/ppermute | solution.py:369
  99.3 7.8 %collective-permute-done.5.far_ref = bf16[2,32,32,128]{3,2,1,0:T(8,128)(2,1)S(1)} collective-permute-done((bf16[2,32,32,128]{3,2,1,0:T(8,128)(2,1)S(1)}, bf16[2,32,32,128]{3,2,1,0:T(8,128)(2,1)S(1)}, u32[]{:S(2)}, u32[]{:S(2)}) %collective-permute-start.5) | collective-permute-done | bytes 524320 | tf_op jit(solution)/shard_map/ppermute | solution.py:361
  107.1 1.2 shard_map.89
  108.3 2.3 %collective-permute-start.10 = (bf16[32,32,128]{2,1,0:T(8,128)(2,1)S(1)}, bf16[32,32,128]{2,1,0:T(8,128)(2,1)S(1)}, u32[]{:S(2)}, u32[]{:S(2)}) collective-permute-start(bf16[32,32,128]{2,1,0:T(8,128)(2,1)S(1)} %get-tuple-element.37.refs_0_), channel_id=1, source_target_pairs={{0,20},{4,16},{8,28},{12,24},{16,4},{20,0},{24,12},{28,8},{1,21},{... | collective-permute-start | bytes 786440 | tf_op jit(solution)/shard_map/ppermute | solution.py:369
  110.6 5.9 %collective-permute-done.11.far_ref = bf16[2,32,32,128]{3,2,1,0:T(8,128)(2,1)S(1)} collective-permute-done((bf16[2,32,32,128]{3,2,1,0:T(8,128)(2,1)S(1)}, bf16[2,32,32,128]{3,2,1,0:T(8,128)(2,1)S(1)}, u32[]{:S(2)}, u32[]{:S(2)}) %collective-permute-start.11) | collective-permute-done | bytes 524320 | tf_op jit(solution)/shard_map/ppermute | solution.py:361
  116.6 1.9 %collective-permute-start.15 = (bf16[32,32,128]{2,1,0:T(8,128)(2,1)S(1)}, bf16[32,32,128]{2,1,0:T(8,128)(2,1)S(1)}, u32[]{:S(2)}, u32[]{:S(2)}) collective-permute-start(bf16[32,32,128]{2,1,0:T(8,128)(2,1)S(1)} %get-tuple-element.41), channel_id=1, source_target_pairs={{0,12},{4,8},{8,4},{12,0},{16,28},{20,24},{24,20},{28,16},{1,13},{... | collective-permute-start | bytes 786440 | tf_op jit(solution)/shard_map/ppermute | solution.py:369
  118.5 1.2 shard_map.92
  119.7 0.6 collective-permute-start.14
  120.3 2.6 %collective-permute-start.16 = (bf16[32,32,128]{2,1,0:T(8,128)(2,1)S(1)}, bf16[32,32,128]{2,1,0:T(8,128)(2,1)S(1)}, u32[]{:S(2)}, u32[]{:S(2)}) collective-permute-start(bf16[32,32,128]{2,1,0:T(8,128)(2,1)S(1)} %get-tuple-element.42), channel_id=1, source_target_pairs={{0,16},{4,20},{8,24},{12,28},{16,0},{20,4},{24,8},{28,12},{1,17},{... | collective-permute-start | bytes 786440 | tf_op jit(solution)/shard_map/ppermute | solution.py:369
  122.9 2.1 %shard_map.82.rows = bf16[256,256]{1,0:T(8,128)(2,1)S(1)} custom-call(s32[512]{0:T(512)S(1)} %copy-done.19, s32[8]{0:T(128)S(1)} %copy-done.20, bf16[512,256]{1,0:T(8,128)(2,1)S(1)} %copy-done.7, bf16[8,128,256]{2,1,0:T(8,128)(2,1)} %get-tuple-element.30.early), custom_call_target="tpu_custom_call" | custom-call | flops 65536 | bytes 262144 | tf_op jit(solution)/shard_map/pallas_call | solution.py:97
  125.0 4.9 %collective-permute-done.15.refs_3_ = bf16[32,32,128]{2,1,0:T(8,128)(2,1)S(1)} collective-permute-done((bf16[32,32,128]{2,1,0:T(8,128)(2,1)S(1)}, bf16[32,32,128]{2,1,0:T(8,128)(2,1)S(1)}, u32[]{:S(2)}, u32[]{:S(2)}) %collective-permute-start.15) | collective-permute-done | bytes 262176 | tf_op jit(solution)/shard_map/ppermute | solution.py:369
  129.9 2.6 %collective-permute-done.14.refs_1_ = bf16[32,32,128]{2,1,0:T(8,128)(2,1)S(1)} collective-permute-done((bf16[32,32,128]{2,1,0:T(8,128)(2,1)S(1)}, bf16[32,32,128]{2,1,0:T(8,128)(2,1)S(1)}, u32[]{:S(2)}, u32[]{:S(2)}) %collective-permute-start.14) | collective-permute-done | bytes 262176 | tf_op jit(solution)/shard_map/ppermute | solution.py:369
  132.5 1.5 %collective-permute-done.16.refs_4_ = bf16[32,32,128]{2,1,0:T(8,128)(2,1)S(1)} collective-permute-done((bf16[32,32,128]{2,1,0:T(8,128)(2,1)S(1)}, bf16[32,32,128]{2,1,0:T(8,128)(2,1)S(1)}, u32[]{:S(2)}, u32[]{:S(2)}) %collective-permute-start.16) | collective-permute-done | bytes 262176 | tf_op jit(solution)/shard_map/ppermute | solution.py:369
  134.0 2.2 %shard_map.93 = (bf16[32,64,256]{2,1,0:T(8,128)(2,1)S(1)}, bf16[32,64,256]{2,1,0:T(8,128)(2,1)S(1)}) custom-call(bf16[256,256]{1,0:T(8,128)(2,1)S(1)} %shard_map.90.rows_ref, bf16[32,32,128]{2,1,0:T(8,128)(2,1)S(1)} %get-tuple-element.38.rest_1_.refs_0_, bf16[32,32,128]{2,1,0:T(8,128)(2,1)S(1)} %collective-permute-done.14.refs_1_, ...), custom_call_target="tpu_custom_call" | custom-call | flops 536870912 | bytes 4325376 | tf_op jit(solution)/shard_map/pallas_call | solution.py:23
  136.3 2.6 %collective-permute-done.18 = bf16[32,64,256]{2,1,0:T(8,128)(2,1)S(1)} collective-permute-done((bf16[32,64,256]{2,1,0:T(8,128)(2,1)S(1)}, bf16[32,64,256]{2,1,0:T(8,128)(2,1)S(1)}, u32[]{:S(2)}, u32[]{:S(2)}) %collective-permute-start.18) | collective-permute-done | bytes 1048608 | tf_op jit(solution)/shard_map/ppermute | solution.py:374
  139.0 1.1 add_bitcast_fusion
  (56 shorter events, 3.9 us)
Async XLA Ops:
  0.0 0.9 copy-start.5
  3.5 3.1 %copy-start.10 = (bf16[32,256,64]{1,2,0:T(8,128)(2,1)S(1)}, bf16[32,256,64]{1,2,0:T(8,128)(2,1)}, u32[]{:S(2)}) copy-start(bf16[32,256,64]{1,2,0:T(8,128)(2,1)} %param.7) | copy-start | bytes 3145732
  3.5 3.5 %copy-start.6 = (bf16[512,256]{1,0:T(8,128)(2,1)S(1)}, bf16[512,256]{1,0:T(8,128)(2,1)}, u32[]{:S(2)}) copy-start(bf16[512,256]{1,0:T(8,128)(2,1)} %orbitals.5) | copy-start | bytes 786436
  3.5 3.4 %copy-start.17 = (s32[512,1]{0,1:T(1,128)S(1)}, s32[512,1]{0,1:T(1,128)}, u32[]{:S(2)}) copy-start(s32[512,1]{0,1:T(1,128)} %param.12) | copy-start | bytes 6148
  3.5 3.4 %copy-start.18 = (s32[512]{0:T(512)S(1)}, s32[512]{0:T(512)}, u32[]{:S(2)}) copy-start(s32[512]{0:T(512)} %sub.1) | copy-start | bytes 6148
  3.6 5.6 %collective-permute-start.1 = (bf16[16,256,128]{2,1,0:T(8,128)(2,1)S(1)}, bf16[16,256,128]{2,1,0:T(8,128)(2,1)S(1)}, u32[]{:S(2)}, u32[]{:S(2)}) collective-permute-start(bf16[16,256,128]{2,1,0:T(8,128)(2,1)S(1)} %shard_map.74.rest_0_), channel_id=1, source_target_pairs={{0,1},{1,0},{2,3},{3,2},{4,5},{5,4},{6,7},{7,6},{8,9},{9,8},{10,11... | collective-permute-start | bytes 3145736 | tf_op jit(solution)/shard_map/ppermute | solution.py:335
  6.4 2.7 %collective-permute-start = (bf16[16,256,128]{2,1,0:T(8,128)(2,1)S(1)}, bf16[16,256,128]{2,1,0:T(8,128)(2,1)S(1)}, u32[]{:S(2)}, u32[]{:S(2)}) collective-permute-start(bf16[16,256,128]{2,1,0:T(8,128)(2,1)S(1)} %shard_map.75.early), channel_id=1, source_target_pairs={{0,1},{1,0},{2,3},{3,2},{4,5},{5,4},{6,7},{7,6},{8,9},{9,8},{10,11... | collective-permute-start | bytes 3145736 | tf_op jit(solution)/shard_map/ppermute | solution.py:335
  6.6 4.0 %collective-permute-start.2 = (bf16[32,64,256]{2,1,0:T(8,128)(2,1)S(1)}, bf16[32,64,256]{2,1,0:T(8,128)(2,1)S(1)}, u32[]{:S(2)}, u32[]{:S(2)}) collective-permute-start(bf16[32,64,256]{2,1,0:T(8,128)(2,1)S(1)} %bitcast.5), channel_id=1, source_target_pairs={{0,1},{1,0},{2,3},{3,2},{4,5},{5,4},{6,7},{7,6},{8,9},{9,8},{10,11... | collective-permute-start | bytes 3145736 | tf_op jit(solution)/shard_map/ppermute | solution.py:326
  9.1 1.5 %copy-start = (bf16[16,256,128]{2,1,0:T(8,128)(2,1)}, bf16[16,256,128]{2,1,0:T(8,128)(2,1)S(1)}, u32[]{:S(2)}) copy-start(bf16[16,256,128]{2,1,0:T(8,128)(2,1)S(1)} %collective-permute-done.rest_1_.other) | copy-start | bytes 3145732
  13.3 55.7 %all-to-all-start = ((bf16[8,32,32,128]{3,2,1,0:T(8,128)(2,1)}), bf16[8,32,32,128]{3,2,1,0:T(8,128)(2,1)S(1)}, u32[]{:S(2)}, u32[]{:S(2)}) async-start(bf16[8,32,32,128]{3,2,1,0:T(8,128)(2,1)} %shard_map.77.rest_0_), calls=%async_computation | async-start | bytes 4194304 | tf_op jit(solution)/shard_map/all_to_all | solution.py:341
  22.5 0.8 copy-start.11
  23.3 14.8 %copy-start.1 = (bf16[16,256,128]{2,1,0:T(8,128)(2,1)S(1)}, bf16[16,256,128]{2,1,0:T(8,128)(2,1)}, u32[]{:S(2)}) copy-start(bf16[16,256,128]{2,1,0:T(8,128)(2,1)} %copy-done) | copy-start | bytes 3145732
  23.3 14.8 %collective-permute-start.3 = (bf16[8,128,256]{2,1,0:T(8,128)(2,1)S(1)}, bf16[8,128,256]{2,1,0:T(8,128)(2,1)S(1)}, u32[]{:S(2)}, u32[]{:S(2)}) collective-permute-start(bf16[8,128,256]{2,1,0:T(8,128)(2,1)S(1)} %get-tuple-element.27.rest_0_), channel_id=1, source_target_pairs={{0,2},{1,3},{2,0},{3,1},{4,6},{5,7},{6,4},{7,5},{8,10},{9,11},{10,... | collective-permute-start | bytes 1572872 | tf_op jit(solution)/shard_map/ppermute | solution.py:353
  27.8 13.5 %copy-start.13 = (bf16[8,128,256]{2,1,0:T(8,128)(2,1)}, bf16[8,128,256]{2,1,0:T(8,128)(2,1)S(1)}, u32[]{:S(2)}) copy-start(bf16[8,128,256]{2,1,0:T(8,128)(2,1)S(1)} %get-tuple-element.32.refs_2_) | copy-start | bytes 1572868
  27.8 21.6 %copy-start.2 = (bf16[16,256,128]{2,1,0:T(8,128)(2,1)S(1)}, bf16[16,256,128]{2,1,0:T(8,128)(2,1)}, u32[]{:S(2)}) copy-start(bf16[16,256,128]{2,1,0:T(8,128)(2,1)} %copy-done) | copy-start | bytes 3145732
  27.8 21.6 %collective-permute-start.4 = (bf16[8,128,256]{2,1,0:T(8,128)(2,1)}, bf16[8,128,256]{2,1,0:T(8,128)(2,1)}, u32[]{:S(2)}, u32[]{:S(2)}) collective-permute-start(bf16[8,128,256]{2,1,0:T(8,128)(2,1)} %get-tuple-element.28.rest_0_), channel_id=1, source_target_pairs={{0,2},{1,3},{2,0},{3,1},{4,6},{5,7},{6,4},{7,5},{8,10},{9,11},{10,... | collective-permute-start | bytes 1572872 | tf_op jit(solution)/shard_map/ppermute | solution.py:353
  38.1 3.2 %copy-start.8 = (bf16[8,128,256]{2,1,0:T(8,128)(2,1)}, bf16[8,128,256]{2,1,0:T(8,128)(2,1)S(1)}, u32[]{:S(2)}) copy-start(bf16[8,128,256]{2,1,0:T(8,128)(2,1)S(1)} %collective-permute-done.3.rest_1_.refs_1_) | copy-start | bytes 1572868
  41.3 0.8 copy-start.15
  42.1 33.3 %collective-permute-start.6 = (bf16[8,128,256]{2,1,0:T(8,128)(2,1)}, bf16[8,128,256]{2,1,0:T(8,128)(2,1)}, u32[]{:S(2)}, u32[]{:S(2)}) collective-permute-start(bf16[8,128,256]{2,1,0:T(8,128)(2,1)} %get-tuple-element.29.rest_0_), channel_id=1, source_target_pairs={{0,2},{1,3},{2,0},{3,1},{4,6},{5,7},{6,4},{7,5},{8,10},{9,11},{10,... | collective-permute-start | bytes 1572872 | tf_op jit(solution)/shard_map/ppermute | solution.py:353
  52.4 0.8 copy-start.3
  53.2 24.2 %collective-permute-start.7 = (bf16[8,128,256]{2,1,0:T(8,128)(2,1)}, bf16[8,128,256]{2,1,0:T(8,128)(2,1)S(1)}, u32[]{:S(2)}, u32[]{:S(2)}) collective-permute-start(bf16[8,128,256]{2,1,0:T(8,128)(2,1)} %get-tuple-element.30.early), channel_id=1, source_target_pairs={{0,2},{1,3},{2,0},{3,1},{4,6},{5,7},{6,4},{7,5},{8,10},{9,11},{10,... | collective-permute-start | bytes 1572872 | tf_op jit(solution)/shard_map/ppermute | solution.py:353
  69.7 14.9 %collective-permute-start.9 = (bf16[2,32,32,128]{3,2,1,0:T(8,128)(2,1)S(1)}, bf16[2,32,32,128]{3,2,1,0:T(8,128)(2,1)S(1)}, u32[]{:S(2)}, u32[]{:S(2)}) collective-permute-start(bf16[2,32,32,128]{3,2,1,0:T(8,128)(2,1)S(1)} %shard_map.83.refs_2_.near_ref), channel_id=1, source_target_pairs={{0,2},{1,3},{2,0},{3,1},{4,6},{5,7},{6,4},{7,5},{8,10},{9,11},{10,... | collective-permute-start | bytes 1572872 | tf_op jit(solution)/shard_map/ppermute | solution.py:361
  71.9 24.0 %collective-permute-start.8 = (bf16[2,32,32,128]{3,2,1,0:T(8,128)(2,1)S(1)}, bf16[2,32,32,128]{3,2,1,0:T(8,128)(2,1)S(1)}, u32[]{:S(2)}, u32[]{:S(2)}) collective-permute-start(bf16[2,32,32,128]{3,2,1,0:T(8,128)(2,1)S(1)} %shard_map.84.refs_2_.near_ref), channel_id=1, source_target_pairs={{0,2},{1,3},{2,0},{3,1},{4,6},{5,7},{6,4},{7,5},{8,10},{9,11},{10,... | collective-permute-start | bytes 1572872 | tf_op jit(solution)/shard_map/ppermute | solution.py:361
  73.1 2.9 %copy-start.9 = (bf16[8,128,256]{2,1,0:T(8,128)(2,1)S(1)}, bf16[8,128,256]{2,1,0:T(8,128)(2,1)}, u32[]{:S(2)}) copy-start(bf16[8,128,256]{2,1,0:T(8,128)(2,1)} %copy-done.8) | copy-start | bytes 1572868
  73.2 2.8 %copy-start.12 = (bf16[8,128,256]{2,1,0:T(8,128)(2,1)S(1)}, bf16[8,128,256]{2,1,0:T(8,128)(2,1)}, u32[]{:S(2)}) copy-start(bf16[8,128,256]{2,1,0:T(8,128)(2,1)} %copy-done.11) | copy-start | bytes 1572868
  73.2 2.8 %copy-start.14 = (bf16[8,128,256]{2,1,0:T(8,128)(2,1)S(1)}, bf16[8,128,256]{2,1,0:T(8,128)(2,1)}, u32[]{:S(2)}) copy-start(bf16[8,128,256]{2,1,0:T(8,128)(2,1)} %copy-done.13) | copy-start | bytes 1572868
  73.2 2.8 %copy-start.16 = (bf16[8,128,256]{2,1,0:T(8,128)(2,1)S(1)}, bf16[8,128,256]{2,1,0:T(8,128)(2,1)}, u32[]{:S(2)}) copy-start(bf16[8,128,256]{2,1,0:T(8,128)(2,1)} %copy-done.15) | copy-start | bytes 1572868
  73.2 33.9 %collective-permute-start.5 = (bf16[2,32,32,128]{3,2,1,0:T(8,128)(2,1)S(1)}, bf16[2,32,32,128]{3,2,1,0:T(8,128)(2,1)S(1)}, u32[]{:S(2)}, u32[]{:S(2)}) collective-permute-start(bf16[2,32,32,128]{3,2,1,0:T(8,128)(2,1)S(1)} %shard_map.85.near_ref.refs_2_), channel_id=1, source_target_pairs={{0,2},{1,3},{2,0},{3,1},{4,6},{5,7},{6,4},{7,5},{8,10},{9,11},{10,... | collective-permute-start | bytes 1572872 | tf_op jit(solution)/shard_map/ppermute | solution.py:361
  75.4 41.2 %collective-permute-start.11 = (bf16[2,32,32,128]{3,2,1,0:T(8,128)(2,1)S(1)}, bf16[2,32,32,128]{3,2,1,0:T(8,128)(2,1)S(1)}, u32[]{:S(2)}, u32[]{:S(2)}) collective-permute-start(bf16[2,32,32,128]{3,2,1,0:T(8,128)(2,1)S(1)} %shard_map.91.near_ref), channel_id=1, source_target_pairs={{0,2},{1,3},{2,0},{3,1},{4,6},{5,7},{6,4},{7,5},{8,10},{9,11},{10,... | collective-permute-start | bytes 1572872 | tf_op jit(solution)/shard_map/ppermute | solution.py:361
  76.0 8.6 %copy-start.4 = (bf16[8,128,256]{2,1,0:T(8,128)(2,1)S(1)}, bf16[8,128,256]{2,1,0:T(8,128)(2,1)}, u32[]{:S(2)}) copy-start(bf16[8,128,256]{2,1,0:T(8,128)(2,1)} %copy-done.3) | copy-start | bytes 1572868
  85.8 32.7 %collective-permute-start.12 = (bf16[32,32,128]{2,1,0:T(8,128)(2,1)S(1)}, bf16[32,32,128]{2,1,0:T(8,128)(2,1)S(1)}, u32[]{:S(2)}, u32[]{:S(2)}) collective-permute-start(bf16[32,32,128]{2,1,0:T(8,128)(2,1)S(1)} %get-tuple-element.35.refs_0_), channel_id=1, source_target_pairs={{0,28},{4,24},{8,20},{12,16},{16,12},{20,8},{24,4},{28,0},{1,29},{... | collective-permute-start | bytes 786440 | tf_op jit(solution)/shard_map/ppermute | solution.py:369
  88.4 30.2 %collective-permute-start.13 = (bf16[32,32,128]{2,1,0:T(8,128)(2,1)S(1)}, bf16[32,32,128]{2,1,0:T(8,128)(2,1)S(1)}, u32[]{:S(2)}, u32[]{:S(2)}) collective-permute-start(bf16[32,32,128]{2,1,0:T(8,128)(2,1)S(1)} %get-tuple-element.39), channel_id=1, source_target_pairs={{0,8},{4,12},{8,0},{12,4},{16,24},{20,28},{24,16},{28,20},{1,9},{5... | collective-permute-start | bytes 786440 | tf_op jit(solution)/shard_map/ppermute | solution.py:369
  97.0 32.9 %collective-permute-start.17 = (bf16[32,32,128]{2,1,0:T(8,128)(2,1)S(1)}, bf16[32,32,128]{2,1,0:T(8,128)(2,1)S(1)}, u32[]{:S(2)}, u32[]{:S(2)}) collective-permute-start(bf16[32,32,128]{2,1,0:T(8,128)(2,1)S(1)} %get-tuple-element.36.refs_0_), channel_id=1, source_target_pairs={{0,24},{4,28},{8,16},{12,20},{16,8},{20,12},{24,0},{28,4},{1,25},{... | collective-permute-start | bytes 786440 | tf_op jit(solution)/shard_map/ppermute | solution.py:369
  108.3 16.7 %collective-permute-start.10 = (bf16[32,32,128]{2,1,0:T(8,128)(2,1)S(1)}, bf16[32,32,128]{2,1,0:T(8,128)(2,1)S(1)}, u32[]{:S(2)}, u32[]{:S(2)}) collective-permute-start(bf16[32,32,128]{2,1,0:T(8,128)(2,1)S(1)} %get-tuple-element.37.refs_0_), channel_id=1, source_target_pairs={{0,20},{4,16},{8,28},{12,24},{16,4},{20,0},{24,12},{28,8},{1,21},{... | collective-permute-start | bytes 786440 | tf_op jit(solution)/shard_map/ppermute | solution.py:369
  116.5 6.3 %copy-start.7 = (bf16[512,256]{1,0:T(8,128)(2,1)S(1)}, bf16[512,256]{1,0:T(8,128)(2,1)}, u32[]{:S(2)}) copy-start(bf16[512,256]{1,0:T(8,128)(2,1)} %orbitals.5) | copy-start | bytes 786436
  116.5 6.3 %copy-start.19 = (s32[512]{0:T(512)S(1)}, s32[512]{0:T(512)}, u32[]{:S(2)}) copy-start(s32[512]{0:T(512)} %row.1) | copy-start | bytes 6148
  116.6 6.3 %copy-start.20 = (s32[8]{0:T(128)S(1)}, s32[8]{0:T(128)}, u32[]{:S(2)}) copy-start(s32[8]{0:T(128)} %count.1) | copy-start | bytes 100
  116.6 13.4 %collective-permute-start.15 = (bf16[32,32,128]{2,1,0:T(8,128)(2,1)S(1)}, bf16[32,32,128]{2,1,0:T(8,128)(2,1)S(1)}, u32[]{:S(2)}, u32[]{:S(2)}) collective-permute-start(bf16[32,32,128]{2,1,0:T(8,128)(2,1)S(1)} %get-tuple-element.41), channel_id=1, source_target_pairs={{0,12},{4,8},{8,4},{12,0},{16,28},{20,24},{24,20},{28,16},{1,13},{... | collective-permute-start | bytes 786440 | tf_op jit(solution)/shard_map/ppermute | solution.py:369
  119.7 12.8 %collective-permute-start.14 = (bf16[32,32,128]{2,1,0:T(8,128)(2,1)S(1)}, bf16[32,32,128]{2,1,0:T(8,128)(2,1)S(1)}, u32[]{:S(2)}, u32[]{:S(2)}) collective-permute-start(bf16[32,32,128]{2,1,0:T(8,128)(2,1)S(1)} %get-tuple-element.40), channel_id=1, source_target_pairs={{0,4},{4,0},{8,12},{12,8},{16,20},{20,16},{24,28},{28,24},{1,5},{5... | collective-permute-start | bytes 786440 | tf_op jit(solution)/shard_map/ppermute | solution.py:369
  120.3 13.7 %collective-permute-start.16 = (bf16[32,32,128]{2,1,0:T(8,128)(2,1)S(1)}, bf16[32,32,128]{2,1,0:T(8,128)(2,1)S(1)}, u32[]{:S(2)}, u32[]{:S(2)}) collective-permute-start(bf16[32,32,128]{2,1,0:T(8,128)(2,1)S(1)} %get-tuple-element.42), channel_id=1, source_target_pairs={{0,16},{4,20},{8,24},{12,28},{16,0},{20,4},{24,8},{28,12},{1,17},{... | collective-permute-start | bytes 786440 | tf_op jit(solution)/shard_map/ppermute | solution.py:369
  136.3 2.7 %collective-permute-start.18 = (bf16[32,64,256]{2,1,0:T(8,128)(2,1)S(1)}, bf16[32,64,256]{2,1,0:T(8,128)(2,1)S(1)}, u32[]{:S(2)}, u32[]{:S(2)}) collective-permute-start(bf16[32,64,256]{2,1,0:T(8,128)(2,1)S(1)} %get-tuple-element.44), channel_id=1, source_target_pairs={{0,1},{1,0},{2,3},{3,2},{4,5},{5,4},{6,7},{7,6},{8,9},{9,8},{10,11... | collective-permute-start | bytes 3145736 | tf_op jit(solution)/shard_map/ppermute | solution.py:374

commit v4 on v3

--- a/solution.py
+++ b/solution.py
@@ -106,26 +106,41 @@
 
 
 def rows_body(rows_ref, mine_ref, other_ref, *rest):
-    out = rest[-1]
-    nodes, occ, slots, width = out.shape
+    out, held, sems = rest[-3:]
+    nodes, occ, slots, width = held.shape
     rows = rows_ref[...]
-
-    def step(n, carry):
-        i = 2 * n
-        right = jnp.concatenate([mine_ref[i], other_ref[i], mine_ref[i + 1], other_ref[i + 1]], 0)
-        product = dot(rows, right, (((1,), (1,)), ((), ()))).astype(BF16)
-        for j in range(2):
-            out[:, i + j] = product[:, j * width:(j + 1) * width].reshape(nodes, slots, width)
-        return carry
-
-    lax.fori_loop(0, occ // 2, step, 0, unroll=4)
+    copies = []
+    part = occ // sems.shape[0]
+    for s in range(sems.shape[0]):
+        for i in range(s * part, (s + 1) * part, 2):
+            right = jnp.concatenate([mine_ref[i], other_ref[i], mine_ref[i + 1], other_ref[i + 1]], 0)
+            product = dot(rows, right, (((1,), (1,)), ((), ()))).astype(BF16)
+            for j in range(2):
+                held[:, i + j] = product[:, j * width:(j + 1) * width].reshape(nodes, slots, width)
+        piece = pl.ds(s * part, part)
+        copies.append(pltpu.make_async_copy(held.at[:, piece], out.at[:, piece], sems.at[s]))
+        copies[-1].start()
+    for copy in copies:
+        copy.wait()
 
 
 def pair_rows(rows, mine, other, nodes, early):
     occ, part, vir = mine.shape
     count = rows.shape[0]
-    outs = [jax.ShapeDtypeStruct((nodes, occ, count // nodes, 2 * part), BF16)]
-    return call(rows_body, outs, (rows, mine, other), 4 * count * occ * vir * part, (), early, TILE_VMEM_LIMIT)[0]
+    shape = (nodes, occ, count // nodes, 2 * part)
+    whole = pl.BlockSpec(memory_space=pltpu.VMEM)
+    away = pl.BlockSpec(memory_space=pl.ANY)
+    return pl.pallas_call(
+        rows_body,
+        out_shape=jax.ShapeDtypeStruct(shape, BF16),
+        in_specs=[whole] * 3 + [away] * len(early),
+        out_specs=pl.BlockSpec(memory_space=pltpu.HBM),
+        scratch_shapes=[pltpu.VMEM(shape, BF16), pltpu.SemaphoreType.DMA((4,))],
+        cost_estimate=pl.CostEstimate(
+            flops=4 * count * occ * vir * part, bytes_accessed=4 * occ * part * vir, transcendentals=0
+        ),
+        compiler_params=pltpu.CompilerParams(vmem_limit_bytes=TILE_VMEM_LIMIT),
+    )(rows, mine, other, *early)
 
 
 def turn_body(groups, meta, *refs):
@@ -335,7 +350,7 @@
         return given, lax.ppermute(given, "ao", near)
 
     given, first_parts = give(0, ())
-    given, second_parts = give(half // 2, [given])
+    given, second_parts = give(half // 2, [given, other])
     source_rows = gather(source_body, (tile_src[:, 0], tile_sub), orbitals, given)
     sent = pair_rows(source_rows, mine, other, nodes, (first_parts, second_parts))
     arrived = lax.all_to_all(sent, "occ", split_axis=0, concat_axis=0, tiled=True)
@@ -353,22 +368,25 @@
         parts += [here, lax.ppermute(there, "ao", far)]
     target_rows = gather(target_body, (tile_row, tile_count), orbitals, early[0])
     tiles_done = [dress(parts[:-2]), *parts[-2:]]
-    units = [[nodes - 1 - n, (n + nodes // 2 - 2) % (nodes // 2)] for n in range(nodes // 2)]
-    wait_for = {2: (0,), 3: (1,)}
+    lower = nodes // 2
+    light = [k for k in ((n + lower // 2) % lower for n in range(lower)) if k] + [0]
+    units = [[nodes - 1]]
+    for n in range(1, lower):
+        units += [[nodes - 1 - n], [light[n - 1]]]
+    units.append([light[-1]])
+    wait_for = {4: (0,), 5: (1,), 6: (2, 3), 7: (4,)}
     blocks_of, far_blocks = [], []
     for unit in units:
         blocks_of.append(turn(own, arrived, unit, blocks_of[-1:]))
         far_blocks.append(lax.ppermute(blocks_of[-1], "ao", far))
-    returned, early = {}, []
+    returned, made = {}, []
     for n, unit in enumerate(units):
+        early = list(made[:1]) + [returned[k] for m in wait_for.get(n, ()) for k in units[m]]
         made = products(blocks_of[n], far_blocks[n], tiles_done, early)
-        early = [made[0]]
-        for m in wait_for.get(n, ()):
-            early += [returned[k] for k in units[m]]
         for k, x in zip(unit, made):
             returned[k] = lax.ppermute(x, "occ", [(o, o ^ k) for o in range(nodes)]) if k else x
-    tied = [returned[k] for m in (2,) for k in units[m]]
-    target_rows = rows_after(target_rows, tied)
+    last_far = [returned[k] for k in (lower, lower + 1)]
+    target_rows = rows_after(target_rows, last_far[:1])
     returned = [returned[k] for k in range(nodes)]
     keep, give_up = back_transform(target_rows, returned)
     return jnp.swapaxes(keep + lax.ppermute(give_up, "ao", near), 1, 2)

time: 140 us -> 134 us (0.957)
  waiting for transfers between devices: 71.2 us -> 56.2 us
  starting transfers between devices: 30.1 us -> 38.5 us
    ppermute x4 -> x8, waiting for transfers between devices: 28.1 us -> 12.6 us  [shards(): far_blocks.append(lax.ppermute(blocks_of[-1], 'ao', far))]
    ppermute x4 -> x8, starting transfers between devices: 4.31 us -> 10.4 us  [shards(): far_blocks.append(lax.ppermute(blocks_of[-1], 'ao', far))]
    ppermute x7, starting transfers between devices: 12.6 us -> 14.5 us  [shards(): lax.ppermute(x, 'occ', [(o, o ^ k) for o in range(nodes)])]
    pallas_call x0 -> x1, Pallas kernels: none -> 1.7 us  [pair_rows(): pl.pallas_call(rows_body, out_shape=jax.ShapeDtypeStruct(shape, BF16), in...]
    ppermute x1, waiting for transfers between devices: 1.49 us -> 0.01 us  [shards(): other = lax.ppermute(mine, 'ao', near)]
    ppermute x4, waiting for transfers between devices: 15.5 us -> 17 us  [shards(): parts += [here, lax.ppermute(there, 'ao', far)]]
    unnamed x42 -> x40, local copies, waits for them, and re-layouts: 3.41 us -> 2.8 us
    pallas_call x9 -> x12, Pallas kernels: 11.3 us -> 10.9 us  [call(): pl.pallas_call(body, out_shape=outs, in_specs=[whole] * len(ins) + [pl.Bl...]
  transfers between devices with their start and end apart: 20 -> 24, of which waited for: 13 -> 14; matrix products, arithmetic and copies ran while one was open for 0% -> 0% of each run, Pallas kernels for 19% -> 23%
where the time goes in v4:
time: 134 us
  waiting for transfers between devices  56.2 us (42%)
  starting transfers between devices  38.5 us (29%)
  Pallas kernels  34.7 us (26%)
  local copies, waits for them, and re-layouts  2.8 us (2%)
    ppermute x4, waiting for transfers between devices, shards(): parts += [here, lax.ppermute(there, 'ao', far)]  17 us
    pallas_call x6, Pallas kernels, tile_call(): pl.pallas_call(body, out_shape=outs, in_specs=[whole, away] + [whole] * (...  15.4 us
    all_to_all x1, waiting for transfers between devices, shards(): lax.all_to_all(sent, 'occ', split_axis=0, concat_axis=0, tiled=True)  14.7 us
    ppermute x7, starting transfers between devices, shards(): lax.ppermute(x, 'occ', [(o, o ^ k) for o in range(nodes)])  14.5 us
    ppermute x8, waiting for transfers between devices, shards(): far_blocks.append(lax.ppermute(blocks_of[-1], 'ao', far))  12.6 us
    pallas_call x12, Pallas kernels, call(): pl.pallas_call(body, out_shape=outs, in_specs=[whole] * len(ins) + [pl.Bl...  10.9 us
    ppermute x8, starting transfers between devices, shards(): far_blocks.append(lax.ppermute(blocks_of[-1], 'ao', far))  10.4 us
    ppermute x7, waiting for transfers between devices, shards(): lax.ppermute(x, 'occ', [(o, o ^ k) for o in range(nodes)])  8.9 us
  transfers between devices with their start and end apart: 24, of which 14 were waited for; matrix products, arithmetic and copies ran while one was open for 0% of the time, Pallas kernels for 23%

profile of v4, /device:TPU:0, one launch (start us, length us, event | category | flops | bytes accessed | tf_op | source)
XLA Modules:
  0.0 133.7 jit_solution(5223234172380529473)
XLA Ops:
  0.5 0.9 copy-done.2
  1.6 2.3 %shard_map.74.rest_0_ = bf16[16,256,128]{2,1,0:T(8,128)(2,1)S(1)} custom-call(bf16[256,512]{1,0:T(8,128)(2,1)S(1)} %get-tuple-element.17.left_ref, bf16[64,512,128]{2,1,0:T(8,128)(2,1)} %tiles.11), custom_call_target="tpu_custom_call" | custom-call | flops 536870912 | bytes 4194304 | tf_op jit(solution)/shard_map/pallas_call | solution.py:239
  4.1 2.3 %shard_map.75.early = bf16[16,256,128]{2,1,0:T(8,128)(2,1)S(1)} custom-call(bf16[256,512]{1,0:T(8,128)(2,1)S(1)} %get-tuple-element.17.left_ref, bf16[64,512,128]{2,1,0:T(8,128)(2,1)} %tiles.11, bf16[16,256,128]{2,1,0:T(8,128)(2,1)S(1)} %shard_map.74.rest_0_, bf16[32,64,256]{2,1,0:T(8,128)(2,1)S(1)} %collective-permute-done.rest_1_.other_ref), custom_call_target="tpu_custom_call" | custom-call | flops 536870912 | bytes 4194304 | tf_op jit(solution)/shard_map/pallas_call | solution.py:239
  7.0 1.9 %shard_map.76.rows_ref = bf16[256,256]{1,0:T(8,128)(2,1)S(1)} custom-call(s32[512]{0:T(512)S(1)} %bitcast.7, s32[512]{0:T(512)S(1)} %copy-done.17, bf16[512,256]{1,0:T(8,128)(2,1)S(1)} %copy-done.3, bf16[16,256,128]{2,1,0:T(8,128)(2,1)S(1)} %shard_map.75.early), custom_call_target="tpu_custom_call" | custom-call | flops 65536 | bytes 262144 | tf_op jit(solution)/shard_map/pallas_call | solution.py:97
  9.3 1.0 copy-done
  10.2 1.7 %shard_map.77.rest_0_ = bf16[8,32,32,128]{3,2,1,0:T(8,128)(2,1)} custom-call(bf16[256,256]{1,0:T(8,128)(2,1)S(1)} %shard_map.76.rows_ref, bf16[32,64,256]{2,1,0:T(8,128)(2,1)S(1)} %bitcast.6, bf16[32,64,256]{2,1,0:T(8,128)(2,1)S(1)} %collective-permute-done.rest_1_.other_ref, bf16[16,256,128]{2,1,0:T(8,128)(2,1)S(1)} %collective-permute-done.2.rest_0_.other, ...), custom_call_target="tpu_custom_call" | custom-call | flops 536870912 | bytes 2097152 | tf_op jit(solution)/shard_map/pallas_call | solution.py:133
  11.9 7.2 %all-to-all-start = ((bf16[8,32,32,128]{3,2,1,0:T(8,128)(2,1)}), bf16[8,32,32,128]{3,2,1,0:T(8,128)(2,1)S(1)}, u32[]{:S(2)}, u32[]{:S(2)}) async-start(bf16[8,32,32,128]{3,2,1,0:T(8,128)(2,1)} %shard_map.77.rest_0_), calls=%async_computation | async-start | bytes 4194304 | tf_op jit(solution)/shard_map/all_to_all | solution.py:356
  19.2 2.2 %shard_map.78 = (bf16[8,128,256]{2,1,0:T(8,128)(2,1)S(1)}, bf16[8,128,256]{2,1,0:T(8,128)(2,1)S(1)}) custom-call(bf16[256,512]{1,0:T(8,128)(2,1)S(1)} %get-tuple-element.17.left_ref, bf16[64,512,128]{2,1,0:T(8,128)(2,1)} %tiles.11, bf16[16,256,128]{2,1,0:T(8,128)(2,1)S(1)} %collective-permute-done.2.rest_0_.other, ...), custom_call_target="tpu_custom_call" | custom-call | flops 536870912 | bytes 2097152 | tf_op jit(solution)/shard_map/pallas_call | solution.py:239
  22.2 1.5 %collective-permute-start.3 = (bf16[8,128,256]{2,1,0:T(8,128)(2,1)S(1)}, bf16[8,128,256]{2,1,0:T(8,128)(2,1)S(1)}, u32[]{:S(2)}, u32[]{:S(2)}) collective-permute-start(bf16[8,128,256]{2,1,0:T(8,128)(2,1)S(1)} %get-tuple-element.19.rest_0_), channel_id=1, source_target_pairs={{0,2},{1,3},{2,0},{3,1},{4,6},{5,7},{6,4},{7,5},{8,10},{9,11},{10,... | collective-permute-start | bytes 1572872 | tf_op jit(solution)/shard_map/ppermute | solution.py:368
  23.7 2.2 %shard_map.79 = (bf16[8,128,256]{2,1,0:T(8,128)(2,1)S(1)}, bf16[8,128,256]{2,1,0:T(8,128)(2,1)S(1)}) custom-call(bf16[256,512]{1,0:T(8,128)(2,1)S(1)} %get-tuple-element.17.left_ref, bf16[64,512,128]{2,1,0:T(8,128)(2,1)} %tiles.11, bf16[16,256,128]{2,1,0:T(8,128)(2,1)S(1)} %collective-permute-done.2.rest_0_.other, ...), custom_call_target="tpu_custom_call" | custom-call | flops 536870912 | bytes 2097152 | tf_op jit(solution)/shard_map/pallas_call | solution.py:239
  26.5 10.5 %collective-permute-done.3.rest_1_.refs_1_ = bf16[8,128,256]{2,1,0:T(8,128)(2,1)S(1)} collective-permute-done((bf16[8,128,256]{2,1,0:T(8,128)(2,1)S(1)}, bf16[8,128,256]{2,1,0:T(8,128)(2,1)S(1)}, u32[]{:S(2)}, u32[]{:S(2)}) %collective-permute-start.3) | collective-permute-done | bytes 524320 | tf_op jit(solution)/shard_map/ppermute | solution.py:368
  37.0 3.2 %shard_map.80 = (bf16[8,128,256]{2,1,0:T(8,128)(2,1)S(1)}, bf16[8,128,256]{2,1,0:T(8,128)(2,1)}) custom-call(bf16[256,512]{1,0:T(8,128)(2,1)S(1)} %get-tuple-element.17.left_ref, bf16[64,512,128]{2,1,0:T(8,128)(2,1)} %tiles.11, bf16[16,256,128]{2,1,0:T(8,128)(2,1)S(1)} %copy-done.1, bf16[256,256]{1,0:T(8,128)(2,1)S(1)} %get-tuple-element.18.right_ref, ...), custom_call_target="tpu_custom_call" | custom-call | flops 536870912 | bytes 2097152 | tf_op jit(solution)/shard_map/pallas_call | solution.py:239
  40.2 1.6 %collective-permute-start.6 = (bf16[8,128,256]{2,1,0:T(8,128)(2,1)}, bf16[8,128,256]{2,1,0:T(8,128)(2,1)}, u32[]{:S(2)}, u32[]{:S(2)}) collective-permute-start(bf16[8,128,256]{2,1,0:T(8,128)(2,1)} %get-tuple-element.21.rest_0_), channel_id=1, source_target_pairs={{0,2},{1,3},{2,0},{3,1},{4,6},{5,7},{6,4},{7,5},{8,10},{9,11},{10,... | collective-permute-start | bytes 1572872 | tf_op jit(solution)/shard_map/ppermute | solution.py:368
  41.8 6.5 %collective-permute-done.4.rest_1_.refs_3_ = bf16[8,128,256]{2,1,0:T(8,128)(2,1)S(1)} collective-permute-done((bf16[8,128,256]{2,1,0:T(8,128)(2,1)S(1)}, bf16[8,128,256]{2,1,0:T(8,128)(2,1)S(1)}, u32[]{:S(2)}, u32[]{:S(2)}) %collective-permute-start.4) | collective-permute-done | bytes 524320 | tf_op jit(solution)/shard_map/ppermute | solution.py:368
  48.2 3.2 %shard_map.81 = (bf16[8,128,256]{2,1,0:T(8,128)(2,1)S(1)}, bf16[8,128,256]{2,1,0:T(8,128)(2,1)}) custom-call(bf16[256,512]{1,0:T(8,128)(2,1)S(1)} %get-tuple-element.17.left_ref, bf16[64,512,128]{2,1,0:T(8,128)(2,1)} %tiles.11, bf16[16,256,128]{2,1,0:T(8,128)(2,1)S(1)} %copy-done.1, bf16[256,256]{1,0:T(8,128)(2,1)S(1)} %get-tuple-element.18.right_ref, ...), custom_call_target="tpu_custom_call" | custom-call | flops 536870912 | bytes 2097152 | tf_op jit(solution)/shard_map/pallas_call | solution.py:239
  51.4 1.6 %collective-permute-start.7 = (bf16[8,128,256]{2,1,0:T(8,128)(2,1)}, bf16[8,128,256]{2,1,0:T(8,128)(2,1)S(1)}, u32[]{:S(2)}, u32[]{:S(2)}) collective-permute-start(bf16[8,128,256]{2,1,0:T(8,128)(2,1)} %get-tuple-element.22.early), channel_id=1, source_target_pairs={{0,2},{1,3},{2,0},{3,1},{4,6},{5,7},{6,4},{7,5},{8,10},{9,11},{10,... | collective-permute-start | bytes 1572872 | tf_op jit(solution)/shard_map/ppermute | solution.py:368
  53.0 14.7 %all-to-all-done.refs_0_ = bf16[8,32,32,128]{3,2,1,0:T(8,128)(2,1)S(1)} async-done(((bf16[8,32,32,128]{3,2,1,0:T(8,128)(2,1)}), bf16[8,32,32,128]{3,2,1,0:T(8,128)(2,1)S(1)}, u32[]{:S(2)}, u32[]{:S(2)}) %all-to-all-start) | async-done | bytes 2097184 | tf_op jit(solution)/shard_map/all_to_all | solution.py:356
  68.1 1.6 %collective-permute-start.12 = (bf16[1,32,32,128]{3,2,1,0:T(8,128)(2,1)S(1)}, bf16[1,32,32,128]{3,2,1,0:T(8,128)(2,1)S(1)}, u32[]{:S(2)}, u32[]{:S(2)}) collective-permute-start(bf16[1,32,32,128]{3,2,1,0:T(8,128)(2,1)S(1)} %shard_map.83.refs_1_.near_ref), channel_id=1, source_target_pairs={{0,2},{1,3},{2,0},{3,1},{4,6},{5,7},{6,4},{7,5},{8,10},{9,11},{10,... | collective-permute-start | bytes 786440 | tf_op jit(solution)/shard_map/ppermute | solution.py:381
  70.9 1.6 %collective-permute-start.10 = (bf16[1,32,32,128]{3,2,1,0:T(8,128)(2,1)S(1)}, bf16[1,32,32,128]{3,2,1,0:T(8,128)(2,1)S(1)}, u32[]{:S(2)}, u32[]{:S(2)}) collective-permute-start(bf16[1,32,32,128]{3,2,1,0:T(8,128)(2,1)S(1)} %shard_map.85.refs_1_.near_ref), channel_id=1, source_target_pairs={{0,2},{1,3},{2,0},{3,1},{4,6},{5,7},{6,4},{7,5},{8,10},{9,11},{10,... | collective-permute-start | bytes 786440 | tf_op jit(solution)/shard_map/ppermute | solution.py:381
  72.5 1.2 shard_map.89.dressed
  75.0 1.6 %collective-permute-start.8 = (bf16[1,32,32,128]{3,2,1,0:T(8,128)(2,1)S(1)}, bf16[1,32,32,128]{3,2,1,0:T(8,128)(2,1)S(1)}, u32[]{:S(2)}, u32[]{:S(2)}) collective-permute-start(bf16[1,32,32,128]{3,2,1,0:T(8,128)(2,1)S(1)} %shard_map.87.refs_1_.near_ref), channel_id=1, source_target_pairs={{0,2},{1,3},{2,0},{3,1},{4,6},{5,7},{6,4},{7,5},{8,10},{9,11},{10,... | collective-permute-start | bytes 786440 | tf_op jit(solution)/shard_map/ppermute | solution.py:381
  77.4 0.9 shard_map.90.refs_0_
  78.3 3.1 %collective-permute-start.13 = (bf16[32,32,128]{2,1,0:T(8,128)(2,1)S(1)}, bf16[32,32,128]{2,1,0:T(8,128)(2,1)S(1)}, u32[]{:S(2)}, u32[]{:S(2)}) collective-permute-start(bf16[32,32,128]{2,1,0:T(8,128)(2,1)S(1)} %shard_map.90.refs_0_), channel_id=1, source_target_pairs={{0,28},{4,24},{8,20},{12,16},{16,12},{20,8},{24,4},{28,0},{1,29},{... | collective-permute-start | bytes 786440 | tf_op jit(solution)/shard_map/ppermute | solution.py:387
  82.1 0.9 collective-permute-done.11.far_ref
  83.0 1.5 %collective-permute-start.5 = (bf16[1,32,32,128]{3,2,1,0:T(8,128)(2,1)S(1)}, bf16[1,32,32,128]{3,2,1,0:T(8,128)(2,1)S(1)}, u32[]{:S(2)}, u32[]{:S(2)}) collective-permute-start(bf16[1,32,32,128]{3,2,1,0:T(8,128)(2,1)S(1)} %shard_map.88.near_ref.refs_1_), channel_id=1, source_target_pairs={{0,2},{1,3},{2,0},{3,1},{4,6},{5,7},{6,4},{7,5},{8,10},{9,11},{10,... | collective-permute-start | bytes 786440 | tf_op jit(solution)/shard_map/ppermute | solution.py:381
  85.4 3.2 %collective-permute-done.10.far_ref = bf16[1,32,32,128]{3,2,1,0:T(8,128)(2,1)S(1)} collective-permute-done((bf16[1,32,32,128]{3,2,1,0:T(8,128)(2,1)S(1)}, bf16[1,32,32,128]{3,2,1,0:T(8,128)(2,1)S(1)}, u32[]{:S(2)}, u32[]{:S(2)}) %collective-permute-start.10) | collective-permute-done | bytes 262176 | tf_op jit(solution)/shard_map/ppermute | solution.py:381
  88.6 2.2 %collective-permute-start.14 = (bf16[32,32,128]{2,1,0:T(8,128)(2,1)S(1)}, bf16[32,32,128]{2,1,0:T(8,128)(2,1)S(1)}, u32[]{:S(2)}, u32[]{:S(2)}) collective-permute-start(bf16[32,32,128]{2,1,0:T(8,128)(2,1)S(1)} %shard_map.91.refs_0_), channel_id=1, source_target_pairs={{0,24},{4,28},{8,16},{12,20},{16,8},{20,12},{24,0},{28,4},{1,25},{... | collective-permute-start | bytes 786440 | tf_op jit(solution)/shard_map/ppermute | solution.py:387
  90.8 0.9 shard_map.92.refs_0_
  91.7 2.5 %collective-permute-done.9.far_ref = bf16[1,32,32,128]{3,2,1,0:T(8,128)(2,1)S(1)} collective-permute-done((bf16[1,32,32,128]{3,2,1,0:T(8,128)(2,1)S(1)}, bf16[1,32,32,128]{3,2,1,0:T(8,128)(2,1)S(1)}, u32[]{:S(2)}, u32[]{:S(2)}) %collective-permute-start.9) | collective-permute-done | bytes 262176 | tf_op jit(solution)/shard_map/ppermute | solution.py:381
  94.2 1.5 %collective-permute-start.17 = (bf16[1,32,32,128]{3,2,1,0:T(8,128)(2,1)S(1)}, bf16[1,32,32,128]{3,2,1,0:T(8,128)(2,1)S(1)}, u32[]{:S(2)}, u32[]{:S(2)}) collective-permute-start(bf16[1,32,32,128]{3,2,1,0:T(8,128)(2,1)S(1)} %shard_map.97.refs_1_.near_ref), channel_id=1, source_target_pairs={{0,2},{1,3},{2,0},{3,1},{4,6},{5,7},{6,4},{7,5},{8,10},{9,11},{10,... | collective-permute-start | bytes 786440 | tf_op jit(solution)/shard_map/ppermute | solution.py:381
  95.7 0.9 shard_map.93.refs_0_
  96.7 3.2 %collective-permute-done.8.far_ref = bf16[1,32,32,128]{3,2,1,0:T(8,128)(2,1)S(1)} collective-permute-done((bf16[1,32,32,128]{3,2,1,0:T(8,128)(2,1)S(1)}, bf16[1,32,32,128]{3,2,1,0:T(8,128)(2,1)S(1)}, u32[]{:S(2)}, u32[]{:S(2)}) %collective-permute-start.8) | collective-permute-done | bytes 262176 | tf_op jit(solution)/shard_map/ppermute | solution.py:381
  100.3 3.2 %collective-permute-start.19 = (bf16[32,32,128]{2,1,0:T(8,128)(2,1)S(1)}, bf16[32,32,128]{2,1,0:T(8,128)(2,1)S(1)}, u32[]{:S(2)}, u32[]{:S(2)}) collective-permute-start(bf16[32,32,128]{2,1,0:T(8,128)(2,1)S(1)} %shard_map.93.refs_0_), channel_id=1, source_target_pairs={{0,20},{4,16},{8,28},{12,24},{16,4},{20,0},{24,12},{28,8},{1,21},{... | collective-permute-start | bytes 786440 | tf_op jit(solution)/shard_map/ppermute | solution.py:387
  103.8 0.9 shard_map.94.refs_0_
  105.5 1.5 %collective-permute-start.16 = (bf16[1,32,32,128]{3,2,1,0:T(8,128)(2,1)S(1)}, bf16[1,32,32,128]{3,2,1,0:T(8,128)(2,1)S(1)}, u32[]{:S(2)}, u32[]{:S(2)}) collective-permute-start(bf16[1,32,32,128]{3,2,1,0:T(8,128)(2,1)S(1)} %shard_map.98.near_ref), channel_id=1, source_target_pairs={{0,2},{1,3},{2,0},{3,1},{4,6},{5,7},{6,4},{7,5},{8,10},{9,11},{10,... | collective-permute-start | bytes 786440 | tf_op jit(solution)/shard_map/ppermute | solution.py:381
  107.0 0.9 shard_map.95.refs_0_
  107.9 1.9 %collective-permute-start.15 = (bf16[32,32,128]{2,1,0:T(8,128)(2,1)S(1)}, bf16[32,32,128]{2,1,0:T(8,128)(2,1)S(1)}, u32[]{:S(2)}, u32[]{:S(2)}) collective-permute-start(bf16[32,32,128]{2,1,0:T(8,128)(2,1)S(1)} %shard_map.95.refs_0_), channel_id=1, source_target_pairs={{0,16},{4,20},{8,24},{12,28},{16,0},{20,4},{24,8},{28,12},{1,17},{... | collective-permute-start | bytes 786440 | tf_op jit(solution)/shard_map/ppermute | solution.py:387
  109.9 1.2 collective-permute-done.17.far_ref
  111.1 1.9 %collective-permute-start.20 = (bf16[32,32,128]{2,1,0:T(8,128)(2,1)S(1)}, bf16[32,32,128]{2,1,0:T(8,128)(2,1)S(1)}, u32[]{:S(2)}, u32[]{:S(2)}) collective-permute-start(bf16[32,32,128]{2,1,0:T(8,128)(2,1)S(1)} %shard_map.94.refs_0_), channel_id=1, source_target_pairs={{0,12},{4,8},{8,4},{12,0},{16,28},{20,24},{24,20},{28,16},{1,13},{... | collective-permute-start | bytes 786440 | tf_op jit(solution)/shard_map/ppermute | solution.py:387
  113.0 7.3 %collective-permute-done.19.refs_2_.refs_5_ = bf16[32,32,128]{2,1,0:T(8,128)(2,1)S(1)} collective-permute-done((bf16[32,32,128]{2,1,0:T(8,128)(2,1)S(1)}, bf16[32,32,128]{2,1,0:T(8,128)(2,1)S(1)}, u32[]{:S(2)}, u32[]{:S(2)}) %collective-permute-start.19) | collective-permute-done | bytes 262176 | tf_op jit(solution)/shard_map/ppermute | solution.py:387
  120.3 0.9 shard_map.99.refs_0_
  121.2 1.7 %collective-permute-start.21 = (bf16[32,32,128]{2,1,0:T(8,128)(2,1)S(1)}, bf16[32,32,128]{2,1,0:T(8,128)(2,1)S(1)}, u32[]{:S(2)}, u32[]{:S(2)}) collective-permute-start(bf16[32,32,128]{2,1,0:T(8,128)(2,1)S(1)} %shard_map.99.refs_0_), channel_id=1, source_target_pairs={{0,4},{4,0},{8,12},{12,8},{16,20},{20,16},{24,28},{28,24},{1,5},{5... | collective-permute-start | bytes 786440 | tf_op jit(solution)/shard_map/ppermute | solution.py:387
  122.9 2.1 %shard_map.82.rows = bf16[256,256]{1,0:T(8,128)(2,1)S(1)} custom-call(s32[512]{0:T(512)S(1)} %copy-done.18, s32[8]{0:T(128)S(1)} %copy-done.19, bf16[512,256]{1,0:T(8,128)(2,1)S(1)} %copy-done.4, bf16[8,128,256]{2,1,0:T(8,128)(2,1)} %get-tuple-element.22.early), custom_call_target="tpu_custom_call" | custom-call | flops 65536 | bytes 262144 | tf_op jit(solution)/shard_map/pallas_call | solution.py:97
  125.1 0.9 shard_map.100.refs_0_
  126.0 1.6 %collective-permute-done.21.refs_1_ = bf16[32,32,128]{2,1,0:T(8,128)(2,1)S(1)} collective-permute-done((bf16[32,32,128]{2,1,0:T(8,128)(2,1)S(1)}, bf16[32,32,128]{2,1,0:T(8,128)(2,1)S(1)}, u32[]{:S(2)}, u32[]{:S(2)}) %collective-permute-start.21) | collective-permute-done | bytes 262176 | tf_op jit(solution)/shard_map/ppermute | solution.py:387
  127.6 2.2 %shard_map.101 = (bf16[32,64,256]{2,1,0:T(8,128)(2,1)S(1)}, bf16[32,64,256]{2,1,0:T(8,128)(2,1)S(1)}) custom-call(bf16[256,256]{1,0:T(8,128)(2,1)S(1)} %shard_map.96.rows_ref, bf16[32,32,128]{2,1,0:T(8,128)(2,1)S(1)} %shard_map.100.refs_0_, bf16[32,32,128]{2,1,0:T(8,128)(2,1)S(1)} %collective-permute-done.21.refs_1_, ...), custom_call_target="tpu_custom_call" | custom-call | flops 536870912 | bytes 4325376 | tf_op jit(solution)/shard_map/pallas_call | solution.py:23
  130.0 2.6 %collective-permute-done.22 = bf16[32,64,256]{2,1,0:T(8,128)(2,1)S(1)} collective-permute-done((bf16[32,64,256]{2,1,0:T(8,128)(2,1)S(1)}, bf16[32,64,256]{2,1,0:T(8,128)(2,1)S(1)}, u32[]{:S(2)}, u32[]{:S(2)}) %collective-permute-start.22) | collective-permute-done | bytes 1048608 | tf_op jit(solution)/shard_map/ppermute | solution.py:392
  132.6 1.1 add_bitcast_fusion
  (70 shorter events, 10.0 us)
Async XLA Ops:
  0.0 4.1 %collective-permute-start = (bf16[32,64,256]{2,1,0:T(8,128)(2,1)}, bf16[32,64,256]{2,1,0:T(8,128)(2,1)S(1)}, u32[]{:S(2)}, u32[]{:S(2)}) collective-permute-start(bf16[32,64,256]{2,1,0:T(8,128)(2,1)} %bitcast.5), channel_id=1, source_target_pairs={{0,1},{1,0},{2,3},{3,2},{4,5},{5,4},{6,7},{7,6},{8,9},{9,8},{10,11... | collective-permute-start | bytes 3145736 | tf_op jit(solution)/shard_map/ppermute | solution.py:341
  0.5 0.9 copy-start.2
  4.0 3.0 %copy-start.3 = (bf16[512,256]{1,0:T(8,128)(2,1)S(1)}, bf16[512,256]{1,0:T(8,128)(2,1)}, u32[]{:S(2)}) copy-start(bf16[512,256]{1,0:T(8,128)(2,1)} %orbitals.5) | copy-start | bytes 786436
  4.0 3.0 %copy-start.16 = (s32[512,1]{0,1:T(1,128)S(1)}, s32[512,1]{0,1:T(1,128)}, u32[]{:S(2)}) copy-start(s32[512,1]{0,1:T(1,128)} %param.12) | copy-start | bytes 6148
  4.0 3.0 %copy-start.17 = (s32[512]{0:T(512)S(1)}, s32[512]{0:T(512)}, u32[]{:S(2)}) copy-start(s32[512]{0:T(512)} %sub.1) | copy-start | bytes 6148
  4.0 4.9 %collective-permute-start.2 = (bf16[16,256,128]{2,1,0:T(8,128)(2,1)S(1)}, bf16[16,256,128]{2,1,0:T(8,128)(2,1)S(1)}, u32[]{:S(2)}, u32[]{:S(2)}) collective-permute-start(bf16[16,256,128]{2,1,0:T(8,128)(2,1)S(1)} %shard_map.74.rest_0_), channel_id=1, source_target_pairs={{0,1},{1,0},{2,3},{3,2},{4,5},{5,4},{6,7},{7,6},{8,9},{9,8},{10,11... | collective-permute-start | bytes 3145736 | tf_op jit(solution)/shard_map/ppermute | solution.py:350
  6.4 3.8 %copy-start.9 = (bf16[32,256,64]{1,2,0:T(8,128)(2,1)S(1)}, bf16[32,256,64]{1,2,0:T(8,128)(2,1)}, u32[]{:S(2)}) copy-start(bf16[32,256,64]{1,2,0:T(8,128)(2,1)} %param.7) | copy-start | bytes 3145732
  6.5 2.8 %collective-permute-start.1 = (bf16[16,256,128]{2,1,0:T(8,128)(2,1)S(1)}, bf16[16,256,128]{2,1,0:T(8,128)(2,1)S(1)}, u32[]{:S(2)}, u32[]{:S(2)}) collective-permute-start(bf16[16,256,128]{2,1,0:T(8,128)(2,1)S(1)} %shard_map.75.early), channel_id=1, source_target_pairs={{0,1},{1,0},{2,3},{3,2},{4,5},{5,4},{6,7},{7,6},{8,9},{9,8},{10,11... | collective-permute-start | bytes 3145736 | tf_op jit(solution)/shard_map/ppermute | solution.py:350
  9.3 1.0 copy-start
  11.9 55.8 %all-to-all-start = ((bf16[8,32,32,128]{3,2,1,0:T(8,128)(2,1)}), bf16[8,32,32,128]{3,2,1,0:T(8,128)(2,1)S(1)}, u32[]{:S(2)}, u32[]{:S(2)}) async-start(bf16[8,32,32,128]{3,2,1,0:T(8,128)(2,1)} %shard_map.77.rest_0_), calls=%async_computation | async-start | bytes 4194304 | tf_op jit(solution)/shard_map/all_to_all | solution.py:356
  21.4 0.8 copy-start.10
  22.2 14.8 %copy-start.1 = (bf16[16,256,128]{2,1,0:T(8,128)(2,1)S(1)}, bf16[16,256,128]{2,1,0:T(8,128)(2,1)}, u32[]{:S(2)}) copy-start(bf16[16,256,128]{2,1,0:T(8,128)(2,1)} %copy-done) | copy-start | bytes 3145732
  22.2 14.8 %collective-permute-start.3 = (bf16[8,128,256]{2,1,0:T(8,128)(2,1)S(1)}, bf16[8,128,256]{2,1,0:T(8,128)(2,1)S(1)}, u32[]{:S(2)}, u32[]{:S(2)}) collective-permute-start(bf16[8,128,256]{2,1,0:T(8,128)(2,1)S(1)} %get-tuple-element.19.rest_0_), channel_id=1, source_target_pairs={{0,2},{1,3},{2,0},{3,1},{4,6},{5,7},{6,4},{7,5},{8,10},{9,11},{10,... | collective-permute-start | bytes 1572872 | tf_op jit(solution)/shard_map/ppermute | solution.py:368
  25.9 14.3 %copy-start.12 = (bf16[8,128,256]{2,1,0:T(8,128)(2,1)}, bf16[8,128,256]{2,1,0:T(8,128)(2,1)S(1)}, u32[]{:S(2)}) copy-start(bf16[8,128,256]{2,1,0:T(8,128)(2,1)S(1)} %get-tuple-element.24.refs_2_) | copy-start | bytes 1572868
  25.9 22.3 %collective-permute-start.4 = (bf16[8,128,256]{2,1,0:T(8,128)(2,1)S(1)}, bf16[8,128,256]{2,1,0:T(8,128)(2,1)S(1)}, u32[]{:S(2)}, u32[]{:S(2)}) collective-permute-start(bf16[8,128,256]{2,1,0:T(8,128)(2,1)S(1)} %get-tuple-element.20.rest_0_), channel_id=1, source_target_pairs={{0,2},{1,3},{2,0},{3,1},{4,6},{5,7},{6,4},{7,5},{8,10},{9,11},{10,... | collective-permute-start | bytes 1572872 | tf_op jit(solution)/shard_map/ppermute | solution.py:368
  37.0 3.2 %copy-start.5 = (bf16[8,128,256]{2,1,0:T(8,128)(2,1)}, bf16[8,128,256]{2,1,0:T(8,128)(2,1)S(1)}, u32[]{:S(2)}) copy-start(bf16[8,128,256]{2,1,0:T(8,128)(2,1)S(1)} %collective-permute-done.3.rest_1_.refs_1_) | copy-start | bytes 1572868
  40.2 11.2 %copy-start.14 = (bf16[8,128,256]{2,1,0:T(8,128)(2,1)}, bf16[8,128,256]{2,1,0:T(8,128)(2,1)S(1)}, u32[]{:S(2)}) copy-start(bf16[8,128,256]{2,1,0:T(8,128)(2,1)S(1)} %get-tuple-element.25.refs_4_) | copy-start | bytes 1572868
  40.2 32.3 %collective-permute-start.6 = (bf16[8,128,256]{2,1,0:T(8,128)(2,1)}, bf16[8,128,256]{2,1,0:T(8,128)(2,1)}, u32[]{:S(2)}, u32[]{:S(2)}) collective-permute-start(bf16[8,128,256]{2,1,0:T(8,128)(2,1)} %get-tuple-element.21.rest_0_), channel_id=1, source_target_pairs={{0,2},{1,3},{2,0},{3,1},{4,6},{5,7},{6,4},{7,5},{8,10},{9,11},{10,... | collective-permute-start | bytes 1572872 | tf_op jit(solution)/shard_map/ppermute | solution.py:368
  48.2 3.2 %copy-start.7 = (bf16[8,128,256]{2,1,0:T(8,128)(2,1)}, bf16[8,128,256]{2,1,0:T(8,128)(2,1)S(1)}, u32[]{:S(2)}) copy-start(bf16[8,128,256]{2,1,0:T(8,128)(2,1)S(1)} %collective-permute-done.4.rest_1_.refs_3_) | copy-start | bytes 1572868
  51.4 23.5 %collective-permute-start.7 = (bf16[8,128,256]{2,1,0:T(8,128)(2,1)}, bf16[8,128,256]{2,1,0:T(8,128)(2,1)S(1)}, u32[]{:S(2)}, u32[]{:S(2)}) collective-permute-start(bf16[8,128,256]{2,1,0:T(8,128)(2,1)} %get-tuple-element.22.early), channel_id=1, source_target_pairs={{0,2},{1,3},{2,0},{3,1},{4,6},{5,7},{6,4},{7,5},{8,10},{9,11},{10,... | collective-permute-start | bytes 1572872 | tf_op jit(solution)/shard_map/ppermute | solution.py:368
  68.0 4.5 %copy-start.6 = (bf16[8,128,256]{2,1,0:T(8,128)(2,1)S(1)}, bf16[8,128,256]{2,1,0:T(8,128)(2,1)}, u32[]{:S(2)}) copy-start(bf16[8,128,256]{2,1,0:T(8,128)(2,1)} %copy-done.5) | copy-start | bytes 1572868
  68.0 4.4 %copy-start.8 = (bf16[8,128,256]{2,1,0:T(8,128)(2,1)S(1)}, bf16[8,128,256]{2,1,0:T(8,128)(2,1)}, u32[]{:S(2)}) copy-start(bf16[8,128,256]{2,1,0:T(8,128)(2,1)} %copy-done.7) | copy-start | bytes 1572868
  68.0 4.4 %copy-start.11 = (bf16[8,128,256]{2,1,0:T(8,128)(2,1)S(1)}, bf16[8,128,256]{2,1,0:T(8,128)(2,1)}, u32[]{:S(2)}) copy-start(bf16[8,128,256]{2,1,0:T(8,128)(2,1)} %copy-done.10) | copy-start | bytes 1572868
  68.1 4.4 %copy-start.13 = (bf16[8,128,256]{2,1,0:T(8,128)(2,1)S(1)}, bf16[8,128,256]{2,1,0:T(8,128)(2,1)}, u32[]{:S(2)}) copy-start(bf16[8,128,256]{2,1,0:T(8,128)(2,1)} %copy-done.12) | copy-start | bytes 1572868
  68.1 4.4 %copy-start.15 = (bf16[8,128,256]{2,1,0:T(8,128)(2,1)S(1)}, bf16[8,128,256]{2,1,0:T(8,128)(2,1)}, u32[]{:S(2)}) copy-start(bf16[8,128,256]{2,1,0:T(8,128)(2,1)} %copy-done.14) | copy-start | bytes 1572868
  68.1 9.3 %collective-permute-start.12 = (bf16[1,32,32,128]{3,2,1,0:T(8,128)(2,1)S(1)}, bf16[1,32,32,128]{3,2,1,0:T(8,128)(2,1)S(1)}, u32[]{:S(2)}, u32[]{:S(2)}) collective-permute-start(bf16[1,32,32,128]{3,2,1,0:T(8,128)(2,1)S(1)} %shard_map.83.refs_1_.near_ref), channel_id=1, source_target_pairs={{0,2},{1,3},{2,0},{3,1},{4,6},{5,7},{6,4},{7,5},{8,10},{9,11},{10,... | collective-permute-start | bytes 786440 | tf_op jit(solution)/shard_map/ppermute | solution.py:381
  70.0 13.0 %collective-permute-start.11 = (bf16[1,32,32,128]{3,2,1,0:T(8,128)(2,1)S(1)}, bf16[1,32,32,128]{3,2,1,0:T(8,128)(2,1)S(1)}, u32[]{:S(2)}, u32[]{:S(2)}) collective-permute-start(bf16[1,32,32,128]{3,2,1,0:T(8,128)(2,1)S(1)} %shard_map.84.refs_1_.near_ref), channel_id=1, source_target_pairs={{0,2},{1,3},{2,0},{3,1},{4,6},{5,7},{6,4},{7,5},{8,10},{9,11},{10,... | collective-permute-start | bytes 786440 | tf_op jit(solution)/shard_map/ppermute | solution.py:381
  70.9 17.7 %collective-permute-start.10 = (bf16[1,32,32,128]{3,2,1,0:T(8,128)(2,1)S(1)}, bf16[1,32,32,128]{3,2,1,0:T(8,128)(2,1)S(1)}, u32[]{:S(2)}, u32[]{:S(2)}) collective-permute-start(bf16[1,32,32,128]{3,2,1,0:T(8,128)(2,1)S(1)} %shard_map.85.refs_1_.near_ref), channel_id=1, source_target_pairs={{0,2},{1,3},{2,0},{3,1},{4,6},{5,7},{6,4},{7,5},{8,10},{9,11},{10,... | collective-permute-start | bytes 786440 | tf_op jit(solution)/shard_map/ppermute | solution.py:381
  74.1 20.2 %collective-permute-start.9 = (bf16[1,32,32,128]{3,2,1,0:T(8,128)(2,1)S(1)}, bf16[1,32,32,128]{3,2,1,0:T(8,128)(2,1)S(1)}, u32[]{:S(2)}, u32[]{:S(2)}) collective-permute-start(bf16[1,32,32,128]{3,2,1,0:T(8,128)(2,1)S(1)} %shard_map.86.refs_1_.near_ref), channel_id=1, source_target_pairs={{0,2},{1,3},{2,0},{3,1},{4,6},{5,7},{6,4},{7,5},{8,10},{9,11},{10,... | collective-permute-start | bytes 786440 | tf_op jit(solution)/shard_map/ppermute | solution.py:381
  75.0 24.9 %collective-permute-start.8 = (bf16[1,32,32,128]{3,2,1,0:T(8,128)(2,1)S(1)}, bf16[1,32,32,128]{3,2,1,0:T(8,128)(2,1)S(1)}, u32[]{:S(2)}, u32[]{:S(2)}) collective-permute-start(bf16[1,32,32,128]{3,2,1,0:T(8,128)(2,1)S(1)} %shard_map.87.refs_1_.near_ref), channel_id=1, source_target_pairs={{0,2},{1,3},{2,0},{3,1},{4,6},{5,7},{6,4},{7,5},{8,10},{9,11},{10,... | collective-permute-start | bytes 786440 | tf_op jit(solution)/shard_map/ppermute | solution.py:381
  78.3 22.0 %collective-permute-start.13 = (bf16[32,32,128]{2,1,0:T(8,128)(2,1)S(1)}, bf16[32,32,128]{2,1,0:T(8,128)(2,1)S(1)}, u32[]{:S(2)}, u32[]{:S(2)}) collective-permute-start(bf16[32,32,128]{2,1,0:T(8,128)(2,1)S(1)} %shard_map.90.refs_0_), channel_id=1, source_target_pairs={{0,28},{4,24},{8,20},{12,16},{16,12},{20,8},{24,4},{28,0},{1,29},{... | collective-permute-start | bytes 786440 | tf_op jit(solution)/shard_map/ppermute | solution.py:387
  83.0 22.5 %collective-permute-start.5 = (bf16[1,32,32,128]{3,2,1,0:T(8,128)(2,1)S(1)}, bf16[1,32,32,128]{3,2,1,0:T(8,128)(2,1)S(1)}, u32[]{:S(2)}, u32[]{:S(2)}) collective-permute-start(bf16[1,32,32,128]{3,2,1,0:T(8,128)(2,1)S(1)} %shard_map.88.near_ref.refs_1_), channel_id=1, source_target_pairs={{0,2},{1,3},{2,0},{3,1},{4,6},{5,7},{6,4},{7,5},{8,10},{9,11},{10,... | collective-permute-start | bytes 786440 | tf_op jit(solution)/shard_map/ppermute | solution.py:381
  88.6 18.3 %collective-permute-start.14 = (bf16[32,32,128]{2,1,0:T(8,128)(2,1)S(1)}, bf16[32,32,128]{2,1,0:T(8,128)(2,1)S(1)}, u32[]{:S(2)}, u32[]{:S(2)}) collective-permute-start(bf16[32,32,128]{2,1,0:T(8,128)(2,1)S(1)} %shard_map.91.refs_0_), channel_id=1, source_target_pairs={{0,24},{4,28},{8,16},{12,20},{16,8},{20,12},{24,0},{28,4},{1,25},{... | collective-permute-start | bytes 786440 | tf_op jit(solution)/shard_map/ppermute | solution.py:387
  94.2 16.9 %collective-permute-start.17 = (bf16[1,32,32,128]{3,2,1,0:T(8,128)(2,1)S(1)}, bf16[1,32,32,128]{3,2,1,0:T(8,128)(2,1)S(1)}, u32[]{:S(2)}, u32[]{:S(2)}) collective-permute-start(bf16[1,32,32,128]{3,2,1,0:T(8,128)(2,1)S(1)} %shard_map.97.refs_1_.near_ref), channel_id=1, source_target_pairs={{0,2},{1,3},{2,0},{3,1},{4,6},{5,7},{6,4},{7,5},{8,10},{9,11},{10,... | collective-permute-start | bytes 786440 | tf_op jit(solution)/shard_map/ppermute | solution.py:381
  99.9 13.1 %collective-permute-start.18 = (bf16[32,32,128]{2,1,0:T(8,128)(2,1)S(1)}, bf16[32,32,128]{2,1,0:T(8,128)(2,1)S(1)}, u32[]{:S(2)}, u32[]{:S(2)}) collective-permute-start(bf16[32,32,128]{2,1,0:T(8,128)(2,1)S(1)} %shard_map.92.refs_0_), channel_id=1, source_target_pairs={{0,8},{4,12},{8,0},{12,4},{16,24},{20,28},{24,16},{28,20},{1,9},{5... | collective-permute-start | bytes 786440 | tf_op jit(solution)/shard_map/ppermute | solution.py:387
  100.3 20.0 %collective-permute-start.19 = (bf16[32,32,128]{2,1,0:T(8,128)(2,1)S(1)}, bf16[32,32,128]{2,1,0:T(8,128)(2,1)S(1)}, u32[]{:S(2)}, u32[]{:S(2)}) collective-permute-start(bf16[32,32,128]{2,1,0:T(8,128)(2,1)S(1)} %shard_map.93.refs_0_), channel_id=1, source_target_pairs={{0,20},{4,16},{8,28},{12,24},{16,4},{20,0},{24,12},{28,8},{1,21},{... | collective-permute-start | bytes 786440 | tf_op jit(solution)/shard_map/ppermute | solution.py:387
  105.5 19.6 %collective-permute-start.16 = (bf16[1,32,32,128]{3,2,1,0:T(8,128)(2,1)S(1)}, bf16[1,32,32,128]{3,2,1,0:T(8,128)(2,1)S(1)}, u32[]{:S(2)}, u32[]{:S(2)}) collective-permute-start(bf16[1,32,32,128]{3,2,1,0:T(8,128)(2,1)S(1)} %shard_map.98.near_ref), channel_id=1, source_target_pairs={{0,2},{1,3},{2,0},{3,1},{4,6},{5,7},{6,4},{7,5},{8,10},{9,11},{10,... | collective-permute-start | bytes 786440 | tf_op jit(solution)/shard_map/ppermute | solution.py:381
  107.9 15.1 %copy-start.4 = (bf16[512,256]{1,0:T(8,128)(2,1)S(1)}, bf16[512,256]{1,0:T(8,128)(2,1)}, u32[]{:S(2)}) copy-start(bf16[512,256]{1,0:T(8,128)(2,1)} %orbitals.5) | copy-start | bytes 786436
  107.9 15.0 %copy-start.18 = (s32[512]{0:T(512)S(1)}, s32[512]{0:T(512)}, u32[]{:S(2)}) copy-start(s32[512]{0:T(512)} %row.1) | copy-start | bytes 6148
  107.9 15.0 %copy-start.19 = (s32[8]{0:T(128)S(1)}, s32[8]{0:T(128)}, u32[]{:S(2)}) copy-start(s32[8]{0:T(128)} %count.1) | copy-start | bytes 100
  107.9 17.2 %collective-permute-start.15 = (bf16[32,32,128]{2,1,0:T(8,128)(2,1)S(1)}, bf16[32,32,128]{2,1,0:T(8,128)(2,1)S(1)}, u32[]{:S(2)}, u32[]{:S(2)}) collective-permute-start(bf16[32,32,128]{2,1,0:T(8,128)(2,1)S(1)} %shard_map.95.refs_0_), channel_id=1, source_target_pairs={{0,16},{4,20},{8,24},{12,28},{16,0},{20,4},{24,8},{28,12},{1,17},{... | collective-permute-start | bytes 786440 | tf_op jit(solution)/shard_map/ppermute | solution.py:387
  111.1 14.0 %collective-permute-start.20 = (bf16[32,32,128]{2,1,0:T(8,128)(2,1)S(1)}, bf16[32,32,128]{2,1,0:T(8,128)(2,1)S(1)}, u32[]{:S(2)}, u32[]{:S(2)}) collective-permute-start(bf16[32,32,128]{2,1,0:T(8,128)(2,1)S(1)} %shard_map.94.refs_0_), channel_id=1, source_target_pairs={{0,12},{4,8},{8,4},{12,0},{16,28},{20,24},{24,20},{28,16},{1,13},{... | collective-permute-start | bytes 786440 | tf_op jit(solution)/shard_map/ppermute | solution.py:387
  121.2 6.4 %collective-permute-start.21 = (bf16[32,32,128]{2,1,0:T(8,128)(2,1)S(1)}, bf16[32,32,128]{2,1,0:T(8,128)(2,1)S(1)}, u32[]{:S(2)}, u32[]{:S(2)}) collective-permute-start(bf16[32,32,128]{2,1,0:T(8,128)(2,1)S(1)} %shard_map.99.refs_0_), channel_id=1, source_target_pairs={{0,4},{4,0},{8,12},{12,8},{16,20},{20,16},{24,28},{28,24},{1,5},{5... | collective-permute-start | bytes 786440 | tf_op jit(solution)/shard_map/ppermute | solution.py:387
  129.9 2.7 %collective-permute-start.22 = (bf16[32,64,256]{2,1,0:T(8,128)(2,1)S(1)}, bf16[32,64,256]{2,1,0:T(8,128)(2,1)S(1)}, u32[]{:S(2)}, u32[]{:S(2)}) collective-permute-start(bf16[32,64,256]{2,1,0:T(8,128)(2,1)S(1)} %get-tuple-element.28), channel_id=1, source_target_pairs={{0,1},{1,0},{2,3},{3,2},{4,5},{5,4},{6,7},{7,6},{8,9},{9,8},{10,11... | collective-permute-start | bytes 3145736 | tf_op jit(solution)/shard_map/ppermute | solution.py:392

commit v5 on v4

--- a/solution.py
+++ b/solution.py
@@ -31,7 +31,7 @@
     )(*ins, *early)
 
 
-def order_body(orbitals, left, side_rows, held):
+def order_orbitals(orbitals, left, side_rows, held):
     vir = orbitals.shape[1]
     part = lax.axis_index("ao")
     nu_part = side_rows.shape[0] // 2
@@ -44,12 +44,6 @@
     for q in range(2):
         start = pl.multiple_of((part ^ q) * nu_part, nu_part)
         side_rows[pl.ds(q * nu_part, nu_part), :] = held[pl.ds(start, nu_part), :]
-
-
-def order_orbitals(orbitals, nu_part):
-    count, vir = orbitals.shape
-    outs = [jax.ShapeDtypeStruct((vir, count), BF16), jax.ShapeDtypeStruct((2 * nu_part, vir), BF16)]
-    return call(order_body, outs, (orbitals,), count * vir, [pltpu.VMEM((count, vir), BF16)])
 
 
 def source_body(src, sub, orbitals, early, source, held, ahead):
@@ -195,15 +189,24 @@
     return product[:, :width].astype(BF16), product[:, width:].astype(BF16)
 
 
-def give_kernel(start, left_ref, tiles, *rest):
-    out, held, sems = rest[-3:]
-    copies = start_copies(True, start, tiles, held, sems)
+def transform_tiles(left_ref, copies, held, out):
     size = out.shape[0] // len(copies)
     left = left_ref[...]
     for n, copy in enumerate(copies):
         copy.wait()
         for t in range(n * size, (n + 1) * size, 2):
             out[t], out[t + 1] = pair_dot(left, held, t)
+
+
+def give_kernel(start, left_ref, tiles, *rest):
+    out, held, sems = rest[-3:]
+    transform_tiles(left_ref, start_copies(True, start, tiles, held, sems), held, out)
+
+
+def first_kernel(start, orbitals, tiles, out, left_ref, side_rows, held, sems, lines):
+    copies = start_copies(True, start, tiles, held, sems)
+    order_orbitals(orbitals, left_ref, side_rows, lines)
+    transform_tiles(left_ref, copies, held, out)
 
 
 def finish_kernel(start, skip, left_ref, tiles, other, right_ref, *rest):
@@ -230,9 +233,9 @@
 PIECE = 4
 
 
-def tile_call(body, count, tiles, ins, outs, early=()):
+def tile_call(body, count, tiles, ins, outs, early=(), scratch=()):
     _, sig, nu = tiles.shape
-    vir = ins[0].shape[0]
+    vir = outs[0].shape[1]
     whole = pl.BlockSpec(memory_space=pltpu.VMEM)
     away = pl.BlockSpec(memory_space=pl.ANY)
     flops = 2 * count * vir * nu * (sig + 2 * vir * (len(outs) - 1))
@@ -241,7 +244,7 @@
         out_shape=outs,
         in_specs=[whole, away] + [whole] * (len(ins) - 1) + [away] * len(early),
         out_specs=[whole] * len(outs),
-        scratch_shapes=[pltpu.VMEM((count, sig, nu), BF16), pltpu.SemaphoreType.DMA((count // PIECE,))],
+        scratch_shapes=[pltpu.VMEM((count, sig, nu), BF16), pltpu.SemaphoreType.DMA((count // PIECE,)), *scratch],
         cost_estimate=pl.CostEstimate(
             flops=flops, bytes_accessed=2 * count * sig * nu * 2, transcendentals=0
         ),
@@ -339,7 +342,6 @@
 
     mine = jnp.swapaxes(amplitudes, 1, 2)
     other = lax.ppermute(mine, "ao", near)
-    left, side_rows = order_orbitals(orbitals, nu_part)
     def tile_shape(count, width):
         return jax.ShapeDtypeStruct((count, vir, width), BF16)
 
@@ -349,7 +351,16 @@
         (given,) = tile_call(body, half // 2, tiles, (left,), outs, early)
         return given, lax.ppermute(given, "ao", near)
 
-    given, first_parts = give(0, ())
+    outs = [
+        tile_shape(half // 2, nu_part),
+        jax.ShapeDtypeStruct((vir, orbitals.shape[0]), BF16),
+        jax.ShapeDtypeStruct((2 * nu_part, vir), BF16),
+    ]
+    scratch = [pltpu.VMEM(orbitals.shape, BF16)]
+    given, left, side_rows = tile_call(
+        functools.partial(first_kernel, 0), half // 2, tiles, (orbitals,), outs, (), scratch
+    )
+    first_parts = lax.ppermute(given, "ao", near)
     given, second_parts = give(half // 2, [given, other])
     source_rows = gather(source_body, (tile_src[:, 0], tile_sub), orbitals, given)
     sent = pair_rows(source_rows, mine, other, nodes, (first_parts, second_parts))
@@ -374,7 +385,7 @@
     for n in range(1, lower):
         units += [[nodes - 1 - n], [light[n - 1]]]
     units.append([light[-1]])
-    wait_for = {4: (0,), 5: (1,), 6: (2, 3), 7: (4,)}
+    wait_for = {4: (0,), 5: (1,), 6: (2, 3)}
     blocks_of, far_blocks = [], []
     for unit in units:
         blocks_of.append(turn(own, arrived, unit, blocks_of[-1:]))
@@ -385,8 +396,8 @@
         made = products(blocks_of[n], far_blocks[n], tiles_done, early)
         for k, x in zip(unit, made):
             returned[k] = lax.ppermute(x, "occ", [(o, o ^ k) for o in range(nodes)]) if k else x
-    last_far = [returned[k] for k in (lower, lower + 1)]
-    target_rows = rows_after(target_rows, last_far[:1])
+    late = [returned[k] for m in (5, 4) if m < len(units) for k in units[m]]
+    target_rows = rows_after(target_rows, late)
     returned = [returned[k] for k in range(nodes)]
     keep, give_up = back_transform(target_rows, returned)
     return jnp.swapaxes(keep + lax.ppermute(give_up, "ao", near), 1, 2)
@@ -446,7 +457,8 @@
     def whole(amplitudes, *rest):
         nodes = mesh.shape["occ"]
         rows = amplitudes.shape[0] // nodes
-        body = shards if rows % 16 == 0 and nodes <= 16 else plain_shards
+        few = nodes <= 16 and nodes & (nodes - 1) == 0
+        body = shards if few and rows % 16 == 0 else plain_shards
         return jax.shard_map(
             body, mesh=mesh, in_specs=placed, out_specs=P("occ", None, "ao"), check_vma=False
         )(amplitudes, *rest)

time: 134 us -> 131 us (0.978)
  waiting for transfers between devices: 56.2 us -> 53.4 us
    ppermute x7, waiting for transfers between devices: 8.9 us -> 5.98 us  [shards(): lax.ppermute(x, 'occ', [(o, o ^ k) for o in range(nodes)])]
    pallas_call x12 -> x11, Pallas kernels: 10.9 us -> 10.7 us  [call(): pl.pallas_call(body, out_shape=outs, in_specs=[whole] * len(ins) + [pl.Bl...]
  transfers between devices with their start and end apart: 24 -> 24, of which waited for: 14 -> 13; matrix products, arithmetic and copies ran while one was open for 0% -> 0% of each run, Pallas kernels for 23% -> 23%
where the time goes in v5:
time: 131 us
  waiting for transfers between devices  53.4 us (41%)
  starting transfers between devices  38.5 us (29%)
  Pallas kernels  34.7 us (26%)
  local copies, waits for them, and re-layouts  2.79 us (2%)
    ppermute x4, waiting for transfers between devices, shards(): parts += [here, lax.ppermute(there, 'ao', far)]  17 us
    pallas_call x6, Pallas kernels, tile_call(): pl.pallas_call(body, out_shape=outs, in_specs=[whole, away] + [whole] * (...  15.6 us
    all_to_all x1, waiting for transfers between devices, shards(): lax.all_to_all(sent, 'occ', split_axis=0, concat_axis=0, tiled=True)  14.7 us
    ppermute x7, starting transfers between devices, shards(): lax.ppermute(x, 'occ', [(o, o ^ k) for o in range(nodes)])  14.5 us
    ppermute x8, waiting for transfers between devices, shards(): far_blocks.append(lax.ppermute(blocks_of[-1], 'ao', far))  12.7 us
    pallas_call x11, Pallas kernels, call(): pl.pallas_call(body, out_shape=outs, in_specs=[whole] * len(ins) + [pl.Bl...  10.7 us
    ppermute x8, starting transfers between devices, shards(): far_blocks.append(lax.ppermute(blocks_of[-1], 'ao', far))  10.4 us
    all_to_all x1, starting transfers between devices, shards(): lax.all_to_all(sent, 'occ', split_axis=0, concat_axis=0, tiled=True)  7.21 us
  transfers between devices with their start and end apart: 24, of which 13 were waited for; matrix products, arithmetic and copies ran while one was open for 0% of the time, Pallas kernels for 23%

profile of v5, /device:TPU:0, one launch (start us, length us, event | category | flops | bytes accessed | tf_op | source)
XLA Modules:
  0.0 130.8 jit_solution(14543717815523399191)
XLA Ops:
  0.5 0.9 copy-done.2
  1.4 2.4 %shard_map.73 = (bf16[16,256,128]{2,1,0:T(8,128)(2,1)S(1)}, bf16[256,512]{1,0:T(8,128)(2,1)S(1)}, bf16[256,256]{1,0:T(8,128)(2,1)S(1)}) custom-call(bf16[512,256]{1,0:T(8,128)(2,1)S(1)} %copy-done.2, bf16[64,512,128]{2,1,0:T(8,128)(2,1)} %tiles.11), custom_call_target="tpu_custom_call" | custom-call | flops 1610612736 | bytes 4194304 | tf_op jit(solution)/shard_map/pallas_call | solution.py:242
  4.0 2.4 %shard_map.74.early = bf16[16,256,128]{2,1,0:T(8,128)(2,1)S(1)} custom-call(bf16[256,512]{1,0:T(8,128)(2,1)S(1)} %get-tuple-element.18.left_ref, bf16[64,512,128]{2,1,0:T(8,128)(2,1)} %tiles.11, bf16[16,256,128]{2,1,0:T(8,128)(2,1)S(1)} %get-tuple-element.19.rest_0_, bf16[32,64,256]{2,1,0:T(8,128)(2,1)S(1)} %collective-permute-done.rest_1_.other_ref), custom_call_target="tpu_custom_call" | custom-call | flops 536870912 | bytes 4194304 | tf_op jit(solution)/shard_map/pallas_call | solution.py:242
  6.9 1.9 %shard_map.75.rows_ref = bf16[256,256]{1,0:T(8,128)(2,1)S(1)} custom-call(s32[512]{0:T(512)S(1)} %bitcast.7, s32[512]{0:T(512)S(1)} %copy-done.17, bf16[512,256]{1,0:T(8,128)(2,1)S(1)} %copy-done.3, bf16[16,256,128]{2,1,0:T(8,128)(2,1)S(1)} %shard_map.74.early), custom_call_target="tpu_custom_call" | custom-call | flops 65536 | bytes 262144 | tf_op jit(solution)/shard_map/pallas_call | solution.py:91
  9.2 1.0 copy-done
  10.1 1.7 %shard_map.76.rest_0_ = bf16[8,32,32,128]{3,2,1,0:T(8,128)(2,1)} custom-call(bf16[256,256]{1,0:T(8,128)(2,1)S(1)} %shard_map.75.rows_ref, bf16[32,64,256]{2,1,0:T(8,128)(2,1)S(1)} %bitcast.6, bf16[32,64,256]{2,1,0:T(8,128)(2,1)S(1)} %collective-permute-done.rest_1_.other_ref, bf16[16,256,128]{2,1,0:T(8,128)(2,1)S(1)} %collective-permute-done.2.rest_0_.other, ...), custom_call_target="tpu_custom_call" | custom-call | flops 536870912 | bytes 2097152 | tf_op jit(solution)/shard_map/pallas_call | solution.py:127
  11.8 7.2 %all-to-all-start = ((bf16[8,32,32,128]{3,2,1,0:T(8,128)(2,1)}), bf16[8,32,32,128]{3,2,1,0:T(8,128)(2,1)S(1)}, u32[]{:S(2)}, u32[]{:S(2)}) async-start(bf16[8,32,32,128]{3,2,1,0:T(8,128)(2,1)} %shard_map.76.rest_0_), calls=%async_computation | async-start | bytes 4194304 | tf_op jit(solution)/shard_map/all_to_all | solution.py:367
  19.1 2.2 %shard_map.77 = (bf16[8,128,256]{2,1,0:T(8,128)(2,1)S(1)}, bf16[8,128,256]{2,1,0:T(8,128)(2,1)S(1)}) custom-call(bf16[256,512]{1,0:T(8,128)(2,1)S(1)} %get-tuple-element.18.left_ref, bf16[64,512,128]{2,1,0:T(8,128)(2,1)} %tiles.11, bf16[16,256,128]{2,1,0:T(8,128)(2,1)S(1)} %collective-permute-done.2.rest_0_.other, ...), custom_call_target="tpu_custom_call" | custom-call | flops 201326592 | bytes 2097152 | tf_op jit(solution)/shard_map/pallas_call | solution.py:242
  22.1 1.5 %collective-permute-start.3 = (bf16[8,128,256]{2,1,0:T(8,128)(2,1)S(1)}, bf16[8,128,256]{2,1,0:T(8,128)(2,1)S(1)}, u32[]{:S(2)}, u32[]{:S(2)}) collective-permute-start(bf16[8,128,256]{2,1,0:T(8,128)(2,1)S(1)} %get-tuple-element.21.rest_0_), channel_id=1, source_target_pairs={{0,2},{1,3},{2,0},{3,1},{4,6},{5,7},{6,4},{7,5},{8,10},{9,11},{10,... | collective-permute-start | bytes 1572872 | tf_op jit(solution)/shard_map/ppermute | solution.py:379
  23.6 2.2 %shard_map.78 = (bf16[8,128,256]{2,1,0:T(8,128)(2,1)S(1)}, bf16[8,128,256]{2,1,0:T(8,128)(2,1)S(1)}) custom-call(bf16[256,512]{1,0:T(8,128)(2,1)S(1)} %get-tuple-element.18.left_ref, bf16[64,512,128]{2,1,0:T(8,128)(2,1)} %tiles.11, bf16[16,256,128]{2,1,0:T(8,128)(2,1)S(1)} %collective-permute-done.2.rest_0_.other, ...), custom_call_target="tpu_custom_call" | custom-call | flops 201326592 | bytes 2097152 | tf_op jit(solution)/shard_map/pallas_call | solution.py:242
  26.4 10.5 %collective-permute-done.3.rest_1_.refs_1_ = bf16[8,128,256]{2,1,0:T(8,128)(2,1)S(1)} collective-permute-done((bf16[8,128,256]{2,1,0:T(8,128)(2,1)S(1)}, bf16[8,128,256]{2,1,0:T(8,128)(2,1)S(1)}, u32[]{:S(2)}, u32[]{:S(2)}) %collective-permute-start.3) | collective-permute-done | bytes 524320 | tf_op jit(solution)/shard_map/ppermute | solution.py:379
  36.9 3.2 %shard_map.79 = (bf16[8,128,256]{2,1,0:T(8,128)(2,1)S(1)}, bf16[8,128,256]{2,1,0:T(8,128)(2,1)}) custom-call(bf16[256,512]{1,0:T(8,128)(2,1)S(1)} %get-tuple-element.18.left_ref, bf16[64,512,128]{2,1,0:T(8,128)(2,1)} %tiles.11, bf16[16,256,128]{2,1,0:T(8,128)(2,1)S(1)} %copy-done.1, bf16[256,256]{1,0:T(8,128)(2,1)S(1)} %get-tuple-element.20.right_ref, ...), custom_call_target="tpu_custom_call" | custom-call | flops 201326592 | bytes 2097152 | tf_op jit(solution)/shard_map/pallas_call | solution.py:242
  40.1 1.5 %collective-permute-start.6 = (bf16[8,128,256]{2,1,0:T(8,128)(2,1)}, bf16[8,128,256]{2,1,0:T(8,128)(2,1)}, u32[]{:S(2)}, u32[]{:S(2)}) collective-permute-start(bf16[8,128,256]{2,1,0:T(8,128)(2,1)} %get-tuple-element.23.rest_0_), channel_id=1, source_target_pairs={{0,2},{1,3},{2,0},{3,1},{4,6},{5,7},{6,4},{7,5},{8,10},{9,11},{10,... | collective-permute-start | bytes 1572872 | tf_op jit(solution)/shard_map/ppermute | solution.py:379
  41.7 6.5 %collective-permute-done.4.rest_1_.refs_3_ = bf16[8,128,256]{2,1,0:T(8,128)(2,1)S(1)} collective-permute-done((bf16[8,128,256]{2,1,0:T(8,128)(2,1)S(1)}, bf16[8,128,256]{2,1,0:T(8,128)(2,1)S(1)}, u32[]{:S(2)}, u32[]{:S(2)}) %collective-permute-start.4) | collective-permute-done | bytes 524320 | tf_op jit(solution)/shard_map/ppermute | solution.py:379
  48.1 3.2 %shard_map.80 = (bf16[8,128,256]{2,1,0:T(8,128)(2,1)S(1)}, bf16[8,128,256]{2,1,0:T(8,128)(2,1)}) custom-call(bf16[256,512]{1,0:T(8,128)(2,1)S(1)} %get-tuple-element.18.left_ref, bf16[64,512,128]{2,1,0:T(8,128)(2,1)} %tiles.11, bf16[16,256,128]{2,1,0:T(8,128)(2,1)S(1)} %copy-done.1, bf16[256,256]{1,0:T(8,128)(2,1)S(1)} %get-tuple-element.20.right_ref, ...), custom_call_target="tpu_custom_call" | custom-call | flops 201326592 | bytes 2097152 | tf_op jit(solution)/shard_map/pallas_call | solution.py:242
  51.3 1.6 %collective-permute-start.7 = (bf16[8,128,256]{2,1,0:T(8,128)(2,1)}, bf16[8,128,256]{2,1,0:T(8,128)(2,1)S(1)}, u32[]{:S(2)}, u32[]{:S(2)}) collective-permute-start(bf16[8,128,256]{2,1,0:T(8,128)(2,1)} %get-tuple-element.24.early), channel_id=1, source_target_pairs={{0,2},{1,3},{2,0},{3,1},{4,6},{5,7},{6,4},{7,5},{8,10},{9,11},{10,... | collective-permute-start | bytes 1572872 | tf_op jit(solution)/shard_map/ppermute | solution.py:379
  52.9 14.7 %all-to-all-done.refs_0_ = bf16[8,32,32,128]{3,2,1,0:T(8,128)(2,1)S(1)} async-done(((bf16[8,32,32,128]{3,2,1,0:T(8,128)(2,1)}), bf16[8,32,32,128]{3,2,1,0:T(8,128)(2,1)S(1)}, u32[]{:S(2)}, u32[]{:S(2)}) %all-to-all-start) | async-done | bytes 2097184 | tf_op jit(solution)/shard_map/all_to_all | solution.py:367
  68.0 1.6 %collective-permute-start.12 = (bf16[1,32,32,128]{3,2,1,0:T(8,128)(2,1)S(1)}, bf16[1,32,32,128]{3,2,1,0:T(8,128)(2,1)S(1)}, u32[]{:S(2)}, u32[]{:S(2)}) collective-permute-start(bf16[1,32,32,128]{3,2,1,0:T(8,128)(2,1)S(1)} %shard_map.82.refs_1_.near_ref), channel_id=1, source_target_pairs={{0,2},{1,3},{2,0},{3,1},{4,6},{5,7},{6,4},{7,5},{8,10},{9,11},{10,... | collective-permute-start | bytes 786440 | tf_op jit(solution)/shard_map/ppermute | solution.py:392
  70.8 1.6 %collective-permute-start.10 = (bf16[1,32,32,128]{3,2,1,0:T(8,128)(2,1)S(1)}, bf16[1,32,32,128]{3,2,1,0:T(8,128)(2,1)S(1)}, u32[]{:S(2)}, u32[]{:S(2)}) collective-permute-start(bf16[1,32,32,128]{3,2,1,0:T(8,128)(2,1)S(1)} %shard_map.84.refs_1_.near_ref), channel_id=1, source_target_pairs={{0,2},{1,3},{2,0},{3,1},{4,6},{5,7},{6,4},{7,5},{8,10},{9,11},{10,... | collective-permute-start | bytes 786440 | tf_op jit(solution)/shard_map/ppermute | solution.py:392
  72.4 1.2 shard_map.88.dressed
  74.9 1.6 %collective-permute-start.8 = (bf16[1,32,32,128]{3,2,1,0:T(8,128)(2,1)S(1)}, bf16[1,32,32,128]{3,2,1,0:T(8,128)(2,1)S(1)}, u32[]{:S(2)}, u32[]{:S(2)}) collective-permute-start(bf16[1,32,32,128]{3,2,1,0:T(8,128)(2,1)S(1)} %shard_map.86.refs_1_.near_ref), channel_id=1, source_target_pairs={{0,2},{1,3},{2,0},{3,1},{4,6},{5,7},{6,4},{7,5},{8,10},{9,11},{10,... | collective-permute-start | bytes 786440 | tf_op jit(solution)/shard_map/ppermute | solution.py:392
  77.3 0.9 shard_map.89.refs_0_
  78.2 3.1 %collective-permute-start.13 = (bf16[32,32,128]{2,1,0:T(8,128)(2,1)S(1)}, bf16[32,32,128]{2,1,0:T(8,128)(2,1)S(1)}, u32[]{:S(2)}, u32[]{:S(2)}) collective-permute-start(bf16[32,32,128]{2,1,0:T(8,128)(2,1)S(1)} %shard_map.89.refs_0_), channel_id=1, source_target_pairs={{0,28},{4,24},{8,20},{12,16},{16,12},{20,8},{24,4},{28,0},{1,29},{... | collective-permute-start | bytes 786440 | tf_op jit(solution)/shard_map/ppermute | solution.py:398
  82.0 0.9 collective-permute-done.11.far_ref
  82.9 1.5 %collective-permute-start.5 = (bf16[1,32,32,128]{3,2,1,0:T(8,128)(2,1)S(1)}, bf16[1,32,32,128]{3,2,1,0:T(8,128)(2,1)S(1)}, u32[]{:S(2)}, u32[]{:S(2)}) collective-permute-start(bf16[1,32,32,128]{3,2,1,0:T(8,128)(2,1)S(1)} %shard_map.87.near_ref.refs_1_), channel_id=1, source_target_pairs={{0,2},{1,3},{2,0},{3,1},{4,6},{5,7},{6,4},{7,5},{8,10},{9,11},{10,... | collective-permute-start | bytes 786440 | tf_op jit(solution)/shard_map/ppermute | solution.py:392
  84.4 0.9 shard_map.90.refs_0_
  85.3 3.2 %collective-permute-done.10.far_ref = bf16[1,32,32,128]{3,2,1,0:T(8,128)(2,1)S(1)} collective-permute-done((bf16[1,32,32,128]{3,2,1,0:T(8,128)(2,1)S(1)}, bf16[1,32,32,128]{3,2,1,0:T(8,128)(2,1)S(1)}, u32[]{:S(2)}, u32[]{:S(2)}) %collective-permute-start.10) | collective-permute-done | bytes 262176 | tf_op jit(solution)/shard_map/ppermute | solution.py:392
  88.5 2.2 %collective-permute-start.14 = (bf16[32,32,128]{2,1,0:T(8,128)(2,1)S(1)}, bf16[32,32,128]{2,1,0:T(8,128)(2,1)S(1)}, u32[]{:S(2)}, u32[]{:S(2)}) collective-permute-start(bf16[32,32,128]{2,1,0:T(8,128)(2,1)S(1)} %shard_map.90.refs_0_), channel_id=1, source_target_pairs={{0,24},{4,28},{8,16},{12,20},{16,8},{20,12},{24,0},{28,4},{1,25},{... | collective-permute-start | bytes 786440 | tf_op jit(solution)/shard_map/ppermute | solution.py:398
  90.7 0.9 shard_map.91.refs_0_
  91.6 2.5 %collective-permute-done.9.far_ref = bf16[1,32,32,128]{3,2,1,0:T(8,128)(2,1)S(1)} collective-permute-done((bf16[1,32,32,128]{3,2,1,0:T(8,128)(2,1)S(1)}, bf16[1,32,32,128]{3,2,1,0:T(8,128)(2,1)S(1)}, u32[]{:S(2)}, u32[]{:S(2)}) %collective-permute-start.9) | collective-permute-done | bytes 262176 | tf_op jit(solution)/shard_map/ppermute | solution.py:392
  94.1 1.5 %collective-permute-start.18 = (bf16[1,32,32,128]{3,2,1,0:T(8,128)(2,1)S(1)}, bf16[1,32,32,128]{3,2,1,0:T(8,128)(2,1)S(1)}, u32[]{:S(2)}, u32[]{:S(2)}) collective-permute-start(bf16[1,32,32,128]{3,2,1,0:T(8,128)(2,1)S(1)} %shard_map.96.refs_1_.near_ref), channel_id=1, source_target_pairs={{0,2},{1,3},{2,0},{3,1},{4,6},{5,7},{6,4},{7,5},{8,10},{9,11},{10,... | collective-permute-start | bytes 786440 | tf_op jit(solution)/shard_map/ppermute | solution.py:392
  95.6 0.9 shard_map.92.refs_0_
  96.6 3.2 %collective-permute-done.8.far_ref = bf16[1,32,32,128]{3,2,1,0:T(8,128)(2,1)S(1)} collective-permute-done((bf16[1,32,32,128]{3,2,1,0:T(8,128)(2,1)S(1)}, bf16[1,32,32,128]{3,2,1,0:T(8,128)(2,1)S(1)}, u32[]{:S(2)}, u32[]{:S(2)}) %collective-permute-start.8) | collective-permute-done | bytes 262176 | tf_op jit(solution)/shard_map/ppermute | solution.py:392
  100.2 3.2 %collective-permute-start.20 = (bf16[32,32,128]{2,1,0:T(8,128)(2,1)S(1)}, bf16[32,32,128]{2,1,0:T(8,128)(2,1)S(1)}, u32[]{:S(2)}, u32[]{:S(2)}) collective-permute-start(bf16[32,32,128]{2,1,0:T(8,128)(2,1)S(1)} %shard_map.92.refs_0_), channel_id=1, source_target_pairs={{0,20},{4,16},{8,28},{12,24},{16,4},{20,0},{24,12},{28,8},{1,21},{... | collective-permute-start | bytes 786440 | tf_op jit(solution)/shard_map/ppermute | solution.py:398
  103.7 0.9 shard_map.93.refs_0_
  105.4 1.5 %collective-permute-start.17 = (bf16[1,32,32,128]{3,2,1,0:T(8,128)(2,1)S(1)}, bf16[1,32,32,128]{3,2,1,0:T(8,128)(2,1)S(1)}, u32[]{:S(2)}, u32[]{:S(2)}) collective-permute-start(bf16[1,32,32,128]{3,2,1,0:T(8,128)(2,1)S(1)} %shard_map.97.near_ref), channel_id=1, source_target_pairs={{0,2},{1,3},{2,0},{3,1},{4,6},{5,7},{6,4},{7,5},{8,10},{9,11},{10,... | collective-permute-start | bytes 786440 | tf_op jit(solution)/shard_map/ppermute | solution.py:392
  106.9 1.9 %collective-permute-start.16 = (bf16[32,32,128]{2,1,0:T(8,128)(2,1)S(1)}, bf16[32,32,128]{2,1,0:T(8,128)(2,1)S(1)}, u32[]{:S(2)}, u32[]{:S(2)}) collective-permute-start(bf16[32,32,128]{2,1,0:T(8,128)(2,1)S(1)} %shard_map.93.refs_0_), channel_id=1, source_target_pairs={{0,12},{4,8},{8,4},{12,0},{16,28},{20,24},{24,20},{28,16},{1,13},{... | collective-permute-start | bytes 786440 | tf_op jit(solution)/shard_map/ppermute | solution.py:398
  108.8 0.9 shard_map.94.refs_0_
  109.7 1.3 collective-permute-done.18.far_ref
  111.0 1.9 %collective-permute-start.15 = (bf16[32,32,128]{2,1,0:T(8,128)(2,1)S(1)}, bf16[32,32,128]{2,1,0:T(8,128)(2,1)S(1)}, u32[]{:S(2)}, u32[]{:S(2)}) collective-permute-start(bf16[32,32,128]{2,1,0:T(8,128)(2,1)S(1)} %shard_map.94.refs_0_), channel_id=1, source_target_pairs={{0,16},{4,20},{8,24},{12,28},{16,0},{20,4},{24,8},{28,12},{1,17},{... | collective-permute-start | bytes 786440 | tf_op jit(solution)/shard_map/ppermute | solution.py:398
  112.9 0.9 shard_map.98.refs_0_
  113.8 1.9 %collective-permute-start.21 = (bf16[32,32,128]{2,1,0:T(8,128)(2,1)S(1)}, bf16[32,32,128]{2,1,0:T(8,128)(2,1)S(1)}, u32[]{:S(2)}, u32[]{:S(2)}) collective-permute-start(bf16[32,32,128]{2,1,0:T(8,128)(2,1)S(1)} %shard_map.98.refs_0_), channel_id=1, source_target_pairs={{0,4},{4,0},{8,12},{12,8},{16,20},{20,16},{24,28},{28,24},{1,5},{5... | collective-permute-start | bytes 786440 | tf_op jit(solution)/shard_map/ppermute | solution.py:398
  115.7 2.1 %shard_map.81.rows = bf16[256,256]{1,0:T(8,128)(2,1)S(1)} custom-call(s32[512]{0:T(512)S(1)} %copy-done.18, s32[8]{0:T(128)S(1)} %copy-done.19, bf16[512,256]{1,0:T(8,128)(2,1)S(1)} %copy-done.4, bf16[8,128,256]{2,1,0:T(8,128)(2,1)} %get-tuple-element.24.early), custom_call_target="tpu_custom_call" | custom-call | flops 65536 | bytes 262144 | tf_op jit(solution)/shard_map/pallas_call | solution.py:91
  117.8 0.9 shard_map.99.refs_0_
  118.7 6.0 %collective-permute-done.15.rest_0_.refs_4_ = bf16[32,32,128]{2,1,0:T(8,128)(2,1)S(1)} collective-permute-done((bf16[32,32,128]{2,1,0:T(8,128)(2,1)S(1)}, bf16[32,32,128]{2,1,0:T(8,128)(2,1)S(1)}, u32[]{:S(2)}, u32[]{:S(2)}) %collective-permute-start.15) | collective-permute-done | bytes 262176 | tf_op jit(solution)/shard_map/ppermute | solution.py:398
  124.7 2.2 %shard_map.100 = (bf16[32,64,256]{2,1,0:T(8,128)(2,1)S(1)}, bf16[32,64,256]{2,1,0:T(8,128)(2,1)S(1)}) custom-call(bf16[256,256]{1,0:T(8,128)(2,1)S(1)} %shard_map.95.rows_ref, bf16[32,32,128]{2,1,0:T(8,128)(2,1)S(1)} %shard_map.99.refs_0_, bf16[32,32,128]{2,1,0:T(8,128)(2,1)S(1)} %collective-permute-done.21.refs_1_, ...), custom_call_target="tpu_custom_call" | custom-call | flops 536870912 | bytes 4325376 | tf_op jit(solution)/shard_map/pallas_call | solution.py:23
  127.0 2.6 %collective-permute-done.22 = bf16[32,64,256]{2,1,0:T(8,128)(2,1)S(1)} collective-permute-done((bf16[32,64,256]{2,1,0:T(8,128)(2,1)S(1)}, bf16[32,64,256]{2,1,0:T(8,128)(2,1)S(1)}, u32[]{:S(2)}, u32[]{:S(2)}) %collective-permute-start.22) | collective-permute-done | bytes 1048608 | tf_op jit(solution)/shard_map/ppermute | solution.py:403
  129.7 1.1 add_bitcast_fusion
  (69 shorter events, 8.9 us)
Async XLA Ops:
  0.0 4.0 %collective-permute-start = (bf16[32,64,256]{2,1,0:T(8,128)(2,1)}, bf16[32,64,256]{2,1,0:T(8,128)(2,1)S(1)}, u32[]{:S(2)}, u32[]{:S(2)}) collective-permute-start(bf16[32,64,256]{2,1,0:T(8,128)(2,1)} %bitcast.5), channel_id=1, source_target_pairs={{0,1},{1,0},{2,3},{3,2},{4,5},{5,4},{6,7},{7,6},{8,9},{9,8},{10,11... | collective-permute-start | bytes 3145736 | tf_op jit(solution)/shard_map/ppermute | solution.py:344
  0.5 0.9 copy-start.2
  3.9 5.0 %collective-permute-start.2 = (bf16[16,256,128]{2,1,0:T(8,128)(2,1)S(1)}, bf16[16,256,128]{2,1,0:T(8,128)(2,1)S(1)}, u32[]{:S(2)}, u32[]{:S(2)}) collective-permute-start(bf16[16,256,128]{2,1,0:T(8,128)(2,1)S(1)} %get-tuple-element.19.rest_0_), channel_id=1, source_target_pairs={{0,1},{1,0},{2,3},{3,2},{4,5},{5,4},{6,7},{7,6},{8,9},{9,8},{10,11... | collective-permute-start | bytes 3145736 | tf_op jit(solution)/shard_map/ppermute | solution.py:363
  4.0 2.9 %copy-start.3 = (bf16[512,256]{1,0:T(8,128)(2,1)S(1)}, bf16[512,256]{1,0:T(8,128)(2,1)}, u32[]{:S(2)}) copy-start(bf16[512,256]{1,0:T(8,128)(2,1)} %orbitals.5) | copy-start | bytes 786436
  4.0 2.9 %copy-start.16 = (s32[512,1]{0,1:T(1,128)S(1)}, s32[512,1]{0,1:T(1,128)}, u32[]{:S(2)}) copy-start(s32[512,1]{0,1:T(1,128)} %param.12) | copy-start | bytes 6148
  4.0 2.9 %copy-start.17 = (s32[512]{0:T(512)S(1)}, s32[512]{0:T(512)}, u32[]{:S(2)}) copy-start(s32[512]{0:T(512)} %sub.1) | copy-start | bytes 6148
  6.3 3.8 %copy-start.9 = (bf16[32,256,64]{1,2,0:T(8,128)(2,1)S(1)}, bf16[32,256,64]{1,2,0:T(8,128)(2,1)}, u32[]{:S(2)}) copy-start(bf16[32,256,64]{1,2,0:T(8,128)(2,1)} %param.7) | copy-start | bytes 3145732
  6.4 2.8 %collective-permute-start.1 = (bf16[16,256,128]{2,1,0:T(8,128)(2,1)S(1)}, bf16[16,256,128]{2,1,0:T(8,128)(2,1)S(1)}, u32[]{:S(2)}, u32[]{:S(2)}) collective-permute-start(bf16[16,256,128]{2,1,0:T(8,128)(2,1)S(1)} %shard_map.74.early), channel_id=1, source_target_pairs={{0,1},{1,0},{2,3},{3,2},{4,5},{5,4},{6,7},{7,6},{8,9},{9,8},{10,11... | collective-permute-start | bytes 3145736 | tf_op jit(solution)/shard_map/ppermute | solution.py:352
  9.2 1.0 copy-start
  11.8 55.8 %all-to-all-start = ((bf16[8,32,32,128]{3,2,1,0:T(8,128)(2,1)}), bf16[8,32,32,128]{3,2,1,0:T(8,128)(2,1)S(1)}, u32[]{:S(2)}, u32[]{:S(2)}) async-start(bf16[8,32,32,128]{3,2,1,0:T(8,128)(2,1)} %shard_map.76.rest_0_), calls=%async_computation | async-start | bytes 4194304 | tf_op jit(solution)/shard_map/all_to_all | solution.py:367
  21.3 0.8 copy-start.10
  22.1 14.8 %copy-start.1 = (bf16[16,256,128]{2,1,0:T(8,128)(2,1)S(1)}, bf16[16,256,128]{2,1,0:T(8,128)(2,1)}, u32[]{:S(2)}) copy-start(bf16[16,256,128]{2,1,0:T(8,128)(2,1)} %copy-done) | copy-start | bytes 3145732
  22.1 14.8 %collective-permute-start.3 = (bf16[8,128,256]{2,1,0:T(8,128)(2,1)S(1)}, bf16[8,128,256]{2,1,0:T(8,128)(2,1)S(1)}, u32[]{:S(2)}, u32[]{:S(2)}) collective-permute-start(bf16[8,128,256]{2,1,0:T(8,128)(2,1)S(1)} %get-tuple-element.21.rest_0_), channel_id=1, source_target_pairs={{0,2},{1,3},{2,0},{3,1},{4,6},{5,7},{6,4},{7,5},{8,10},{9,11},{10,... | collective-permute-start | bytes 1572872 | tf_op jit(solution)/shard_map/ppermute | solution.py:379
  25.8 14.3 %copy-start.12 = (bf16[8,128,256]{2,1,0:T(8,128)(2,1)}, bf16[8,128,256]{2,1,0:T(8,128)(2,1)S(1)}, u32[]{:S(2)}) copy-start(bf16[8,128,256]{2,1,0:T(8,128)(2,1)S(1)} %get-tuple-element.26.refs_2_) | copy-start | bytes 1572868
  25.8 22.3 %collective-permute-start.4 = (bf16[8,128,256]{2,1,0:T(8,128)(2,1)S(1)}, bf16[8,128,256]{2,1,0:T(8,128)(2,1)S(1)}, u32[]{:S(2)}, u32[]{:S(2)}) collective-permute-start(bf16[8,128,256]{2,1,0:T(8,128)(2,1)S(1)} %get-tuple-element.22.rest_0_), channel_id=1, source_target_pairs={{0,2},{1,3},{2,0},{3,1},{4,6},{5,7},{6,4},{7,5},{8,10},{9,11},{10,... | collective-permute-start | bytes 1572872 | tf_op jit(solution)/shard_map/ppermute | solution.py:379
  36.9 3.2 %copy-start.5 = (bf16[8,128,256]{2,1,0:T(8,128)(2,1)}, bf16[8,128,256]{2,1,0:T(8,128)(2,1)S(1)}, u32[]{:S(2)}) copy-start(bf16[8,128,256]{2,1,0:T(8,128)(2,1)S(1)} %collective-permute-done.3.rest_1_.refs_1_) | copy-start | bytes 1572868
  40.1 11.2 %copy-start.14 = (bf16[8,128,256]{2,1,0:T(8,128)(2,1)}, bf16[8,128,256]{2,1,0:T(8,128)(2,1)S(1)}, u32[]{:S(2)}) copy-start(bf16[8,128,256]{2,1,0:T(8,128)(2,1)S(1)} %get-tuple-element.27.refs_4_) | copy-start | bytes 1572868
  40.1 32.3 %collective-permute-start.6 = (bf16[8,128,256]{2,1,0:T(8,128)(2,1)}, bf16[8,128,256]{2,1,0:T(8,128)(2,1)}, u32[]{:S(2)}, u32[]{:S(2)}) collective-permute-start(bf16[8,128,256]{2,1,0:T(8,128)(2,1)} %get-tuple-element.23.rest_0_), channel_id=1, source_target_pairs={{0,2},{1,3},{2,0},{3,1},{4,6},{5,7},{6,4},{7,5},{8,10},{9,11},{10,... | collective-permute-start | bytes 1572872 | tf_op jit(solution)/shard_map/ppermute | solution.py:379
  48.1 3.2 %copy-start.7 = (bf16[8,128,256]{2,1,0:T(8,128)(2,1)}, bf16[8,128,256]{2,1,0:T(8,128)(2,1)S(1)}, u32[]{:S(2)}) copy-start(bf16[8,128,256]{2,1,0:T(8,128)(2,1)S(1)} %collective-permute-done.4.rest_1_.refs_3_) | copy-start | bytes 1572868
  51.3 23.6 %collective-permute-start.7 = (bf16[8,128,256]{2,1,0:T(8,128)(2,1)}, bf16[8,128,256]{2,1,0:T(8,128)(2,1)S(1)}, u32[]{:S(2)}, u32[]{:S(2)}) collective-permute-start(bf16[8,128,256]{2,1,0:T(8,128)(2,1)} %get-tuple-element.24.early), channel_id=1, source_target_pairs={{0,2},{1,3},{2,0},{3,1},{4,6},{5,7},{6,4},{7,5},{8,10},{9,11},{10,... | collective-permute-start | bytes 1572872 | tf_op jit(solution)/shard_map/ppermute | solution.py:379
  67.9 4.4 %copy-start.6 = (bf16[8,128,256]{2,1,0:T(8,128)(2,1)S(1)}, bf16[8,128,256]{2,1,0:T(8,128)(2,1)}, u32[]{:S(2)}) copy-start(bf16[8,128,256]{2,1,0:T(8,128)(2,1)} %copy-done.5) | copy-start | bytes 1572868
  67.9 4.4 %copy-start.8 = (bf16[8,128,256]{2,1,0:T(8,128)(2,1)S(1)}, bf16[8,128,256]{2,1,0:T(8,128)(2,1)}, u32[]{:S(2)}) copy-start(bf16[8,128,256]{2,1,0:T(8,128)(2,1)} %copy-done.7) | copy-start | bytes 1572868
  68.0 4.4 %copy-start.11 = (bf16[8,128,256]{2,1,0:T(8,128)(2,1)S(1)}, bf16[8,128,256]{2,1,0:T(8,128)(2,1)}, u32[]{:S(2)}) copy-start(bf16[8,128,256]{2,1,0:T(8,128)(2,1)} %copy-done.10) | copy-start | bytes 1572868
  68.0 4.4 %copy-start.13 = (bf16[8,128,256]{2,1,0:T(8,128)(2,1)S(1)}, bf16[8,128,256]{2,1,0:T(8,128)(2,1)}, u32[]{:S(2)}) copy-start(bf16[8,128,256]{2,1,0:T(8,128)(2,1)} %copy-done.12) | copy-start | bytes 1572868
  68.0 4.4 %copy-start.15 = (bf16[8,128,256]{2,1,0:T(8,128)(2,1)S(1)}, bf16[8,128,256]{2,1,0:T(8,128)(2,1)}, u32[]{:S(2)}) copy-start(bf16[8,128,256]{2,1,0:T(8,128)(2,1)} %copy-done.14) | copy-start | bytes 1572868
  68.0 9.3 %collective-permute-start.12 = (bf16[1,32,32,128]{3,2,1,0:T(8,128)(2,1)S(1)}, bf16[1,32,32,128]{3,2,1,0:T(8,128)(2,1)S(1)}, u32[]{:S(2)}, u32[]{:S(2)}) collective-permute-start(bf16[1,32,32,128]{3,2,1,0:T(8,128)(2,1)S(1)} %shard_map.82.refs_1_.near_ref), channel_id=1, source_target_pairs={{0,2},{1,3},{2,0},{3,1},{4,6},{5,7},{6,4},{7,5},{8,10},{9,11},{10,... | collective-permute-start | bytes 786440 | tf_op jit(solution)/shard_map/ppermute | solution.py:392
  69.9 13.0 %collective-permute-start.11 = (bf16[1,32,32,128]{3,2,1,0:T(8,128)(2,1)S(1)}, bf16[1,32,32,128]{3,2,1,0:T(8,128)(2,1)S(1)}, u32[]{:S(2)}, u32[]{:S(2)}) collective-permute-start(bf16[1,32,32,128]{3,2,1,0:T(8,128)(2,1)S(1)} %shard_map.83.refs_1_.near_ref), channel_id=1, source_target_pairs={{0,2},{1,3},{2,0},{3,1},{4,6},{5,7},{6,4},{7,5},{8,10},{9,11},{10,... | collective-permute-start | bytes 786440 | tf_op jit(solution)/shard_map/ppermute | solution.py:392
  70.8 17.7 %collective-permute-start.10 = (bf16[1,32,32,128]{3,2,1,0:T(8,128)(2,1)S(1)}, bf16[1,32,32,128]{3,2,1,0:T(8,128)(2,1)S(1)}, u32[]{:S(2)}, u32[]{:S(2)}) collective-permute-start(bf16[1,32,32,128]{3,2,1,0:T(8,128)(2,1)S(1)} %shard_map.84.refs_1_.near_ref), channel_id=1, source_target_pairs={{0,2},{1,3},{2,0},{3,1},{4,6},{5,7},{6,4},{7,5},{8,10},{9,11},{10,... | collective-permute-start | bytes 786440 | tf_op jit(solution)/shard_map/ppermute | solution.py:392
  74.0 20.2 %collective-permute-start.9 = (bf16[1,32,32,128]{3,2,1,0:T(8,128)(2,1)S(1)}, bf16[1,32,32,128]{3,2,1,0:T(8,128)(2,1)S(1)}, u32[]{:S(2)}, u32[]{:S(2)}) collective-permute-start(bf16[1,32,32,128]{3,2,1,0:T(8,128)(2,1)S(1)} %shard_map.85.refs_1_.near_ref), channel_id=1, source_target_pairs={{0,2},{1,3},{2,0},{3,1},{4,6},{5,7},{6,4},{7,5},{8,10},{9,11},{10,... | collective-permute-start | bytes 786440 | tf_op jit(solution)/shard_map/ppermute | solution.py:392
  74.9 24.9 %collective-permute-start.8 = (bf16[1,32,32,128]{3,2,1,0:T(8,128)(2,1)S(1)}, bf16[1,32,32,128]{3,2,1,0:T(8,128)(2,1)S(1)}, u32[]{:S(2)}, u32[]{:S(2)}) collective-permute-start(bf16[1,32,32,128]{3,2,1,0:T(8,128)(2,1)S(1)} %shard_map.86.refs_1_.near_ref), channel_id=1, source_target_pairs={{0,2},{1,3},{2,0},{3,1},{4,6},{5,7},{6,4},{7,5},{8,10},{9,11},{10,... | collective-permute-start | bytes 786440 | tf_op jit(solution)/shard_map/ppermute | solution.py:392
  78.2 22.0 %collective-permute-start.13 = (bf16[32,32,128]{2,1,0:T(8,128)(2,1)S(1)}, bf16[32,32,128]{2,1,0:T(8,128)(2,1)S(1)}, u32[]{:S(2)}, u32[]{:S(2)}) collective-permute-start(bf16[32,32,128]{2,1,0:T(8,128)(2,1)S(1)} %shard_map.89.refs_0_), channel_id=1, source_target_pairs={{0,28},{4,24},{8,20},{12,16},{16,12},{20,8},{24,4},{28,0},{1,29},{... | collective-permute-start | bytes 786440 | tf_op jit(solution)/shard_map/ppermute | solution.py:398
  82.9 22.5 %collective-permute-start.5 = (bf16[1,32,32,128]{3,2,1,0:T(8,128)(2,1)S(1)}, bf16[1,32,32,128]{3,2,1,0:T(8,128)(2,1)S(1)}, u32[]{:S(2)}, u32[]{:S(2)}) collective-permute-start(bf16[1,32,32,128]{3,2,1,0:T(8,128)(2,1)S(1)} %shard_map.87.near_ref.refs_1_), channel_id=1, source_target_pairs={{0,2},{1,3},{2,0},{3,1},{4,6},{5,7},{6,4},{7,5},{8,10},{9,11},{10,... | collective-permute-start | bytes 786440 | tf_op jit(solution)/shard_map/ppermute | solution.py:392
  88.5 18.3 %collective-permute-start.14 = (bf16[32,32,128]{2,1,0:T(8,128)(2,1)S(1)}, bf16[32,32,128]{2,1,0:T(8,128)(2,1)S(1)}, u32[]{:S(2)}, u32[]{:S(2)}) collective-permute-start(bf16[32,32,128]{2,1,0:T(8,128)(2,1)S(1)} %shard_map.90.refs_0_), channel_id=1, source_target_pairs={{0,24},{4,28},{8,16},{12,20},{16,8},{20,12},{24,0},{28,4},{1,25},{... | collective-permute-start | bytes 786440 | tf_op jit(solution)/shard_map/ppermute | solution.py:398
  94.1 16.9 %collective-permute-start.18 = (bf16[1,32,32,128]{3,2,1,0:T(8,128)(2,1)S(1)}, bf16[1,32,32,128]{3,2,1,0:T(8,128)(2,1)S(1)}, u32[]{:S(2)}, u32[]{:S(2)}) collective-permute-start(bf16[1,32,32,128]{3,2,1,0:T(8,128)(2,1)S(1)} %shard_map.96.refs_1_.near_ref), channel_id=1, source_target_pairs={{0,2},{1,3},{2,0},{3,1},{4,6},{5,7},{6,4},{7,5},{8,10},{9,11},{10,... | collective-permute-start | bytes 786440 | tf_op jit(solution)/shard_map/ppermute | solution.py:392
  99.8 13.1 %collective-permute-start.19 = (bf16[32,32,128]{2,1,0:T(8,128)(2,1)S(1)}, bf16[32,32,128]{2,1,0:T(8,128)(2,1)S(1)}, u32[]{:S(2)}, u32[]{:S(2)}) collective-permute-start(bf16[32,32,128]{2,1,0:T(8,128)(2,1)S(1)} %shard_map.91.refs_0_), channel_id=1, source_target_pairs={{0,8},{4,12},{8,0},{12,4},{16,24},{20,28},{24,16},{28,20},{1,9},{5... | collective-permute-start | bytes 786440 | tf_op jit(solution)/shard_map/ppermute | solution.py:398
  100.2 12.7 %collective-permute-start.20 = (bf16[32,32,128]{2,1,0:T(8,128)(2,1)S(1)}, bf16[32,32,128]{2,1,0:T(8,128)(2,1)S(1)}, u32[]{:S(2)}, u32[]{:S(2)}) collective-permute-start(bf16[32,32,128]{2,1,0:T(8,128)(2,1)S(1)} %shard_map.92.refs_0_), channel_id=1, source_target_pairs={{0,20},{4,16},{8,28},{12,24},{16,4},{20,0},{24,12},{28,8},{1,21},{... | collective-permute-start | bytes 786440 | tf_op jit(solution)/shard_map/ppermute | solution.py:398
  105.4 12.4 %collective-permute-start.17 = (bf16[1,32,32,128]{3,2,1,0:T(8,128)(2,1)S(1)}, bf16[1,32,32,128]{3,2,1,0:T(8,128)(2,1)S(1)}, u32[]{:S(2)}, u32[]{:S(2)}) collective-permute-start(bf16[1,32,32,128]{3,2,1,0:T(8,128)(2,1)S(1)} %shard_map.97.near_ref), channel_id=1, source_target_pairs={{0,2},{1,3},{2,0},{3,1},{4,6},{5,7},{6,4},{7,5},{8,10},{9,11},{10,... | collective-permute-start | bytes 786440 | tf_op jit(solution)/shard_map/ppermute | solution.py:392
  106.9 17.8 %collective-permute-start.16 = (bf16[32,32,128]{2,1,0:T(8,128)(2,1)S(1)}, bf16[32,32,128]{2,1,0:T(8,128)(2,1)S(1)}, u32[]{:S(2)}, u32[]{:S(2)}) collective-permute-start(bf16[32,32,128]{2,1,0:T(8,128)(2,1)S(1)} %shard_map.93.refs_0_), channel_id=1, source_target_pairs={{0,12},{4,8},{8,4},{12,0},{16,28},{20,24},{24,20},{28,16},{1,13},{... | collective-permute-start | bytes 786440 | tf_op jit(solution)/shard_map/ppermute | solution.py:398
  109.7 6.0 %copy-start.4 = (bf16[512,256]{1,0:T(8,128)(2,1)S(1)}, bf16[512,256]{1,0:T(8,128)(2,1)}, u32[]{:S(2)}) copy-start(bf16[512,256]{1,0:T(8,128)(2,1)} %orbitals.5) | copy-start | bytes 786436
  109.7 6.0 %copy-start.18 = (s32[512]{0:T(512)S(1)}, s32[512]{0:T(512)}, u32[]{:S(2)}) copy-start(s32[512]{0:T(512)} %row.1) | copy-start | bytes 6148
  109.7 6.0 %copy-start.19 = (s32[8]{0:T(128)S(1)}, s32[8]{0:T(128)}, u32[]{:S(2)}) copy-start(s32[8]{0:T(128)} %count.1) | copy-start | bytes 100
  111.0 13.7 %collective-permute-start.15 = (bf16[32,32,128]{2,1,0:T(8,128)(2,1)S(1)}, bf16[32,32,128]{2,1,0:T(8,128)(2,1)S(1)}, u32[]{:S(2)}, u32[]{:S(2)}) collective-permute-start(bf16[32,32,128]{2,1,0:T(8,128)(2,1)S(1)} %shard_map.94.refs_0_), channel_id=1, source_target_pairs={{0,16},{4,20},{8,24},{12,28},{16,0},{20,4},{24,8},{28,12},{1,17},{... | collective-permute-start | bytes 786440 | tf_op jit(solution)/shard_map/ppermute | solution.py:398
  113.8 10.9 %collective-permute-start.21 = (bf16[32,32,128]{2,1,0:T(8,128)(2,1)S(1)}, bf16[32,32,128]{2,1,0:T(8,128)(2,1)S(1)}, u32[]{:S(2)}, u32[]{:S(2)}) collective-permute-start(bf16[32,32,128]{2,1,0:T(8,128)(2,1)S(1)} %shard_map.98.refs_0_), channel_id=1, source_target_pairs={{0,4},{4,0},{8,12},{12,8},{16,20},{20,16},{24,28},{28,24},{1,5},{5... | collective-permute-start | bytes 786440 | tf_op jit(solution)/shard_map/ppermute | solution.py:398
  127.0 2.7 %collective-permute-start.22 = (bf16[32,64,256]{2,1,0:T(8,128)(2,1)S(1)}, bf16[32,64,256]{2,1,0:T(8,128)(2,1)S(1)}, u32[]{:S(2)}, u32[]{:S(2)}) collective-permute-start(bf16[32,64,256]{2,1,0:T(8,128)(2,1)S(1)} %get-tuple-element.30), channel_id=1, source_target_pairs={{0,1},{1,0},{2,3},{3,2},{4,5},{5,4},{6,7},{7,6},{8,9},{9,8},{10,11... | collective-permute-start | bytes 3145736 | tf_op jit(solution)/shard_map/ppermute | solution.py:403

commit v6 on v5

--- a/solution.py
+++ b/solution.py
@@ -230,7 +230,7 @@
         there[piece] = jnp.concatenate([away[:, :, width:], away[:, :, :width]], 2)
 
 
-PIECE = 4
+PIECE = 8
 
 
 def tile_call(body, count, tiles, ins, outs, early=(), scratch=()):
@@ -313,7 +313,7 @@
         give[i] = jnp.where(core == 0, high, low)
         return carry
 
-    lax.fori_loop(0, occ, step, 0, unroll=4)
+    lax.fori_loop(0, occ, step, 0, unroll=8)
 
 
 def back_transform(rows, values):

time: 131 us -> 130 us (level)
  waiting for transfers between devices: 53.4 us -> 55.7 us
  Pallas kernels: 34.7 us -> 32.8 us
  starting transfers between devices: 38.5 us -> 36.7 us
    ppermute x7, starting transfers between devices: 14.5 us -> 12.7 us  [shards(): lax.ppermute(x, 'occ', [(o, o ^ k) for o in range(nodes)])]
  transfers between devices with their start and end apart: 24 -> 24, of which waited for: 13 -> 14; matrix products, arithmetic and copies ran while one was open for 0% -> 0% of each run, Pallas kernels for 23% -> 23%
where the time goes in v6:
time: 130 us; the launch traced here: 129 us
  waiting for transfers between devices  55.7 us (43%)
  starting transfers between devices  36.7 us (28%)
  Pallas kernels  32.8 us (25%)
  local copies, waits for them, and re-layouts  2.79 us (2%)
    ppermute x4, waiting for transfers between devices, shards(): parts += [here, lax.ppermute(there, 'ao', far)]  17.3 us
    all_to_all x1, waiting for transfers between devices, shards(): lax.all_to_all(sent, 'occ', split_axis=0, concat_axis=0, tiled=True)  15.1 us
    pallas_call x6, Pallas kernels, tile_call(): pl.pallas_call(body, out_shape=outs, in_specs=[whole, away] + [whole] * (...  14.5 us
    ppermute x8, waiting for transfers between devices, shards(): far_blocks.append(lax.ppermute(blocks_of[-1], 'ao', far))  13.7 us
    ppermute x7, starting transfers between devices, shards(): lax.ppermute(x, 'occ', [(o, o ^ k) for o in range(nodes)])  12.7 us
    ppermute x8, starting transfers between devices, shards(): far_blocks.append(lax.ppermute(blocks_of[-1], 'ao', far))  10.4 us
    pallas_call x11, Pallas kernels, call(): pl.pallas_call(body, out_shape=outs, in_specs=[whole] * len(ins) + [pl.Bl...  9.91 us
    all_to_all x1, starting transfers between devices, shards(): lax.all_to_all(sent, 'occ', split_axis=0, concat_axis=0, tiled=True)  7.22 us
  transfers between devices with their start and end apart: 24, of which 14 were waited for; matrix products, arithmetic and copies ran while one was open for 0% of the time, Pallas kernels for 23%

profile of v6, /device:TPU:0, one launch (start us, length us, event | category | flops | bytes accessed | tf_op | source)
XLA Modules:
  0.0 129.4 jit_solution(17669332458364903011)
XLA Ops:
  0.5 0.9 copy-done.2
  1.4 2.3 %shard_map.73 = (bf16[16,256,128]{2,1,0:T(8,128)(2,1)S(1)}, bf16[256,512]{1,0:T(8,128)(2,1)S(1)}, bf16[256,256]{1,0:T(8,128)(2,1)S(1)}) custom-call(bf16[512,256]{1,0:T(8,128)(2,1)S(1)} %copy-done.2, bf16[64,512,128]{2,1,0:T(8,128)(2,1)} %tiles.11), custom_call_target="tpu_custom_call" | custom-call | flops 1610612736 | bytes 4194304 | tf_op jit(solution)/shard_map/pallas_call | solution.py:242
  3.8 2.2 %shard_map.74.early = bf16[16,256,128]{2,1,0:T(8,128)(2,1)S(1)} custom-call(bf16[256,512]{1,0:T(8,128)(2,1)S(1)} %get-tuple-element.18.left_ref, bf16[64,512,128]{2,1,0:T(8,128)(2,1)} %tiles.11, bf16[16,256,128]{2,1,0:T(8,128)(2,1)S(1)} %get-tuple-element.19.rest_0_, bf16[32,64,256]{2,1,0:T(8,128)(2,1)S(1)} %collective-permute-done.rest_1_.other_ref), custom_call_target="tpu_custom_call" | custom-call | flops 536870912 | bytes 4194304 | tf_op jit(solution)/shard_map/pallas_call | solution.py:242
  6.5 1.9 %shard_map.75.rows_ref = bf16[256,256]{1,0:T(8,128)(2,1)S(1)} custom-call(s32[512]{0:T(512)S(1)} %bitcast.7, s32[512]{0:T(512)S(1)} %copy-done.17, bf16[512,256]{1,0:T(8,128)(2,1)S(1)} %copy-done.3, bf16[16,256,128]{2,1,0:T(8,128)(2,1)S(1)} %shard_map.74.early), custom_call_target="tpu_custom_call" | custom-call | flops 65536 | bytes 262144 | tf_op jit(solution)/shard_map/pallas_call | solution.py:91
  8.8 1.0 copy-done
  9.8 1.7 %shard_map.76.rest_0_ = bf16[8,32,32,128]{3,2,1,0:T(8,128)(2,1)} custom-call(bf16[256,256]{1,0:T(8,128)(2,1)S(1)} %shard_map.75.rows_ref, bf16[32,64,256]{2,1,0:T(8,128)(2,1)S(1)} %bitcast.6, bf16[32,64,256]{2,1,0:T(8,128)(2,1)S(1)} %collective-permute-done.rest_1_.other_ref, bf16[16,256,128]{2,1,0:T(8,128)(2,1)S(1)} %collective-permute-done.2.rest_0_.other, ...), custom_call_target="tpu_custom_call" | custom-call | flops 536870912 | bytes 2097152 | tf_op jit(solution)/shard_map/pallas_call | solution.py:127
  11.5 7.2 %all-to-all-start = ((bf16[8,32,32,128]{3,2,1,0:T(8,128)(2,1)}), bf16[8,32,32,128]{3,2,1,0:T(8,128)(2,1)S(1)}, u32[]{:S(2)}, u32[]{:S(2)}) async-start(bf16[8,32,32,128]{3,2,1,0:T(8,128)(2,1)} %shard_map.76.rest_0_), calls=%async_computation | async-start | bytes 4194304 | tf_op jit(solution)/shard_map/all_to_all | solution.py:367
  18.7 2.0 %shard_map.77 = (bf16[8,128,256]{2,1,0:T(8,128)(2,1)S(1)}, bf16[8,128,256]{2,1,0:T(8,128)(2,1)S(1)}) custom-call(bf16[256,512]{1,0:T(8,128)(2,1)S(1)} %get-tuple-element.18.left_ref, bf16[64,512,128]{2,1,0:T(8,128)(2,1)} %tiles.11, bf16[16,256,128]{2,1,0:T(8,128)(2,1)S(1)} %collective-permute-done.2.rest_0_.other, ...), custom_call_target="tpu_custom_call" | custom-call | flops 201326592 | bytes 2097152 | tf_op jit(solution)/shard_map/pallas_call | solution.py:242
  21.5 1.5 %collective-permute-start.3 = (bf16[8,128,256]{2,1,0:T(8,128)(2,1)S(1)}, bf16[8,128,256]{2,1,0:T(8,128)(2,1)S(1)}, u32[]{:S(2)}, u32[]{:S(2)}) collective-permute-start(bf16[8,128,256]{2,1,0:T(8,128)(2,1)S(1)} %get-tuple-element.21.rest_0_), channel_id=1, source_target_pairs={{0,2},{1,3},{2,0},{3,1},{4,6},{5,7},{6,4},{7,5},{8,10},{9,11},{10,... | collective-permute-start | bytes 1572872 | tf_op jit(solution)/shard_map/ppermute | solution.py:379
  23.0 2.0 %shard_map.78 = (bf16[8,128,256]{2,1,0:T(8,128)(2,1)S(1)}, bf16[8,128,256]{2,1,0:T(8,128)(2,1)S(1)}) custom-call(bf16[256,512]{1,0:T(8,128)(2,1)S(1)} %get-tuple-element.18.left_ref, bf16[64,512,128]{2,1,0:T(8,128)(2,1)} %tiles.11, bf16[16,256,128]{2,1,0:T(8,128)(2,1)S(1)} %collective-permute-done.2.rest_0_.other, ...), custom_call_target="tpu_custom_call" | custom-call | flops 201326592 | bytes 2097152 | tf_op jit(solution)/shard_map/pallas_call | solution.py:242
  25.7 10.7 %collective-permute-done.3.rest_1_.refs_1_ = bf16[8,128,256]{2,1,0:T(8,128)(2,1)S(1)} collective-permute-done((bf16[8,128,256]{2,1,0:T(8,128)(2,1)S(1)}, bf16[8,128,256]{2,1,0:T(8,128)(2,1)S(1)}, u32[]{:S(2)}, u32[]{:S(2)}) %collective-permute-start.3) | collective-permute-done | bytes 524320 | tf_op jit(solution)/shard_map/ppermute | solution.py:379
  36.4 3.0 %shard_map.79 = (bf16[8,128,256]{2,1,0:T(8,128)(2,1)S(1)}, bf16[8,128,256]{2,1,0:T(8,128)(2,1)}) custom-call(bf16[256,512]{1,0:T(8,128)(2,1)S(1)} %get-tuple-element.18.left_ref, bf16[64,512,128]{2,1,0:T(8,128)(2,1)} %tiles.11, bf16[16,256,128]{2,1,0:T(8,128)(2,1)S(1)} %copy-done.1, bf16[256,256]{1,0:T(8,128)(2,1)S(1)} %get-tuple-element.20.right_ref, ...), custom_call_target="tpu_custom_call" | custom-call | flops 201326592 | bytes 2097152 | tf_op jit(solution)/shard_map/pallas_call | solution.py:242
  39.4 1.6 %collective-permute-start.6 = (bf16[8,128,256]{2,1,0:T(8,128)(2,1)}, bf16[8,128,256]{2,1,0:T(8,128)(2,1)}, u32[]{:S(2)}, u32[]{:S(2)}) collective-permute-start(bf16[8,128,256]{2,1,0:T(8,128)(2,1)} %get-tuple-element.23.rest_0_), channel_id=1, source_target_pairs={{0,2},{1,3},{2,0},{3,1},{4,6},{5,7},{6,4},{7,5},{8,10},{9,11},{10,... | collective-permute-start | bytes 1572872 | tf_op jit(solution)/shard_map/ppermute | solution.py:379
  40.9 6.6 %collective-permute-done.4.rest_1_.refs_3_ = bf16[8,128,256]{2,1,0:T(8,128)(2,1)S(1)} collective-permute-done((bf16[8,128,256]{2,1,0:T(8,128)(2,1)S(1)}, bf16[8,128,256]{2,1,0:T(8,128)(2,1)S(1)}, u32[]{:S(2)}, u32[]{:S(2)}) %collective-permute-start.4) | collective-permute-done | bytes 524320 | tf_op jit(solution)/shard_map/ppermute | solution.py:379
  47.6 3.0 %shard_map.80 = (bf16[8,128,256]{2,1,0:T(8,128)(2,1)S(1)}, bf16[8,128,256]{2,1,0:T(8,128)(2,1)}) custom-call(bf16[256,512]{1,0:T(8,128)(2,1)S(1)} %get-tuple-element.18.left_ref, bf16[64,512,128]{2,1,0:T(8,128)(2,1)} %tiles.11, bf16[16,256,128]{2,1,0:T(8,128)(2,1)S(1)} %copy-done.1, bf16[256,256]{1,0:T(8,128)(2,1)S(1)} %get-tuple-element.20.right_ref, ...), custom_call_target="tpu_custom_call" | custom-call | flops 201326592 | bytes 2097152 | tf_op jit(solution)/shard_map/pallas_call | solution.py:242
  50.6 1.6 %collective-permute-start.7 = (bf16[8,128,256]{2,1,0:T(8,128)(2,1)}, bf16[8,128,256]{2,1,0:T(8,128)(2,1)S(1)}, u32[]{:S(2)}, u32[]{:S(2)}) collective-permute-start(bf16[8,128,256]{2,1,0:T(8,128)(2,1)} %get-tuple-element.24.early), channel_id=1, source_target_pairs={{0,2},{1,3},{2,0},{3,1},{4,6},{5,7},{6,4},{7,5},{8,10},{9,11},{10,... | collective-permute-start | bytes 1572872 | tf_op jit(solution)/shard_map/ppermute | solution.py:379
  52.2 15.1 %all-to-all-done.refs_0_ = bf16[8,32,32,128]{3,2,1,0:T(8,128)(2,1)S(1)} async-done(((bf16[8,32,32,128]{3,2,1,0:T(8,128)(2,1)}), bf16[8,32,32,128]{3,2,1,0:T(8,128)(2,1)S(1)}, u32[]{:S(2)}, u32[]{:S(2)}) %all-to-all-start) | async-done | bytes 2097184 | tf_op jit(solution)/shard_map/all_to_all | solution.py:367
  67.6 1.6 %collective-permute-start.12 = (bf16[1,32,32,128]{3,2,1,0:T(8,128)(2,1)S(1)}, bf16[1,32,32,128]{3,2,1,0:T(8,128)(2,1)S(1)}, u32[]{:S(2)}, u32[]{:S(2)}) collective-permute-start(bf16[1,32,32,128]{3,2,1,0:T(8,128)(2,1)S(1)} %shard_map.82.refs_1_.near_ref), channel_id=1, source_target_pairs={{0,2},{1,3},{2,0},{3,1},{4,6},{5,7},{6,4},{7,5},{8,10},{9,11},{10,... | collective-permute-start | bytes 786440 | tf_op jit(solution)/shard_map/ppermute | solution.py:392
  70.5 1.6 %collective-permute-start.10 = (bf16[1,32,32,128]{3,2,1,0:T(8,128)(2,1)S(1)}, bf16[1,32,32,128]{3,2,1,0:T(8,128)(2,1)S(1)}, u32[]{:S(2)}, u32[]{:S(2)}) collective-permute-start(bf16[1,32,32,128]{3,2,1,0:T(8,128)(2,1)S(1)} %shard_map.84.refs_1_.near_ref), channel_id=1, source_target_pairs={{0,2},{1,3},{2,0},{3,1},{4,6},{5,7},{6,4},{7,5},{8,10},{9,11},{10,... | collective-permute-start | bytes 786440 | tf_op jit(solution)/shard_map/ppermute | solution.py:392
  72.1 1.2 shard_map.88.dressed
  74.6 1.6 %collective-permute-start.8 = (bf16[1,32,32,128]{3,2,1,0:T(8,128)(2,1)S(1)}, bf16[1,32,32,128]{3,2,1,0:T(8,128)(2,1)S(1)}, u32[]{:S(2)}, u32[]{:S(2)}) collective-permute-start(bf16[1,32,32,128]{3,2,1,0:T(8,128)(2,1)S(1)} %shard_map.86.refs_1_.near_ref), channel_id=1, source_target_pairs={{0,2},{1,3},{2,0},{3,1},{4,6},{5,7},{6,4},{7,5},{8,10},{9,11},{10,... | collective-permute-start | bytes 786440 | tf_op jit(solution)/shard_map/ppermute | solution.py:392
  76.9 0.9 shard_map.89.refs_0_
  77.9 2.7 %collective-permute-start.13 = (bf16[32,32,128]{2,1,0:T(8,128)(2,1)S(1)}, bf16[32,32,128]{2,1,0:T(8,128)(2,1)S(1)}, u32[]{:S(2)}, u32[]{:S(2)}) collective-permute-start(bf16[32,32,128]{2,1,0:T(8,128)(2,1)S(1)} %shard_map.89.refs_0_), channel_id=1, source_target_pairs={{0,28},{4,24},{8,20},{12,16},{16,12},{20,8},{24,4},{28,0},{1,29},{... | collective-permute-start | bytes 786440 | tf_op jit(solution)/shard_map/ppermute | solution.py:398
  81.3 1.3 %collective-permute-done.11.far_ref = bf16[1,32,32,128]{3,2,1,0:T(8,128)(2,1)S(1)} collective-permute-done((bf16[1,32,32,128]{3,2,1,0:T(8,128)(2,1)S(1)}, bf16[1,32,32,128]{3,2,1,0:T(8,128)(2,1)S(1)}, u32[]{:S(2)}, u32[]{:S(2)}) %collective-permute-start.11) | collective-permute-done | bytes 262176 | tf_op jit(solution)/shard_map/ppermute | solution.py:392
  82.6 1.5 %collective-permute-start.5 = (bf16[1,32,32,128]{3,2,1,0:T(8,128)(2,1)S(1)}, bf16[1,32,32,128]{3,2,1,0:T(8,128)(2,1)S(1)}, u32[]{:S(2)}, u32[]{:S(2)}) collective-permute-start(bf16[1,32,32,128]{3,2,1,0:T(8,128)(2,1)S(1)} %shard_map.87.near_ref.refs_1_), channel_id=1, source_target_pairs={{0,2},{1,3},{2,0},{3,1},{4,6},{5,7},{6,4},{7,5},{8,10},{9,11},{10,... | collective-permute-start | bytes 786440 | tf_op jit(solution)/shard_map/ppermute | solution.py:392
  84.1 0.9 shard_map.90.refs_0_
  85.0 3.2 %collective-permute-done.10.far_ref = bf16[1,32,32,128]{3,2,1,0:T(8,128)(2,1)S(1)} collective-permute-done((bf16[1,32,32,128]{3,2,1,0:T(8,128)(2,1)S(1)}, bf16[1,32,32,128]{3,2,1,0:T(8,128)(2,1)S(1)}, u32[]{:S(2)}, u32[]{:S(2)}) %collective-permute-start.10) | collective-permute-done | bytes 262176 | tf_op jit(solution)/shard_map/ppermute | solution.py:392
  88.2 2.2 %collective-permute-start.14 = (bf16[32,32,128]{2,1,0:T(8,128)(2,1)S(1)}, bf16[32,32,128]{2,1,0:T(8,128)(2,1)S(1)}, u32[]{:S(2)}, u32[]{:S(2)}) collective-permute-start(bf16[32,32,128]{2,1,0:T(8,128)(2,1)S(1)} %shard_map.90.refs_0_), channel_id=1, source_target_pairs={{0,24},{4,28},{8,16},{12,20},{16,8},{20,12},{24,0},{28,4},{1,25},{... | collective-permute-start | bytes 786440 | tf_op jit(solution)/shard_map/ppermute | solution.py:398
  90.4 0.9 shard_map.91.refs_0_
  91.3 2.5 %collective-permute-done.9.far_ref = bf16[1,32,32,128]{3,2,1,0:T(8,128)(2,1)S(1)} collective-permute-done((bf16[1,32,32,128]{3,2,1,0:T(8,128)(2,1)S(1)}, bf16[1,32,32,128]{3,2,1,0:T(8,128)(2,1)S(1)}, u32[]{:S(2)}, u32[]{:S(2)}) %collective-permute-start.9) | collective-permute-done | bytes 262176 | tf_op jit(solution)/shard_map/ppermute | solution.py:392
  93.8 1.5 %collective-permute-start.18 = (bf16[1,32,32,128]{3,2,1,0:T(8,128)(2,1)S(1)}, bf16[1,32,32,128]{3,2,1,0:T(8,128)(2,1)S(1)}, u32[]{:S(2)}, u32[]{:S(2)}) collective-permute-start(bf16[1,32,32,128]{3,2,1,0:T(8,128)(2,1)S(1)} %shard_map.96.refs_1_.near_ref), channel_id=1, source_target_pairs={{0,2},{1,3},{2,0},{3,1},{4,6},{5,7},{6,4},{7,5},{8,10},{9,11},{10,... | collective-permute-start | bytes 786440 | tf_op jit(solution)/shard_map/ppermute | solution.py:392
  95.3 0.9 shard_map.92.refs_0_
  96.2 3.2 %collective-permute-done.8.far_ref = bf16[1,32,32,128]{3,2,1,0:T(8,128)(2,1)S(1)} collective-permute-done((bf16[1,32,32,128]{3,2,1,0:T(8,128)(2,1)S(1)}, bf16[1,32,32,128]{3,2,1,0:T(8,128)(2,1)S(1)}, u32[]{:S(2)}, u32[]{:S(2)}) %collective-permute-start.8) | collective-permute-done | bytes 262176 | tf_op jit(solution)/shard_map/ppermute | solution.py:392
  99.5 3.2 %collective-permute-start.20 = (bf16[32,32,128]{2,1,0:T(8,128)(2,1)S(1)}, bf16[32,32,128]{2,1,0:T(8,128)(2,1)S(1)}, u32[]{:S(2)}, u32[]{:S(2)}) collective-permute-start(bf16[32,32,128]{2,1,0:T(8,128)(2,1)S(1)} %shard_map.92.refs_0_), channel_id=1, source_target_pairs={{0,20},{4,16},{8,28},{12,24},{16,4},{20,0},{24,12},{28,8},{1,21},{... | collective-permute-start | bytes 786440 | tf_op jit(solution)/shard_map/ppermute | solution.py:398
  103.0 0.9 shard_map.93.refs_0_
  103.9 1.1 collective-permute-done.5.far_ref
  105.0 1.5 %collective-permute-start.17 = (bf16[1,32,32,128]{3,2,1,0:T(8,128)(2,1)S(1)}, bf16[1,32,32,128]{3,2,1,0:T(8,128)(2,1)S(1)}, u32[]{:S(2)}, u32[]{:S(2)}) collective-permute-start(bf16[1,32,32,128]{3,2,1,0:T(8,128)(2,1)S(1)} %shard_map.97.near_ref), channel_id=1, source_target_pairs={{0,2},{1,3},{2,0},{3,1},{4,6},{5,7},{6,4},{7,5},{8,10},{9,11},{10,... | collective-permute-start | bytes 786440 | tf_op jit(solution)/shard_map/ppermute | solution.py:392
  106.5 1.7 %collective-permute-start.16 = (bf16[32,32,128]{2,1,0:T(8,128)(2,1)S(1)}, bf16[32,32,128]{2,1,0:T(8,128)(2,1)S(1)}, u32[]{:S(2)}, u32[]{:S(2)}) collective-permute-start(bf16[32,32,128]{2,1,0:T(8,128)(2,1)S(1)} %shard_map.93.refs_0_), channel_id=1, source_target_pairs={{0,12},{4,8},{8,4},{12,0},{16,28},{20,24},{24,20},{28,16},{1,13},{... | collective-permute-start | bytes 786440 | tf_op jit(solution)/shard_map/ppermute | solution.py:398
  109.2 1.5 %collective-permute-done.18.far_ref = bf16[1,32,32,128]{3,2,1,0:T(8,128)(2,1)S(1)} collective-permute-done((bf16[1,32,32,128]{3,2,1,0:T(8,128)(2,1)S(1)}, bf16[1,32,32,128]{3,2,1,0:T(8,128)(2,1)S(1)}, u32[]{:S(2)}, u32[]{:S(2)}) %collective-permute-start.18) | collective-permute-done | bytes 262176 | tf_op jit(solution)/shard_map/ppermute | solution.py:392
  110.6 1.7 %collective-permute-start.15 = (bf16[32,32,128]{2,1,0:T(8,128)(2,1)S(1)}, bf16[32,32,128]{2,1,0:T(8,128)(2,1)S(1)}, u32[]{:S(2)}, u32[]{:S(2)}) collective-permute-start(bf16[32,32,128]{2,1,0:T(8,128)(2,1)S(1)} %shard_map.94.refs_0_), channel_id=1, source_target_pairs={{0,16},{4,20},{8,24},{12,28},{16,0},{20,4},{24,8},{28,12},{1,17},{... | collective-permute-start | bytes 786440 | tf_op jit(solution)/shard_map/ppermute | solution.py:398
  112.8 0.9 shard_map.98.refs_0_
  113.7 1.2 collective-permute-start.21
  115.0 2.1 %shard_map.81.rows = bf16[256,256]{1,0:T(8,128)(2,1)S(1)} custom-call(s32[512]{0:T(512)S(1)} %copy-done.18, s32[8]{0:T(128)S(1)} %copy-done.19, bf16[512,256]{1,0:T(8,128)(2,1)S(1)} %copy-done.4, bf16[8,128,256]{2,1,0:T(8,128)(2,1)} %get-tuple-element.24.early), custom_call_target="tpu_custom_call" | custom-call | flops 65536 | bytes 262144 | tf_op jit(solution)/shard_map/pallas_call | solution.py:91
  117.1 0.9 shard_map.99.refs_0_
  118.0 6.1 %collective-permute-done.15.rest_0_.refs_4_ = bf16[32,32,128]{2,1,0:T(8,128)(2,1)S(1)} collective-permute-done((bf16[32,32,128]{2,1,0:T(8,128)(2,1)S(1)}, bf16[32,32,128]{2,1,0:T(8,128)(2,1)S(1)}, u32[]{:S(2)}, u32[]{:S(2)}) %collective-permute-start.15) | collective-permute-done | bytes 262176 | tf_op jit(solution)/shard_map/ppermute | solution.py:398
  124.2 1.4 %shard_map.100 = (bf16[32,64,256]{2,1,0:T(8,128)(2,1)S(1)}, bf16[32,64,256]{2,1,0:T(8,128)(2,1)S(1)}) custom-call(bf16[256,256]{1,0:T(8,128)(2,1)S(1)} %shard_map.95.rows_ref, bf16[32,32,128]{2,1,0:T(8,128)(2,1)S(1)} %shard_map.99.refs_0_, bf16[32,32,128]{2,1,0:T(8,128)(2,1)S(1)} %collective-permute-done.21.refs_1_, ...), custom_call_target="tpu_custom_call" | custom-call | flops 536870912 | bytes 4325376 | tf_op jit(solution)/shard_map/pallas_call | solution.py:23
  125.7 2.6 %collective-permute-done.22 = bf16[32,64,256]{2,1,0:T(8,128)(2,1)S(1)} collective-permute-done((bf16[32,64,256]{2,1,0:T(8,128)(2,1)S(1)}, bf16[32,64,256]{2,1,0:T(8,128)(2,1)S(1)}, u32[]{:S(2)}, u32[]{:S(2)}) %collective-permute-start.22) | collective-permute-done | bytes 1048608 | tf_op jit(solution)/shard_map/ppermute | solution.py:403
  128.4 1.1 add_bitcast_fusion
  (69 shorter events, 9.1 us)
Async XLA Ops:
  0.0 3.8 %collective-permute-start = (bf16[32,64,256]{2,1,0:T(8,128)(2,1)}, bf16[32,64,256]{2,1,0:T(8,128)(2,1)S(1)}, u32[]{:S(2)}, u32[]{:S(2)}) collective-permute-start(bf16[32,64,256]{2,1,0:T(8,128)(2,1)} %bitcast.5), channel_id=1, source_target_pairs={{0,1},{1,0},{2,3},{3,2},{4,5},{5,4},{6,7},{7,6},{8,9},{9,8},{10,11... | collective-permute-start | bytes 3145736 | tf_op jit(solution)/shard_map/ppermute | solution.py:344
  0.5 0.9 copy-start.2
  3.7 4.8 %collective-permute-start.2 = (bf16[16,256,128]{2,1,0:T(8,128)(2,1)S(1)}, bf16[16,256,128]{2,1,0:T(8,128)(2,1)S(1)}, u32[]{:S(2)}, u32[]{:S(2)}) collective-permute-start(bf16[16,256,128]{2,1,0:T(8,128)(2,1)S(1)} %get-tuple-element.19.rest_0_), channel_id=1, source_target_pairs={{0,1},{1,0},{2,3},{3,2},{4,5},{5,4},{6,7},{7,6},{8,9},{9,8},{10,11... | collective-permute-start | bytes 3145736 | tf_op jit(solution)/shard_map/ppermute | solution.py:363
  3.8 2.7 %copy-start.3 = (bf16[512,256]{1,0:T(8,128)(2,1)S(1)}, bf16[512,256]{1,0:T(8,128)(2,1)}, u32[]{:S(2)}) copy-start(bf16[512,256]{1,0:T(8,128)(2,1)} %orbitals.5) | copy-start | bytes 786436
  3.8 2.7 %copy-start.16 = (s32[512,1]{0,1:T(1,128)S(1)}, s32[512,1]{0,1:T(1,128)}, u32[]{:S(2)}) copy-start(s32[512,1]{0,1:T(1,128)} %param.12) | copy-start | bytes 6148
  3.8 2.7 %copy-start.17 = (s32[512]{0:T(512)S(1)}, s32[512]{0:T(512)}, u32[]{:S(2)}) copy-start(s32[512]{0:T(512)} %sub.1) | copy-start | bytes 6148
  6.0 3.8 %copy-start.9 = (bf16[32,256,64]{1,2,0:T(8,128)(2,1)S(1)}, bf16[32,256,64]{1,2,0:T(8,128)(2,1)}, u32[]{:S(2)}) copy-start(bf16[32,256,64]{1,2,0:T(8,128)(2,1)} %param.7) | copy-start | bytes 3145732
  6.0 2.8 %collective-permute-start.1 = (bf16[16,256,128]{2,1,0:T(8,128)(2,1)S(1)}, bf16[16,256,128]{2,1,0:T(8,128)(2,1)S(1)}, u32[]{:S(2)}, u32[]{:S(2)}) collective-permute-start(bf16[16,256,128]{2,1,0:T(8,128)(2,1)S(1)} %shard_map.74.early), channel_id=1, source_target_pairs={{0,1},{1,0},{2,3},{3,2},{4,5},{5,4},{6,7},{7,6},{8,9},{9,8},{10,11... | collective-permute-start | bytes 3145736 | tf_op jit(solution)/shard_map/ppermute | solution.py:352
  8.8 1.0 copy-start
  11.5 55.8 %all-to-all-start = ((bf16[8,32,32,128]{3,2,1,0:T(8,128)(2,1)}), bf16[8,32,32,128]{3,2,1,0:T(8,128)(2,1)S(1)}, u32[]{:S(2)}, u32[]{:S(2)}) async-start(bf16[8,32,32,128]{3,2,1,0:T(8,128)(2,1)} %shard_map.76.rest_0_), calls=%async_computation | async-start | bytes 4194304 | tf_op jit(solution)/shard_map/all_to_all | solution.py:367
  20.7 0.8 copy-start.10
  21.5 14.8 %copy-start.1 = (bf16[16,256,128]{2,1,0:T(8,128)(2,1)S(1)}, bf16[16,256,128]{2,1,0:T(8,128)(2,1)}, u32[]{:S(2)}) copy-start(bf16[16,256,128]{2,1,0:T(8,128)(2,1)} %copy-done) | copy-start | bytes 3145732
  21.5 14.8 %collective-permute-start.3 = (bf16[8,128,256]{2,1,0:T(8,128)(2,1)S(1)}, bf16[8,128,256]{2,1,0:T(8,128)(2,1)S(1)}, u32[]{:S(2)}, u32[]{:S(2)}) collective-permute-start(bf16[8,128,256]{2,1,0:T(8,128)(2,1)S(1)} %get-tuple-element.21.rest_0_), channel_id=1, source_target_pairs={{0,2},{1,3},{2,0},{3,1},{4,6},{5,7},{6,4},{7,5},{8,10},{9,11},{10,... | collective-permute-start | bytes 1572872 | tf_op jit(solution)/shard_map/ppermute | solution.py:379
  25.0 14.3 %copy-start.12 = (bf16[8,128,256]{2,1,0:T(8,128)(2,1)}, bf16[8,128,256]{2,1,0:T(8,128)(2,1)S(1)}, u32[]{:S(2)}) copy-start(bf16[8,128,256]{2,1,0:T(8,128)(2,1)S(1)} %get-tuple-element.26.refs_2_) | copy-start | bytes 1572868
  25.1 22.5 %collective-permute-start.4 = (bf16[8,128,256]{2,1,0:T(8,128)(2,1)S(1)}, bf16[8,128,256]{2,1,0:T(8,128)(2,1)S(1)}, u32[]{:S(2)}, u32[]{:S(2)}) collective-permute-start(bf16[8,128,256]{2,1,0:T(8,128)(2,1)S(1)} %get-tuple-element.22.rest_0_), channel_id=1, source_target_pairs={{0,2},{1,3},{2,0},{3,1},{4,6},{5,7},{6,4},{7,5},{8,10},{9,11},{10,... | collective-permute-start | bytes 1572872 | tf_op jit(solution)/shard_map/ppermute | solution.py:379
  36.4 3.0 %copy-start.5 = (bf16[8,128,256]{2,1,0:T(8,128)(2,1)}, bf16[8,128,256]{2,1,0:T(8,128)(2,1)S(1)}, u32[]{:S(2)}) copy-start(bf16[8,128,256]{2,1,0:T(8,128)(2,1)S(1)} %collective-permute-done.3.rest_1_.refs_1_) | copy-start | bytes 1572868
  39.4 11.2 %copy-start.14 = (bf16[8,128,256]{2,1,0:T(8,128)(2,1)}, bf16[8,128,256]{2,1,0:T(8,128)(2,1)S(1)}, u32[]{:S(2)}) copy-start(bf16[8,128,256]{2,1,0:T(8,128)(2,1)S(1)} %get-tuple-element.27.refs_4_) | copy-start | bytes 1572868
  39.4 32.6 %collective-permute-start.6 = (bf16[8,128,256]{2,1,0:T(8,128)(2,1)}, bf16[8,128,256]{2,1,0:T(8,128)(2,1)}, u32[]{:S(2)}, u32[]{:S(2)}) collective-permute-start(bf16[8,128,256]{2,1,0:T(8,128)(2,1)} %get-tuple-element.23.rest_0_), channel_id=1, source_target_pairs={{0,2},{1,3},{2,0},{3,1},{4,6},{5,7},{6,4},{7,5},{8,10},{9,11},{10,... | collective-permute-start | bytes 1572872 | tf_op jit(solution)/shard_map/ppermute | solution.py:379
  47.6 3.0 %copy-start.7 = (bf16[8,128,256]{2,1,0:T(8,128)(2,1)}, bf16[8,128,256]{2,1,0:T(8,128)(2,1)S(1)}, u32[]{:S(2)}) copy-start(bf16[8,128,256]{2,1,0:T(8,128)(2,1)S(1)} %collective-permute-done.4.rest_1_.refs_3_) | copy-start | bytes 1572868
  50.6 23.9 %collective-permute-start.7 = (bf16[8,128,256]{2,1,0:T(8,128)(2,1)}, bf16[8,128,256]{2,1,0:T(8,128)(2,1)S(1)}, u32[]{:S(2)}, u32[]{:S(2)}) collective-permute-start(bf16[8,128,256]{2,1,0:T(8,128)(2,1)} %get-tuple-element.24.early), channel_id=1, source_target_pairs={{0,2},{1,3},{2,0},{3,1},{4,6},{5,7},{6,4},{7,5},{8,10},{9,11},{10,... | collective-permute-start | bytes 1572872 | tf_op jit(solution)/shard_map/ppermute | solution.py:379
  67.6 4.5 %copy-start.6 = (bf16[8,128,256]{2,1,0:T(8,128)(2,1)S(1)}, bf16[8,128,256]{2,1,0:T(8,128)(2,1)}, u32[]{:S(2)}) copy-start(bf16[8,128,256]{2,1,0:T(8,128)(2,1)} %copy-done.5) | copy-start | bytes 1572868
  67.6 4.4 %copy-start.8 = (bf16[8,128,256]{2,1,0:T(8,128)(2,1)S(1)}, bf16[8,128,256]{2,1,0:T(8,128)(2,1)}, u32[]{:S(2)}) copy-start(bf16[8,128,256]{2,1,0:T(8,128)(2,1)} %copy-done.7) | copy-start | bytes 1572868
  67.6 4.4 %copy-start.11 = (bf16[8,128,256]{2,1,0:T(8,128)(2,1)S(1)}, bf16[8,128,256]{2,1,0:T(8,128)(2,1)}, u32[]{:S(2)}) copy-start(bf16[8,128,256]{2,1,0:T(8,128)(2,1)} %copy-done.10) | copy-start | bytes 1572868
  67.6 4.4 %copy-start.13 = (bf16[8,128,256]{2,1,0:T(8,128)(2,1)S(1)}, bf16[8,128,256]{2,1,0:T(8,128)(2,1)}, u32[]{:S(2)}) copy-start(bf16[8,128,256]{2,1,0:T(8,128)(2,1)} %copy-done.12) | copy-start | bytes 1572868
  67.6 4.4 %copy-start.15 = (bf16[8,128,256]{2,1,0:T(8,128)(2,1)S(1)}, bf16[8,128,256]{2,1,0:T(8,128)(2,1)}, u32[]{:S(2)}) copy-start(bf16[8,128,256]{2,1,0:T(8,128)(2,1)} %copy-done.14) | copy-start | bytes 1572868
  67.6 9.3 %collective-permute-start.12 = (bf16[1,32,32,128]{3,2,1,0:T(8,128)(2,1)S(1)}, bf16[1,32,32,128]{3,2,1,0:T(8,128)(2,1)S(1)}, u32[]{:S(2)}, u32[]{:S(2)}) collective-permute-start(bf16[1,32,32,128]{3,2,1,0:T(8,128)(2,1)S(1)} %shard_map.82.refs_1_.near_ref), channel_id=1, source_target_pairs={{0,2},{1,3},{2,0},{3,1},{4,6},{5,7},{6,4},{7,5},{8,10},{9,11},{10,... | collective-permute-start | bytes 786440 | tf_op jit(solution)/shard_map/ppermute | solution.py:392
  69.5 13.0 %collective-permute-start.11 = (bf16[1,32,32,128]{3,2,1,0:T(8,128)(2,1)S(1)}, bf16[1,32,32,128]{3,2,1,0:T(8,128)(2,1)S(1)}, u32[]{:S(2)}, u32[]{:S(2)}) collective-permute-start(bf16[1,32,32,128]{3,2,1,0:T(8,128)(2,1)S(1)} %shard_map.83.refs_1_.near_ref), channel_id=1, source_target_pairs={{0,2},{1,3},{2,0},{3,1},{4,6},{5,7},{6,4},{7,5},{8,10},{9,11},{10,... | collective-permute-start | bytes 786440 | tf_op jit(solution)/shard_map/ppermute | solution.py:392
  70.5 17.7 %collective-permute-start.10 = (bf16[1,32,32,128]{3,2,1,0:T(8,128)(2,1)S(1)}, bf16[1,32,32,128]{3,2,1,0:T(8,128)(2,1)S(1)}, u32[]{:S(2)}, u32[]{:S(2)}) collective-permute-start(bf16[1,32,32,128]{3,2,1,0:T(8,128)(2,1)S(1)} %shard_map.84.refs_1_.near_ref), channel_id=1, source_target_pairs={{0,2},{1,3},{2,0},{3,1},{4,6},{5,7},{6,4},{7,5},{8,10},{9,11},{10,... | collective-permute-start | bytes 786440 | tf_op jit(solution)/shard_map/ppermute | solution.py:392
  73.6 20.2 %collective-permute-start.9 = (bf16[1,32,32,128]{3,2,1,0:T(8,128)(2,1)S(1)}, bf16[1,32,32,128]{3,2,1,0:T(8,128)(2,1)S(1)}, u32[]{:S(2)}, u32[]{:S(2)}) collective-permute-start(bf16[1,32,32,128]{3,2,1,0:T(8,128)(2,1)S(1)} %shard_map.85.refs_1_.near_ref), channel_id=1, source_target_pairs={{0,2},{1,3},{2,0},{3,1},{4,6},{5,7},{6,4},{7,5},{8,10},{9,11},{10,... | collective-permute-start | bytes 786440 | tf_op jit(solution)/shard_map/ppermute | solution.py:392
  74.6 24.9 %collective-permute-start.8 = (bf16[1,32,32,128]{3,2,1,0:T(8,128)(2,1)S(1)}, bf16[1,32,32,128]{3,2,1,0:T(8,128)(2,1)S(1)}, u32[]{:S(2)}, u32[]{:S(2)}) collective-permute-start(bf16[1,32,32,128]{3,2,1,0:T(8,128)(2,1)S(1)} %shard_map.86.refs_1_.near_ref), channel_id=1, source_target_pairs={{0,2},{1,3},{2,0},{3,1},{4,6},{5,7},{6,4},{7,5},{8,10},{9,11},{10,... | collective-permute-start | bytes 786440 | tf_op jit(solution)/shard_map/ppermute | solution.py:392
  77.9 21.6 %collective-permute-start.13 = (bf16[32,32,128]{2,1,0:T(8,128)(2,1)S(1)}, bf16[32,32,128]{2,1,0:T(8,128)(2,1)S(1)}, u32[]{:S(2)}, u32[]{:S(2)}) collective-permute-start(bf16[32,32,128]{2,1,0:T(8,128)(2,1)S(1)} %shard_map.89.refs_0_), channel_id=1, source_target_pairs={{0,28},{4,24},{8,20},{12,16},{16,12},{20,8},{24,4},{28,0},{1,29},{... | collective-permute-start | bytes 786440 | tf_op jit(solution)/shard_map/ppermute | solution.py:398
  82.6 22.5 %collective-permute-start.5 = (bf16[1,32,32,128]{3,2,1,0:T(8,128)(2,1)S(1)}, bf16[1,32,32,128]{3,2,1,0:T(8,128)(2,1)S(1)}, u32[]{:S(2)}, u32[]{:S(2)}) collective-permute-start(bf16[1,32,32,128]{3,2,1,0:T(8,128)(2,1)S(1)} %shard_map.87.near_ref.refs_1_), channel_id=1, source_target_pairs={{0,2},{1,3},{2,0},{3,1},{4,6},{5,7},{6,4},{7,5},{8,10},{9,11},{10,... | collective-permute-start | bytes 786440 | tf_op jit(solution)/shard_map/ppermute | solution.py:392
  88.2 18.4 %collective-permute-start.14 = (bf16[32,32,128]{2,1,0:T(8,128)(2,1)S(1)}, bf16[32,32,128]{2,1,0:T(8,128)(2,1)S(1)}, u32[]{:S(2)}, u32[]{:S(2)}) collective-permute-start(bf16[32,32,128]{2,1,0:T(8,128)(2,1)S(1)} %shard_map.90.refs_0_), channel_id=1, source_target_pairs={{0,24},{4,28},{8,16},{12,20},{16,8},{20,12},{24,0},{28,4},{1,25},{... | collective-permute-start | bytes 786440 | tf_op jit(solution)/shard_map/ppermute | solution.py:398
  93.8 16.9 %collective-permute-start.18 = (bf16[1,32,32,128]{3,2,1,0:T(8,128)(2,1)S(1)}, bf16[1,32,32,128]{3,2,1,0:T(8,128)(2,1)S(1)}, u32[]{:S(2)}, u32[]{:S(2)}) collective-permute-start(bf16[1,32,32,128]{3,2,1,0:T(8,128)(2,1)S(1)} %shard_map.96.refs_1_.near_ref), channel_id=1, source_target_pairs={{0,2},{1,3},{2,0},{3,1},{4,6},{5,7},{6,4},{7,5},{8,10},{9,11},{10,... | collective-permute-start | bytes 786440 | tf_op jit(solution)/shard_map/ppermute | solution.py:392
  99.4 13.4 %collective-permute-start.19 = (bf16[32,32,128]{2,1,0:T(8,128)(2,1)S(1)}, bf16[32,32,128]{2,1,0:T(8,128)(2,1)S(1)}, u32[]{:S(2)}, u32[]{:S(2)}) collective-permute-start(bf16[32,32,128]{2,1,0:T(8,128)(2,1)S(1)} %shard_map.91.refs_0_), channel_id=1, source_target_pairs={{0,8},{4,12},{8,0},{12,4},{16,24},{20,28},{24,16},{28,20},{1,9},{5... | collective-permute-start | bytes 786440 | tf_op jit(solution)/shard_map/ppermute | solution.py:398
  99.5 13.3 %collective-permute-start.20 = (bf16[32,32,128]{2,1,0:T(8,128)(2,1)S(1)}, bf16[32,32,128]{2,1,0:T(8,128)(2,1)S(1)}, u32[]{:S(2)}, u32[]{:S(2)}) collective-permute-start(bf16[32,32,128]{2,1,0:T(8,128)(2,1)S(1)} %shard_map.92.refs_0_), channel_id=1, source_target_pairs={{0,20},{4,16},{8,28},{12,24},{16,4},{20,0},{24,12},{28,8},{1,21},{... | collective-permute-start | bytes 786440 | tf_op jit(solution)/shard_map/ppermute | solution.py:398
  105.0 12.1 %collective-permute-start.17 = (bf16[1,32,32,128]{3,2,1,0:T(8,128)(2,1)S(1)}, bf16[1,32,32,128]{3,2,1,0:T(8,128)(2,1)S(1)}, u32[]{:S(2)}, u32[]{:S(2)}) collective-permute-start(bf16[1,32,32,128]{3,2,1,0:T(8,128)(2,1)S(1)} %shard_map.97.near_ref), channel_id=1, source_target_pairs={{0,2},{1,3},{2,0},{3,1},{4,6},{5,7},{6,4},{7,5},{8,10},{9,11},{10,... | collective-permute-start | bytes 786440 | tf_op jit(solution)/shard_map/ppermute | solution.py:392
  106.5 17.6 %collective-permute-start.16 = (bf16[32,32,128]{2,1,0:T(8,128)(2,1)S(1)}, bf16[32,32,128]{2,1,0:T(8,128)(2,1)S(1)}, u32[]{:S(2)}, u32[]{:S(2)}) collective-permute-start(bf16[32,32,128]{2,1,0:T(8,128)(2,1)S(1)} %shard_map.93.refs_0_), channel_id=1, source_target_pairs={{0,12},{4,8},{8,4},{12,0},{16,28},{20,24},{24,20},{28,16},{1,13},{... | collective-permute-start | bytes 786440 | tf_op jit(solution)/shard_map/ppermute | solution.py:398
  109.1 5.8 %copy-start.4 = (bf16[512,256]{1,0:T(8,128)(2,1)S(1)}, bf16[512,256]{1,0:T(8,128)(2,1)}, u32[]{:S(2)}) copy-start(bf16[512,256]{1,0:T(8,128)(2,1)} %orbitals.5) | copy-start | bytes 786436
  109.1 5.8 %copy-start.18 = (s32[512]{0:T(512)S(1)}, s32[512]{0:T(512)}, u32[]{:S(2)}) copy-start(s32[512]{0:T(512)} %row.1) | copy-start | bytes 6148
  109.2 5.8 %copy-start.19 = (s32[8]{0:T(128)S(1)}, s32[8]{0:T(128)}, u32[]{:S(2)}) copy-start(s32[8]{0:T(128)} %count.1) | copy-start | bytes 100
  110.6 13.5 %collective-permute-start.15 = (bf16[32,32,128]{2,1,0:T(8,128)(2,1)S(1)}, bf16[32,32,128]{2,1,0:T(8,128)(2,1)S(1)}, u32[]{:S(2)}, u32[]{:S(2)}) collective-permute-start(bf16[32,32,128]{2,1,0:T(8,128)(2,1)S(1)} %shard_map.94.refs_0_), channel_id=1, source_target_pairs={{0,16},{4,20},{8,24},{12,28},{16,0},{20,4},{24,8},{28,12},{1,17},{... | collective-permute-start | bytes 786440 | tf_op jit(solution)/shard_map/ppermute | solution.py:398
  113.7 10.4 %collective-permute-start.21 = (bf16[32,32,128]{2,1,0:T(8,128)(2,1)S(1)}, bf16[32,32,128]{2,1,0:T(8,128)(2,1)S(1)}, u32[]{:S(2)}, u32[]{:S(2)}) collective-permute-start(bf16[32,32,128]{2,1,0:T(8,128)(2,1)S(1)} %shard_map.98.refs_0_), channel_id=1, source_target_pairs={{0,4},{4,0},{8,12},{12,8},{16,20},{20,16},{24,28},{28,24},{1,5},{5... | collective-permute-start | bytes 786440 | tf_op jit(solution)/shard_map/ppermute | solution.py:398
  125.6 2.7 %collective-permute-start.22 = (bf16[32,64,256]{2,1,0:T(8,128)(2,1)S(1)}, bf16[32,64,256]{2,1,0:T(8,128)(2,1)S(1)}, u32[]{:S(2)}, u32[]{:S(2)}) collective-permute-start(bf16[32,64,256]{2,1,0:T(8,128)(2,1)S(1)} %get-tuple-element.30), channel_id=1, source_target_pairs={{0,1},{1,0},{2,3},{3,2},{4,5},{5,4},{6,7},{7,6},{8,9},{9,8},{10,11... | collective-permute-start | bytes 3145736 | tf_op jit(solution)/shard_map/ppermute | solution.py:403

commit v7 on v6

--- a/solution.py
+++ b/solution.py
@@ -129,7 +129,7 @@
         out_shape=jax.ShapeDtypeStruct(shape, BF16),
         in_specs=[whole] * 3 + [away] * len(early),
         out_specs=pl.BlockSpec(memory_space=pltpu.HBM),
-        scratch_shapes=[pltpu.VMEM(shape, BF16), pltpu.SemaphoreType.DMA((4,))],
+        scratch_shapes=[pltpu.VMEM(shape, BF16), pltpu.SemaphoreType.DMA((8,))],
         cost_estimate=pl.CostEstimate(
             flops=4 * count * occ * vir * part, bytes_accessed=4 * occ * part * vir, transcendentals=0
         ),
@@ -203,9 +203,12 @@
     transform_tiles(left_ref, start_copies(True, start, tiles, held, sems), held, out)
 
 
-def first_kernel(start, orbitals, tiles, out, left_ref, side_rows, held, sems, lines):
+def first_kernel(start, orbitals, tiles, out, left_ref, side_rows, held, sems, lines, whole, sem):
+    fetch = pltpu.make_async_copy(orbitals, whole, sem)
+    fetch.start()
     copies = start_copies(True, start, tiles, held, sems)
-    order_orbitals(orbitals, left_ref, side_rows, lines)
+    fetch.wait()
+    order_orbitals(whole, left_ref, side_rows, lines)
     transform_tiles(left_ref, copies, held, out)
 
 
@@ -233,7 +236,7 @@
 PIECE = 8
 
 
-def tile_call(body, count, tiles, ins, outs, early=(), scratch=()):
+def tile_call(body, count, tiles, ins, outs, early=(), scratch=(), first=None):
     _, sig, nu = tiles.shape
     vir = outs[0].shape[1]
     whole = pl.BlockSpec(memory_space=pltpu.VMEM)
@@ -242,7 +245,7 @@
     return pl.pallas_call(
         body,
         out_shape=outs,
-        in_specs=[whole, away] + [whole] * (len(ins) - 1) + [away] * len(early),
+        in_specs=[first or whole, away] + [whole] * (len(ins) - 1) + [away] * len(early),
         out_specs=[whole] * len(outs),
         scratch_shapes=[pltpu.VMEM((count, sig, nu), BF16), pltpu.SemaphoreType.DMA((count // PIECE,)), *scratch],
         cost_estimate=pl.CostEstimate(
@@ -313,7 +316,7 @@
         give[i] = jnp.where(core == 0, high, low)
         return carry
 
-    lax.fori_loop(0, occ, step, 0, unroll=8)
+    lax.fori_loop(0, occ, step, 0, unroll=16)
 
 
 def back_transform(rows, values):
@@ -356,9 +359,10 @@
         jax.ShapeDtypeStruct((vir, orbitals.shape[0]), BF16),
         jax.ShapeDtypeStruct((2 * nu_part, vir), BF16),
     ]
-    scratch = [pltpu.VMEM(orbitals.shape, BF16)]
+    scratch = [pltpu.VMEM(orbitals.shape, BF16)] * 2 + [pltpu.SemaphoreType.DMA]
     given, left, side_rows = tile_call(
-        functools.partial(first_kernel, 0), half // 2, tiles, (orbitals,), outs, (), scratch
+        functools.partial(first_kernel, 0), half // 2, tiles, (orbitals,), outs, (), scratch,
+        pl.BlockSpec(memory_space=pltpu.HBM),
     )
     first_parts = lax.ppermute(given, "ao", near)
     given, second_parts = give(half // 2, [given, other])

time: 130 us -> 129 us (level)
  no operation moved by 1% of the time
where the time goes in v7:
time: 129 us
  waiting for transfers between devices  55.7 us (43%)
  starting transfers between devices  36.7 us (28%)
  Pallas kernels  32.2 us (25%)
  local copies, waits for them, and re-layouts  2.79 us (2%)
    ppermute x4, waiting for transfers between devices, shards(): parts += [here, lax.ppermute(there, 'ao', far)]  17.3 us
    all_to_all x1, waiting for transfers between devices, shards(): lax.all_to_all(sent, 'occ', split_axis=0, concat_axis=0, tiled=True)  15.1 us
    pallas_call x6, Pallas kernels, tile_call(): pl.pallas_call(body, out_shape=outs, in_specs=[first or whole, away] + [w...  14.3 us
    ppermute x8, waiting for transfers between devices, shards(): far_blocks.append(lax.ppermute(blocks_of[-1], 'ao', far))  13.7 us
    ppermute x7, starting transfers between devices, shards(): lax.ppermute(x, 'occ', [(o, o ^ k) for o in range(nodes)])  12.7 us
    ppermute x8, starting transfers between devices, shards(): far_blocks.append(lax.ppermute(blocks_of[-1], 'ao', far))  10.4 us
    pallas_call x11, Pallas kernels, call(): pl.pallas_call(body, out_shape=outs, in_specs=[whole] * len(ins) + [pl.Bl...  9.48 us
    all_to_all x1, starting transfers between devices, shards(): lax.all_to_all(sent, 'occ', split_axis=0, concat_axis=0, tiled=True)  7.22 us
  transfers between devices with their start and end apart: 24, of which 14 were waited for; matrix products, arithmetic and copies ran while one was open for 0% of the time, Pallas kernels for 23%

profile of v7, /device:TPU:0, one launch (start us, length us, event | category | flops | bytes accessed | tf_op | source)
XLA Modules:
  0.0 128.9 jit_solution(9817623603024389811)
XLA Ops:
  0.5 0.9 copy-done.2
  1.4 2.2 %shard_map.73 = (bf16[16,256,128]{2,1,0:T(8,128)(2,1)S(1)}, bf16[256,512]{1,0:T(8,128)(2,1)S(1)}, bf16[256,256]{1,0:T(8,128)(2,1)S(1)}) custom-call(bf16[512,256]{1,0:T(8,128)(2,1)S(1)} %copy-done.2, bf16[64,512,128]{2,1,0:T(8,128)(2,1)} %tiles.11), custom_call_target="tpu_custom_call" | custom-call | flops 1610612736 | bytes 4194304 | tf_op jit(solution)/shard_map/pallas_call | solution.py:245
  3.7 2.2 %shard_map.74.early = bf16[16,256,128]{2,1,0:T(8,128)(2,1)S(1)} custom-call(bf16[256,512]{1,0:T(8,128)(2,1)S(1)} %get-tuple-element.18.left_ref, bf16[64,512,128]{2,1,0:T(8,128)(2,1)} %tiles.11, bf16[16,256,128]{2,1,0:T(8,128)(2,1)S(1)} %get-tuple-element.19.rest_0_, bf16[32,64,256]{2,1,0:T(8,128)(2,1)S(1)} %collective-permute-done.rest_1_.other_ref), custom_call_target="tpu_custom_call" | custom-call | flops 536870912 | bytes 4194304 | tf_op jit(solution)/shard_map/pallas_call | solution.py:245
  6.4 1.9 %shard_map.75.rows_ref = bf16[256,256]{1,0:T(8,128)(2,1)S(1)} custom-call(s32[512]{0:T(512)S(1)} %bitcast.7, s32[512]{0:T(512)S(1)} %copy-done.17, bf16[512,256]{1,0:T(8,128)(2,1)S(1)} %copy-done.3, bf16[16,256,128]{2,1,0:T(8,128)(2,1)S(1)} %shard_map.74.early), custom_call_target="tpu_custom_call" | custom-call | flops 65536 | bytes 262144 | tf_op jit(solution)/shard_map/pallas_call | solution.py:91
  8.7 1.0 copy-done
  9.7 1.7 %shard_map.76.rest_0_ = bf16[8,32,32,128]{3,2,1,0:T(8,128)(2,1)} custom-call(bf16[256,256]{1,0:T(8,128)(2,1)S(1)} %shard_map.75.rows_ref, bf16[32,64,256]{2,1,0:T(8,128)(2,1)S(1)} %bitcast.6, bf16[32,64,256]{2,1,0:T(8,128)(2,1)S(1)} %collective-permute-done.rest_1_.other_ref, bf16[16,256,128]{2,1,0:T(8,128)(2,1)S(1)} %collective-permute-done.2.rest_0_.other, ...), custom_call_target="tpu_custom_call" | custom-call | flops 536870912 | bytes 2097152 | tf_op jit(solution)/shard_map/pallas_call | solution.py:127
  11.4 7.2 %all-to-all-start = ((bf16[8,32,32,128]{3,2,1,0:T(8,128)(2,1)}), bf16[8,32,32,128]{3,2,1,0:T(8,128)(2,1)S(1)}, u32[]{:S(2)}, u32[]{:S(2)}) async-start(bf16[8,32,32,128]{3,2,1,0:T(8,128)(2,1)} %shard_map.76.rest_0_), calls=%async_computation | async-start | bytes 4194304 | tf_op jit(solution)/shard_map/all_to_all | solution.py:371
  18.6 2.0 %shard_map.77 = (bf16[8,128,256]{2,1,0:T(8,128)(2,1)S(1)}, bf16[8,128,256]{2,1,0:T(8,128)(2,1)S(1)}) custom-call(bf16[256,512]{1,0:T(8,128)(2,1)S(1)} %get-tuple-element.18.left_ref, bf16[64,512,128]{2,1,0:T(8,128)(2,1)} %tiles.11, bf16[16,256,128]{2,1,0:T(8,128)(2,1)S(1)} %collective-permute-done.2.rest_0_.other, ...), custom_call_target="tpu_custom_call" | custom-call | flops 201326592 | bytes 2097152 | tf_op jit(solution)/shard_map/pallas_call | solution.py:245
  21.4 1.5 %collective-permute-start.3 = (bf16[8,128,256]{2,1,0:T(8,128)(2,1)S(1)}, bf16[8,128,256]{2,1,0:T(8,128)(2,1)S(1)}, u32[]{:S(2)}, u32[]{:S(2)}) collective-permute-start(bf16[8,128,256]{2,1,0:T(8,128)(2,1)S(1)} %get-tuple-element.21.rest_0_), channel_id=1, source_target_pairs={{0,2},{1,3},{2,0},{3,1},{4,6},{5,7},{6,4},{7,5},{8,10},{9,11},{10,... | collective-permute-start | bytes 1572872 | tf_op jit(solution)/shard_map/ppermute | solution.py:383
  22.9 2.0 %shard_map.78 = (bf16[8,128,256]{2,1,0:T(8,128)(2,1)S(1)}, bf16[8,128,256]{2,1,0:T(8,128)(2,1)S(1)}) custom-call(bf16[256,512]{1,0:T(8,128)(2,1)S(1)} %get-tuple-element.18.left_ref, bf16[64,512,128]{2,1,0:T(8,128)(2,1)} %tiles.11, bf16[16,256,128]{2,1,0:T(8,128)(2,1)S(1)} %collective-permute-done.2.rest_0_.other, ...), custom_call_target="tpu_custom_call" | custom-call | flops 201326592 | bytes 2097152 | tf_op jit(solution)/shard_map/pallas_call | solution.py:245
  25.5 10.7 %collective-permute-done.3.rest_1_.refs_1_ = bf16[8,128,256]{2,1,0:T(8,128)(2,1)S(1)} collective-permute-done((bf16[8,128,256]{2,1,0:T(8,128)(2,1)S(1)}, bf16[8,128,256]{2,1,0:T(8,128)(2,1)S(1)}, u32[]{:S(2)}, u32[]{:S(2)}) %collective-permute-start.3) | collective-permute-done | bytes 524320 | tf_op jit(solution)/shard_map/ppermute | solution.py:383
  36.2 3.0 %shard_map.79 = (bf16[8,128,256]{2,1,0:T(8,128)(2,1)S(1)}, bf16[8,128,256]{2,1,0:T(8,128)(2,1)}) custom-call(bf16[256,512]{1,0:T(8,128)(2,1)S(1)} %get-tuple-element.18.left_ref, bf16[64,512,128]{2,1,0:T(8,128)(2,1)} %tiles.11, bf16[16,256,128]{2,1,0:T(8,128)(2,1)S(1)} %copy-done.1, bf16[256,256]{1,0:T(8,128)(2,1)S(1)} %get-tuple-element.20.right_ref, ...), custom_call_target="tpu_custom_call" | custom-call | flops 201326592 | bytes 2097152 | tf_op jit(solution)/shard_map/pallas_call | solution.py:245
  39.2 1.5 %collective-permute-start.6 = (bf16[8,128,256]{2,1,0:T(8,128)(2,1)}, bf16[8,128,256]{2,1,0:T(8,128)(2,1)}, u32[]{:S(2)}, u32[]{:S(2)}) collective-permute-start(bf16[8,128,256]{2,1,0:T(8,128)(2,1)} %get-tuple-element.23.rest_0_), channel_id=1, source_target_pairs={{0,2},{1,3},{2,0},{3,1},{4,6},{5,7},{6,4},{7,5},{8,10},{9,11},{10,... | collective-permute-start | bytes 1572872 | tf_op jit(solution)/shard_map/ppermute | solution.py:383
  40.8 6.6 %collective-permute-done.4.rest_1_.refs_3_ = bf16[8,128,256]{2,1,0:T(8,128)(2,1)S(1)} collective-permute-done((bf16[8,128,256]{2,1,0:T(8,128)(2,1)S(1)}, bf16[8,128,256]{2,1,0:T(8,128)(2,1)S(1)}, u32[]{:S(2)}, u32[]{:S(2)}) %collective-permute-start.4) | collective-permute-done | bytes 524320 | tf_op jit(solution)/shard_map/ppermute | solution.py:383
  47.4 3.0 %shard_map.80 = (bf16[8,128,256]{2,1,0:T(8,128)(2,1)S(1)}, bf16[8,128,256]{2,1,0:T(8,128)(2,1)}) custom-call(bf16[256,512]{1,0:T(8,128)(2,1)S(1)} %get-tuple-element.18.left_ref, bf16[64,512,128]{2,1,0:T(8,128)(2,1)} %tiles.11, bf16[16,256,128]{2,1,0:T(8,128)(2,1)S(1)} %copy-done.1, bf16[256,256]{1,0:T(8,128)(2,1)S(1)} %get-tuple-element.20.right_ref, ...), custom_call_target="tpu_custom_call" | custom-call | flops 201326592 | bytes 2097152 | tf_op jit(solution)/shard_map/pallas_call | solution.py:245
  50.5 1.6 %collective-permute-start.7 = (bf16[8,128,256]{2,1,0:T(8,128)(2,1)}, bf16[8,128,256]{2,1,0:T(8,128)(2,1)S(1)}, u32[]{:S(2)}, u32[]{:S(2)}) collective-permute-start(bf16[8,128,256]{2,1,0:T(8,128)(2,1)} %get-tuple-element.24.early), channel_id=1, source_target_pairs={{0,2},{1,3},{2,0},{3,1},{4,6},{5,7},{6,4},{7,5},{8,10},{9,11},{10,... | collective-permute-start | bytes 1572872 | tf_op jit(solution)/shard_map/ppermute | solution.py:383
  52.0 15.1 %all-to-all-done.refs_0_ = bf16[8,32,32,128]{3,2,1,0:T(8,128)(2,1)S(1)} async-done(((bf16[8,32,32,128]{3,2,1,0:T(8,128)(2,1)}), bf16[8,32,32,128]{3,2,1,0:T(8,128)(2,1)S(1)}, u32[]{:S(2)}, u32[]{:S(2)}) %all-to-all-start) | async-done | bytes 2097184 | tf_op jit(solution)/shard_map/all_to_all | solution.py:371
  67.5 1.6 %collective-permute-start.12 = (bf16[1,32,32,128]{3,2,1,0:T(8,128)(2,1)S(1)}, bf16[1,32,32,128]{3,2,1,0:T(8,128)(2,1)S(1)}, u32[]{:S(2)}, u32[]{:S(2)}) collective-permute-start(bf16[1,32,32,128]{3,2,1,0:T(8,128)(2,1)S(1)} %shard_map.82.refs_1_.near_ref), channel_id=1, source_target_pairs={{0,2},{1,3},{2,0},{3,1},{4,6},{5,7},{6,4},{7,5},{8,10},{9,11},{10,... | collective-permute-start | bytes 786440 | tf_op jit(solution)/shard_map/ppermute | solution.py:396
  70.3 1.6 %collective-permute-start.10 = (bf16[1,32,32,128]{3,2,1,0:T(8,128)(2,1)S(1)}, bf16[1,32,32,128]{3,2,1,0:T(8,128)(2,1)S(1)}, u32[]{:S(2)}, u32[]{:S(2)}) collective-permute-start(bf16[1,32,32,128]{3,2,1,0:T(8,128)(2,1)S(1)} %shard_map.84.refs_1_.near_ref), channel_id=1, source_target_pairs={{0,2},{1,3},{2,0},{3,1},{4,6},{5,7},{6,4},{7,5},{8,10},{9,11},{10,... | collective-permute-start | bytes 786440 | tf_op jit(solution)/shard_map/ppermute | solution.py:396
  71.9 1.2 shard_map.88.dressed
  74.4 1.6 %collective-permute-start.8 = (bf16[1,32,32,128]{3,2,1,0:T(8,128)(2,1)S(1)}, bf16[1,32,32,128]{3,2,1,0:T(8,128)(2,1)S(1)}, u32[]{:S(2)}, u32[]{:S(2)}) collective-permute-start(bf16[1,32,32,128]{3,2,1,0:T(8,128)(2,1)S(1)} %shard_map.86.refs_1_.near_ref), channel_id=1, source_target_pairs={{0,2},{1,3},{2,0},{3,1},{4,6},{5,7},{6,4},{7,5},{8,10},{9,11},{10,... | collective-permute-start | bytes 786440 | tf_op jit(solution)/shard_map/ppermute | solution.py:396
  76.8 0.9 shard_map.89.refs_0_
  77.7 2.7 %collective-permute-start.13 = (bf16[32,32,128]{2,1,0:T(8,128)(2,1)S(1)}, bf16[32,32,128]{2,1,0:T(8,128)(2,1)S(1)}, u32[]{:S(2)}, u32[]{:S(2)}) collective-permute-start(bf16[32,32,128]{2,1,0:T(8,128)(2,1)S(1)} %shard_map.89.refs_0_), channel_id=1, source_target_pairs={{0,28},{4,24},{8,20},{12,16},{16,12},{20,8},{24,4},{28,0},{1,29},{... | collective-permute-start | bytes 786440 | tf_op jit(solution)/shard_map/ppermute | solution.py:402
  81.1 1.3 %collective-permute-done.11.far_ref = bf16[1,32,32,128]{3,2,1,0:T(8,128)(2,1)S(1)} collective-permute-done((bf16[1,32,32,128]{3,2,1,0:T(8,128)(2,1)S(1)}, bf16[1,32,32,128]{3,2,1,0:T(8,128)(2,1)S(1)}, u32[]{:S(2)}, u32[]{:S(2)}) %collective-permute-start.11) | collective-permute-done | bytes 262176 | tf_op jit(solution)/shard_map/ppermute | solution.py:396
  82.4 1.5 %collective-permute-start.5 = (bf16[1,32,32,128]{3,2,1,0:T(8,128)(2,1)S(1)}, bf16[1,32,32,128]{3,2,1,0:T(8,128)(2,1)S(1)}, u32[]{:S(2)}, u32[]{:S(2)}) collective-permute-start(bf16[1,32,32,128]{3,2,1,0:T(8,128)(2,1)S(1)} %shard_map.87.near_ref.refs_1_), channel_id=1, source_target_pairs={{0,2},{1,3},{2,0},{3,1},{4,6},{5,7},{6,4},{7,5},{8,10},{9,11},{10,... | collective-permute-start | bytes 786440 | tf_op jit(solution)/shard_map/ppermute | solution.py:396
  84.8 3.2 %collective-permute-done.10.far_ref = bf16[1,32,32,128]{3,2,1,0:T(8,128)(2,1)S(1)} collective-permute-done((bf16[1,32,32,128]{3,2,1,0:T(8,128)(2,1)S(1)}, bf16[1,32,32,128]{3,2,1,0:T(8,128)(2,1)S(1)}, u32[]{:S(2)}, u32[]{:S(2)}) %collective-permute-start.10) | collective-permute-done | bytes 262176 | tf_op jit(solution)/shard_map/ppermute | solution.py:396
  88.0 2.2 %collective-permute-start.14 = (bf16[32,32,128]{2,1,0:T(8,128)(2,1)S(1)}, bf16[32,32,128]{2,1,0:T(8,128)(2,1)S(1)}, u32[]{:S(2)}, u32[]{:S(2)}) collective-permute-start(bf16[32,32,128]{2,1,0:T(8,128)(2,1)S(1)} %shard_map.90.refs_0_), channel_id=1, source_target_pairs={{0,24},{4,28},{8,16},{12,20},{16,8},{20,12},{24,0},{28,4},{1,25},{... | collective-permute-start | bytes 786440 | tf_op jit(solution)/shard_map/ppermute | solution.py:402
  90.2 0.9 shard_map.91.refs_0_
  91.2 2.5 %collective-permute-done.9.far_ref = bf16[1,32,32,128]{3,2,1,0:T(8,128)(2,1)S(1)} collective-permute-done((bf16[1,32,32,128]{3,2,1,0:T(8,128)(2,1)S(1)}, bf16[1,32,32,128]{3,2,1,0:T(8,128)(2,1)S(1)}, u32[]{:S(2)}, u32[]{:S(2)}) %collective-permute-start.9) | collective-permute-done | bytes 262176 | tf_op jit(solution)/shard_map/ppermute | solution.py:396
  93.7 1.5 %collective-permute-start.18 = (bf16[1,32,32,128]{3,2,1,0:T(8,128)(2,1)S(1)}, bf16[1,32,32,128]{3,2,1,0:T(8,128)(2,1)S(1)}, u32[]{:S(2)}, u32[]{:S(2)}) collective-permute-start(bf16[1,32,32,128]{3,2,1,0:T(8,128)(2,1)S(1)} %shard_map.96.refs_1_.near_ref), channel_id=1, source_target_pairs={{0,2},{1,3},{2,0},{3,1},{4,6},{5,7},{6,4},{7,5},{8,10},{9,11},{10,... | collective-permute-start | bytes 786440 | tf_op jit(solution)/shard_map/ppermute | solution.py:396
  95.2 0.9 shard_map.92.refs_0_
  96.1 3.2 %collective-permute-done.8.far_ref = bf16[1,32,32,128]{3,2,1,0:T(8,128)(2,1)S(1)} collective-permute-done((bf16[1,32,32,128]{3,2,1,0:T(8,128)(2,1)S(1)}, bf16[1,32,32,128]{3,2,1,0:T(8,128)(2,1)S(1)}, u32[]{:S(2)}, u32[]{:S(2)}) %collective-permute-start.8) | collective-permute-done | bytes 262176 | tf_op jit(solution)/shard_map/ppermute | solution.py:396
  99.3 3.2 %collective-permute-start.20 = (bf16[32,32,128]{2,1,0:T(8,128)(2,1)S(1)}, bf16[32,32,128]{2,1,0:T(8,128)(2,1)S(1)}, u32[]{:S(2)}, u32[]{:S(2)}) collective-permute-start(bf16[32,32,128]{2,1,0:T(8,128)(2,1)S(1)} %shard_map.92.refs_0_), channel_id=1, source_target_pairs={{0,20},{4,16},{8,28},{12,24},{16,4},{20,0},{24,12},{28,8},{1,21},{... | collective-permute-start | bytes 786440 | tf_op jit(solution)/shard_map/ppermute | solution.py:402
  102.8 0.9 shard_map.93.refs_0_
  103.8 1.1 collective-permute-done.5.far_ref
  104.9 1.5 %collective-permute-start.17 = (bf16[1,32,32,128]{3,2,1,0:T(8,128)(2,1)S(1)}, bf16[1,32,32,128]{3,2,1,0:T(8,128)(2,1)S(1)}, u32[]{:S(2)}, u32[]{:S(2)}) collective-permute-start(bf16[1,32,32,128]{3,2,1,0:T(8,128)(2,1)S(1)} %shard_map.97.near_ref), channel_id=1, source_target_pairs={{0,2},{1,3},{2,0},{3,1},{4,6},{5,7},{6,4},{7,5},{8,10},{9,11},{10,... | collective-permute-start | bytes 786440 | tf_op jit(solution)/shard_map/ppermute | solution.py:396
  106.4 1.7 %collective-permute-start.16 = (bf16[32,32,128]{2,1,0:T(8,128)(2,1)S(1)}, bf16[32,32,128]{2,1,0:T(8,128)(2,1)S(1)}, u32[]{:S(2)}, u32[]{:S(2)}) collective-permute-start(bf16[32,32,128]{2,1,0:T(8,128)(2,1)S(1)} %shard_map.93.refs_0_), channel_id=1, source_target_pairs={{0,12},{4,8},{8,4},{12,0},{16,28},{20,24},{24,20},{28,16},{1,13},{... | collective-permute-start | bytes 786440 | tf_op jit(solution)/shard_map/ppermute | solution.py:402
  108.1 0.9 shard_map.94.refs_0_
  109.0 1.5 %collective-permute-done.18.far_ref = bf16[1,32,32,128]{3,2,1,0:T(8,128)(2,1)S(1)} collective-permute-done((bf16[1,32,32,128]{3,2,1,0:T(8,128)(2,1)S(1)}, bf16[1,32,32,128]{3,2,1,0:T(8,128)(2,1)S(1)}, u32[]{:S(2)}, u32[]{:S(2)}) %collective-permute-start.18) | collective-permute-done | bytes 262176 | tf_op jit(solution)/shard_map/ppermute | solution.py:396
  110.5 1.7 %collective-permute-start.15 = (bf16[32,32,128]{2,1,0:T(8,128)(2,1)S(1)}, bf16[32,32,128]{2,1,0:T(8,128)(2,1)S(1)}, u32[]{:S(2)}, u32[]{:S(2)}) collective-permute-start(bf16[32,32,128]{2,1,0:T(8,128)(2,1)S(1)} %shard_map.94.refs_0_), channel_id=1, source_target_pairs={{0,16},{4,20},{8,24},{12,28},{16,0},{20,4},{24,8},{28,12},{1,17},{... | collective-permute-start | bytes 786440 | tf_op jit(solution)/shard_map/ppermute | solution.py:402
  112.7 0.9 shard_map.98.refs_0_
  113.6 1.2 collective-permute-start.21
  114.8 2.1 %shard_map.81.rows = bf16[256,256]{1,0:T(8,128)(2,1)S(1)} custom-call(s32[512]{0:T(512)S(1)} %copy-done.18, s32[8]{0:T(128)S(1)} %copy-done.19, bf16[512,256]{1,0:T(8,128)(2,1)S(1)} %copy-done.4, bf16[8,128,256]{2,1,0:T(8,128)(2,1)} %get-tuple-element.24.early), custom_call_target="tpu_custom_call" | custom-call | flops 65536 | bytes 262144 | tf_op jit(solution)/shard_map/pallas_call | solution.py:91
  117.0 0.9 shard_map.99.refs_0_
  117.9 6.1 %collective-permute-done.15.rest_0_.refs_4_ = bf16[32,32,128]{2,1,0:T(8,128)(2,1)S(1)} collective-permute-done((bf16[32,32,128]{2,1,0:T(8,128)(2,1)S(1)}, bf16[32,32,128]{2,1,0:T(8,128)(2,1)S(1)}, u32[]{:S(2)}, u32[]{:S(2)}) %collective-permute-start.15) | collective-permute-done | bytes 262176 | tf_op jit(solution)/shard_map/ppermute | solution.py:402
  124.0 1.0 shard_map.100
  125.1 2.6 %collective-permute-done.22 = bf16[32,64,256]{2,1,0:T(8,128)(2,1)S(1)} collective-permute-done((bf16[32,64,256]{2,1,0:T(8,128)(2,1)S(1)}, bf16[32,64,256]{2,1,0:T(8,128)(2,1)S(1)}, u32[]{:S(2)}, u32[]{:S(2)}) %collective-permute-start.22) | collective-permute-done | bytes 1048608 | tf_op jit(solution)/shard_map/ppermute | solution.py:407
  127.8 1.1 add_bitcast_fusion
  (69 shorter events, 9.1 us)
Async XLA Ops:
  0.0 3.7 %collective-permute-start = (bf16[32,64,256]{2,1,0:T(8,128)(2,1)}, bf16[32,64,256]{2,1,0:T(8,128)(2,1)S(1)}, u32[]{:S(2)}, u32[]{:S(2)}) collective-permute-start(bf16[32,64,256]{2,1,0:T(8,128)(2,1)} %bitcast.5), channel_id=1, source_target_pairs={{0,1},{1,0},{2,3},{3,2},{4,5},{5,4},{6,7},{7,6},{8,9},{9,8},{10,11... | collective-permute-start | bytes 3145736 | tf_op jit(solution)/shard_map/ppermute | solution.py:347
  0.5 0.9 copy-start.2
  3.6 4.8 %collective-permute-start.2 = (bf16[16,256,128]{2,1,0:T(8,128)(2,1)S(1)}, bf16[16,256,128]{2,1,0:T(8,128)(2,1)S(1)}, u32[]{:S(2)}, u32[]{:S(2)}) collective-permute-start(bf16[16,256,128]{2,1,0:T(8,128)(2,1)S(1)} %get-tuple-element.19.rest_0_), channel_id=1, source_target_pairs={{0,1},{1,0},{2,3},{3,2},{4,5},{5,4},{6,7},{7,6},{8,9},{9,8},{10,11... | collective-permute-start | bytes 3145736 | tf_op jit(solution)/shard_map/ppermute | solution.py:367
  3.7 2.7 %copy-start.3 = (bf16[512,256]{1,0:T(8,128)(2,1)S(1)}, bf16[512,256]{1,0:T(8,128)(2,1)}, u32[]{:S(2)}) copy-start(bf16[512,256]{1,0:T(8,128)(2,1)} %orbitals.5) | copy-start | bytes 786436
  3.7 2.7 %copy-start.16 = (s32[512,1]{0,1:T(1,128)S(1)}, s32[512,1]{0,1:T(1,128)}, u32[]{:S(2)}) copy-start(s32[512,1]{0,1:T(1,128)} %param.12) | copy-start | bytes 6148
  3.7 2.7 %copy-start.17 = (s32[512]{0:T(512)S(1)}, s32[512]{0:T(512)}, u32[]{:S(2)}) copy-start(s32[512]{0:T(512)} %sub.1) | copy-start | bytes 6148
  5.9 3.8 %copy-start.9 = (bf16[32,256,64]{1,2,0:T(8,128)(2,1)S(1)}, bf16[32,256,64]{1,2,0:T(8,128)(2,1)}, u32[]{:S(2)}) copy-start(bf16[32,256,64]{1,2,0:T(8,128)(2,1)} %param.7) | copy-start | bytes 3145732
  5.9 2.8 %collective-permute-start.1 = (bf16[16,256,128]{2,1,0:T(8,128)(2,1)S(1)}, bf16[16,256,128]{2,1,0:T(8,128)(2,1)S(1)}, u32[]{:S(2)}, u32[]{:S(2)}) collective-permute-start(bf16[16,256,128]{2,1,0:T(8,128)(2,1)S(1)} %shard_map.74.early), channel_id=1, source_target_pairs={{0,1},{1,0},{2,3},{3,2},{4,5},{5,4},{6,7},{7,6},{8,9},{9,8},{10,11... | collective-permute-start | bytes 3145736 | tf_op jit(solution)/shard_map/ppermute | solution.py:355
  8.7 1.0 copy-start
  11.4 55.8 %all-to-all-start = ((bf16[8,32,32,128]{3,2,1,0:T(8,128)(2,1)}), bf16[8,32,32,128]{3,2,1,0:T(8,128)(2,1)S(1)}, u32[]{:S(2)}, u32[]{:S(2)}) async-start(bf16[8,32,32,128]{3,2,1,0:T(8,128)(2,1)} %shard_map.76.rest_0_), calls=%async_computation | async-start | bytes 4194304 | tf_op jit(solution)/shard_map/all_to_all | solution.py:371
  20.6 0.8 copy-start.10
  21.4 14.8 %copy-start.1 = (bf16[16,256,128]{2,1,0:T(8,128)(2,1)S(1)}, bf16[16,256,128]{2,1,0:T(8,128)(2,1)}, u32[]{:S(2)}) copy-start(bf16[16,256,128]{2,1,0:T(8,128)(2,1)} %copy-done) | copy-start | bytes 3145732
  21.4 14.8 %collective-permute-start.3 = (bf16[8,128,256]{2,1,0:T(8,128)(2,1)S(1)}, bf16[8,128,256]{2,1,0:T(8,128)(2,1)S(1)}, u32[]{:S(2)}, u32[]{:S(2)}) collective-permute-start(bf16[8,128,256]{2,1,0:T(8,128)(2,1)S(1)} %get-tuple-element.21.rest_0_), channel_id=1, source_target_pairs={{0,2},{1,3},{2,0},{3,1},{4,6},{5,7},{6,4},{7,5},{8,10},{9,11},{10,... | collective-permute-start | bytes 1572872 | tf_op jit(solution)/shard_map/ppermute | solution.py:383
  24.9 14.3 %copy-start.12 = (bf16[8,128,256]{2,1,0:T(8,128)(2,1)}, bf16[8,128,256]{2,1,0:T(8,128)(2,1)S(1)}, u32[]{:S(2)}) copy-start(bf16[8,128,256]{2,1,0:T(8,128)(2,1)S(1)} %get-tuple-element.26.refs_2_) | copy-start | bytes 1572868
  24.9 22.5 %collective-permute-start.4 = (bf16[8,128,256]{2,1,0:T(8,128)(2,1)S(1)}, bf16[8,128,256]{2,1,0:T(8,128)(2,1)S(1)}, u32[]{:S(2)}, u32[]{:S(2)}) collective-permute-start(bf16[8,128,256]{2,1,0:T(8,128)(2,1)S(1)} %get-tuple-element.22.rest_0_), channel_id=1, source_target_pairs={{0,2},{1,3},{2,0},{3,1},{4,6},{5,7},{6,4},{7,5},{8,10},{9,11},{10,... | collective-permute-start | bytes 1572872 | tf_op jit(solution)/shard_map/ppermute | solution.py:383
  36.2 3.0 %copy-start.5 = (bf16[8,128,256]{2,1,0:T(8,128)(2,1)}, bf16[8,128,256]{2,1,0:T(8,128)(2,1)S(1)}, u32[]{:S(2)}) copy-start(bf16[8,128,256]{2,1,0:T(8,128)(2,1)S(1)} %collective-permute-done.3.rest_1_.refs_1_) | copy-start | bytes 1572868
  39.2 11.2 %copy-start.14 = (bf16[8,128,256]{2,1,0:T(8,128)(2,1)}, bf16[8,128,256]{2,1,0:T(8,128)(2,1)S(1)}, u32[]{:S(2)}) copy-start(bf16[8,128,256]{2,1,0:T(8,128)(2,1)S(1)} %get-tuple-element.27.refs_4_) | copy-start | bytes 1572868
  39.2 32.6 %collective-permute-start.6 = (bf16[8,128,256]{2,1,0:T(8,128)(2,1)}, bf16[8,128,256]{2,1,0:T(8,128)(2,1)}, u32[]{:S(2)}, u32[]{:S(2)}) collective-permute-start(bf16[8,128,256]{2,1,0:T(8,128)(2,1)} %get-tuple-element.23.rest_0_), channel_id=1, source_target_pairs={{0,2},{1,3},{2,0},{3,1},{4,6},{5,7},{6,4},{7,5},{8,10},{9,11},{10,... | collective-permute-start | bytes 1572872 | tf_op jit(solution)/shard_map/ppermute | solution.py:383
  47.4 3.0 %copy-start.7 = (bf16[8,128,256]{2,1,0:T(8,128)(2,1)}, bf16[8,128,256]{2,1,0:T(8,128)(2,1)S(1)}, u32[]{:S(2)}) copy-start(bf16[8,128,256]{2,1,0:T(8,128)(2,1)S(1)} %collective-permute-done.4.rest_1_.refs_3_) | copy-start | bytes 1572868
  50.5 23.9 %collective-permute-start.7 = (bf16[8,128,256]{2,1,0:T(8,128)(2,1)}, bf16[8,128,256]{2,1,0:T(8,128)(2,1)S(1)}, u32[]{:S(2)}, u32[]{:S(2)}) collective-permute-start(bf16[8,128,256]{2,1,0:T(8,128)(2,1)} %get-tuple-element.24.early), channel_id=1, source_target_pairs={{0,2},{1,3},{2,0},{3,1},{4,6},{5,7},{6,4},{7,5},{8,10},{9,11},{10,... | collective-permute-start | bytes 1572872 | tf_op jit(solution)/shard_map/ppermute | solution.py:383
  67.4 4.5 %copy-start.6 = (bf16[8,128,256]{2,1,0:T(8,128)(2,1)S(1)}, bf16[8,128,256]{2,1,0:T(8,128)(2,1)}, u32[]{:S(2)}) copy-start(bf16[8,128,256]{2,1,0:T(8,128)(2,1)} %copy-done.5) | copy-start | bytes 1572868
  67.5 4.4 %copy-start.8 = (bf16[8,128,256]{2,1,0:T(8,128)(2,1)S(1)}, bf16[8,128,256]{2,1,0:T(8,128)(2,1)}, u32[]{:S(2)}) copy-start(bf16[8,128,256]{2,1,0:T(8,128)(2,1)} %copy-done.7) | copy-start | bytes 1572868
  67.5 4.4 %copy-start.11 = (bf16[8,128,256]{2,1,0:T(8,128)(2,1)S(1)}, bf16[8,128,256]{2,1,0:T(8,128)(2,1)}, u32[]{:S(2)}) copy-start(bf16[8,128,256]{2,1,0:T(8,128)(2,1)} %copy-done.10) | copy-start | bytes 1572868
  67.5 4.4 %copy-start.13 = (bf16[8,128,256]{2,1,0:T(8,128)(2,1)S(1)}, bf16[8,128,256]{2,1,0:T(8,128)(2,1)}, u32[]{:S(2)}) copy-start(bf16[8,128,256]{2,1,0:T(8,128)(2,1)} %copy-done.12) | copy-start | bytes 1572868
  67.5 4.4 %copy-start.15 = (bf16[8,128,256]{2,1,0:T(8,128)(2,1)S(1)}, bf16[8,128,256]{2,1,0:T(8,128)(2,1)}, u32[]{:S(2)}) copy-start(bf16[8,128,256]{2,1,0:T(8,128)(2,1)} %copy-done.14) | copy-start | bytes 1572868
  67.5 9.3 %collective-permute-start.12 = (bf16[1,32,32,128]{3,2,1,0:T(8,128)(2,1)S(1)}, bf16[1,32,32,128]{3,2,1,0:T(8,128)(2,1)S(1)}, u32[]{:S(2)}, u32[]{:S(2)}) collective-permute-start(bf16[1,32,32,128]{3,2,1,0:T(8,128)(2,1)S(1)} %shard_map.82.refs_1_.near_ref), channel_id=1, source_target_pairs={{0,2},{1,3},{2,0},{3,1},{4,6},{5,7},{6,4},{7,5},{8,10},{9,11},{10,... | collective-permute-start | bytes 786440 | tf_op jit(solution)/shard_map/ppermute | solution.py:396
  69.4 13.0 %collective-permute-start.11 = (bf16[1,32,32,128]{3,2,1,0:T(8,128)(2,1)S(1)}, bf16[1,32,32,128]{3,2,1,0:T(8,128)(2,1)S(1)}, u32[]{:S(2)}, u32[]{:S(2)}) collective-permute-start(bf16[1,32,32,128]{3,2,1,0:T(8,128)(2,1)S(1)} %shard_map.83.refs_1_.near_ref), channel_id=1, source_target_pairs={{0,2},{1,3},{2,0},{3,1},{4,6},{5,7},{6,4},{7,5},{8,10},{9,11},{10,... | collective-permute-start | bytes 786440 | tf_op jit(solution)/shard_map/ppermute | solution.py:396
  70.3 17.7 %collective-permute-start.10 = (bf16[1,32,32,128]{3,2,1,0:T(8,128)(2,1)S(1)}, bf16[1,32,32,128]{3,2,1,0:T(8,128)(2,1)S(1)}, u32[]{:S(2)}, u32[]{:S(2)}) collective-permute-start(bf16[1,32,32,128]{3,2,1,0:T(8,128)(2,1)S(1)} %shard_map.84.refs_1_.near_ref), channel_id=1, source_target_pairs={{0,2},{1,3},{2,0},{3,1},{4,6},{5,7},{6,4},{7,5},{8,10},{9,11},{10,... | collective-permute-start | bytes 786440 | tf_op jit(solution)/shard_map/ppermute | solution.py:396
  73.5 20.2 %collective-permute-start.9 = (bf16[1,32,32,128]{3,2,1,0:T(8,128)(2,1)S(1)}, bf16[1,32,32,128]{3,2,1,0:T(8,128)(2,1)S(1)}, u32[]{:S(2)}, u32[]{:S(2)}) collective-permute-start(bf16[1,32,32,128]{3,2,1,0:T(8,128)(2,1)S(1)} %shard_map.85.refs_1_.near_ref), channel_id=1, source_target_pairs={{0,2},{1,3},{2,0},{3,1},{4,6},{5,7},{6,4},{7,5},{8,10},{9,11},{10,... | collective-permute-start | bytes 786440 | tf_op jit(solution)/shard_map/ppermute | solution.py:396
  74.4 24.9 %collective-permute-start.8 = (bf16[1,32,32,128]{3,2,1,0:T(8,128)(2,1)S(1)}, bf16[1,32,32,128]{3,2,1,0:T(8,128)(2,1)S(1)}, u32[]{:S(2)}, u32[]{:S(2)}) collective-permute-start(bf16[1,32,32,128]{3,2,1,0:T(8,128)(2,1)S(1)} %shard_map.86.refs_1_.near_ref), channel_id=1, source_target_pairs={{0,2},{1,3},{2,0},{3,1},{4,6},{5,7},{6,4},{7,5},{8,10},{9,11},{10,... | collective-permute-start | bytes 786440 | tf_op jit(solution)/shard_map/ppermute | solution.py:396
  77.7 21.6 %collective-permute-start.13 = (bf16[32,32,128]{2,1,0:T(8,128)(2,1)S(1)}, bf16[32,32,128]{2,1,0:T(8,128)(2,1)S(1)}, u32[]{:S(2)}, u32[]{:S(2)}) collective-permute-start(bf16[32,32,128]{2,1,0:T(8,128)(2,1)S(1)} %shard_map.89.refs_0_), channel_id=1, source_target_pairs={{0,28},{4,24},{8,20},{12,16},{16,12},{20,8},{24,4},{28,0},{1,29},{... | collective-permute-start | bytes 786440 | tf_op jit(solution)/shard_map/ppermute | solution.py:402
  82.4 22.5 %collective-permute-start.5 = (bf16[1,32,32,128]{3,2,1,0:T(8,128)(2,1)S(1)}, bf16[1,32,32,128]{3,2,1,0:T(8,128)(2,1)S(1)}, u32[]{:S(2)}, u32[]{:S(2)}) collective-permute-start(bf16[1,32,32,128]{3,2,1,0:T(8,128)(2,1)S(1)} %shard_map.87.near_ref.refs_1_), channel_id=1, source_target_pairs={{0,2},{1,3},{2,0},{3,1},{4,6},{5,7},{6,4},{7,5},{8,10},{9,11},{10,... | collective-permute-start | bytes 786440 | tf_op jit(solution)/shard_map/ppermute | solution.py:396
  88.0 18.4 %collective-permute-start.14 = (bf16[32,32,128]{2,1,0:T(8,128)(2,1)S(1)}, bf16[32,32,128]{2,1,0:T(8,128)(2,1)S(1)}, u32[]{:S(2)}, u32[]{:S(2)}) collective-permute-start(bf16[32,32,128]{2,1,0:T(8,128)(2,1)S(1)} %shard_map.90.refs_0_), channel_id=1, source_target_pairs={{0,24},{4,28},{8,16},{12,20},{16,8},{20,12},{24,0},{28,4},{1,25},{... | collective-permute-start | bytes 786440 | tf_op jit(solution)/shard_map/ppermute | solution.py:402
  93.7 16.9 %collective-permute-start.18 = (bf16[1,32,32,128]{3,2,1,0:T(8,128)(2,1)S(1)}, bf16[1,32,32,128]{3,2,1,0:T(8,128)(2,1)S(1)}, u32[]{:S(2)}, u32[]{:S(2)}) collective-permute-start(bf16[1,32,32,128]{3,2,1,0:T(8,128)(2,1)S(1)} %shard_map.96.refs_1_.near_ref), channel_id=1, source_target_pairs={{0,2},{1,3},{2,0},{3,1},{4,6},{5,7},{6,4},{7,5},{8,10},{9,11},{10,... | collective-permute-start | bytes 786440 | tf_op jit(solution)/shard_map/ppermute | solution.py:396
  99.3 13.4 %collective-permute-start.19 = (bf16[32,32,128]{2,1,0:T(8,128)(2,1)S(1)}, bf16[32,32,128]{2,1,0:T(8,128)(2,1)S(1)}, u32[]{:S(2)}, u32[]{:S(2)}) collective-permute-start(bf16[32,32,128]{2,1,0:T(8,128)(2,1)S(1)} %shard_map.91.refs_0_), channel_id=1, source_target_pairs={{0,8},{4,12},{8,0},{12,4},{16,24},{20,28},{24,16},{28,20},{1,9},{5... | collective-permute-start | bytes 786440 | tf_op jit(solution)/shard_map/ppermute | solution.py:402
  99.3 13.3 %collective-permute-start.20 = (bf16[32,32,128]{2,1,0:T(8,128)(2,1)S(1)}, bf16[32,32,128]{2,1,0:T(8,128)(2,1)S(1)}, u32[]{:S(2)}, u32[]{:S(2)}) collective-permute-start(bf16[32,32,128]{2,1,0:T(8,128)(2,1)S(1)} %shard_map.92.refs_0_), channel_id=1, source_target_pairs={{0,20},{4,16},{8,28},{12,24},{16,4},{20,0},{24,12},{28,8},{1,21},{... | collective-permute-start | bytes 786440 | tf_op jit(solution)/shard_map/ppermute | solution.py:402
  104.9 12.1 %collective-permute-start.17 = (bf16[1,32,32,128]{3,2,1,0:T(8,128)(2,1)S(1)}, bf16[1,32,32,128]{3,2,1,0:T(8,128)(2,1)S(1)}, u32[]{:S(2)}, u32[]{:S(2)}) collective-permute-start(bf16[1,32,32,128]{3,2,1,0:T(8,128)(2,1)S(1)} %shard_map.97.near_ref), channel_id=1, source_target_pairs={{0,2},{1,3},{2,0},{3,1},{4,6},{5,7},{6,4},{7,5},{8,10},{9,11},{10,... | collective-permute-start | bytes 786440 | tf_op jit(solution)/shard_map/ppermute | solution.py:396
  106.4 17.6 %collective-permute-start.16 = (bf16[32,32,128]{2,1,0:T(8,128)(2,1)S(1)}, bf16[32,32,128]{2,1,0:T(8,128)(2,1)S(1)}, u32[]{:S(2)}, u32[]{:S(2)}) collective-permute-start(bf16[32,32,128]{2,1,0:T(8,128)(2,1)S(1)} %shard_map.93.refs_0_), channel_id=1, source_target_pairs={{0,12},{4,8},{8,4},{12,0},{16,28},{20,24},{24,20},{28,16},{1,13},{... | collective-permute-start | bytes 786440 | tf_op jit(solution)/shard_map/ppermute | solution.py:402
  109.0 5.8 %copy-start.4 = (bf16[512,256]{1,0:T(8,128)(2,1)S(1)}, bf16[512,256]{1,0:T(8,128)(2,1)}, u32[]{:S(2)}) copy-start(bf16[512,256]{1,0:T(8,128)(2,1)} %orbitals.5) | copy-start | bytes 786436
  109.0 5.8 %copy-start.18 = (s32[512]{0:T(512)S(1)}, s32[512]{0:T(512)}, u32[]{:S(2)}) copy-start(s32[512]{0:T(512)} %row.1) | copy-start | bytes 6148
  109.0 5.8 %copy-start.19 = (s32[8]{0:T(128)S(1)}, s32[8]{0:T(128)}, u32[]{:S(2)}) copy-start(s32[8]{0:T(128)} %count.1) | copy-start | bytes 100
  110.5 13.5 %collective-permute-start.15 = (bf16[32,32,128]{2,1,0:T(8,128)(2,1)S(1)}, bf16[32,32,128]{2,1,0:T(8,128)(2,1)S(1)}, u32[]{:S(2)}, u32[]{:S(2)}) collective-permute-start(bf16[32,32,128]{2,1,0:T(8,128)(2,1)S(1)} %shard_map.94.refs_0_), channel_id=1, source_target_pairs={{0,16},{4,20},{8,24},{12,28},{16,0},{20,4},{24,8},{28,12},{1,17},{... | collective-permute-start | bytes 786440 | tf_op jit(solution)/shard_map/ppermute | solution.py:402
  113.6 10.4 %collective-permute-start.21 = (bf16[32,32,128]{2,1,0:T(8,128)(2,1)S(1)}, bf16[32,32,128]{2,1,0:T(8,128)(2,1)S(1)}, u32[]{:S(2)}, u32[]{:S(2)}) collective-permute-start(bf16[32,32,128]{2,1,0:T(8,128)(2,1)S(1)} %shard_map.98.refs_0_), channel_id=1, source_target_pairs={{0,4},{4,0},{8,12},{12,8},{16,20},{20,16},{24,28},{28,24},{1,5},{5... | collective-permute-start | bytes 786440 | tf_op jit(solution)/shard_map/ppermute | solution.py:402
  125.1 2.7 %collective-permute-start.22 = (bf16[32,64,256]{2,1,0:T(8,128)(2,1)S(1)}, bf16[32,64,256]{2,1,0:T(8,128)(2,1)S(1)}, u32[]{:S(2)}, u32[]{:S(2)}) collective-permute-start(bf16[32,64,256]{2,1,0:T(8,128)(2,1)S(1)} %get-tuple-element.30), channel_id=1, source_target_pairs={{0,1},{1,0},{2,3},{3,2},{4,5},{5,4},{6,7},{7,6},{8,9},{9,8},{10,11... | collective-permute-start | bytes 3145736 | tf_op jit(solution)/shard_map/ppermute | solution.py:407

commit v8 on v7

--- a/solution.py
+++ b/solution.py
@@ -316,7 +316,7 @@
         give[i] = jnp.where(core == 0, high, low)
         return carry
 
-    lax.fori_loop(0, occ, step, 0, unroll=16)
+    lax.fori_loop(0, occ, step, 0, unroll=32)
 
 
 def back_transform(rows, values):

time: 129 us -> 129 us (level)
  no operation moved by 1% of the time
where the time goes in v8:
time: 129 us
  waiting for transfers between devices  55.7 us (43%)
  starting transfers between devices  36.7 us (28%)
  Pallas kernels  31.9 us (25%)
  local copies, waits for them, and re-layouts  2.79 us (2%)
    ppermute x4, waiting for transfers between devices, shards(): parts += [here, lax.ppermute(there, 'ao', far)]  17.3 us
    all_to_all x1, waiting for transfers between devices, shards(): lax.all_to_all(sent, 'occ', split_axis=0, concat_axis=0, tiled=True)  15.1 us
    pallas_call x6, Pallas kernels, tile_call(): pl.pallas_call(body, out_shape=outs, in_specs=[first or whole, away] + [w...  14.3 us
    ppermute x8, waiting for transfers between devices, shards(): far_blocks.append(lax.ppermute(blocks_of[-1], 'ao', far))  13.7 us
    ppermute x7, starting transfers between devices, shards(): lax.ppermute(x, 'occ', [(o, o ^ k) for o in range(nodes)])  12.7 us
    ppermute x8, starting transfers between devices, shards(): far_blocks.append(lax.ppermute(blocks_of[-1], 'ao', far))  10.4 us
    pallas_call x11, Pallas kernels, call(): pl.pallas_call(body, out_shape=outs, in_specs=[whole] * len(ins) + [pl.Bl...  9.24 us
    all_to_all x1, starting transfers between devices, shards(): lax.all_to_all(sent, 'occ', split_axis=0, concat_axis=0, tiled=True)  7.22 us
  transfers between devices with their start and end apart: 24, of which 14 were waited for; matrix products, arithmetic and copies ran while one was open for 0% of the time, Pallas kernels for 23%

profile of v8, /device:TPU:0, one launch (start us, length us, event | category | flops | bytes accessed | tf_op | source)
XLA Modules:
  0.0 128.6 jit_solution(11045697093371322065)
XLA Ops:
  0.5 0.9 copy-done.2
  1.4 2.2 %shard_map.73 = (bf16[16,256,128]{2,1,0:T(8,128)(2,1)S(1)}, bf16[256,512]{1,0:T(8,128)(2,1)S(1)}, bf16[256,256]{1,0:T(8,128)(2,1)S(1)}) custom-call(bf16[512,256]{1,0:T(8,128)(2,1)S(1)} %copy-done.2, bf16[64,512,128]{2,1,0:T(8,128)(2,1)} %tiles.11), custom_call_target="tpu_custom_call" | custom-call | flops 1610612736 | bytes 4194304 | tf_op jit(solution)/shard_map/pallas_call | solution.py:245
  3.7 2.2 %shard_map.74.early = bf16[16,256,128]{2,1,0:T(8,128)(2,1)S(1)} custom-call(bf16[256,512]{1,0:T(8,128)(2,1)S(1)} %get-tuple-element.18.left_ref, bf16[64,512,128]{2,1,0:T(8,128)(2,1)} %tiles.11, bf16[16,256,128]{2,1,0:T(8,128)(2,1)S(1)} %get-tuple-element.19.rest_0_, bf16[32,64,256]{2,1,0:T(8,128)(2,1)S(1)} %collective-permute-done.rest_1_.other_ref), custom_call_target="tpu_custom_call" | custom-call | flops 536870912 | bytes 4194304 | tf_op jit(solution)/shard_map/pallas_call | solution.py:245
  6.4 1.9 %shard_map.75.rows_ref = bf16[256,256]{1,0:T(8,128)(2,1)S(1)} custom-call(s32[512]{0:T(512)S(1)} %bitcast.7, s32[512]{0:T(512)S(1)} %copy-done.17, bf16[512,256]{1,0:T(8,128)(2,1)S(1)} %copy-done.3, bf16[16,256,128]{2,1,0:T(8,128)(2,1)S(1)} %shard_map.74.early), custom_call_target="tpu_custom_call" | custom-call | flops 65536 | bytes 262144 | tf_op jit(solution)/shard_map/pallas_call | solution.py:91
  8.7 1.0 copy-done
  9.7 1.7 %shard_map.76.rest_0_ = bf16[8,32,32,128]{3,2,1,0:T(8,128)(2,1)} custom-call(bf16[256,256]{1,0:T(8,128)(2,1)S(1)} %shard_map.75.rows_ref, bf16[32,64,256]{2,1,0:T(8,128)(2,1)S(1)} %bitcast.6, bf16[32,64,256]{2,1,0:T(8,128)(2,1)S(1)} %collective-permute-done.rest_1_.other_ref, bf16[16,256,128]{2,1,0:T(8,128)(2,1)S(1)} %collective-permute-done.2.rest_0_.other, ...), custom_call_target="tpu_custom_call" | custom-call | flops 536870912 | bytes 2097152 | tf_op jit(solution)/shard_map/pallas_call | solution.py:127
  11.4 7.2 %all-to-all-start = ((bf16[8,32,32,128]{3,2,1,0:T(8,128)(2,1)}), bf16[8,32,32,128]{3,2,1,0:T(8,128)(2,1)S(1)}, u32[]{:S(2)}, u32[]{:S(2)}) async-start(bf16[8,32,32,128]{3,2,1,0:T(8,128)(2,1)} %shard_map.76.rest_0_), calls=%async_computation | async-start | bytes 4194304 | tf_op jit(solution)/shard_map/all_to_all | solution.py:371
  18.6 2.0 %shard_map.77 = (bf16[8,128,256]{2,1,0:T(8,128)(2,1)S(1)}, bf16[8,128,256]{2,1,0:T(8,128)(2,1)S(1)}) custom-call(bf16[256,512]{1,0:T(8,128)(2,1)S(1)} %get-tuple-element.18.left_ref, bf16[64,512,128]{2,1,0:T(8,128)(2,1)} %tiles.11, bf16[16,256,128]{2,1,0:T(8,128)(2,1)S(1)} %collective-permute-done.2.rest_0_.other, ...), custom_call_target="tpu_custom_call" | custom-call | flops 201326592 | bytes 2097152 | tf_op jit(solution)/shard_map/pallas_call | solution.py:245
  21.4 1.5 %collective-permute-start.3 = (bf16[8,128,256]{2,1,0:T(8,128)(2,1)S(1)}, bf16[8,128,256]{2,1,0:T(8,128)(2,1)S(1)}, u32[]{:S(2)}, u32[]{:S(2)}) collective-permute-start(bf16[8,128,256]{2,1,0:T(8,128)(2,1)S(1)} %get-tuple-element.21.rest_0_), channel_id=1, source_target_pairs={{0,2},{1,3},{2,0},{3,1},{4,6},{5,7},{6,4},{7,5},{8,10},{9,11},{10,... | collective-permute-start | bytes 1572872 | tf_op jit(solution)/shard_map/ppermute | solution.py:383
  22.9 2.0 %shard_map.78 = (bf16[8,128,256]{2,1,0:T(8,128)(2,1)S(1)}, bf16[8,128,256]{2,1,0:T(8,128)(2,1)S(1)}) custom-call(bf16[256,512]{1,0:T(8,128)(2,1)S(1)} %get-tuple-element.18.left_ref, bf16[64,512,128]{2,1,0:T(8,128)(2,1)} %tiles.11, bf16[16,256,128]{2,1,0:T(8,128)(2,1)S(1)} %collective-permute-done.2.rest_0_.other, ...), custom_call_target="tpu_custom_call" | custom-call | flops 201326592 | bytes 2097152 | tf_op jit(solution)/shard_map/pallas_call | solution.py:245
  25.5 10.7 %collective-permute-done.3.rest_1_.refs_1_ = bf16[8,128,256]{2,1,0:T(8,128)(2,1)S(1)} collective-permute-done((bf16[8,128,256]{2,1,0:T(8,128)(2,1)S(1)}, bf16[8,128,256]{2,1,0:T(8,128)(2,1)S(1)}, u32[]{:S(2)}, u32[]{:S(2)}) %collective-permute-start.3) | collective-permute-done | bytes 524320 | tf_op jit(solution)/shard_map/ppermute | solution.py:383
  36.2 3.0 %shard_map.79 = (bf16[8,128,256]{2,1,0:T(8,128)(2,1)S(1)}, bf16[8,128,256]{2,1,0:T(8,128)(2,1)}) custom-call(bf16[256,512]{1,0:T(8,128)(2,1)S(1)} %get-tuple-element.18.left_ref, bf16[64,512,128]{2,1,0:T(8,128)(2,1)} %tiles.11, bf16[16,256,128]{2,1,0:T(8,128)(2,1)S(1)} %copy-done.1, bf16[256,256]{1,0:T(8,128)(2,1)S(1)} %get-tuple-element.20.right_ref, ...), custom_call_target="tpu_custom_call" | custom-call | flops 201326592 | bytes 2097152 | tf_op jit(solution)/shard_map/pallas_call | solution.py:245
  39.2 1.5 %collective-permute-start.6 = (bf16[8,128,256]{2,1,0:T(8,128)(2,1)}, bf16[8,128,256]{2,1,0:T(8,128)(2,1)}, u32[]{:S(2)}, u32[]{:S(2)}) collective-permute-start(bf16[8,128,256]{2,1,0:T(8,128)(2,1)} %get-tuple-element.23.rest_0_), channel_id=1, source_target_pairs={{0,2},{1,3},{2,0},{3,1},{4,6},{5,7},{6,4},{7,5},{8,10},{9,11},{10,... | collective-permute-start | bytes 1572872 | tf_op jit(solution)/shard_map/ppermute | solution.py:383
  40.8 6.6 %collective-permute-done.4.rest_1_.refs_3_ = bf16[8,128,256]{2,1,0:T(8,128)(2,1)S(1)} collective-permute-done((bf16[8,128,256]{2,1,0:T(8,128)(2,1)S(1)}, bf16[8,128,256]{2,1,0:T(8,128)(2,1)S(1)}, u32[]{:S(2)}, u32[]{:S(2)}) %collective-permute-start.4) | collective-permute-done | bytes 524320 | tf_op jit(solution)/shard_map/ppermute | solution.py:383
  47.4 3.0 %shard_map.80 = (bf16[8,128,256]{2,1,0:T(8,128)(2,1)S(1)}, bf16[8,128,256]{2,1,0:T(8,128)(2,1)}) custom-call(bf16[256,512]{1,0:T(8,128)(2,1)S(1)} %get-tuple-element.18.left_ref, bf16[64,512,128]{2,1,0:T(8,128)(2,1)} %tiles.11, bf16[16,256,128]{2,1,0:T(8,128)(2,1)S(1)} %copy-done.1, bf16[256,256]{1,0:T(8,128)(2,1)S(1)} %get-tuple-element.20.right_ref, ...), custom_call_target="tpu_custom_call" | custom-call | flops 201326592 | bytes 2097152 | tf_op jit(solution)/shard_map/pallas_call | solution.py:245
  50.5 1.6 %collective-permute-start.7 = (bf16[8,128,256]{2,1,0:T(8,128)(2,1)}, bf16[8,128,256]{2,1,0:T(8,128)(2,1)S(1)}, u32[]{:S(2)}, u32[]{:S(2)}) collective-permute-start(bf16[8,128,256]{2,1,0:T(8,128)(2,1)} %get-tuple-element.24.early), channel_id=1, source_target_pairs={{0,2},{1,3},{2,0},{3,1},{4,6},{5,7},{6,4},{7,5},{8,10},{9,11},{10,... | collective-permute-start | bytes 1572872 | tf_op jit(solution)/shard_map/ppermute | solution.py:383
  52.0 15.1 %all-to-all-done.refs_0_ = bf16[8,32,32,128]{3,2,1,0:T(8,128)(2,1)S(1)} async-done(((bf16[8,32,32,128]{3,2,1,0:T(8,128)(2,1)}), bf16[8,32,32,128]{3,2,1,0:T(8,128)(2,1)S(1)}, u32[]{:S(2)}, u32[]{:S(2)}) %all-to-all-start) | async-done | bytes 2097184 | tf_op jit(solution)/shard_map/all_to_all | solution.py:371
  67.5 1.6 %collective-permute-start.12 = (bf16[1,32,32,128]{3,2,1,0:T(8,128)(2,1)S(1)}, bf16[1,32,32,128]{3,2,1,0:T(8,128)(2,1)S(1)}, u32[]{:S(2)}, u32[]{:S(2)}) collective-permute-start(bf16[1,32,32,128]{3,2,1,0:T(8,128)(2,1)S(1)} %shard_map.82.refs_1_.near_ref), channel_id=1, source_target_pairs={{0,2},{1,3},{2,0},{3,1},{4,6},{5,7},{6,4},{7,5},{8,10},{9,11},{10,... | collective-permute-start | bytes 786440 | tf_op jit(solution)/shard_map/ppermute | solution.py:396
  70.3 1.6 %collective-permute-start.10 = (bf16[1,32,32,128]{3,2,1,0:T(8,128)(2,1)S(1)}, bf16[1,32,32,128]{3,2,1,0:T(8,128)(2,1)S(1)}, u32[]{:S(2)}, u32[]{:S(2)}) collective-permute-start(bf16[1,32,32,128]{3,2,1,0:T(8,128)(2,1)S(1)} %shard_map.84.refs_1_.near_ref), channel_id=1, source_target_pairs={{0,2},{1,3},{2,0},{3,1},{4,6},{5,7},{6,4},{7,5},{8,10},{9,11},{10,... | collective-permute-start | bytes 786440 | tf_op jit(solution)/shard_map/ppermute | solution.py:396
  71.9 1.2 shard_map.88.dressed
  74.4 1.6 %collective-permute-start.8 = (bf16[1,32,32,128]{3,2,1,0:T(8,128)(2,1)S(1)}, bf16[1,32,32,128]{3,2,1,0:T(8,128)(2,1)S(1)}, u32[]{:S(2)}, u32[]{:S(2)}) collective-permute-start(bf16[1,32,32,128]{3,2,1,0:T(8,128)(2,1)S(1)} %shard_map.86.refs_1_.near_ref), channel_id=1, source_target_pairs={{0,2},{1,3},{2,0},{3,1},{4,6},{5,7},{6,4},{7,5},{8,10},{9,11},{10,... | collective-permute-start | bytes 786440 | tf_op jit(solution)/shard_map/ppermute | solution.py:396
  76.8 0.9 shard_map.89.refs_0_
  77.7 2.7 %collective-permute-start.13 = (bf16[32,32,128]{2,1,0:T(8,128)(2,1)S(1)}, bf16[32,32,128]{2,1,0:T(8,128)(2,1)S(1)}, u32[]{:S(2)}, u32[]{:S(2)}) collective-permute-start(bf16[32,32,128]{2,1,0:T(8,128)(2,1)S(1)} %shard_map.89.refs_0_), channel_id=1, source_target_pairs={{0,28},{4,24},{8,20},{12,16},{16,12},{20,8},{24,4},{28,0},{1,29},{... | collective-permute-start | bytes 786440 | tf_op jit(solution)/shard_map/ppermute | solution.py:402
  81.1 1.3 %collective-permute-done.11.far_ref = bf16[1,32,32,128]{3,2,1,0:T(8,128)(2,1)S(1)} collective-permute-done((bf16[1,32,32,128]{3,2,1,0:T(8,128)(2,1)S(1)}, bf16[1,32,32,128]{3,2,1,0:T(8,128)(2,1)S(1)}, u32[]{:S(2)}, u32[]{:S(2)}) %collective-permute-start.11) | collective-permute-done | bytes 262176 | tf_op jit(solution)/shard_map/ppermute | solution.py:396
  82.4 1.5 %collective-permute-start.5 = (bf16[1,32,32,128]{3,2,1,0:T(8,128)(2,1)S(1)}, bf16[1,32,32,128]{3,2,1,0:T(8,128)(2,1)S(1)}, u32[]{:S(2)}, u32[]{:S(2)}) collective-permute-start(bf16[1,32,32,128]{3,2,1,0:T(8,128)(2,1)S(1)} %shard_map.87.near_ref.refs_1_), channel_id=1, source_target_pairs={{0,2},{1,3},{2,0},{3,1},{4,6},{5,7},{6,4},{7,5},{8,10},{9,11},{10,... | collective-permute-start | bytes 786440 | tf_op jit(solution)/shard_map/ppermute | solution.py:396
  83.9 0.9 shard_map.90.refs_0_
  84.8 3.2 %collective-permute-done.10.far_ref = bf16[1,32,32,128]{3,2,1,0:T(8,128)(2,1)S(1)} collective-permute-done((bf16[1,32,32,128]{3,2,1,0:T(8,128)(2,1)S(1)}, bf16[1,32,32,128]{3,2,1,0:T(8,128)(2,1)S(1)}, u32[]{:S(2)}, u32[]{:S(2)}) %collective-permute-start.10) | collective-permute-done | bytes 262176 | tf_op jit(solution)/shard_map/ppermute | solution.py:396
  88.0 2.2 %collective-permute-start.14 = (bf16[32,32,128]{2,1,0:T(8,128)(2,1)S(1)}, bf16[32,32,128]{2,1,0:T(8,128)(2,1)S(1)}, u32[]{:S(2)}, u32[]{:S(2)}) collective-permute-start(bf16[32,32,128]{2,1,0:T(8,128)(2,1)S(1)} %shard_map.90.refs_0_), channel_id=1, source_target_pairs={{0,24},{4,28},{8,16},{12,20},{16,8},{20,12},{24,0},{28,4},{1,25},{... | collective-permute-start | bytes 786440 | tf_op jit(solution)/shard_map/ppermute | solution.py:402
  90.2 0.9 shard_map.91.refs_0_
  91.2 2.5 %collective-permute-done.9.far_ref = bf16[1,32,32,128]{3,2,1,0:T(8,128)(2,1)S(1)} collective-permute-done((bf16[1,32,32,128]{3,2,1,0:T(8,128)(2,1)S(1)}, bf16[1,32,32,128]{3,2,1,0:T(8,128)(2,1)S(1)}, u32[]{:S(2)}, u32[]{:S(2)}) %collective-permute-start.9) | collective-permute-done | bytes 262176 | tf_op jit(solution)/shard_map/ppermute | solution.py:396
  93.7 1.5 %collective-permute-start.18 = (bf16[1,32,32,128]{3,2,1,0:T(8,128)(2,1)S(1)}, bf16[1,32,32,128]{3,2,1,0:T(8,128)(2,1)S(1)}, u32[]{:S(2)}, u32[]{:S(2)}) collective-permute-start(bf16[1,32,32,128]{3,2,1,0:T(8,128)(2,1)S(1)} %shard_map.96.refs_1_.near_ref), channel_id=1, source_target_pairs={{0,2},{1,3},{2,0},{3,1},{4,6},{5,7},{6,4},{7,5},{8,10},{9,11},{10,... | collective-permute-start | bytes 786440 | tf_op jit(solution)/shard_map/ppermute | solution.py:396
  95.2 0.9 shard_map.92.refs_0_
  96.1 3.2 %collective-permute-done.8.far_ref = bf16[1,32,32,128]{3,2,1,0:T(8,128)(2,1)S(1)} collective-permute-done((bf16[1,32,32,128]{3,2,1,0:T(8,128)(2,1)S(1)}, bf16[1,32,32,128]{3,2,1,0:T(8,128)(2,1)S(1)}, u32[]{:S(2)}, u32[]{:S(2)}) %collective-permute-start.8) | collective-permute-done | bytes 262176 | tf_op jit(solution)/shard_map/ppermute | solution.py:396
  99.3 3.2 %collective-permute-start.20 = (bf16[32,32,128]{2,1,0:T(8,128)(2,1)S(1)}, bf16[32,32,128]{2,1,0:T(8,128)(2,1)S(1)}, u32[]{:S(2)}, u32[]{:S(2)}) collective-permute-start(bf16[32,32,128]{2,1,0:T(8,128)(2,1)S(1)} %shard_map.92.refs_0_), channel_id=1, source_target_pairs={{0,20},{4,16},{8,28},{12,24},{16,4},{20,0},{24,12},{28,8},{1,21},{... | collective-permute-start | bytes 786440 | tf_op jit(solution)/shard_map/ppermute | solution.py:402
  102.8 0.9 shard_map.93.refs_0_
  103.8 1.1 collective-permute-done.5.far_ref
  104.9 1.5 %collective-permute-start.17 = (bf16[1,32,32,128]{3,2,1,0:T(8,128)(2,1)S(1)}, bf16[1,32,32,128]{3,2,1,0:T(8,128)(2,1)S(1)}, u32[]{:S(2)}, u32[]{:S(2)}) collective-permute-start(bf16[1,32,32,128]{3,2,1,0:T(8,128)(2,1)S(1)} %shard_map.97.near_ref), channel_id=1, source_target_pairs={{0,2},{1,3},{2,0},{3,1},{4,6},{5,7},{6,4},{7,5},{8,10},{9,11},{10,... | collective-permute-start | bytes 786440 | tf_op jit(solution)/shard_map/ppermute | solution.py:396
  106.4 1.7 %collective-permute-start.16 = (bf16[32,32,128]{2,1,0:T(8,128)(2,1)S(1)}, bf16[32,32,128]{2,1,0:T(8,128)(2,1)S(1)}, u32[]{:S(2)}, u32[]{:S(2)}) collective-permute-start(bf16[32,32,128]{2,1,0:T(8,128)(2,1)S(1)} %shard_map.93.refs_0_), channel_id=1, source_target_pairs={{0,12},{4,8},{8,4},{12,0},{16,28},{20,24},{24,20},{28,16},{1,13},{... | collective-permute-start | bytes 786440 | tf_op jit(solution)/shard_map/ppermute | solution.py:402
  108.1 0.9 shard_map.94.refs_0_
  109.0 1.5 %collective-permute-done.18.far_ref = bf16[1,32,32,128]{3,2,1,0:T(8,128)(2,1)S(1)} collective-permute-done((bf16[1,32,32,128]{3,2,1,0:T(8,128)(2,1)S(1)}, bf16[1,32,32,128]{3,2,1,0:T(8,128)(2,1)S(1)}, u32[]{:S(2)}, u32[]{:S(2)}) %collective-permute-start.18) | collective-permute-done | bytes 262176 | tf_op jit(solution)/shard_map/ppermute | solution.py:396
  110.5 1.7 %collective-permute-start.15 = (bf16[32,32,128]{2,1,0:T(8,128)(2,1)S(1)}, bf16[32,32,128]{2,1,0:T(8,128)(2,1)S(1)}, u32[]{:S(2)}, u32[]{:S(2)}) collective-permute-start(bf16[32,32,128]{2,1,0:T(8,128)(2,1)S(1)} %shard_map.94.refs_0_), channel_id=1, source_target_pairs={{0,16},{4,20},{8,24},{12,28},{16,0},{20,4},{24,8},{28,12},{1,17},{... | collective-permute-start | bytes 786440 | tf_op jit(solution)/shard_map/ppermute | solution.py:402
  112.7 0.9 shard_map.98.refs_0_
  113.6 1.2 collective-permute-start.21
  114.8 2.1 %shard_map.81.rows = bf16[256,256]{1,0:T(8,128)(2,1)S(1)} custom-call(s32[512]{0:T(512)S(1)} %copy-done.18, s32[8]{0:T(128)S(1)} %copy-done.19, bf16[512,256]{1,0:T(8,128)(2,1)S(1)} %copy-done.4, bf16[8,128,256]{2,1,0:T(8,128)(2,1)} %get-tuple-element.24.early), custom_call_target="tpu_custom_call" | custom-call | flops 65536 | bytes 262144 | tf_op jit(solution)/shard_map/pallas_call | solution.py:91
  117.0 0.9 shard_map.99.refs_0_
  117.9 6.1 %collective-permute-done.15.rest_0_.refs_4_ = bf16[32,32,128]{2,1,0:T(8,128)(2,1)S(1)} collective-permute-done((bf16[32,32,128]{2,1,0:T(8,128)(2,1)S(1)}, bf16[32,32,128]{2,1,0:T(8,128)(2,1)S(1)}, u32[]{:S(2)}, u32[]{:S(2)}) %collective-permute-start.15) | collective-permute-done | bytes 262176 | tf_op jit(solution)/shard_map/ppermute | solution.py:402
  124.9 2.6 %collective-permute-done.22 = bf16[32,64,256]{2,1,0:T(8,128)(2,1)S(1)} collective-permute-done((bf16[32,64,256]{2,1,0:T(8,128)(2,1)S(1)}, bf16[32,64,256]{2,1,0:T(8,128)(2,1)S(1)}, u32[]{:S(2)}, u32[]{:S(2)}) %collective-permute-start.22) | collective-permute-done | bytes 1048608 | tf_op jit(solution)/shard_map/ppermute | solution.py:407
  127.5 1.1 add_bitcast_fusion
  (69 shorter events, 9.0 us)
Async XLA Ops:
  0.0 3.7 %collective-permute-start = (bf16[32,64,256]{2,1,0:T(8,128)(2,1)}, bf16[32,64,256]{2,1,0:T(8,128)(2,1)S(1)}, u32[]{:S(2)}, u32[]{:S(2)}) collective-permute-start(bf16[32,64,256]{2,1,0:T(8,128)(2,1)} %bitcast.5), channel_id=1, source_target_pairs={{0,1},{1,0},{2,3},{3,2},{4,5},{5,4},{6,7},{7,6},{8,9},{9,8},{10,11... | collective-permute-start | bytes 3145736 | tf_op jit(solution)/shard_map/ppermute | solution.py:347
  0.5 0.9 copy-start.2
  3.6 4.8 %collective-permute-start.2 = (bf16[16,256,128]{2,1,0:T(8,128)(2,1)S(1)}, bf16[16,256,128]{2,1,0:T(8,128)(2,1)S(1)}, u32[]{:S(2)}, u32[]{:S(2)}) collective-permute-start(bf16[16,256,128]{2,1,0:T(8,128)(2,1)S(1)} %get-tuple-element.19.rest_0_), channel_id=1, source_target_pairs={{0,1},{1,0},{2,3},{3,2},{4,5},{5,4},{6,7},{7,6},{8,9},{9,8},{10,11... | collective-permute-start | bytes 3145736 | tf_op jit(solution)/shard_map/ppermute | solution.py:367
  3.7 2.7 %copy-start.3 = (bf16[512,256]{1,0:T(8,128)(2,1)S(1)}, bf16[512,256]{1,0:T(8,128)(2,1)}, u32[]{:S(2)}) copy-start(bf16[512,256]{1,0:T(8,128)(2,1)} %orbitals.5) | copy-start | bytes 786436
  3.7 2.7 %copy-start.16 = (s32[512,1]{0,1:T(1,128)S(1)}, s32[512,1]{0,1:T(1,128)}, u32[]{:S(2)}) copy-start(s32[512,1]{0,1:T(1,128)} %param.12) | copy-start | bytes 6148
  3.7 2.7 %copy-start.17 = (s32[512]{0:T(512)S(1)}, s32[512]{0:T(512)}, u32[]{:S(2)}) copy-start(s32[512]{0:T(512)} %sub.1) | copy-start | bytes 6148
  5.9 3.8 %copy-start.9 = (bf16[32,256,64]{1,2,0:T(8,128)(2,1)S(1)}, bf16[32,256,64]{1,2,0:T(8,128)(2,1)}, u32[]{:S(2)}) copy-start(bf16[32,256,64]{1,2,0:T(8,128)(2,1)} %param.7) | copy-start | bytes 3145732
  5.9 2.8 %collective-permute-start.1 = (bf16[16,256,128]{2,1,0:T(8,128)(2,1)S(1)}, bf16[16,256,128]{2,1,0:T(8,128)(2,1)S(1)}, u32[]{:S(2)}, u32[]{:S(2)}) collective-permute-start(bf16[16,256,128]{2,1,0:T(8,128)(2,1)S(1)} %shard_map.74.early), channel_id=1, source_target_pairs={{0,1},{1,0},{2,3},{3,2},{4,5},{5,4},{6,7},{7,6},{8,9},{9,8},{10,11... | collective-permute-start | bytes 3145736 | tf_op jit(solution)/shard_map/ppermute | solution.py:355
  8.7 1.0 copy-start
  11.4 55.8 %all-to-all-start = ((bf16[8,32,32,128]{3,2,1,0:T(8,128)(2,1)}), bf16[8,32,32,128]{3,2,1,0:T(8,128)(2,1)S(1)}, u32[]{:S(2)}, u32[]{:S(2)}) async-start(bf16[8,32,32,128]{3,2,1,0:T(8,128)(2,1)} %shard_map.76.rest_0_), calls=%async_computation | async-start | bytes 4194304 | tf_op jit(solution)/shard_map/all_to_all | solution.py:371
  20.6 0.8 copy-start.10
  21.4 14.8 %copy-start.1 = (bf16[16,256,128]{2,1,0:T(8,128)(2,1)S(1)}, bf16[16,256,128]{2,1,0:T(8,128)(2,1)}, u32[]{:S(2)}) copy-start(bf16[16,256,128]{2,1,0:T(8,128)(2,1)} %copy-done) | copy-start | bytes 3145732
  21.4 14.8 %collective-permute-start.3 = (bf16[8,128,256]{2,1,0:T(8,128)(2,1)S(1)}, bf16[8,128,256]{2,1,0:T(8,128)(2,1)S(1)}, u32[]{:S(2)}, u32[]{:S(2)}) collective-permute-start(bf16[8,128,256]{2,1,0:T(8,128)(2,1)S(1)} %get-tuple-element.21.rest_0_), channel_id=1, source_target_pairs={{0,2},{1,3},{2,0},{3,1},{4,6},{5,7},{6,4},{7,5},{8,10},{9,11},{10,... | collective-permute-start | bytes 1572872 | tf_op jit(solution)/shard_map/ppermute | solution.py:383
  24.9 14.3 %copy-start.12 = (bf16[8,128,256]{2,1,0:T(8,128)(2,1)}, bf16[8,128,256]{2,1,0:T(8,128)(2,1)S(1)}, u32[]{:S(2)}) copy-start(bf16[8,128,256]{2,1,0:T(8,128)(2,1)S(1)} %get-tuple-element.26.refs_2_) | copy-start | bytes 1572868
  24.9 22.5 %collective-permute-start.4 = (bf16[8,128,256]{2,1,0:T(8,128)(2,1)S(1)}, bf16[8,128,256]{2,1,0:T(8,128)(2,1)S(1)}, u32[]{:S(2)}, u32[]{:S(2)}) collective-permute-start(bf16[8,128,256]{2,1,0:T(8,128)(2,1)S(1)} %get-tuple-element.22.rest_0_), channel_id=1, source_target_pairs={{0,2},{1,3},{2,0},{3,1},{4,6},{5,7},{6,4},{7,5},{8,10},{9,11},{10,... | collective-permute-start | bytes 1572872 | tf_op jit(solution)/shard_map/ppermute | solution.py:383
  36.2 3.0 %copy-start.5 = (bf16[8,128,256]{2,1,0:T(8,128)(2,1)}, bf16[8,128,256]{2,1,0:T(8,128)(2,1)S(1)}, u32[]{:S(2)}) copy-start(bf16[8,128,256]{2,1,0:T(8,128)(2,1)S(1)} %collective-permute-done.3.rest_1_.refs_1_) | copy-start | bytes 1572868
  39.2 11.2 %copy-start.14 = (bf16[8,128,256]{2,1,0:T(8,128)(2,1)}, bf16[8,128,256]{2,1,0:T(8,128)(2,1)S(1)}, u32[]{:S(2)}) copy-start(bf16[8,128,256]{2,1,0:T(8,128)(2,1)S(1)} %get-tuple-element.27.refs_4_) | copy-start | bytes 1572868
  39.2 32.6 %collective-permute-start.6 = (bf16[8,128,256]{2,1,0:T(8,128)(2,1)}, bf16[8,128,256]{2,1,0:T(8,128)(2,1)}, u32[]{:S(2)}, u32[]{:S(2)}) collective-permute-start(bf16[8,128,256]{2,1,0:T(8,128)(2,1)} %get-tuple-element.23.rest_0_), channel_id=1, source_target_pairs={{0,2},{1,3},{2,0},{3,1},{4,6},{5,7},{6,4},{7,5},{8,10},{9,11},{10,... | collective-permute-start | bytes 1572872 | tf_op jit(solution)/shard_map/ppermute | solution.py:383
  47.4 3.0 %copy-start.7 = (bf16[8,128,256]{2,1,0:T(8,128)(2,1)}, bf16[8,128,256]{2,1,0:T(8,128)(2,1)S(1)}, u32[]{:S(2)}) copy-start(bf16[8,128,256]{2,1,0:T(8,128)(2,1)S(1)} %collective-permute-done.4.rest_1_.refs_3_) | copy-start | bytes 1572868
  50.5 23.9 %collective-permute-start.7 = (bf16[8,128,256]{2,1,0:T(8,128)(2,1)}, bf16[8,128,256]{2,1,0:T(8,128)(2,1)S(1)}, u32[]{:S(2)}, u32[]{:S(2)}) collective-permute-start(bf16[8,128,256]{2,1,0:T(8,128)(2,1)} %get-tuple-element.24.early), channel_id=1, source_target_pairs={{0,2},{1,3},{2,0},{3,1},{4,6},{5,7},{6,4},{7,5},{8,10},{9,11},{10,... | collective-permute-start | bytes 1572872 | tf_op jit(solution)/shard_map/ppermute | solution.py:383
  67.4 4.5 %copy-start.6 = (bf16[8,128,256]{2,1,0:T(8,128)(2,1)S(1)}, bf16[8,128,256]{2,1,0:T(8,128)(2,1)}, u32[]{:S(2)}) copy-start(bf16[8,128,256]{2,1,0:T(8,128)(2,1)} %copy-done.5) | copy-start | bytes 1572868
  67.5 4.4 %copy-start.8 = (bf16[8,128,256]{2,1,0:T(8,128)(2,1)S(1)}, bf16[8,128,256]{2,1,0:T(8,128)(2,1)}, u32[]{:S(2)}) copy-start(bf16[8,128,256]{2,1,0:T(8,128)(2,1)} %copy-done.7) | copy-start | bytes 1572868
  67.5 4.4 %copy-start.11 = (bf16[8,128,256]{2,1,0:T(8,128)(2,1)S(1)}, bf16[8,128,256]{2,1,0:T(8,128)(2,1)}, u32[]{:S(2)}) copy-start(bf16[8,128,256]{2,1,0:T(8,128)(2,1)} %copy-done.10) | copy-start | bytes 1572868
  67.5 4.4 %copy-start.13 = (bf16[8,128,256]{2,1,0:T(8,128)(2,1)S(1)}, bf16[8,128,256]{2,1,0:T(8,128)(2,1)}, u32[]{:S(2)}) copy-start(bf16[8,128,256]{2,1,0:T(8,128)(2,1)} %copy-done.12) | copy-start | bytes 1572868
  67.5 4.4 %copy-start.15 = (bf16[8,128,256]{2,1,0:T(8,128)(2,1)S(1)}, bf16[8,128,256]{2,1,0:T(8,128)(2,1)}, u32[]{:S(2)}) copy-start(bf16[8,128,256]{2,1,0:T(8,128)(2,1)} %copy-done.14) | copy-start | bytes 1572868
  67.5 9.3 %collective-permute-start.12 = (bf16[1,32,32,128]{3,2,1,0:T(8,128)(2,1)S(1)}, bf16[1,32,32,128]{3,2,1,0:T(8,128)(2,1)S(1)}, u32[]{:S(2)}, u32[]{:S(2)}) collective-permute-start(bf16[1,32,32,128]{3,2,1,0:T(8,128)(2,1)S(1)} %shard_map.82.refs_1_.near_ref), channel_id=1, source_target_pairs={{0,2},{1,3},{2,0},{3,1},{4,6},{5,7},{6,4},{7,5},{8,10},{9,11},{10,... | collective-permute-start | bytes 786440 | tf_op jit(solution)/shard_map/ppermute | solution.py:396
  69.4 13.0 %collective-permute-start.11 = (bf16[1,32,32,128]{3,2,1,0:T(8,128)(2,1)S(1)}, bf16[1,32,32,128]{3,2,1,0:T(8,128)(2,1)S(1)}, u32[]{:S(2)}, u32[]{:S(2)}) collective-permute-start(bf16[1,32,32,128]{3,2,1,0:T(8,128)(2,1)S(1)} %shard_map.83.refs_1_.near_ref), channel_id=1, source_target_pairs={{0,2},{1,3},{2,0},{3,1},{4,6},{5,7},{6,4},{7,5},{8,10},{9,11},{10,... | collective-permute-start | bytes 786440 | tf_op jit(solution)/shard_map/ppermute | solution.py:396
  70.3 17.7 %collective-permute-start.10 = (bf16[1,32,32,128]{3,2,1,0:T(8,128)(2,1)S(1)}, bf16[1,32,32,128]{3,2,1,0:T(8,128)(2,1)S(1)}, u32[]{:S(2)}, u32[]{:S(2)}) collective-permute-start(bf16[1,32,32,128]{3,2,1,0:T(8,128)(2,1)S(1)} %shard_map.84.refs_1_.near_ref), channel_id=1, source_target_pairs={{0,2},{1,3},{2,0},{3,1},{4,6},{5,7},{6,4},{7,5},{8,10},{9,11},{10,... | collective-permute-start | bytes 786440 | tf_op jit(solution)/shard_map/ppermute | solution.py:396
  73.5 20.2 %collective-permute-start.9 = (bf16[1,32,32,128]{3,2,1,0:T(8,128)(2,1)S(1)}, bf16[1,32,32,128]{3,2,1,0:T(8,128)(2,1)S(1)}, u32[]{:S(2)}, u32[]{:S(2)}) collective-permute-start(bf16[1,32,32,128]{3,2,1,0:T(8,128)(2,1)S(1)} %shard_map.85.refs_1_.near_ref), channel_id=1, source_target_pairs={{0,2},{1,3},{2,0},{3,1},{4,6},{5,7},{6,4},{7,5},{8,10},{9,11},{10,... | collective-permute-start | bytes 786440 | tf_op jit(solution)/shard_map/ppermute | solution.py:396
  74.4 24.9 %collective-permute-start.8 = (bf16[1,32,32,128]{3,2,1,0:T(8,128)(2,1)S(1)}, bf16[1,32,32,128]{3,2,1,0:T(8,128)(2,1)S(1)}, u32[]{:S(2)}, u32[]{:S(2)}) collective-permute-start(bf16[1,32,32,128]{3,2,1,0:T(8,128)(2,1)S(1)} %shard_map.86.refs_1_.near_ref), channel_id=1, source_target_pairs={{0,2},{1,3},{2,0},{3,1},{4,6},{5,7},{6,4},{7,5},{8,10},{9,11},{10,... | collective-permute-start | bytes 786440 | tf_op jit(solution)/shard_map/ppermute | solution.py:396
  77.7 21.6 %collective-permute-start.13 = (bf16[32,32,128]{2,1,0:T(8,128)(2,1)S(1)}, bf16[32,32,128]{2,1,0:T(8,128)(2,1)S(1)}, u32[]{:S(2)}, u32[]{:S(2)}) collective-permute-start(bf16[32,32,128]{2,1,0:T(8,128)(2,1)S(1)} %shard_map.89.refs_0_), channel_id=1, source_target_pairs={{0,28},{4,24},{8,20},{12,16},{16,12},{20,8},{24,4},{28,0},{1,29},{... | collective-permute-start | bytes 786440 | tf_op jit(solution)/shard_map/ppermute | solution.py:402
  82.4 22.5 %collective-permute-start.5 = (bf16[1,32,32,128]{3,2,1,0:T(8,128)(2,1)S(1)}, bf16[1,32,32,128]{3,2,1,0:T(8,128)(2,1)S(1)}, u32[]{:S(2)}, u32[]{:S(2)}) collective-permute-start(bf16[1,32,32,128]{3,2,1,0:T(8,128)(2,1)S(1)} %shard_map.87.near_ref.refs_1_), channel_id=1, source_target_pairs={{0,2},{1,3},{2,0},{3,1},{4,6},{5,7},{6,4},{7,5},{8,10},{9,11},{10,... | collective-permute-start | bytes 786440 | tf_op jit(solution)/shard_map/ppermute | solution.py:396
  88.0 18.4 %collective-permute-start.14 = (bf16[32,32,128]{2,1,0:T(8,128)(2,1)S(1)}, bf16[32,32,128]{2,1,0:T(8,128)(2,1)S(1)}, u32[]{:S(2)}, u32[]{:S(2)}) collective-permute-start(bf16[32,32,128]{2,1,0:T(8,128)(2,1)S(1)} %shard_map.90.refs_0_), channel_id=1, source_target_pairs={{0,24},{4,28},{8,16},{12,20},{16,8},{20,12},{24,0},{28,4},{1,25},{... | collective-permute-start | bytes 786440 | tf_op jit(solution)/shard_map/ppermute | solution.py:402
  93.7 16.9 %collective-permute-start.18 = (bf16[1,32,32,128]{3,2,1,0:T(8,128)(2,1)S(1)}, bf16[1,32,32,128]{3,2,1,0:T(8,128)(2,1)S(1)}, u32[]{:S(2)}, u32[]{:S(2)}) collective-permute-start(bf16[1,32,32,128]{3,2,1,0:T(8,128)(2,1)S(1)} %shard_map.96.refs_1_.near_ref), channel_id=1, source_target_pairs={{0,2},{1,3},{2,0},{3,1},{4,6},{5,7},{6,4},{7,5},{8,10},{9,11},{10,... | collective-permute-start | bytes 786440 | tf_op jit(solution)/shard_map/ppermute | solution.py:396
  99.3 13.4 %collective-permute-start.19 = (bf16[32,32,128]{2,1,0:T(8,128)(2,1)S(1)}, bf16[32,32,128]{2,1,0:T(8,128)(2,1)S(1)}, u32[]{:S(2)}, u32[]{:S(2)}) collective-permute-start(bf16[32,32,128]{2,1,0:T(8,128)(2,1)S(1)} %shard_map.91.refs_0_), channel_id=1, source_target_pairs={{0,8},{4,12},{8,0},{12,4},{16,24},{20,28},{24,16},{28,20},{1,9},{5... | collective-permute-start | bytes 786440 | tf_op jit(solution)/shard_map/ppermute | solution.py:402
  99.3 13.3 %collective-permute-start.20 = (bf16[32,32,128]{2,1,0:T(8,128)(2,1)S(1)}, bf16[32,32,128]{2,1,0:T(8,128)(2,1)S(1)}, u32[]{:S(2)}, u32[]{:S(2)}) collective-permute-start(bf16[32,32,128]{2,1,0:T(8,128)(2,1)S(1)} %shard_map.92.refs_0_), channel_id=1, source_target_pairs={{0,20},{4,16},{8,28},{12,24},{16,4},{20,0},{24,12},{28,8},{1,21},{... | collective-permute-start | bytes 786440 | tf_op jit(solution)/shard_map/ppermute | solution.py:402
  104.9 12.1 %collective-permute-start.17 = (bf16[1,32,32,128]{3,2,1,0:T(8,128)(2,1)S(1)}, bf16[1,32,32,128]{3,2,1,0:T(8,128)(2,1)S(1)}, u32[]{:S(2)}, u32[]{:S(2)}) collective-permute-start(bf16[1,32,32,128]{3,2,1,0:T(8,128)(2,1)S(1)} %shard_map.97.near_ref), channel_id=1, source_target_pairs={{0,2},{1,3},{2,0},{3,1},{4,6},{5,7},{6,4},{7,5},{8,10},{9,11},{10,... | collective-permute-start | bytes 786440 | tf_op jit(solution)/shard_map/ppermute | solution.py:396
  106.4 17.6 %collective-permute-start.16 = (bf16[32,32,128]{2,1,0:T(8,128)(2,1)S(1)}, bf16[32,32,128]{2,1,0:T(8,128)(2,1)S(1)}, u32[]{:S(2)}, u32[]{:S(2)}) collective-permute-start(bf16[32,32,128]{2,1,0:T(8,128)(2,1)S(1)} %shard_map.93.refs_0_), channel_id=1, source_target_pairs={{0,12},{4,8},{8,4},{12,0},{16,28},{20,24},{24,20},{28,16},{1,13},{... | collective-permute-start | bytes 786440 | tf_op jit(solution)/shard_map/ppermute | solution.py:402
  109.0 5.8 %copy-start.4 = (bf16[512,256]{1,0:T(8,128)(2,1)S(1)}, bf16[512,256]{1,0:T(8,128)(2,1)}, u32[]{:S(2)}) copy-start(bf16[512,256]{1,0:T(8,128)(2,1)} %orbitals.5) | copy-start | bytes 786436
  109.0 5.8 %copy-start.18 = (s32[512]{0:T(512)S(1)}, s32[512]{0:T(512)}, u32[]{:S(2)}) copy-start(s32[512]{0:T(512)} %row.1) | copy-start | bytes 6148
  109.0 5.8 %copy-start.19 = (s32[8]{0:T(128)S(1)}, s32[8]{0:T(128)}, u32[]{:S(2)}) copy-start(s32[8]{0:T(128)} %count.1) | copy-start | bytes 100
  110.5 13.5 %collective-permute-start.15 = (bf16[32,32,128]{2,1,0:T(8,128)(2,1)S(1)}, bf16[32,32,128]{2,1,0:T(8,128)(2,1)S(1)}, u32[]{:S(2)}, u32[]{:S(2)}) collective-permute-start(bf16[32,32,128]{2,1,0:T(8,128)(2,1)S(1)} %shard_map.94.refs_0_), channel_id=1, source_target_pairs={{0,16},{4,20},{8,24},{12,28},{16,0},{20,4},{24,8},{28,12},{1,17},{... | collective-permute-start | bytes 786440 | tf_op jit(solution)/shard_map/ppermute | solution.py:402
  113.6 10.4 %collective-permute-start.21 = (bf16[32,32,128]{2,1,0:T(8,128)(2,1)S(1)}, bf16[32,32,128]{2,1,0:T(8,128)(2,1)S(1)}, u32[]{:S(2)}, u32[]{:S(2)}) collective-permute-start(bf16[32,32,128]{2,1,0:T(8,128)(2,1)S(1)} %shard_map.98.refs_0_), channel_id=1, source_target_pairs={{0,4},{4,0},{8,12},{12,8},{16,20},{20,16},{24,28},{28,24},{1,5},{5... | collective-permute-start | bytes 786440 | tf_op jit(solution)/shard_map/ppermute | solution.py:402
  124.8 2.7 %collective-permute-start.22 = (bf16[32,64,256]{2,1,0:T(8,128)(2,1)S(1)}, bf16[32,64,256]{2,1,0:T(8,128)(2,1)S(1)}, u32[]{:S(2)}, u32[]{:S(2)}) collective-permute-start(bf16[32,64,256]{2,1,0:T(8,128)(2,1)S(1)} %get-tuple-element.30), channel_id=1, source_target_pairs={{0,1},{1,0},{2,3},{3,2},{4,5},{5,4},{6,7},{7,6},{8,9},{9,8},{10,11... | collective-permute-start | bytes 3145736 | tf_op jit(solution)/shard_map/ppermute | solution.py:407
